TPU v7x, 32 devices: a whole 2x2x4 slice. The times are simulated.
32 devices in a mesh: grp: 2 (over y), ep: 8 (over z, x), tp: 2 (over core).
Axes of the slice: x: 2, y: 2, z: 4, core: 2. Of those that a mesh axis runs over, the one named last changes fastest.
Arguments:
- residual: bfloat16 [128, 7168], P(('grp', 'ep')), parts along dimension 0, may hold values from -12 to 12
- queries: bfloat16 [128, 16384], P(('grp', 'ep'), 'tp'), parts along dimension 0, may hold values from -8 to 8
- new_kv: bfloat16 [128, 512], P(('grp', 'ep')), parts along dimension 0, may hold values from -4 to 4
- cache: bfloat16 [128, 384, 512], P(('grp', 'ep')), parts along dimension 0, may hold values from -8 to 8
- lengths: int32 [128], P(('grp', 'ep')), parts along dimension 0, may hold values from 2 to 384, as said below
- w_out: bfloat16 [16384, 7168], P('tp', 'ep'), may hold values from -0.046875 to 0.046875
- gain: float32 [7168], replicated, may hold values from 0.5 to 1.5
- route_ids: int32 [128, 3], P(('grp', 'ep')), parts along dimension 0, may hold values from 0 to 3, all different within a row; in each aligned block of 8 rows (0 to 7, 8 to 15, ...) at most 8 rows name the same one
- route_weights: float32 [128, 3], P(('grp', 'ep')), parts along dimension 0, may hold values from 0.2 to 1
- w_gate: bfloat16 [7168, 2560], P(None, ('ep', 'tp')), may hold values from -0.0625 to 0.0625
- w_up: bfloat16 [7168, 2560], P(None, ('ep', 'tp')), may hold values from -0.0625 to 0.0625
- w_down: bfloat16 [2560, 7168], P(('ep', 'tp')), may hold values from -0.25 to 0.25
Outputs:
- output: bfloat16 [128, 7168], P(('grp', 'ep'), 'tp'), parts along dimension 0
There are 2 independent parts, one for each index of `grp`. A program takes and returns all parts, laid end to end along the dimension named above; an argument that names none is the same for every part. Nothing has to cross between parts.
Inputs may be any that keep to these rules, and one draw needn't show every extreme that they name: `route_ids`: a row names 3 different experts; in the rows of one device (aligned blocks of 8 rows) no expert is named by more than 8 rows. `lengths`: some row holds exactly 384 cached tokens.
All inputs are finite; a program needn't handle non-finite values.
Results may differ from a plain program's by a relative error of at most 0.006.
Values may be sent and summed in bfloat16 or wider, within the bound.
No kernel may reach another device: no remote copies, remote signals or barrier semaphores. Data moves between devices by JAX's collectives and lax.ppermute only.
A program may use at most 128 MiB of HBM per device.

v0:
```python
import jax
import jax.numpy as jnp
from jax import lax
from jax.sharding import PartitionSpec as P

HD = 256
TOPK = 3
EXPERTS = 4
CAP = 8


def body(
    residual,
    queries,
    new_kv,
    cache,
    lengths,
    w_out,
    gain,
    route_ids,
    route_weights,
    w_gate,
    w_up,
    w_down,
):
    row_count = queries.shape[0]
    head_count = queries.shape[1] // HD
    scaling = HD ** (-0.5)
    query_heads = queries.reshape(row_count, head_count, HD)
    key_rows = cache[:, :, :HD]
    value_rows = cache[:, :, HD:]
    scores = (
        jnp.einsum("rhd,rpd->rhp", query_heads, key_rows, preferred_element_type=jnp.float32)
        * scaling
    )
    usable = jnp.arange(cache.shape[1], dtype=jnp.int32)[None, :] < lengths[:, None]
    scores = jnp.where(usable[:, None, :], scores, -jnp.inf)
    own_score = (
        jnp.einsum("rhd,rd->rh", query_heads, new_kv[:, :HD], preferred_element_type=jnp.float32)
        * scaling
    )
    peak_score = jnp.maximum(jnp.max(scores, axis=2), own_score)
    cache_weight = jnp.exp(scores - peak_score[:, :, None])
    own_weight = jnp.exp(own_score - peak_score)
    denominator = jnp.sum(cache_weight, axis=2) + own_weight
    probabilities = (cache_weight / denominator[:, :, None]).astype(jnp.bfloat16)
    own_prob = (own_weight / denominator).astype(jnp.bfloat16)
    context = jnp.einsum(
        "rhp,rpd->rhd", probabilities, value_rows, preferred_element_type=jnp.float32
    )
    context = context + own_prob.astype(jnp.float32)[:, :, None] * new_kv[:, None, HD:].astype(
        jnp.float32
    )
    context = context.astype(jnp.bfloat16).reshape(row_count, head_count * HD)
    attn_cols = jnp.dot(
        lax.all_gather(context, "ep", axis=0, tiled=True), w_out, preferred_element_type=jnp.float32
    )
    attn_rows = lax.all_to_all(attn_cols, "ep", split_axis=0, concat_axis=1, tiled=True)
    attention = lax.psum(attn_rows, "tp")
    stream = residual.astype(jnp.float32) + attention
    mean_square = jnp.mean(stream * stream, axis=1, keepdims=True)
    normed = (stream * lax.rsqrt(mean_square + 1e-06) * gain[None, :]).astype(jnp.bfloat16)
    width = normed.shape[1]
    ep_size = lax.axis_size("ep")
    members = ep_size // EXPERTS
    slot_count = EXPERTS * CAP
    flat_ids = route_ids.reshape(-1)
    one_hot = (flat_ids[:, None] == jnp.arange(EXPERTS, dtype=jnp.int32)[None, :]).astype(jnp.int32)
    earlier = jnp.cumsum(one_hot, axis=0) - one_hot
    slot_index = jnp.sum(earlier * one_hot, axis=1)
    target = (flat_ids * CAP + slot_index).reshape(row_count, TOPK)
    placed = (target[:, :, None] == jnp.arange(slot_count, dtype=jnp.int32)[None, None, :]).astype(
        jnp.float32
    )
    chosen = jnp.sum(placed, axis=1).reshape(row_count, EXPERTS, CAP).astype(jnp.bfloat16)
    mixing = jnp.sum(placed * route_weights[:, :, None], axis=1).reshape(row_count, EXPERTS, CAP)
    outgoing = jnp.einsum("rec,rd->ecd", chosen, normed, preferred_element_type=jnp.float32).astype(
        jnp.bfloat16
    )
    outgoing = jnp.broadcast_to(outgoing[:, None], (EXPERTS, members, CAP, width)).reshape(
        ep_size * CAP, width
    )
    arrived = lax.all_to_all(outgoing, "ep", split_axis=0, concat_axis=0, tiled=True)
    gate_act = jnp.dot(arrived, w_gate, preferred_element_type=jnp.float32)
    up_act = jnp.dot(arrived, w_up, preferred_element_type=jnp.float32)
    hidden = (jax.nn.silu(gate_act) * up_act).astype(jnp.bfloat16)
    partial_value = jnp.dot(hidden, w_down, preferred_element_type=jnp.float32)
    halves = lax.psum_scatter(partial_value, "tp", scatter_dimension=1, tiled=True)
    returned = lax.all_to_all(halves, "ep", split_axis=0, concat_axis=0, tiled=True)
    returned = returned.reshape(EXPERTS, members, CAP, returned.shape[1])
    mixed = jnp.einsum("rec,egcw->rw", mixing, returned, precision=lax.Precision.HIGHEST)
    tp_start = lax.axis_index("tp") * mixed.shape[1]
    stream_part = lax.dynamic_slice_in_dim(stream, tp_start, mixed.shape[1], 1)
    return (stream_part + mixed).astype(jnp.bfloat16)


def solution(mesh):
    placed = (
        P(("grp", "ep"), None),
        P(("grp", "ep"), "tp"),
        P(("grp", "ep"), None),
        P(("grp", "ep"), None, None),
        P(("grp", "ep")),
        P("tp", "ep"),
        P(),
        P(("grp", "ep"), None),
        P(("grp", "ep"), None),
        P(None, ("ep", "tp")),
        P(None, ("ep", "tp")),
        P(("ep", "tp"), None),
    )
    return jax.shard_map(
        body, mesh=mesh, in_specs=placed, out_specs=P(("grp", "ep"), "tp"), check_vma=False
    )
```

profile of v0, /device:TPU:0, one launch (start us, length us, event | category | flops | bytes accessed | tf_op | source)
XLA Modules:
  0.0 176.8 jit_solution(8321067404957458068)
XLA Ops:
  6.5 0.0 copy-start
  6.5 0.0 all-gather.2.cloned.1.call-start
  6.5 0.9 iota_compare_fusion.2
  7.4 0.7 slice_convert_fusion
  8.1 1.0 fusion.30
  9.2 2.1 %fusion.50 = (f32[8,32]{1,0:T(8,128)S(1)}, f32[8,32,384]{2,1,0:T(8,128)S(1)}) fusion(bf16[8,384,512]{2,1,0:T(8,128)(2,1)} %param.15, bf16[8,32,256]{2,0,1:T(8,128)(2,1)} %bitcast.48, pred[8,384]{1,0:T(8,128)(4,1)S(1)} %iota_compare_fusion.2), kind=kOutput, calls=%fused_computation.61 | convolution fusion | flops 50626304 | bytes 2101248 | tf_op jit(solution)/shard_map/rhd,rpd->rhp/dot_general | solution.py:33
  11.3 0.2 fusion.27
  11.5 1.8 %fusion.18 = bf16[1,8,32,256]{3,2,1,0:T(8,128)(2,1)S(1)} fusion(bf16[8,384,512]{2,1,0:T(8,128)(2,1)} %param.15, f32[8,32,384]{2,1,0:T(8,128)S(1)} %get-tuple-element.14, f32[8,32]{1,0:T(8,128)S(1)} %get-tuple-element.10, f32[8,32]{1,0:T(8,128)S(1)} %multiply_maximum_fusion, f32[8,256]{1,0:T(8,128)S(1)} %get-tuple-element.11, f32[8,32]{1,0:T(8,128)S(1)} %get-tuple-element.9), kind=kOutput, calls=%fused_computation.13 | convolution fusion | flops 50823168 | bytes 2108416 | tf_op jit(solution)/shard_map/rhp,rpd->rhd/dot_general | solution.py:48
  13.4 0.7 copy.31
  14.1 0.0 all-gather.2.cloned.1.call-update
  14.1 0.0 copy-start.5
  14.1 0.0 copy-start.6
  14.2 0.0 copy-start.3
  14.2 0.0 copy-start.4
  14.2 43.0 %all-gather.2.cloned.1.call-done = bf16[64,8192]{1,0:T(8,128)(2,1)} async-done(((bf16[8,8192]{1,0:T(8,128)(2,1)}), bf16[64,8192]{1,0:T(8,128)(2,1)}) %all-gather.2.cloned.1.call-update) | async-done | bytes 1048592 | tf_op jit(solution)/shard_map/all_gather | solution.py:56
  57.1 8.6 %convolution_bitcast_fusion.1 = f32[8,8,896]{2,1,0:T(8,128)} fusion(bf16[64,8192]{1,0:T(8,128)(2,1)} %all-gather.2.cloned.1.call-done, bf16[8192,896]{1,0:T(8,128)(2,1)} %param.17), kind=kOutput, calls=%fused_computation.11 | convolution fusion | flops 939524096 | bytes 15958016 | tf_op jit(solution)/shard_map/dot_general | solution.py:55
  65.7 3.4 %all-to-all-start = ((f32[8,8,896]{2,1,0:T(8,128)}), f32[8,8,896]{2,1,0:T(8,128)S(1)}, u32[]{:S(2)}, u32[]{:S(2)}) async-start(f32[8,8,896]{2,1,0:T(8,128)} %convolution_bitcast_fusion.1), calls=%async_computation | async-start | bytes 458752 | tf_op jit(solution)/shard_map/all_to_all | solution.py:58
  69.1 0.0 all-reduce.2.cloned.1.call-start
  69.2 0.0 copy-done.5
  69.2 0.1 copy.23
  69.3 0.1 eq.28
  69.4 0.1 fusion.44
  69.5 0.2 select_reduce_fusion.1
  69.7 0.1 reduce_sum.58
  69.8 7.4 %all-to-all-done = f32[8,8,896]{2,1,0:T(8,128)S(1)} async-done(((f32[8,8,896]{2,1,0:T(8,128)}), f32[8,8,896]{2,1,0:T(8,128)S(1)}, u32[]{:S(2)}, u32[]{:S(2)}) %all-to-all-start) | async-done | bytes 229408 | tf_op jit(solution)/shard_map/all_to_all | solution.py:58
  77.1 0.0 copy-start.2
  77.1 0.7 copy-done.2
  77.8 0.0 all-reduce.2.cloned.1.call-update
  77.8 0.0 reduce-scatter.2.cloned.1.call-start
  77.9 0.1 copy.25
  78.0 0.0 copy-done.6
  78.0 0.1 select_reduce_fusion
  78.1 0.1 copy.30
  78.1 16.4 %all-reduce.2.cloned.1.call-done = f32[8,7168]{1,0:T(8,128)} async-done(((f32[8,7168]{1,0:T(8,128)}), f32[8,7168]{1,0:T(8,128)}) %all-reduce.2.cloned.1.call-update) | async-done | bytes 229392 | tf_op jit(solution)/shard_map/psum | solution.py:59
  94.6 0.0 copy-done.3
  94.6 0.0 copy-start.1
  94.6 1.3 multiply_reduce_fusion
  95.9 0.0 copy-done.4
  95.9 0.3 convolution_convert_fusion
  96.2 0.1 broadcast_in_dim.16
  96.3 29.3 %all_to_all.40 = bf16[8,8,7168]{2,1,0:T(8,128)(2,1)S(1)} all-to-all(bf16[8,8,7168]{2,1,0:T(8,128)(2,1)S(1)} %bitcast.41), channel_id=1, replica_groups=mesh['grp'=2,'ep'=8,'tp'=2] {'ep'}, dimensions={0} | all-to-all | bytes 1835008 | tf_op jit(solution)/shard_map/all_to_all | solution.py:83
  125.6 0.0 copy-done.1
  125.6 0.9 fusion.25
  126.5 0.0 copy-done
  126.5 4.7 %fusion.22 = f32[64,7168]{1,0:T(8,128)} fusion(bf16[160,7168]{1,0:T(8,128)(2,1)S(1)} %copy-done, bf16[7168,160]{0,1:T(8,128)(2,1)} %param.22, bf16[8,8,7168]{2,1,0:T(8,128)(2,1)S(1)} %all_to_all.40, f32[64,160]{1,0:T(8,128)S(1)} %fusion.25), kind=kOutput, calls=%fused_computation.16 | convolution fusion | flops 293662720 | bytes 7380992 | tf_op jit(solution)/shard_map/dot_general | solution.py:87
  131.2 0.0 reduce-scatter.2.cloned.1.call-update
  131.2 8.2 %reduce-scatter.2.cloned.1.call-done = f32[64,3584]{1,0:T(8,128)} async-done(((f32[64,7168]{1,0:T(8,128)}), f32[64,3584]{1,0:T(8,128)}) %reduce-scatter.2.cloned.1.call-update) | async-done | bytes 917520 | tf_op jit(solution)/shard_map/reduce_scatter | solution.py:88
  139.4 5.7 %all-to-all-start.2 = ((f32[8,8,3584]{2,1,0:T(8,128)}), f32[8,8,3584]{2,1,0:T(8,128)S(1)}, u32[]{:S(2)}, u32[]{:S(2)}) async-start(f32[8,8,3584]{2,1,0:T(8,128)} %bitcast.42), calls=%async_computation.3 | async-start | bytes 1835008 | tf_op jit(solution)/shard_map/all_to_all | solution.py:89
  145.1 0.1 reshape.67
  145.2 23.4 %all-to-all-done.2 = f32[8,8,3584]{2,1,0:T(8,128)S(1)} async-done(((f32[8,8,3584]{2,1,0:T(8,128)}), f32[8,8,3584]{2,1,0:T(8,128)S(1)}, u32[]{:S(2)}, u32[]{:S(2)}) %all-to-all-start.2) | async-done | bytes 917536 | tf_op jit(solution)/shard_map/all_to_all | solution.py:89
  168.6 1.6 fusion.1
  (6 shorter events, 0.1 us)
Async XLA Ops:
  6.5 120.0 %copy-start = (bf16[160,7168]{1,0:T(8,128)(2,1)S(1)}, bf16[160,7168]{1,0:T(8,128)(2,1)}, u32[]{:S(2)}) copy-start(bf16[160,7168]{1,0:T(8,128)(2,1)} %param.23) | copy-start | bytes 6881284
  6.5 50.6 %all-gather.2.cloned.1.call-start = ((), (), s32[]{:S(2)}) async-start(), calls=%async_computation.4 | async-start | bytes 1179648 | tf_op jit(solution)/shard_map/all_gather | solution.py:56
  14.1 55.1 %copy-start.5 = (s32[8,3]{0,1:T(4,128)S(1)}, s32[8,3]{0,1:T(4,128)}, u32[]{:S(2)}) copy-start(s32[8,3]{0,1:T(4,128)} %param.19) | copy-start | bytes 292
  14.1 63.8 %copy-start.6 = (f32[8,3]{0,1:T(4,128)S(1)}, f32[8,3]{0,1:T(4,128)}, u32[]{:S(2)}) copy-start(f32[8,3]{0,1:T(4,128)} %param.20) | copy-start | bytes 292
  14.2 80.4 %copy-start.3 = (bf16[8,7168]{1,0:T(8,128)(2,1)S(1)}, bf16[8,7168]{1,0:T(8,128)(2,1)}, u32[]{:S(2)}) copy-start(bf16[8,7168]{1,0:T(8,128)(2,1)} %param.12) | copy-start | bytes 344068
  14.2 81.7 %copy-start.4 = (f32[7168]{0:T(1024)S(1)}, f32[7168]{0:T(1024)}, u32[]{:S(2)}) copy-start(f32[7168]{0:T(1024)} %param.18) | copy-start | bytes 86020
  65.7 11.4 %all-to-all-start = ((f32[8,8,896]{2,1,0:T(8,128)}), f32[8,8,896]{2,1,0:T(8,128)S(1)}, u32[]{:S(2)}, u32[]{:S(2)}) async-start(f32[8,8,896]{2,1,0:T(8,128)} %convolution_bitcast_fusion.1), calls=%async_computation | async-start | bytes 458752 | tf_op jit(solution)/shard_map/all_to_all | solution.py:58
  69.1 25.4 %all-reduce.2.cloned.1.call-start = ((), (), s32[]{:S(2)}) async-start(), calls=%async_computation.5 | async-start | bytes 458752 | tf_op jit(solution)/shard_map/psum | solution.py:59
  77.1 0.7 copy-start.2
  77.8 61.6 %reduce-scatter.2.cloned.1.call-start = ((), (), s32[]{:S(2)}) async-start(), calls=%async_computation.6 | async-start | bytes 2752512 | tf_op jit(solution)/shard_map/reduce_scatter | solution.py:88
  94.6 31.0 %copy-start.1 = (bf16[7168,160]{0,1:T(8,128)(2,1)S(1)}, bf16[7168,160]{0,1:T(8,128)(2,1)}, u32[]{:S(2)}) copy-start(bf16[7168,160]{0,1:T(8,128)(2,1)} %param.21) | copy-start | bytes 6881284
  139.4 29.2 %all-to-all-start.2 = ((f32[8,8,3584]{2,1,0:T(8,128)}), f32[8,8,3584]{2,1,0:T(8,128)S(1)}, u32[]{:S(2)}, u32[]{:S(2)}) async-start(f32[8,8,3584]{2,1,0:T(8,128)} %bitcast.42), calls=%async_computation.3 | async-start | bytes 1835008 | tf_op jit(solution)/shard_map/all_to_all | solution.py:89
Sparse Core Ops, SparseCore 0:
  14.2 42.8 all-gather.1
  78.0 16.5 all-reduce.1
  131.3 8.0 reduce-scatter.1
where the time goes:
time: 177 us
  waiting for transfers between devices  98.4 us (56%)
  blocking collectives  29.3 us (17%)
  matrix products  21.1 us (12%)
  between operations  13.2 us (7%)
  starting transfers between devices  9.21 us (5%)
  other arithmetic  3.51 us (2%)
  local copies, waits for them, and re-layouts  2.02 us (1%)
    all_gather x1, waiting for transfers between devices, body(): lax.all_gather(context, 'ep', axis=0, tiled=True)  43 us
    all_to_all x1, blocking collectives, body(): lax.all_to_all(outgoing, 'ep', split_axis=0, concat_axis=0, tiled=True)  29.3 us
    all_to_all x1, waiting for transfers between devices, body(): lax.all_to_all(halves, 'ep', split_axis=0, concat_axis=0, tiled=True)  23.4 us
    psum x1, waiting for transfers between devices, body(): attention = lax.psum(attn_rows, 'tp')  16.4 us
    dot_general x1, matrix products, body(): jnp.dot(lax.all_gather(context, 'ep', axis=0, tiled=True), w_out, preferr...  8.59 us
    reduce_scatter x1, waiting for transfers between devices, body(): lax.psum_scatter(partial_value, 'tp', scatter_dimension=1, tiled=True)  8.19 us
    all_to_all x1, waiting for transfers between devices, body(): lax.all_to_all(attn_cols, 'ep', split_axis=0, concat_axis=1, tiled=True)  7.36 us
    all_to_all x1, starting transfers between devices, body(): lax.all_to_all(halves, 'ep', split_axis=0, concat_axis=0, tiled=True)  5.73 us
  transfers between devices with their start and end apart: 5, of which 5 were waited for; matrix products, arithmetic and copies ran while one was open for 0% of the time, Pallas kernels for 0%

commit v1 on v0

v1 whole, which is shorter than its diff:
```python
import jax
import jax.numpy as jnp
from jax import lax
from jax.sharding import PartitionSpec as P

HD = 256
EXPERTS = 4


def grid_of(ep_size):
    x_size = 1 << ((ep_size.bit_length() - 1) // 3)
    return ep_size // x_size, x_size


def shift_z(arr, step, z_size, x_size):
    pairs = [
        (z * x_size + x, (z + step) % z_size * x_size + x)
        for z in range(z_size)
        for x in range(x_size)
    ]
    return lax.ppermute(arr, "ep", pairs)


def shift_x(arr, step, z_size, x_size):
    pairs = [
        (z * x_size + x, z * x_size + (x + step) % x_size)
        for z in range(z_size)
        for x in range(x_size)
    ]
    return lax.ppermute(arr, "ep", pairs)


def swap(arr):
    return lax.ppermute(arr, "tp", [(0, 1), (1, 0)])


def spread(own, z_size, x_size):
    column = [own]
    for _ in range(1, z_size):
        column.append(shift_z(column[-1], 1, z_size, x_size))
    return [
        [chunk] + [shift_x(chunk, u, z_size, x_size) for u in range(1, x_size)] for chunk in column
    ]


def attend(queries, new_kv, cache, lengths):
    row_count = queries.shape[0]
    head_count = queries.shape[1] // HD
    scaling = HD ** (-0.5)
    query_heads = queries.reshape(row_count, head_count, HD)
    key_rows = cache[:, :, :HD]
    value_rows = cache[:, :, HD:]
    scores = (
        jnp.einsum("rhd,rpd->rhp", query_heads, key_rows, preferred_element_type=jnp.float32)
        * scaling
    )
    usable = jnp.arange(cache.shape[1], dtype=jnp.int32)[None, :] < lengths[:, None]
    scores = jnp.where(usable[:, None, :], scores, -jnp.inf)
    own_score = (
        jnp.einsum("rhd,rd->rh", query_heads, new_kv[:, :HD], preferred_element_type=jnp.float32)
        * scaling
    )
    peak_score = jnp.maximum(jnp.max(scores, axis=2), own_score)
    cache_weight = jnp.exp(scores - peak_score[:, :, None])
    own_weight = jnp.exp(own_score - peak_score)
    denominator = jnp.sum(cache_weight, axis=2) + own_weight
    probabilities = (cache_weight / denominator[:, :, None]).astype(jnp.bfloat16)
    own_prob = (own_weight / denominator).astype(jnp.bfloat16)
    context = jnp.einsum(
        "rhp,rpd->rhd", probabilities, value_rows, preferred_element_type=jnp.float32
    )
    context = context + own_prob.astype(jnp.float32)[:, :, None] * new_kv[:, None, HD:].astype(
        jnp.float32
    )
    return context.astype(jnp.bfloat16).reshape(row_count, head_count * HD)


def body(
    residual,
    queries,
    new_kv,
    cache,
    lengths,
    w_out,
    gain,
    route_ids,
    route_weights,
    w_gate,
    w_up,
    w_down,
):
    ep_size = lax.axis_size("ep")
    z_size, x_size = grid_of(ep_size)
    me = lax.axis_index("ep")
    z_me, x_me = me // x_size, me % x_size
    core = lax.axis_index("tp")
    rows = residual.shape[0]
    width = residual.shape[1]
    cols = w_out.shape[1]
    half = cols // 2

    experts = jnp.arange(EXPERTS, dtype=jnp.int32)
    coefficient = jnp.sum(
        (route_ids[:, :, None] == experts[None, None, :]).astype(jnp.float32)
        * route_weights[:, :, None],
        axis=1,
    )
    mine = lax.dynamic_slice_in_dim(residual.reshape(rows, ep_size, cols), core * half, half, 2)
    residual_cols = lax.all_to_all(mine, "ep", split_axis=1, concat_axis=0, tiled=True)
    residual_cols = residual_cols.reshape(ep_size, rows, half)
    first = lax.all_gather(coefficient, "ep", axis=0, tiled=True)
    weight = lax.dynamic_slice_in_dim(first, me * EXPERTS // ep_size, 1, 1)

    context = attend(queries, new_kv, cache, lengths)
    chunks = spread(context, z_size, x_size)
    gathered = jnp.concatenate([c for line in chunks for c in line], axis=0)
    attn = jnp.dot(gathered, w_out, preferred_element_type=jnp.float32)
    attn = attn.reshape(z_size, x_size, rows, cols)
    z_order = (z_me - jnp.arange(z_size)) % z_size
    x_order = (x_me - jnp.arange(x_size)) % x_size
    attn = jnp.take(jnp.take(attn, z_order, axis=0), x_order, axis=1)
    attn = attn.reshape(ep_size, rows, cols)
    theirs = lax.dynamic_slice_in_dim(attn, (1 - core) * half, half, 2)
    ours = lax.dynamic_slice_in_dim(attn, core * half, half, 2)
    stream_cols = residual_cols.astype(jnp.float32) + (ours + swap(theirs))
    stream_cols = stream_cols.astype(jnp.bfloat16).reshape(ep_size * rows, half)

    blocks = spread(stream_cols, z_size, x_size)
    stream_half = jnp.stack([b for line in blocks for b in line]).reshape(
        z_size, x_size, ep_size * rows, half
    )
    stream_half = jnp.take(jnp.take(stream_half, z_order, axis=0), x_order, axis=1)
    stream_half = stream_half.reshape(ep_size, ep_size * rows, half)
    other_half = swap(stream_half)
    low = jnp.where(core == 0, stream_half, other_half)
    high = jnp.where(core == 0, other_half, stream_half)
    stream = jnp.concatenate([low, high], axis=2).transpose(1, 0, 2).reshape(ep_size * rows, width)
    stream = stream.astype(jnp.float32)
    mean_square = jnp.mean(stream * stream, axis=1, keepdims=True)
    normed = (stream * lax.rsqrt(mean_square + 1e-06) * gain[None, :]).astype(jnp.bfloat16)

    gate_act = jnp.dot(normed, w_gate, preferred_element_type=jnp.float32)
    up_act = jnp.dot(normed, w_up, preferred_element_type=jnp.float32)
    hidden = (jax.nn.silu(gate_act) * up_act).astype(jnp.bfloat16)
    partial_value = weight * jnp.dot(hidden, w_down, preferred_element_type=jnp.float32)
    out_width = width // 2
    ours = lax.dynamic_slice_in_dim(partial_value, core * out_width, out_width, 1)
    theirs = lax.dynamic_slice_in_dim(partial_value, (1 - core) * out_width, out_width, 1)
    mixed = ours + swap(theirs.astype(jnp.bfloat16)).astype(jnp.float32)
    mixed = mixed.reshape(z_size, x_size, rows, out_width)
    total = lax.dynamic_index_in_dim(mixed, x_me, 1, keepdims=False)
    for u in range(1, x_size):
        leaving = lax.dynamic_index_in_dim(mixed, (x_me + u) % x_size, 1, keepdims=False)
        total = total + shift_x(leaving.astype(jnp.bfloat16), u, z_size, x_size).astype(jnp.float32)
    result = lax.dynamic_index_in_dim(total, z_me, 0, keepdims=False)
    for s in range(1, z_size):
        leaving = lax.dynamic_index_in_dim(total, (z_me + s) % z_size, 0, keepdims=False)
        result = result + shift_z(leaving.astype(jnp.bfloat16), s, z_size, x_size).astype(
            jnp.float32
        )
    home = lax.dynamic_slice(stream, (me * rows, core * out_width), (rows, out_width))
    return (home + result).astype(jnp.bfloat16)


def solution(mesh):
    placed = (
        P(("grp", "ep"), None),
        P(("grp", "ep"), "tp"),
        P(("grp", "ep"), None),
        P(("grp", "ep"), None, None),
        P(("grp", "ep")),
        P("tp", "ep"),
        P(),
        P(("grp", "ep"), None),
        P(("grp", "ep"), None),
        P(None, ("ep", "tp")),
        P(None, ("ep", "tp")),
        P(("ep", "tp"), None),
    )
    return jax.shard_map(
        body, mesh=mesh, in_specs=placed, out_specs=P(("grp", "ep"), "tp"), check_vma=False
    )
```

time: 177 us -> 146 us (0.82)
  waiting for transfers between devices: 98.4 us -> 55.1 us
  between operations: 13.2 us -> 0.52 us
  local copies, waits for them, and re-layouts: 2.02 us -> 11.1 us
  blocking collectives: 29.3 us -> 35.3 us
  starting transfers between devices: 9.21 us -> 15 us
  other arithmetic: 3.51 us -> 9.24 us
    ppermute x0 -> x21, waiting for transfers between devices: none -> 55.1 us  [the longest x9 37.2 us: shift_z(): return lax.ppermute(arr, 'ep', pairs)]
    all_gather x1 -> x0, waiting for transfers between devices: 43 us -> none  [body(): lax.all_gather(context, 'ep', axis=0, tiled=True)]
    all_to_all x2 -> x0, waiting for transfers between devices: 30.7 us -> none  [the longest x1 23.4 us: body(): lax.all_to_all(halves, 'ep', split_axis=0, concat_axis=0, tiled=True)]
    all_gather x0 -> x1, blocking collectives: none -> 26 us  [body(): first = lax.all_gather(coefficient, 'ep', axis=0, tiled=True)]
    all_to_all x1, blocking collectives: 29.3 us -> 9.33 us  [body(): lax.all_to_all(mine, 'ep', split_axis=1, concat_axis=0, tiled=True)]
    psum x1 -> x0, waiting for transfers between devices: 16.4 us -> none  [body(): attention = lax.psum(attn_rows, 'tp')]
    ppermute x0 -> x21, starting transfers between devices: none -> 15 us  [the longest x9 9.08 us: shift_x(): return lax.ppermute(arr, 'ep', pairs)]
    all_to_all x2 -> x0, starting transfers between devices: 9.13 us -> none  [the longest x1 5.73 us: body(): lax.all_to_all(halves, 'ep', split_axis=0, concat_axis=0, tiled=True)]
  transfers between devices with their start and end apart: 5 -> 21, of which waited for: 5 -> 12; matrix products, arithmetic and copies ran while one was open for 0% -> 2% of each run, Pallas kernels for 0% -> 0%
where the time goes in v1:
time: 146 us
  waiting for transfers between devices  55.1 us (38%)
  blocking collectives  35.3 us (24%)
  matrix products  19.5 us (13%)
  starting transfers between devices  15 us (10%)
  local copies, waits for them, and re-layouts  11.1 us (8%)
  other arithmetic  9.24 us (6%)
    ppermute x9, waiting for transfers between devices, shift_z(): return lax.ppermute(arr, 'ep', pairs)  37.2 us
    all_gather x1, blocking collectives, body(): first = lax.all_gather(coefficient, 'ep', axis=0, tiled=True)  26 us
    ppermute x9, waiting for transfers between devices, shift_x(): return lax.ppermute(arr, 'ep', pairs)  15.9 us
    all_to_all x1, blocking collectives, body(): lax.all_to_all(mine, 'ep', split_axis=1, concat_axis=0, tiled=True)  9.33 us
    ppermute x9, starting transfers between devices, shift_x(): return lax.ppermute(arr, 'ep', pairs)  9.08 us
    dot_general x1, matrix products, body(): attn = jnp.dot(gathered, w_out, preferred_element_type=jnp.float32)  8.25 us
    ppermute x9, starting transfers between devices, shift_z(): return lax.ppermute(arr, 'ep', pairs)  5.7 us
    dot_general x1, matrix products, body(): jnp.dot(hidden, w_down, preferred_element_type=jnp.float32)  5.29 us
  transfers between devices with their start and end apart: 21, of which 12 were waited for; matrix products, arithmetic and copies ran while one was open for 2% of the time, Pallas kernels for 0%

profile of v1, /device:TPU:0, one launch (start us, length us, event | category | flops | bytes accessed | tf_op | source)
XLA Modules:
  0.0 145.7 jit_solution(13800947019348797082)
XLA Ops:
  0.0 0.9 iota_compare_fusion
  0.9 0.7 slice_convert_fusion
  1.6 1.0 fusion.26
  2.6 2.1 %fusion.55 = (f32[8,32]{1,0:T(8,128)S(1)}, f32[8,32,384]{2,1,0:T(8,128)S(1)}) fusion(bf16[8,384,512]{2,1,0:T(8,128)(2,1)} %param.15, bf16[8,32,256]{2,0,1:T(8,128)(2,1)} %bitcast.109, pred[8,384]{1,0:T(8,128)(4,1)S(1)} %iota_compare_fusion), kind=kOutput, calls=%fused_computation.119 | convolution fusion | flops 50626304 | bytes 2101248 | tf_op jit(solution)/shard_map/rhd,rpd->rhp/dot_general | solution.py:54
  4.8 0.2 fusion.21
  5.0 1.8 %fusion.17 = bf16[1,8,32,256]{3,2,1,0:T(8,128)(2,1)S(1)} fusion(bf16[8,384,512]{2,1,0:T(8,128)(2,1)} %param.15, f32[8,32,384]{2,1,0:T(8,128)S(1)} %get-tuple-element.17, f32[8,32]{1,0:T(8,128)S(1)} %get-tuple-element.13, f32[8,32]{1,0:T(8,128)S(1)} %multiply_maximum_fusion, f32[8,256]{1,0:T(8,128)S(1)} %get-tuple-element.14, f32[8,32]{1,0:T(8,128)S(1)} %get-tuple-element.12), kind=kOutput, calls=%fused_computation.17 | convolution fusion | flops 50823168 | bytes 2108416 | tf_op jit(solution)/shard_map/rhp,rpd->rhd/dot_general | solution.py:69
  6.8 0.1 copy.55
  6.9 3.0 %collective-permute-start = (bf16[8,8192]{1,0:T(8,128)(2,1)S(1)}, bf16[8,8192]{1,0:T(8,128)(2,1)}, u32[]{:S(2)}, u32[]{:S(2)}) collective-permute-start(bf16[8,8192]{1,0:T(8,128)(2,1)S(1)} %bitcast.99), channel_id=1, source_target_pairs={{0,2},{2,0},{4,6},{6,4},{8,10},{10,8},{12,14},{14,12},{1,3},{3,1},... | collective-permute-start | bytes 393224 | tf_op jit(solution)/shard_map/ppermute | solution.py:30
  9.9 1.6 %collective-permute-start.1 = (bf16[8,8192]{1,0:T(8,128)(2,1)S(1)}, bf16[8,8192]{1,0:T(8,128)(2,1)}, u32[]{:S(2)}, u32[]{:S(2)}) collective-permute-start(bf16[8,8192]{1,0:T(8,128)(2,1)S(1)} %bitcast.100), channel_id=1, source_target_pairs={{0,4},{2,6},{4,8},{6,10},{8,12},{10,14},{12,0},{14,2},{1,5},{3,7},... | collective-permute-start | bytes 393224 | tf_op jit(solution)/shard_map/ppermute | solution.py:21
  11.6 0.1 broadcast_in_dim.69
  11.7 5.1 %collective-permute-done.1 = bf16[8,8192]{1,0:T(8,128)(2,1)} collective-permute-done((bf16[8,8192]{1,0:T(8,128)(2,1)S(1)}, bf16[8,8192]{1,0:T(8,128)(2,1)}, u32[]{:S(2)}, u32[]{:S(2)}) %collective-permute-start.1) | collective-permute-done | bytes 131104 | tf_op jit(solution)/shard_map/ppermute | solution.py:21
  16.9 0.5 collective-permute-start.2
  17.4 0.9 constant_dynamic-update-slice_fusion.6
  18.3 0.9 constant_dynamic-update-slice_fusion.5
  19.2 5.1 %collective-permute-done.3 = bf16[8,8192]{1,0:T(8,128)(2,1)S(1)} collective-permute-done((bf16[8,8192]{1,0:T(8,128)(2,1)}, bf16[8,8192]{1,0:T(8,128)(2,1)S(1)}, u32[]{:S(2)}, u32[]{:S(2)}) %collective-permute-start.3) | collective-permute-done | bytes 131104 | tf_op jit(solution)/shard_map/ppermute | solution.py:21
  24.4 1.5 %collective-permute-start.4 = (bf16[8,8192]{1,0:T(8,128)(2,1)S(1)}, bf16[8,8192]{1,0:T(8,128)(2,1)S(1)}, u32[]{:S(2)}, u32[]{:S(2)}) collective-permute-start(bf16[8,8192]{1,0:T(8,128)(2,1)S(1)} %collective-permute-done.3), channel_id=1, source_target_pairs={{0,2},{2,0},{4,6},{6,4},{8,10},{10,8},{12,14},{14,12},{1,3},{3,1},... | collective-permute-start | bytes 393224 | tf_op jit(solution)/shard_map/ppermute | solution.py:30
  25.9 6.7 %collective-permute-done.5 = bf16[8,8192]{1,0:T(8,128)(2,1)S(1)} collective-permute-done((bf16[8,8192]{1,0:T(8,128)(2,1)S(1)}, bf16[8,8192]{1,0:T(8,128)(2,1)S(1)}, u32[]{:S(2)}, u32[]{:S(2)}) %collective-permute-start.5) | collective-permute-done | bytes 131104 | tf_op jit(solution)/shard_map/ppermute | solution.py:21
  32.6 0.5 collective-permute-start.6
  33.2 4.4 %collective-permute-done.6 = bf16[8,8192]{1,0:T(8,128)(2,1)S(1)} collective-permute-done((bf16[8,8192]{1,0:T(8,128)(2,1)S(1)}, bf16[8,8192]{1,0:T(8,128)(2,1)S(1)}, u32[]{:S(2)}, u32[]{:S(2)}) %collective-permute-start.6) | collective-permute-done | bytes 131104 | tf_op jit(solution)/shard_map/ppermute | solution.py:30
  37.6 8.2 %fusion.56 = f32[64,896]{1,0:T(8,128)} fusion(bf16[64,8192]{1,0:T(8,128)(2,1)S(1)} %constant_dynamic-update-slice_fusion, bf16[8192,896]{1,0:T(8,128)(2,1)} %param.17), kind=kOutput, calls=%fused_computation.120 | convolution fusion | flops 939524096 | bytes 15958016 | tf_op jit(solution)/shard_map/dot_general | solution.py:117
  45.9 1.5 %gather_fusion = f32[4,2,8,896]{3,2,1,0:T(8,128)S(1)} fusion(f32[4,2,8,896]{3,2,1,0:T(8,128)} %bitcast.96, s32[1024]{0:T(1024)S(1)} %get-tuple-element.19), kind=kCustom, calls=%fused_computation | custom fusion | bytes 458768 | tf_op jit(solution)/shard_map/jit(_take)/gather | solution.py:121
  47.4 0.1 broadcast_select_fusion.3
  47.5 0.6 gather_fusion.1
  48.1 0.1 bitcast_select_fusion.1
  48.2 0.1 constant_dynamic-slice_fusion.1
  48.4 0.1 constant_dynamic-slice_fusion.2
  48.5 9.3 %all_to_all.4 = bf16[8,8,448]{2,0,1:T(8,128)(2,1)S(1)} all-to-all(bf16[8,8,448]{2,0,1:T(8,128)(2,1)S(1)} %constant_dynamic-slice_fusion.2), channel_id=1, replica_groups=mesh['grp'=2,'ep'=8,'tp'=2] {'ep'}, dimensions={1} | all-to-all | bytes 114688 | tf_op jit(solution)/shard_map/all_to_all | solution.py:109
  57.8 0.1 bitcast_dynamic-update-slice_fusion.7
  57.9 0.2 collective-permute-start.9
  58.2 1.0 collective-permute-start.8
  59.2 4.8 %collective-permute-done.9 = bf16[64,448]{1,0:T(8,128)(2,1)S(1)} collective-permute-done((bf16[64,448]{1,0:T(8,128)(2,1)S(1)}, bf16[64,448]{1,0:T(8,128)(2,1)S(1)}, u32[]{:S(2)}, u32[]{:S(2)}) %collective-permute-start.9) | collective-permute-done | bytes 57376 | tf_op jit(solution)/shard_map/ppermute | solution.py:21
  64.0 0.4 collective-permute-start.10
  64.4 6.0 %collective-permute-done.11 = bf16[64,448]{1,0:T(8,128)(2,1)S(1)} collective-permute-done((bf16[64,448]{1,0:T(8,128)(2,1)S(1)}, bf16[64,448]{1,0:T(8,128)(2,1)S(1)}, u32[]{:S(2)}, u32[]{:S(2)}) %collective-permute-start.11) | collective-permute-done | bytes 57376 | tf_op jit(solution)/shard_map/ppermute | solution.py:21
  70.5 1.6 %collective-permute-start.12 = (bf16[64,448]{1,0:T(8,128)(2,1)S(1)}, bf16[64,448]{1,0:T(8,128)(2,1)S(1)}, u32[]{:S(2)}, u32[]{:S(2)}) collective-permute-start(bf16[64,448]{1,0:T(8,128)(2,1)S(1)} %collective-permute-done.11), channel_id=1, source_target_pairs={{0,2},{2,0},{4,6},{6,4},{8,10},{10,8},{12,14},{14,12},{1,3},{3,1},... | collective-permute-start | bytes 172040 | tf_op jit(solution)/shard_map/ppermute | solution.py:30
  72.2 6.0 %collective-permute-done.13 = bf16[64,448]{1,0:T(8,128)(2,1)S(1)} collective-permute-done((bf16[64,448]{1,0:T(8,128)(2,1)S(1)}, bf16[64,448]{1,0:T(8,128)(2,1)S(1)}, u32[]{:S(2)}, u32[]{:S(2)}) %collective-permute-start.13) | collective-permute-done | bytes 57376 | tf_op jit(solution)/shard_map/ppermute | solution.py:21
  78.2 0.4 collective-permute-start.14
  78.6 3.9 %collective-permute-done.14 = bf16[64,448]{1,0:T(8,128)(2,1)S(1)} collective-permute-done((bf16[64,448]{1,0:T(8,128)(2,1)S(1)}, bf16[64,448]{1,0:T(8,128)(2,1)S(1)}, u32[]{:S(2)}, u32[]{:S(2)}) %collective-permute-start.14) | collective-permute-done | bytes 57376 | tf_op jit(solution)/shard_map/ppermute | solution.py:30
  82.5 0.6 gather_fusion.2
  83.0 0.9 broadcast_select_fusion
  84.0 1.6 %gather_fusion.3 = bf16[2,4,64,448]{3,2,1,0:T(8,128)(2,1)S(1)} fusion(bf16[4,2,64,448]{3,2,1,0:T(8,128)(2,1)} %broadcast_select_fusion, s32[1024]{0:T(1024)S(1)} %get-tuple-element.18), kind=kCustom, calls=%fused_computation.3 | custom fusion | bytes 917512 | tf_op jit(solution)/shard_map/jit(_take)/gather | solution.py:132
  85.7 0.1 bitcast_select_fusion
  85.8 0.1 collective-permute-start.15
  85.9 26.0 %all-gather = f32[8,8,4]{1,2,0:T(4,128)S(1)} all-gather(f32[1,8,4]{1,2,0:T(4,128)S(1)} %bitcast.107), channel_id=1, replica_groups=mesh['grp'=2,'ep'=8,'tp'=2] {'ep'}, dimensions={0}, use_global_device_ids=true | all-gather | bytes 1152 | tf_op jit(solution)/shard_map/all_gather | solution.py:111
  111.9 0.1 reshape.224
  112.0 1.2 broadcast_select_fusion.2
  113.2 0.5 fusion
  113.7 0.3 convert_bitcast_fusion
  114.1 0.1 copy.54
  114.3 1.3 copy-done.1
  115.5 0.9 copy-done.2
  116.4 0.9 fusion.53
  117.3 5.3 %convolution_multiply_fusion = f32[64,7168]{1,0:T(8,128)} fusion(bf16[160,7168]{1,0:T(8,128)(2,1)S(1)} %copy-done, bf16[7168,160]{0,1:T(8,128)(2,1)} %param.22, f32[64]{0:T(128)S(1)} %fusion.51, f32[64,160]{1,0:T(8,128)S(1)} %fusion.53, f32[64,7168]{1,0:T(8,128)} %bitcast.91, f32[7168]{0:T(1024)S(1)} %copy-done.4, f32[64]{0:T(128)S(1)} %add_rsqrt_fusion), kind=kOutput, calls=%fused_computation.4 | convolution fusion | flops 295497728 | bytes 8327680 | tf_op jit(solution)/shard_map/dot_general | solution.py:145
  122.6 1.2 dynamic-slice_convert_fusion
  123.9 0.1 collective-permute-start.16
  123.9 1.9 %collective-permute-done.16 = bf16[64,3584]{1,0:T(8,128)(2,1)} collective-permute-done((bf16[64,3584]{1,0:T(8,128)(2,1)S(1)}, bf16[64,3584]{1,0:T(8,128)(2,1)}, u32[]{:S(2)}, u32[]{:S(2)}) %collective-permute-start.16) | collective-permute-done | bytes 458784 | tf_op jit(solution)/shard_map/ppermute | solution.py:34
  125.9 1.4 convert_add_fusion
  127.5 7.7 %collective-permute-done.17 = bf16[4,8,3584]{2,1,0:T(8,128)(2,1)} collective-permute-done((bf16[4,8,3584]{2,1,0:T(8,128)(2,1)S(1)}, bf16[4,8,3584]{2,1,0:T(8,128)(2,1)}, u32[]{:S(2)}, u32[]{:S(2)}) %collective-permute-start.17) | collective-permute-done | bytes 229408 | tf_op jit(solution)/shard_map/ppermute | solution.py:30
  135.1 1.0 bitcast_add_fusion
  136.1 0.8 copy-done.3
  136.9 0.3 collective-permute-start.18
  137.2 3.6 %collective-permute-start.20 = (bf16[8,3584]{1,0:T(8,128)(2,1)S(1)}, bf16[8,3584]{1,0:T(8,128)(2,1)S(1)}, u32[]{:S(2)}, u32[]{:S(2)}) collective-permute-start(bf16[8,3584]{1,0:T(8,128)(2,1)S(1)} %get-tuple-element.10), channel_id=1, source_target_pairs={{0,12},{2,14},{4,0},{6,2},{8,4},{10,6},{12,8},{14,10},{1,13},{3,15... | collective-permute-start | bytes 172040 | tf_op jit(solution)/shard_map/ppermute | solution.py:21
  140.8 2.5 %collective-permute-done.18 = bf16[8,3584]{1,0:T(8,128)(2,1)S(1)} collective-permute-done((bf16[8,3584]{1,0:T(8,128)(2,1)S(1)}, bf16[8,3584]{1,0:T(8,128)(2,1)S(1)}, u32[]{:S(2)}, u32[]{:S(2)}) %collective-permute-start.18) | collective-permute-done | bytes 57376 | tf_op jit(solution)/shard_map/ppermute | solution.py:21
  143.2 0.9 collective-permute-done.19
  144.1 1.6 %fusion.32 = bf16[8,3584]{1,0:T(8,128)(2,1)} fusion(bf16[8,3584]{1,0:T(8,128)(2,1)S(1)} %collective-permute-done.20, bf16[8,3584]{1,0:T(8,128)(2,1)S(1)} %collective-permute-done.19, bf16[8,3584]{1,0:T(8,128)(2,1)S(1)} %collective-permute-done.18, f32[4,8,3584]{2,1,0:T(8,128)} %copy-done.3, s32[]{:T(128)S(6)} %select_n.202, f32[64,7168]{1,0:T(8,128)} %bitcast.92, ...), kind=kLoop, calls=%fused_computation.45 | loop fusion | flops 229376 | bytes 458764 | tf_op jit(solution)/shard_map/convert_element_type | solution.py:162
  (58 shorter events, 0.5 us)
Async XLA Ops:
  0.0 117.3 %copy-start = (bf16[160,7168]{1,0:T(8,128)(2,1)S(1)}, bf16[160,7168]{1,0:T(8,128)(2,1)}, u32[]{:S(2)}) copy-start(bf16[160,7168]{1,0:T(8,128)(2,1)} %param.23) | copy-start | bytes 6881284
  6.9 10.5 %collective-permute-start = (bf16[8,8192]{1,0:T(8,128)(2,1)S(1)}, bf16[8,8192]{1,0:T(8,128)(2,1)}, u32[]{:S(2)}, u32[]{:S(2)}) collective-permute-start(bf16[8,8192]{1,0:T(8,128)(2,1)S(1)} %bitcast.99), channel_id=1, source_target_pairs={{0,2},{2,0},{4,6},{6,4},{8,10},{10,8},{12,14},{14,12},{1,3},{3,1},... | collective-permute-start | bytes 393224 | tf_op jit(solution)/shard_map/ppermute | solution.py:30
  9.9 6.9 %collective-permute-start.1 = (bf16[8,8192]{1,0:T(8,128)(2,1)S(1)}, bf16[8,8192]{1,0:T(8,128)(2,1)}, u32[]{:S(2)}, u32[]{:S(2)}) collective-permute-start(bf16[8,8192]{1,0:T(8,128)(2,1)S(1)} %bitcast.100), channel_id=1, source_target_pairs={{0,4},{2,6},{4,8},{6,10},{8,12},{10,14},{12,0},{14,2},{1,5},{3,7},... | collective-permute-start | bytes 393224 | tf_op jit(solution)/shard_map/ppermute | solution.py:21
  16.9 9.0 %collective-permute-start.2 = (bf16[8,8192]{1,0:T(8,128)(2,1)}, bf16[8,8192]{1,0:T(8,128)(2,1)S(1)}, u32[]{:S(2)}, u32[]{:S(2)}) collective-permute-start(bf16[8,8192]{1,0:T(8,128)(2,1)} %collective-permute-done.1), channel_id=1, source_target_pairs={{0,2},{2,0},{4,6},{6,4},{8,10},{10,8},{12,14},{14,12},{1,3},{3,1},... | collective-permute-start | bytes 393224 | tf_op jit(solution)/shard_map/ppermute | solution.py:30
  17.4 7.0 %collective-permute-start.3 = (bf16[8,8192]{1,0:T(8,128)(2,1)}, bf16[8,8192]{1,0:T(8,128)(2,1)S(1)}, u32[]{:S(2)}, u32[]{:S(2)}) collective-permute-start(bf16[8,8192]{1,0:T(8,128)(2,1)} %collective-permute-done.1), channel_id=1, source_target_pairs={{0,4},{2,6},{4,8},{6,10},{8,12},{10,14},{12,0},{14,2},{1,5},{3,7},... | collective-permute-start | bytes 393224 | tf_op jit(solution)/shard_map/ppermute | solution.py:21
  24.4 8.8 %collective-permute-start.4 = (bf16[8,8192]{1,0:T(8,128)(2,1)S(1)}, bf16[8,8192]{1,0:T(8,128)(2,1)S(1)}, u32[]{:S(2)}, u32[]{:S(2)}) collective-permute-start(bf16[8,8192]{1,0:T(8,128)(2,1)S(1)} %collective-permute-done.3), channel_id=1, source_target_pairs={{0,2},{2,0},{4,6},{6,4},{8,10},{10,8},{12,14},{14,12},{1,3},{3,1},... | collective-permute-start | bytes 393224 | tf_op jit(solution)/shard_map/ppermute | solution.py:30
  25.9 6.8 %collective-permute-start.5 = (bf16[8,8192]{1,0:T(8,128)(2,1)S(1)}, bf16[8,8192]{1,0:T(8,128)(2,1)S(1)}, u32[]{:S(2)}, u32[]{:S(2)}) collective-permute-start(bf16[8,8192]{1,0:T(8,128)(2,1)S(1)} %collective-permute-done.3), channel_id=1, source_target_pairs={{0,4},{2,6},{4,8},{6,10},{8,12},{10,14},{12,0},{14,2},{1,5},{3,7},... | collective-permute-start | bytes 393224 | tf_op jit(solution)/shard_map/ppermute | solution.py:21
  32.6 5.0 %collective-permute-start.6 = (bf16[8,8192]{1,0:T(8,128)(2,1)S(1)}, bf16[8,8192]{1,0:T(8,128)(2,1)S(1)}, u32[]{:S(2)}, u32[]{:S(2)}) collective-permute-start(bf16[8,8192]{1,0:T(8,128)(2,1)S(1)} %collective-permute-done.5), channel_id=1, source_target_pairs={{0,2},{2,0},{4,6},{6,4},{8,10},{10,8},{12,14},{14,12},{1,3},{3,1},... | collective-permute-start | bytes 393224 | tf_op jit(solution)/shard_map/ppermute | solution.py:30
  45.9 2.5 %copy-start.5 = (bf16[8,7168]{1,0:T(8,128)(2,1)S(1)}, bf16[8,7168]{1,0:T(8,128)(2,1)}, u32[]{:S(2)}) copy-start(bf16[8,7168]{1,0:T(8,128)(2,1)} %param.12) | copy-start | bytes 344068
  48.3 9.5 %collective-permute-start.7 = (f32[8,8,448]{2,1,0:T(8,128)S(1)}, f32[8,8,448]{2,1,0:T(8,128)S(1)}, u32[]{:S(2)}, u32[]{:S(2)}) collective-permute-start(f32[8,8,448]{2,1,0:T(8,128)S(1)} %constant_dynamic-slice_fusion.1), channel_id=1, source_target_pairs={{0,1},{1,0},{2,3},{3,2},{4,5},{5,4},{6,7},{7,6},{8,9},{9,8},{10,11... | collective-permute-start | bytes 344072 | tf_op jit(solution)/shard_map/ppermute | solution.py:34
  57.9 6.1 %collective-permute-start.9 = (bf16[64,448]{1,0:T(8,128)(2,1)S(1)}, bf16[64,448]{1,0:T(8,128)(2,1)S(1)}, u32[]{:S(2)}, u32[]{:S(2)}) collective-permute-start(bf16[64,448]{1,0:T(8,128)(2,1)S(1)} %bitcast.102), channel_id=1, source_target_pairs={{0,4},{2,6},{4,8},{6,10},{8,12},{10,14},{12,0},{14,2},{1,5},{3,7},... | collective-permute-start | bytes 172040 | tf_op jit(solution)/shard_map/ppermute | solution.py:21
  58.2 6.3 %collective-permute-start.8 = (bf16[64,448]{1,0:T(8,128)(2,1)S(1)}, bf16[64,448]{1,0:T(8,128)(2,1)S(1)}, u32[]{:S(2)}, u32[]{:S(2)}) collective-permute-start(bf16[64,448]{1,0:T(8,128)(2,1)S(1)} %bitcast.103), channel_id=1, source_target_pairs={{0,2},{2,0},{4,6},{6,4},{8,10},{10,8},{12,14},{14,12},{1,3},{3,1},... | collective-permute-start | bytes 172040 | tf_op jit(solution)/shard_map/ppermute | solution.py:30
  64.0 8.1 %collective-permute-start.10 = (bf16[64,448]{1,0:T(8,128)(2,1)S(1)}, bf16[64,448]{1,0:T(8,128)(2,1)S(1)}, u32[]{:S(2)}, u32[]{:S(2)}) collective-permute-start(bf16[64,448]{1,0:T(8,128)(2,1)S(1)} %collective-permute-done.9), channel_id=1, source_target_pairs={{0,2},{2,0},{4,6},{6,4},{8,10},{10,8},{12,14},{14,12},{1,3},{3,1},... | collective-permute-start | bytes 172040 | tf_op jit(solution)/shard_map/ppermute | solution.py:30
  64.4 6.1 %collective-permute-start.11 = (bf16[64,448]{1,0:T(8,128)(2,1)S(1)}, bf16[64,448]{1,0:T(8,128)(2,1)S(1)}, u32[]{:S(2)}, u32[]{:S(2)}) collective-permute-start(bf16[64,448]{1,0:T(8,128)(2,1)S(1)} %collective-permute-done.9), channel_id=1, source_target_pairs={{0,4},{2,6},{4,8},{6,10},{8,12},{10,14},{12,0},{14,2},{1,5},{3,7},... | collective-permute-start | bytes 172040 | tf_op jit(solution)/shard_map/ppermute | solution.py:21
  70.5 8.1 %collective-permute-start.12 = (bf16[64,448]{1,0:T(8,128)(2,1)S(1)}, bf16[64,448]{1,0:T(8,128)(2,1)S(1)}, u32[]{:S(2)}, u32[]{:S(2)}) collective-permute-start(bf16[64,448]{1,0:T(8,128)(2,1)S(1)} %collective-permute-done.11), channel_id=1, source_target_pairs={{0,2},{2,0},{4,6},{6,4},{8,10},{10,8},{12,14},{14,12},{1,3},{3,1},... | collective-permute-start | bytes 172040 | tf_op jit(solution)/shard_map/ppermute | solution.py:30
  72.1 6.1 %collective-permute-start.13 = (bf16[64,448]{1,0:T(8,128)(2,1)S(1)}, bf16[64,448]{1,0:T(8,128)(2,1)S(1)}, u32[]{:S(2)}, u32[]{:S(2)}) collective-permute-start(bf16[64,448]{1,0:T(8,128)(2,1)S(1)} %collective-permute-done.11), channel_id=1, source_target_pairs={{0,4},{2,6},{4,8},{6,10},{8,12},{10,14},{12,0},{14,2},{1,5},{3,7},... | collective-permute-start | bytes 172040 | tf_op jit(solution)/shard_map/ppermute | solution.py:21
  78.2 4.3 %collective-permute-start.14 = (bf16[64,448]{1,0:T(8,128)(2,1)S(1)}, bf16[64,448]{1,0:T(8,128)(2,1)S(1)}, u32[]{:S(2)}, u32[]{:S(2)}) collective-permute-start(bf16[64,448]{1,0:T(8,128)(2,1)S(1)} %collective-permute-done.13), channel_id=1, source_target_pairs={{0,2},{2,0},{4,6},{6,4},{8,10},{10,8},{12,14},{14,12},{1,3},{3,1},... | collective-permute-start | bytes 172040 | tf_op jit(solution)/shard_map/ppermute | solution.py:30
  84.0 1.9 %copy-start.6 = (f32[8,3]{0,1:T(4,128)S(1)}, f32[8,3]{0,1:T(4,128)}, u32[]{:S(2)}) copy-start(f32[8,3]{0,1:T(4,128)} %param.20) | copy-start | bytes 292
  84.0 1.9 %copy-start.7 = (s32[8,3]{0,1:T(4,128)S(1)}, s32[8,3]{0,1:T(4,128)}, u32[]{:S(2)}) copy-start(s32[8,3]{0,1:T(4,128)} %param.19) | copy-start | bytes 292
  85.8 26.2 %collective-permute-start.15 = (bf16[8,64,448]{2,1,0:T(8,128)(2,1)S(1)}, bf16[8,64,448]{2,1,0:T(8,128)(2,1)}, u32[]{:S(2)}, u32[]{:S(2)}) collective-permute-start(bf16[8,64,448]{2,1,0:T(8,128)(2,1)S(1)} %bitcast_select_fusion), channel_id=1, source_target_pairs={{0,1},{1,0},{2,3},{3,2},{4,5},{5,4},{6,7},{7,6},{8,9},{9,8},{10,11... | collective-permute-start | bytes 1376264 | tf_op jit(solution)/shard_map/ppermute | solution.py:34
  114.1 2.3 %copy-start.2 = (bf16[7168,160]{0,1:T(8,128)(2,1)S(1)}, bf16[7168,160]{0,1:T(8,128)(2,1)}, u32[]{:S(2)}) copy-start(bf16[7168,160]{0,1:T(8,128)(2,1)} %param.21) | copy-start | bytes 6881284
  114.1 2.3 %copy-start.4 = (f32[7168]{0:T(1024)S(1)}, f32[7168]{0:T(1024)}, u32[]{:S(2)}) copy-start(f32[7168]{0:T(1024)} %param.18) | copy-start | bytes 86020
  114.3 1.3 copy-start.1
  123.9 2.0 %collective-permute-start.16 = (bf16[64,3584]{1,0:T(8,128)(2,1)S(1)}, bf16[64,3584]{1,0:T(8,128)(2,1)}, u32[]{:S(2)}, u32[]{:S(2)}) collective-permute-start(bf16[64,3584]{1,0:T(8,128)(2,1)S(1)} %dynamic-slice_convert_fusion), channel_id=1, source_target_pairs={{0,1},{1,0},{2,3},{3,2},{4,5},{5,4},{6,7},{7,6},{8,9},{9,8},{10,11... | collective-permute-start | bytes 1376264 | tf_op jit(solution)/shard_map/ppermute | solution.py:34
  127.3 7.8 %collective-permute-start.17 = (bf16[4,8,3584]{2,1,0:T(8,128)(2,1)S(1)}, bf16[4,8,3584]{2,1,0:T(8,128)(2,1)}, u32[]{:S(2)}, u32[]{:S(2)}) collective-permute-start(bf16[4,8,3584]{2,1,0:T(8,128)(2,1)S(1)} %fusion.22), channel_id=1, source_target_pairs={{0,2},{2,0},{4,6},{6,4},{8,10},{10,8},{12,14},{14,12},{1,3},{3,1},... | collective-permute-start | bytes 688136 | tf_op jit(solution)/shard_map/ppermute | solution.py:30
  136.1 0.8 copy-start.3
  136.9 6.3 %collective-permute-start.18 = (bf16[8,3584]{1,0:T(8,128)(2,1)S(1)}, bf16[8,3584]{1,0:T(8,128)(2,1)S(1)}, u32[]{:S(2)}, u32[]{:S(2)}) collective-permute-start(bf16[8,3584]{1,0:T(8,128)(2,1)S(1)} %get-tuple-element.9), channel_id=1, source_target_pairs={{0,4},{2,6},{4,8},{6,10},{8,12},{10,14},{12,0},{14,2},{1,5},{3,7},... | collective-permute-start | bytes 172040 | tf_op jit(solution)/shard_map/ppermute | solution.py:21
  137.2 6.9 %collective-permute-start.19 = (bf16[8,3584]{1,0:T(8,128)(2,1)S(1)}, bf16[8,3584]{1,0:T(8,128)(2,1)S(1)}, u32[]{:S(2)}, u32[]{:S(2)}) collective-permute-start(bf16[8,3584]{1,0:T(8,128)(2,1)S(1)} %get-tuple-element.11), channel_id=1, source_target_pairs={{0,8},{2,10},{4,12},{6,14},{8,0},{10,2},{12,4},{14,6},{1,9},{3,11}... | collective-permute-start | bytes 172040 | tf_op jit(solution)/shard_map/ppermute | solution.py:21
  137.2 6.9 %collective-permute-start.20 = (bf16[8,3584]{1,0:T(8,128)(2,1)S(1)}, bf16[8,3584]{1,0:T(8,128)(2,1)S(1)}, u32[]{:S(2)}, u32[]{:S(2)}) collective-permute-start(bf16[8,3584]{1,0:T(8,128)(2,1)S(1)} %get-tuple-element.10), channel_id=1, source_target_pairs={{0,12},{2,14},{4,0},{6,2},{8,4},{10,6},{12,8},{14,10},{1,13},{3,15... | collective-permute-start | bytes 172040 | tf_op jit(solution)/shard_map/ppermute | solution.py:21

commit v2 on v0

--- a/solution.py
+++ b/solution.py
@@ -1,15 +1,450 @@
+import functools
+
 import jax
 import jax.numpy as jnp
 from jax import lax
+from jax.experimental import pallas as pl
+from jax.experimental.pallas import tpu as pltpu
 from jax.sharding import PartitionSpec as P
 
 HD = 256
 TOPK = 3
 EXPERTS = 4
 CAP = 8
-
-
-def body(
+LANES = 128
+VMEM_BYTES = 48 * 1024 * 1024
+
+
+def params():
+    return pltpu.CompilerParams(vmem_limit_bytes=VMEM_BYTES)
+
+
+def vmem():
+    return pl.BlockSpec(memory_space=pltpu.VMEM)
+
+
+def shape_of(shape, dtype):
+    return jax.ShapeDtypeStruct(shape, dtype)
+
+
+class Grid:
+    def __init__(self, ep_size, x_size):
+        self.ep, self.x, self.z = ep_size, x_size, ep_size // x_size
+        self.steps = [(s, u) for s in range(self.z) for u in range(x_size)]
+
+    def send(self, arr, s, u):
+        pairs = [
+            (z * self.x + x, (z + s) % self.z * self.x + (x + u) % self.x)
+            for z in range(self.z)
+            for x in range(self.x)
+        ]
+        return lax.ppermute(arr, "ep", pairs)
+
+    def spread(self, own):
+        got = {(0, 0): own}
+        for s in range(1, self.z):
+            got[s, 0] = self.send(own, s, 0)
+        for s in range(self.z):
+            for u in range(1, self.x):
+                got[s, u] = self.send(got[s, 0], 0, u)
+        return [got[step] for step in self.steps]
+
+    def source(self, step):
+        me = lax.axis_index("ep")
+        z = lax.rem(me // self.x - step[0] + self.z, self.z)
+        return z * self.x + lax.rem(lax.rem(me, self.x) - step[1] + self.x, self.x)
+
+    def target(self, step):
+        return self.source((-step[0] % self.z, -step[1] % self.x))
+
+
+def swap(arr):
+    return lax.ppermute(arr, "tp", [(0, 1), (1, 0)])
+
+
+def nt_dot(a, b):
+    return lax.dot_general(a, b, (((1,), (1,)), ((), ())), preferred_element_type=jnp.float32)
+
+
+def attention(grid, piece, cols, queries, new_kv, cache, lengths, residual, route_ids, route_weights):
+    rows, width = queries.shape
+    heads = width // HD
+    ctx = cache.shape[1]
+    tall = rows * heads
+    scaling = HD ** (-0.5)
+
+    def kernel(len_ref, q_ref, kv_ref, cache_ref, res_ref, ids_ref, wts_ref, *rest):
+        out_refs, msg_refs = rest[:2], rest[2 : 2 + grid.ep]
+        kept, score, sems = rest[2 + grid.ep :]
+        copies = [
+            pltpu.make_async_copy(cache_ref.at[r], kept.at[r], sems.at[r]) for r in range(rows)
+        ]
+        for copy in copies:
+            copy.start()
+
+        other = lax.axis_index("tp") * (cols - piece)
+        lane = lax.broadcasted_iota(jnp.int32, (rows, LANES), 1)
+        for i, step in enumerate(grid.steps):
+            to = grid.target(step)
+            begin = pl.multiple_of(to * cols + other, LANES)
+            msg_refs[i][:, :piece] = res_ref[:, pl.ds(begin, piece)]
+            expert = to * EXPERTS // grid.ep
+            weight = jnp.sum(jnp.where(ids_ref[...] == expert, wts_ref[...], 0.0), axis=1, keepdims=True)
+            high = weight.astype(jnp.bfloat16)
+            left = weight - high.astype(jnp.float32)
+            middle = left.astype(jnp.bfloat16)
+            low = (left - middle.astype(jnp.float32)).astype(jnp.bfloat16)
+            tile = jnp.where(
+                lane == 0,
+                high.astype(jnp.float32),
+                jnp.where(
+                    lane == 1,
+                    middle.astype(jnp.float32),
+                    jnp.where(lane == 2, low.astype(jnp.float32), 0.0),
+                ),
+            )
+            msg_refs[i][:, piece:] = tile.astype(jnp.bfloat16)
+
+        q = q_ref[...].astype(jnp.float32)
+        stacked = jnp.concatenate([q[:, h * HD : (h + 1) * HD] for h in range(heads)], axis=0)
+        narrow = stacked.astype(jnp.bfloat16)
+        new_kv_f = kv_ref[...].astype(jnp.float32)
+        new_k = jnp.concatenate([new_kv_f[:, :HD]] * heads, axis=0)
+        new_v = jnp.concatenate([new_kv_f[:, HD:]] * heads, axis=0)
+        own = jnp.sum(stacked * new_k, axis=1, keepdims=True) * scaling
+        row_of = lax.rem(lax.broadcasted_iota(jnp.int32, (tall, 1), 0), rows)
+        row_wide = lax.rem(lax.broadcasted_iota(jnp.int32, (tall, ctx), 0), rows)
+        length = jnp.zeros((tall, 1), jnp.int32)
+        for r in range(rows):
+            length = jnp.where(row_of == r, len_ref[r], length)
+        for r in range(rows):
+            copies[r].wait()
+            part = nt_dot(narrow, kept[r, :, :HD])
+            score[...] = jnp.where(row_wide == r, part, score[...]) if r else part
+        place = lax.broadcasted_iota(jnp.int32, (tall, ctx), 1)
+        scores = jnp.where(place < length, score[...] * scaling, -jnp.inf)
+        peak = jnp.maximum(jnp.max(scores, axis=1, keepdims=True), own)
+        exps = jnp.exp(scores - peak)
+        own_exp = jnp.exp(own - peak)
+        denominator = jnp.sum(exps, axis=1, keepdims=True) + own_exp
+        prob = exps / denominator
+        own_prob = (own_exp / denominator).astype(jnp.bfloat16).astype(jnp.float32)
+        total = own_prob * new_v
+        for r in range(rows):
+            only = jnp.where(row_wide == r, prob, 0.0).astype(jnp.bfloat16)
+            total = total + jnp.dot(only, kept[r, :, HD:], preferred_element_type=jnp.float32)
+        for h in range(heads):
+            part, at = divmod(h, heads // 2)
+            out_refs[part][:, at * HD : (at + 1) * HD] = total[h * rows : (h + 1) * rows].astype(
+                jnp.bfloat16
+            )
+
+    outs = pl.pallas_call(
+        kernel,
+        name="attention",
+        out_shape=[shape_of((rows, width // 2), jnp.bfloat16)] * 2
+        + [shape_of((rows, piece + LANES), jnp.bfloat16)] * grid.ep,
+        in_specs=[pl.BlockSpec(memory_space=pltpu.SMEM), vmem(), vmem(), pl.BlockSpec(memory_space=pl.ANY)]
+        + [vmem()] * 3,
+        out_specs=[vmem()] * (2 + grid.ep),
+        scratch_shapes=[
+            pltpu.VMEM(cache.shape[:2] + (2 * HD,), jnp.bfloat16),
+            pltpu.VMEM((tall, ctx), jnp.float32),
+            pltpu.SemaphoreType.DMA((rows,)),
+        ],
+        compiler_params=params(),
+    )(lengths, queries, new_kv, cache, residual, route_ids, route_weights)
+    return outs[0], outs[1], outs[2:]
+
+
+def project(grid, piece, part, chunks, w_out, before=None, messages=()):
+    rows, depth = chunks[0].shape
+    cols = w_out.shape[1]
+    count = len(chunks)
+    tall = rows * count
+    block = depth // 4
+    last = before is not None
+
+    def kernel(*refs):
+        chunk_refs, rest = refs[:count], refs[count:]
+        w_ref, rest = rest[0], rest[1:]
+        if last:
+            before_ref, message_refs, rest = rest[0], rest[1 : 1 + count], rest[1 + count :]
+            ours_ref, theirs_ref, weight_ref = rest[:3]
+            stacked, total = rest[3:]
+        else:
+            out_ref, stacked, total = rest
+        k = pl.program_id(0)
+
+        @pl.when(k == 0)
+        def _():
+            both = jnp.concatenate([ref[...] for ref in chunk_refs], axis=0)
+            for i in range(depth // block):
+                stacked[i] = both[:, i * block : (i + 1) * block]
+
+        product = jnp.dot(stacked[k], w_ref[...], preferred_element_type=jnp.float32)
+
+        @pl.when(k == 0)
+        def _():
+            total[...] = product + before_ref[...] if last else product
+
+        @pl.when(k > 0)
+        def _():
+            total[...] += product
+
+        @pl.when(k == depth // block - 1)
+        def _():
+            if not last:
+                out_ref[...] = total[...]
+                return
+            core = lax.axis_index("tp")
+            mine = pl.multiple_of(core * (cols - piece), LANES)
+            other = pl.multiple_of((1 - core) * (cols - piece), LANES)
+            for i, step in enumerate(grid.steps):
+                here = pl.ds(pl.multiple_of(grid.source(step) * rows, rows), rows)
+                message = message_refs[i][...].astype(jnp.float32)
+                ours_ref[here, :] = total[i * rows : (i + 1) * rows, pl.ds(mine, piece)] + message[:, :piece]
+                theirs_ref[here, :] = total[i * rows : (i + 1) * rows, pl.ds(other, piece)]
+                weight_ref[here, :] = jnp.broadcast_to(
+                    jnp.sum(message[:, piece:], axis=1, keepdims=True), (rows, LANES)
+                )
+
+    def whole(arr):
+        return pl.BlockSpec(arr.shape, lambda k: (0, 0))
+
+    outs = (
+        [shape_of((tall, piece), jnp.float32)] * 2 + [shape_of((tall, LANES), jnp.float32)]
+        if last
+        else [shape_of((tall, cols), jnp.float32)]
+    )
+    extra = ([before] if last else []) + list(messages)
+    result = pl.pallas_call(
+        kernel,
+        name="project",
+        grid=(depth // block,),
+        out_shape=outs,
+        in_specs=[whole(c) for c in chunks]
+        + [pl.BlockSpec((block, cols), lambda k: (part * (depth // block) + k, 0))]
+        + [whole(e) for e in extra],
+        out_specs=[whole(o) for o in outs],
+        scratch_shapes=[
+            pltpu.VMEM((depth // block, tall, block), jnp.bfloat16),
+            pltpu.VMEM((tall, cols), jnp.float32),
+        ],
+        compiler_params=params(),
+    )(*chunks, w_out, *extra)
+    return result if last else result[0]
+
+
+def pack_weights(grid, piece, cols, gate_t, up_t, w_down):
+    units, width = gate_t.shape
+    out_width = width // 2
+
+    def kernel(gate_ref, up_ref, down_ref, pack_ref, half_ref, sems):
+        other = 1 - lax.axis_index("tp")
+        copies = []
+        for j in range(grid.ep):
+            begin = pl.multiple_of(j * cols + other * (cols - piece), LANES)
+            for i, ref in enumerate((gate_ref, up_ref)):
+                copies.append(
+                    pltpu.make_async_copy(
+                        ref.at[:, pl.ds(begin, piece)],
+                        pack_ref.at[j, pl.ds(i * units, units), :],
+                        sems.at[len(copies)],
+                    )
+                )
+        begin = pl.multiple_of(other * out_width, LANES)
+        copies.append(
+            pltpu.make_async_copy(down_ref.at[:, pl.ds(begin, out_width)], half_ref, sems.at[len(copies)])
+        )
+        for copy in copies:
+            copy.start()
+        for copy in copies:
+            copy.wait()
+
+    anywhere = pl.BlockSpec(memory_space=pl.ANY)
+    return pl.pallas_call(
+        kernel,
+        name="pack_weights",
+        out_shape=[
+            shape_of((grid.ep, 2 * units, piece), jnp.bfloat16),
+            shape_of((units, out_width), jnp.bfloat16),
+        ],
+        in_specs=[anywhere] * 3,
+        out_specs=[anywhere] * 2,
+        scratch_shapes=[pltpu.SemaphoreType.DMA((2 * grid.ep + 1,))],
+        compiler_params=params(),
+    )(gate_t, up_t, w_down)
+
+
+def gate_up(grid, piece, cols, rows, pieces, gain, gate_t, up_t, other):
+    tall = pieces[0].shape[0]
+    units = gate_t.shape[0]
+    slot = -(-units // LANES) * LANES
+    count = grid.ep
+    dup = 2 * piece - cols
+    per_half = count // 2
+
+    def kernel(*refs):
+        piece_refs, rest = refs[:count], refs[count:]
+        gain_ref, gate_ref, up_ref, other_ref, sums_ref, home_ref, held = rest
+        core = lax.axis_index("tp")
+        me = lax.axis_index("ep")
+        fresh = lax.broadcasted_iota(jnp.int32, (tall, piece), 1) >= core * dup
+        square = jnp.zeros((tall, 1), jnp.float32)
+        own_gate = jnp.zeros((tall, units), jnp.float32)
+        own_up = jnp.zeros((tall, units), jnp.float32)
+        far = jnp.zeros((tall, 2 * units), jnp.float32)
+        for i, step in enumerate(grid.steps):
+            j = grid.source(step)
+            lanes = pl.ds(pl.multiple_of(j * cols + core * (cols - piece), LANES), piece)
+            stream = piece_refs[i][...].astype(jnp.float32)
+            held[...] = stream
+            mine = held[pl.ds(pl.multiple_of(me * rows, rows), rows), :]
+            side = lax.rem(j // per_half + core, 2)
+            at = pl.multiple_of(lax.rem(j, per_half) * piece, LANES)
+            home_ref[side, :, pl.ds(at, piece)] = mine.astype(jnp.bfloat16)
+            stream = jnp.where(fresh, stream, 0.0)
+            square = square + jnp.sum(stream * stream, axis=1, keepdims=True)
+            scaled = (stream * gain_ref[:, lanes]).astype(jnp.bfloat16)
+            own_gate = own_gate + nt_dot(scaled, gate_ref[:, lanes])
+            own_up = own_up + nt_dot(scaled, up_ref[:, lanes])
+            far = far + nt_dot(scaled, other_ref[j])
+        sums_ref[0, :, :units] = own_gate
+        sums_ref[1, :, :units] = own_up
+        sums_ref[2, :, :units] = far[:, :units]
+        sums_ref[3, :, :units] = far[:, units:]
+        sums_ref[4] = jnp.broadcast_to(square, (tall, slot))
+
+    return pl.pallas_call(
+        kernel,
+        name="gate_up",
+        out_shape=[
+            shape_of((5, tall, slot), jnp.float32),
+            shape_of((2, rows, per_half * piece), jnp.bfloat16),
+        ],
+        in_specs=[vmem()] * (count + 4),
+        out_specs=[vmem()] * 2,
+        scratch_shapes=[pltpu.VMEM((tall, piece), jnp.float32)],
+        compiler_params=params(),
+    )(*pieces, gain, gate_t, up_t, other)
+
+
+def down(grid, rows, sums, far_sums, weight, w_down, far_down):
+    tall = weight.shape[0]
+    units, width = w_down.shape
+    out_width = width // 2
+    count = grid.ep
+
+    def kernel(sums_ref, far_ref, weight_ref, down_ref, far_down_ref, *rest):
+        out_refs, total, down_half, sem = rest[:count], rest[count], rest[count + 1], rest[count + 2]
+        begin = pl.multiple_of(lax.axis_index("tp") * out_width, LANES)
+        copy = pltpu.make_async_copy(down_ref.at[:, pl.ds(begin, out_width)], down_half, sem)
+        copy.start()
+        square = sums_ref[4][:, :1] + far_ref[4][:, :1]
+        scale = lax.rsqrt(square / width + 1e-06)
+
+        def hidden(a, b):
+            gate = (sums_ref[a][:, :units] + far_ref[b][:, :units]) * scale
+            up = (sums_ref[a + 1][:, :units] + far_ref[b + 1][:, :units]) * scale
+            return (gate / (1.0 + jnp.exp(-gate)) * up).astype(jnp.bfloat16)
+
+        near, far = hidden(0, 2), hidden(2, 0)
+        copy.wait()
+        value = jnp.dot(near, down_half[...], preferred_element_type=jnp.float32)
+        value = value + jnp.dot(far, far_down_ref[...], preferred_element_type=jnp.float32)
+        total[...] = value * weight_ref[:, :1]
+        for i, step in enumerate(grid.steps):
+            there = pl.ds(pl.multiple_of(grid.target(step) * rows, rows), rows)
+            out_refs[i][...] = total[there, :].astype(out_refs[i].dtype)
+
+    return pl.pallas_call(
+        kernel,
+        name="down",
+        out_shape=[
+            shape_of((rows, out_width), jnp.bfloat16 if i else jnp.float32) for i in range(count)
+        ],
+        in_specs=[vmem()] * 3 + [pl.BlockSpec(memory_space=pl.ANY), vmem()],
+        out_specs=[vmem()] * count,
+        scratch_shapes=[
+            pltpu.VMEM((tall, out_width), jnp.float32),
+            pltpu.VMEM((units, out_width), jnp.bfloat16),
+            pltpu.SemaphoreType.DMA(()),
+        ],
+        compiler_params=params(),
+    )(sums, far_sums, weight, w_down, far_down)
+
+
+def finish(piece, cols, near, far, parts):
+    rows, out_width = parts[0].shape
+    dup = 2 * piece - cols
+
+    def kernel(near_ref, far_ref, *rest):
+        part_refs, out_ref = rest[:-1], rest[-1]
+        first = lax.axis_index("tp") == 0
+        for c in range(out_width // cols):
+            span = slice(c * piece, (c + 1) * piece)
+            a = near_ref[:, span].astype(jnp.float32)
+            b = far_ref[:, span].astype(jnp.float32)
+            low = jnp.where(first, a, b)
+            high = jnp.where(first, b, a)[:, dup:]
+            value = jnp.concatenate([low, high], axis=1)
+            for ref in part_refs:
+                value = value + ref[:, c * cols : (c + 1) * cols].astype(jnp.float32)
+            out_ref[:, c * cols : (c + 1) * cols] = value.astype(jnp.bfloat16)
+
+    return pl.pallas_call(
+        kernel,
+        name="finish",
+        out_shape=shape_of((rows, out_width), jnp.bfloat16),
+        in_specs=[vmem()] * (2 + len(parts)),
+        out_specs=vmem(),
+        compiler_params=params(),
+    )(near, far, *parts)
+
+
+def tuned_body(
+    grid,
+    residual,
+    queries,
+    new_kv,
+    cache,
+    lengths,
+    w_out,
+    gain,
+    route_ids,
+    route_weights,
+    w_gate,
+    w_up,
+    w_down,
+):
+    rows, width = residual.shape
+    cols = w_out.shape[1]
+    piece = -(-cols // (2 * LANES)) * LANES
+    first, second, messages = attention(
+        grid, piece, cols, queries, new_kv, cache, lengths, residual, route_ids, route_weights
+    )
+    first_chunks = grid.spread(first)
+    second_chunks = grid.spread(second)
+    arrived = [grid.send(m, s, u) if s or u else m for m, (s, u) in zip(messages, grid.steps)]
+    gate_t, up_t = w_gate.T, w_up.T
+    late = lax.optimization_barrier((gate_t, up_t, w_down, first))
+    packed, down_half = pack_weights(grid, piece, cols, *late[:3])
+    far_weights, far_down = swap(packed), swap(down_half)
+    before = project(grid, piece, 0, first_chunks, w_out)
+    ours, theirs, weight = project(grid, piece, 1, second_chunks, w_out, before, arrived)
+    stream = (ours + swap(theirs)).astype(jnp.bfloat16)
+    pieces = grid.spread(stream)
+    sums, home = gate_up(
+        grid, piece, cols, rows, pieces, gain.reshape(1, width), gate_t, up_t, far_weights
+    )
+    far_home = swap(home[1])
+    parts = down(grid, rows, sums, swap(sums), weight, w_down, far_down)
+    shares = [grid.send(p, s, u) if s or u else p for p, (s, u) in zip(parts, grid.steps)]
+    return finish(piece, cols, home[0], far_home, shares)
+
+
+def general_body(
     residual,
     queries,
     new_kv,
@@ -94,6 +529,13 @@
     return (stream_part + mixed).astype(jnp.bfloat16)
 
 
+def body(*args):
+    ep_size, cols, heads_width = lax.axis_size("ep"), args[5].shape[1], args[5].shape[0]
+    if ep_size == 8 and lax.axis_size("tp") == 2 and cols % LANES == 0 and heads_width % (8 * HD) == 0:
+        return tuned_body(Grid(ep_size, 2), *args)
+    return general_body(*args)
+
+
 def solution(mesh):
     placed = (
         P(("grp", "ep"), None),

time: 177 us -> 111 us (0.63)
  waiting for transfers between devices: 98.4 us -> 33.8 us
  starting transfers between devices: 9.21 us -> 43.7 us
  blocking collectives: 29.3 us -> 0 us
  Pallas kernels: 0 us -> 23.1 us
  matrix products: 21.1 us -> 0 us
  between operations: 13.2 us -> 0.2 us
  local copies, waits for them, and re-layouts: 2.02 us -> 9.85 us
  other arithmetic: 3.51 us -> 0.02 us
    ppermute x0 -> x40, starting transfers between devices: none -> 43.7 us  [the longest x35 43 us: send(): return lax.ppermute(arr, 'ep', pairs)]
    all_gather x1 -> x0, waiting for transfers between devices: 43 us -> none  [body(): lax.all_gather(context, 'ep', axis=0, tiled=True)]
    ppermute x0 -> x40, waiting for transfers between devices: none -> 33.8 us  [the longest x35 30.8 us: send(): return lax.ppermute(arr, 'ep', pairs)]
    all_to_all x2 -> x0, waiting for transfers between devices: 30.7 us -> none  [the longest x1 23.4 us: body(): lax.all_to_all(halves, 'ep', split_axis=0, concat_axis=0, tiled=True)]
    all_to_all x1 -> x0, blocking collectives: 29.3 us -> none  [body(): lax.all_to_all(outgoing, 'ep', split_axis=0, concat_axis=0, tiled=True)]
    pallas_call x0 -> x7, Pallas kernels: none -> 23.1 us  [the longest x2 9.59 us: project(): pl.pallas_call(kernel, name='project', grid=(depth // block,), out_shape=...]
    dot_general x8 -> x0, matrix products: 21.1 us -> none  [the longest x1 8.59 us: body(): jnp.dot(lax.all_gather(context, 'ep', axis=0, tiled=True), w_out, preferr...]
    psum x1 -> x0, waiting for transfers between devices: 16.4 us -> none  [body(): attention = lax.psum(attn_rows, 'tp')]
  transfers between devices with their start and end apart: 5 -> 40, of which waited for: 5 -> 21; matrix products, arithmetic and copies ran while one was open for 0% -> 0% of each run, Pallas kernels for 0% -> 12%
where the time goes in v2:
time: 111 us
  starting transfers between devices  43.7 us (39%)
  waiting for transfers between devices  33.8 us (30%)
  Pallas kernels  23.1 us (21%)
  local copies, waits for them, and re-layouts  9.85 us (9%)
    ppermute x35, starting transfers between devices, send(): return lax.ppermute(arr, 'ep', pairs)  43 us
    ppermute x35, waiting for transfers between devices, send(): return lax.ppermute(arr, 'ep', pairs)  30.8 us
    unnamed x24, local copies, waits for them, and re-layouts  9.84 us
    pallas_call x2, Pallas kernels, project(): pl.pallas_call(kernel, name='project', grid=(depth // block,), out_shape=...  9.59 us
    pallas_call x1, Pallas kernels, attention(): pl.pallas_call(kernel, name='attention', out_shape=[shape_of((rows, width...  6.13 us
    pallas_call x1, Pallas kernels, gate_up(): pl.pallas_call(kernel, name='gate_up', out_shape=[shape_of((5, tall, slot...  3.7 us
    ppermute x5, waiting for transfers between devices, swap(): return lax.ppermute(arr, 'tp', [(0, 1), (1, 0)])  2.95 us
    pallas_call x1, Pallas kernels, pack_weights(): pl.pallas_call(kernel, name='pack_weights', out_shape=[shape_of((grid.ep,...  2.25 us
  transfers between devices with their start and end apart: 40, of which 21 were waited for; matrix products, arithmetic and copies ran while one was open for 0% of the time, Pallas kernels for 12%

profile of v2, /device:TPU:0, one launch (start us, length us, event | category | flops | bytes accessed | tf_op | source)
XLA Modules:
  0.0 110.7 jit_solution(16060969908954768071)
XLA Ops:
  0.0 0.9 copy.13.ids_ref
  0.9 0.8 copy.14.wts_ref
  1.7 1.9 %copy-done.4 = bf16[8,384,512]{2,1,0:T(8,128)(2,1)S(1)} copy-done((bf16[8,384,512]{2,1,0:T(8,128)(2,1)S(1)}, bf16[8,384,512]{2,1,0:T(8,128)(2,1)}, u32[]{:S(2)}) %copy-start.4) | copy-done | bytes 3145752
  3.6 0.9 copy-done.5
  4.5 0.9 copy-done.6
  5.4 0.7 copy-done.8
  6.1 0.7 copy-done.9
  6.7 6.1 %attention.1 = (bf16[8,4096]{1,0:T(8,128)(2,1)S(1)}, bf16[8,4096]{1,0:T(8,128)(2,1)S(1)}, bf16[8,640]{1,0:T(8,128)(2,1)S(1)}, bf16[8,640]{1,0:T(8,128)(2,1)S(1)}...) custom-call(s32[8]{0:T(128)S(1)} %copy-done.9, ...), custom_call_target="tpu_custom_call" | custom-call | tf_op jit(solution)/shard_map/attention/pallas_call | solution.py:142
  12.9 1.6 %copy-done.1 = bf16[7168,160]{0,1:T(8,128)(2,1)S(1)} copy-done((bf16[7168,160]{0,1:T(8,128)(2,1)S(1)}, bf16[7168,160]{0,1:T(8,128)(2,1)}, u32[]{:S(2)}) %copy-start.1) | copy-done | bytes 2293784
  14.5 2.2 %pack_weights.1 = (bf16[8,320,512]{2,1,0:T(8,128)(2,1)}, bf16[160,3584]{1,0:T(8,128)(2,1)S(1)}) custom-call(bf16[160,7168]{1,0:T(8,128)(2,1)S(1)} %bitcast.7, bf16[160,7168]{1,0:T(8,128)(2,1)S(1)} %bitcast.9, bf16[160,7168]{1,0:T(8,128)(2,1)} %down_ref.2), custom_call_target="tpu_custom_call" | custom-call | tf_op jit(solution)/shard_map/pack_weights/pallas_call | solution.py:266
  17.3 4.7 %collective-permute-start.5 = (bf16[8,4096]{1,0:T(8,128)(2,1)S(1)}, bf16[8,4096]{1,0:T(8,128)(2,1)S(1)}, u32[]{:S(2)}, u32[]{:S(2)}) collective-permute-start(bf16[8,4096]{1,0:T(8,128)(2,1)S(1)} %get-tuple-element.33.refs_0_), channel_id=1, source_target_pairs={{0,12},{2,14},{4,0},{6,2},{8,4},{10,6},{12,8},{14,10},{1,13},{3,15... | collective-permute-start | bytes 196616 | tf_op jit(solution)/shard_map/ppermute | solution.py:41
  21.9 1.5 %collective-permute-start.14 = (bf16[8,640]{1,0:T(8,128)(2,1)S(1)}, bf16[8,640]{1,0:T(8,128)(2,1)S(1)}, u32[]{:S(2)}, u32[]{:S(2)}) collective-permute-start(bf16[8,640]{1,0:T(8,128)(2,1)S(1)} %get-tuple-element.36), channel_id=1, source_target_pairs={{0,2},{2,0},{4,6},{6,4},{8,10},{10,8},{12,14},{14,12},{1,3},{3,1},... | collective-permute-start | bytes 30728 | tf_op jit(solution)/shard_map/ppermute | solution.py:41
  23.4 1.0 collective-permute-start.15
  24.4 1.2 %collective-permute-done.14.refs_11_ = bf16[8,640]{1,0:T(8,128)(2,1)S(1)} collective-permute-done((bf16[8,640]{1,0:T(8,128)(2,1)S(1)}, bf16[8,640]{1,0:T(8,128)(2,1)S(1)}, u32[]{:S(2)}, u32[]{:S(2)}) %collective-permute-start.14) | collective-permute-done | bytes 10272 | tf_op jit(solution)/shard_map/ppermute | solution.py:41
  25.6 1.9 %collective-permute-start.16 = (bf16[8,640]{1,0:T(8,128)(2,1)S(1)}, bf16[8,640]{1,0:T(8,128)(2,1)S(1)}, u32[]{:S(2)}, u32[]{:S(2)}) collective-permute-start(bf16[8,640]{1,0:T(8,128)(2,1)S(1)} %get-tuple-element.38), channel_id=1, source_target_pairs={{0,6},{2,4},{4,10},{6,8},{8,14},{10,12},{12,2},{14,0},{1,7},{3,5},... | collective-permute-start | bytes 30728 | tf_op jit(solution)/shard_map/ppermute | solution.py:41
  27.6 1.4 %collective-permute-done.15.refs_12_ = bf16[8,640]{1,0:T(8,128)(2,1)S(1)} collective-permute-done((bf16[8,640]{1,0:T(8,128)(2,1)S(1)}, bf16[8,640]{1,0:T(8,128)(2,1)S(1)}, u32[]{:S(2)}, u32[]{:S(2)}) %collective-permute-start.15) | collective-permute-done | bytes 10272 | tf_op jit(solution)/shard_map/ppermute | solution.py:41
  28.9 1.1 %collective-permute-start.17 = (bf16[8,640]{1,0:T(8,128)(2,1)S(1)}, bf16[8,640]{1,0:T(8,128)(2,1)S(1)}, u32[]{:S(2)}, u32[]{:S(2)}) collective-permute-start(bf16[8,640]{1,0:T(8,128)(2,1)S(1)} %get-tuple-element.39), channel_id=1, source_target_pairs={{0,8},{2,10},{4,12},{6,14},{8,0},{10,2},{12,4},{14,6},{1,9},{3,11}... | collective-permute-start | bytes 30728 | tf_op jit(solution)/shard_map/ppermute | solution.py:41
  30.0 2.0 %collective-permute-done.16.refs_13_ = bf16[8,640]{1,0:T(8,128)(2,1)S(1)} collective-permute-done((bf16[8,640]{1,0:T(8,128)(2,1)S(1)}, bf16[8,640]{1,0:T(8,128)(2,1)S(1)}, u32[]{:S(2)}, u32[]{:S(2)}) %collective-permute-start.16) | collective-permute-done | bytes 10272 | tf_op jit(solution)/shard_map/ppermute | solution.py:41
  32.0 2.0 %collective-permute-start.18 = (bf16[8,640]{1,0:T(8,128)(2,1)S(1)}, bf16[8,640]{1,0:T(8,128)(2,1)S(1)}, u32[]{:S(2)}, u32[]{:S(2)}) collective-permute-start(bf16[8,640]{1,0:T(8,128)(2,1)S(1)} %get-tuple-element.40), channel_id=1, source_target_pairs={{0,10},{2,8},{4,14},{6,12},{8,2},{10,0},{12,6},{14,4},{1,11},{3,9}... | collective-permute-start | bytes 30728 | tf_op jit(solution)/shard_map/ppermute | solution.py:41
  34.0 0.9 collective-permute-start.19
  35.0 2.5 %collective-permute-done.18.refs_15_ = bf16[8,640]{1,0:T(8,128)(2,1)S(1)} collective-permute-done((bf16[8,640]{1,0:T(8,128)(2,1)S(1)}, bf16[8,640]{1,0:T(8,128)(2,1)S(1)}, u32[]{:S(2)}, u32[]{:S(2)}) %collective-permute-start.18) | collective-permute-done | bytes 10272 | tf_op jit(solution)/shard_map/ppermute | solution.py:41
  38.0 2.4 %collective-permute-start.1 = (bf16[8,4096]{1,0:T(8,128)(2,1)S(1)}, bf16[8,4096]{1,0:T(8,128)(2,1)S(1)}, u32[]{:S(2)}, u32[]{:S(2)}) collective-permute-start(bf16[8,4096]{1,0:T(8,128)(2,1)S(1)} %get-tuple-element.33.refs_0_), channel_id=1, source_target_pairs={{0,4},{2,6},{4,8},{6,10},{8,12},{10,14},{12,0},{14,2},{1,5},{3,7},... | collective-permute-start | bytes 196616 | tf_op jit(solution)/shard_map/ppermute | solution.py:41
  40.4 1.7 %collective-permute-done.20.refs_17_ = bf16[8,640]{1,0:T(8,128)(2,1)S(1)} collective-permute-done((bf16[8,640]{1,0:T(8,128)(2,1)S(1)}, bf16[8,640]{1,0:T(8,128)(2,1)S(1)}, u32[]{:S(2)}, u32[]{:S(2)}) %collective-permute-start.20) | collective-permute-done | bytes 10272 | tf_op jit(solution)/shard_map/ppermute | solution.py:41
  42.1 1.5 %collective-permute-start = (bf16[8,4096]{1,0:T(8,128)(2,1)S(1)}, bf16[8,4096]{1,0:T(8,128)(2,1)S(1)}, u32[]{:S(2)}, u32[]{:S(2)}) collective-permute-start(bf16[8,4096]{1,0:T(8,128)(2,1)S(1)} %get-tuple-element.33.refs_0_), channel_id=1, source_target_pairs={{0,2},{2,0},{4,6},{6,4},{8,10},{10,8},{12,14},{14,12},{1,3},{3,1},... | collective-permute-start | bytes 196616 | tf_op jit(solution)/shard_map/ppermute | solution.py:41
  43.6 1.4 %collective-permute-start.12 = (bf16[8,4096]{1,0:T(8,128)(2,1)S(1)}, bf16[8,4096]{1,0:T(8,128)(2,1)S(1)}, u32[]{:S(2)}, u32[]{:S(2)}) collective-permute-start(bf16[8,4096]{1,0:T(8,128)(2,1)S(1)} %get-tuple-element.34.refs_0_), channel_id=1, source_target_pairs={{0,12},{2,14},{4,0},{6,2},{8,4},{10,6},{12,8},{14,10},{1,13},{3,15... | collective-permute-start | bytes 196616 | tf_op jit(solution)/shard_map/ppermute | solution.py:41
  45.1 1.3 %collective-permute-done.refs_1_ = bf16[8,4096]{1,0:T(8,128)(2,1)S(1)} collective-permute-done((bf16[8,4096]{1,0:T(8,128)(2,1)S(1)}, bf16[8,4096]{1,0:T(8,128)(2,1)S(1)}, u32[]{:S(2)}, u32[]{:S(2)}) %collective-permute-start) | collective-permute-done | bytes 65568 | tf_op jit(solution)/shard_map/ppermute | solution.py:41
  46.3 0.6 collective-permute-start.8
  46.9 0.9 collective-permute-done.12.refs_6_
  47.8 1.3 %collective-permute-start.7 = (bf16[8,4096]{1,0:T(8,128)(2,1)S(1)}, bf16[8,4096]{1,0:T(8,128)(2,1)S(1)}, u32[]{:S(2)}, u32[]{:S(2)}) collective-permute-start(bf16[8,4096]{1,0:T(8,128)(2,1)S(1)} %get-tuple-element.34.refs_0_), channel_id=1, source_target_pairs={{0,2},{2,0},{4,6},{6,4},{8,10},{10,8},{12,14},{14,12},{1,3},{3,1},... | collective-permute-start | bytes 196616 | tf_op jit(solution)/shard_map/ppermute | solution.py:41
  49.1 4.1 %collective-permute-done.10.refs_4_ = bf16[8,4096]{1,0:T(8,128)(2,1)S(1)} collective-permute-done((bf16[8,4096]{1,0:T(8,128)(2,1)S(1)}, bf16[8,4096]{1,0:T(8,128)(2,1)S(1)}, u32[]{:S(2)}, u32[]{:S(2)}) %collective-permute-start.10) | collective-permute-done | bytes 65568 | tf_op jit(solution)/shard_map/ppermute | solution.py:41
  53.2 2.0 %collective-permute-start.11 = (bf16[8,4096]{1,0:T(8,128)(2,1)S(1)}, bf16[8,4096]{1,0:T(8,128)(2,1)S(1)}, u32[]{:S(2)}, u32[]{:S(2)}) collective-permute-start(bf16[8,4096]{1,0:T(8,128)(2,1)S(1)} %collective-permute-done.10.refs_4_), channel_id=1, source_target_pairs={{0,2},{2,0},{4,6},{6,4},{8,10},{10,8},{12,14},{14,12},{1,3},{3,1},... | collective-permute-start | bytes 196616 | tf_op jit(solution)/shard_map/ppermute | solution.py:41
  55.3 2.9 %collective-permute-done.13.refs_7_ = bf16[8,4096]{1,0:T(8,128)(2,1)S(1)} collective-permute-done((bf16[8,4096]{1,0:T(8,128)(2,1)S(1)}, bf16[8,4096]{1,0:T(8,128)(2,1)S(1)}, u32[]{:S(2)}, u32[]{:S(2)}) %collective-permute-start.13) | collective-permute-done | bytes 65568 | tf_op jit(solution)/shard_map/ppermute | solution.py:41
  58.2 1.4 %collective-permute-done.11.refs_5_ = bf16[8,4096]{1,0:T(8,128)(2,1)S(1)} collective-permute-done((bf16[8,4096]{1,0:T(8,128)(2,1)S(1)}, bf16[8,4096]{1,0:T(8,128)(2,1)S(1)}, u32[]{:S(2)}, u32[]{:S(2)}) %collective-permute-start.11) | collective-permute-done | bytes 65568 | tf_op jit(solution)/shard_map/ppermute | solution.py:41
  59.6 0.6 collective-permute-start.4
  60.2 0.8 collective-permute-done.9.refs_3_
  61.0 0.6 collective-permute-start.2
  61.6 4.7 %project.2.refs_9_ = f32[64,896]{1,0:T(8,128)S(1)} custom-call(bf16[8,4096]{1,0:T(8,128)(2,1)S(1)} %get-tuple-element.34.refs_0_, bf16[8,4096]{1,0:T(8,128)(2,1)S(1)} %collective-permute-done.7.refs_1_, bf16[8,4096]{1,0:T(8,128)(2,1)S(1)} %collective-permute-done.8.refs_2_, bf16[8,4096]{1,0:T(8,128)(2,1)S(1)} %collective-permute-done.9.refs_3_, ...), custom_call_target="tpu_custom_call" | custom-call | tf_op jit(solution)/shard_map/project/pallas_call | solution.py:221
  66.3 4.9 %project.3 = (f32[64,512]{1,0:T(8,128)S(1)}, f32[64,512]{1,0:T(8,128)S(1)}, f32[64,128]{1,0:T(8,128)S(1)}) custom-call(bf16[8,4096]{1,0:T(8,128)(2,1)S(1)} %get-tuple-element.33.refs_0_, bf16[8,4096]{1,0:T(8,128)(2,1)S(1)} %collective-permute-done.refs_1_, bf16[8,4096]{1,0:T(8,128)(2,1)S(1)} %collective-permute-done.1.refs_2_, ...), custom_call_target="tpu_custom_call" | custom-call | tf_op jit(solution)/shard_map/project/pallas_call | solution.py:221
  71.3 1.3 %collective-permute-done.21 = f32[64,512]{1,0:T(8,128)S(1)} collective-permute-done((f32[64,512]{1,0:T(8,128)S(1)}, f32[64,512]{1,0:T(8,128)S(1)}, u32[]{:S(2)}, u32[]{:S(2)}) %collective-permute-start.21) | collective-permute-done | bytes 131104 | tf_op jit(solution)/shard_map/ppermute | solution.py:62
  72.7 0.9 collective-permute-start.27
  73.6 1.2 %collective-permute-start.23 = (bf16[64,512]{1,0:T(8,128)(2,1)S(1)}, bf16[64,512]{1,0:T(8,128)(2,1)S(1)}, u32[]{:S(2)}, u32[]{:S(2)}) collective-permute-start(bf16[64,512]{1,0:T(8,128)(2,1)S(1)} %add_convert_fusion.refs_0_), channel_id=1, source_target_pairs={{0,4},{2,6},{4,8},{6,10},{8,12},{10,14},{12,0},{14,2},{1,5},{3,7},... | collective-permute-start | bytes 196616 | tf_op jit(solution)/shard_map/ppermute | solution.py:41
  74.8 2.2 %collective-permute-done.27.refs_6_ = bf16[64,512]{1,0:T(8,128)(2,1)S(1)} collective-permute-done((bf16[64,512]{1,0:T(8,128)(2,1)S(1)}, bf16[64,512]{1,0:T(8,128)(2,1)S(1)}, u32[]{:S(2)}, u32[]{:S(2)}) %collective-permute-start.27) | collective-permute-done | bytes 65568 | tf_op jit(solution)/shard_map/ppermute | solution.py:41
  77.0 2.1 %collective-permute-start.22 = (bf16[64,512]{1,0:T(8,128)(2,1)S(1)}, bf16[64,512]{1,0:T(8,128)(2,1)S(1)}, u32[]{:S(2)}, u32[]{:S(2)}) collective-permute-start(bf16[64,512]{1,0:T(8,128)(2,1)S(1)} %add_convert_fusion.refs_0_), channel_id=1, source_target_pairs={{0,2},{2,0},{4,6},{6,4},{8,10},{10,8},{12,14},{14,12},{1,3},{3,1},... | collective-permute-start | bytes 196616 | tf_op jit(solution)/shard_map/ppermute | solution.py:41
  79.1 2.0 %collective-permute-done.25.refs_4_ = bf16[64,512]{1,0:T(8,128)(2,1)S(1)} collective-permute-done((bf16[64,512]{1,0:T(8,128)(2,1)S(1)}, bf16[64,512]{1,0:T(8,128)(2,1)S(1)}, u32[]{:S(2)}, u32[]{:S(2)}) %collective-permute-start.25) | collective-permute-done | bytes 65568 | tf_op jit(solution)/shard_map/ppermute | solution.py:41
  81.2 1.3 %collective-permute-start.28 = (bf16[64,512]{1,0:T(8,128)(2,1)S(1)}, bf16[64,512]{1,0:T(8,128)(2,1)S(1)}, u32[]{:S(2)}, u32[]{:S(2)}) collective-permute-start(bf16[64,512]{1,0:T(8,128)(2,1)S(1)} %collective-permute-done.27.refs_6_), channel_id=1, source_target_pairs={{0,2},{2,0},{4,6},{6,4},{8,10},{10,8},{12,14},{14,12},{1,3},{3,1},... | collective-permute-start | bytes 196616 | tf_op jit(solution)/shard_map/ppermute | solution.py:41
  82.5 0.7 collective-permute-start.26
  83.2 1.3 %collective-permute-start.24 = (bf16[64,512]{1,0:T(8,128)(2,1)S(1)}, bf16[64,512]{1,0:T(8,128)(2,1)S(1)}, u32[]{:S(2)}, u32[]{:S(2)}) collective-permute-start(bf16[64,512]{1,0:T(8,128)(2,1)S(1)} %collective-permute-done.23.refs_2_), channel_id=1, source_target_pairs={{0,2},{2,0},{4,6},{6,4},{8,10},{10,8},{12,14},{14,12},{1,3},{3,1},... | collective-permute-start | bytes 196616 | tf_op jit(solution)/shard_map/ppermute | solution.py:41
  84.5 0.9 collective-permute-done.28.refs_7_
  85.4 1.3 %collective-permute-done.26.refs_5_ = bf16[64,512]{1,0:T(8,128)(2,1)S(1)} collective-permute-done((bf16[64,512]{1,0:T(8,128)(2,1)S(1)}, bf16[64,512]{1,0:T(8,128)(2,1)S(1)}, u32[]{:S(2)}, u32[]{:S(2)}) %collective-permute-start.26) | collective-permute-done | bytes 65568 | tf_op jit(solution)/shard_map/ppermute | solution.py:41
  86.8 0.7 collective-permute-done.24.refs_3_
  87.5 1.5 %copy-done.10 = bf16[8,320,512]{2,1,0:T(8,128)(2,1)} copy-done((bf16[8,320,512]{2,1,0:T(8,128)(2,1)}, bf16[8,320,512]{2,1,0:T(8,128)(2,1)S(1)}, u32[]{:S(2)}) %copy-start.10) | copy-done | bytes 2621464
  89.0 3.7 %gate_up.1 = (f32[5,64,256]{2,1,0:T(8,128)S(1)}, bf16[2,8,2048]{2,1,0:T(8,128)(2,1)S(1)}) custom-call(bf16[64,512]{1,0:T(8,128)(2,1)S(1)} %add_convert_fusion.refs_0_, bf16[64,512]{1,0:T(8,128)(2,1)S(1)} %collective-permute-done.22.refs_1_, bf16[64,512]{1,0:T(8,128)(2,1)S(1)} %collective-permute-done.23.refs_2_, ...), custom_call_target="tpu_custom_call" | custom-call | tf_op jit(solution)/shard_map/gate_up/pallas_call | solution.py:319
  92.8 1.6 %collective-permute-done.31.far_ref = f32[5,64,256]{2,1,0:T(8,128)S(1)} collective-permute-done((f32[5,64,256]{2,1,0:T(8,128)S(1)}, f32[5,64,256]{2,1,0:T(8,128)S(1)}, u32[]{:S(2)}, u32[]{:S(2)}) %collective-permute-start.31) | collective-permute-done | bytes 327712 | tf_op jit(solution)/shard_map/ppermute | solution.py:62
  94.4 0.8 down.1
  95.1 1.4 %collective-permute-start.33 = (bf16[8,3584]{1,0:T(8,128)(2,1)S(1)}, bf16[8,3584]{1,0:T(8,128)(2,1)S(1)}, u32[]{:S(2)}, u32[]{:S(2)}) collective-permute-start(bf16[8,3584]{1,0:T(8,128)(2,1)S(1)} %get-tuple-element.54), channel_id=1, source_target_pairs={{0,2},{2,0},{4,6},{6,4},{8,10},{10,8},{12,14},{14,12},{1,3},{3,1},... | collective-permute-start | bytes 172040 | tf_op jit(solution)/shard_map/ppermute | solution.py:41
  96.6 1.5 %collective-permute-start.35 = (bf16[8,3584]{1,0:T(8,128)(2,1)S(1)}, bf16[8,3584]{1,0:T(8,128)(2,1)S(1)}, u32[]{:S(2)}, u32[]{:S(2)}) collective-permute-start(bf16[8,3584]{1,0:T(8,128)(2,1)S(1)} %get-tuple-element.56), channel_id=1, source_target_pairs={{0,6},{2,4},{4,10},{6,8},{8,14},{10,12},{12,2},{14,0},{1,7},{3,5},... | collective-permute-start | bytes 172040 | tf_op jit(solution)/shard_map/ppermute | solution.py:41
  98.0 3.1 %collective-permute-start.36 = (bf16[8,3584]{1,0:T(8,128)(2,1)S(1)}, bf16[8,3584]{1,0:T(8,128)(2,1)S(1)}, u32[]{:S(2)}, u32[]{:S(2)}) collective-permute-start(bf16[8,3584]{1,0:T(8,128)(2,1)S(1)} %get-tuple-element.57), channel_id=1, source_target_pairs={{0,8},{2,10},{4,12},{6,14},{8,0},{10,2},{12,4},{14,6},{1,9},{3,11}... | collective-permute-start | bytes 172040 | tf_op jit(solution)/shard_map/ppermute | solution.py:41
  101.1 0.7 collective-permute-start.37
  101.9 2.4 %collective-permute-start.38 = (bf16[8,3584]{1,0:T(8,128)(2,1)S(1)}, bf16[8,3584]{1,0:T(8,128)(2,1)S(1)}, u32[]{:S(2)}, u32[]{:S(2)}) collective-permute-start(bf16[8,3584]{1,0:T(8,128)(2,1)S(1)} %get-tuple-element.59), channel_id=1, source_target_pairs={{0,12},{2,14},{4,0},{6,2},{8,4},{10,6},{12,8},{14,10},{1,13},{3,15... | collective-permute-start | bytes 172040 | tf_op jit(solution)/shard_map/ppermute | solution.py:41
  104.3 2.1 %collective-permute-start.39 = (bf16[8,3584]{1,0:T(8,128)(2,1)S(1)}, bf16[8,3584]{1,0:T(8,128)(2,1)S(1)}, u32[]{:S(2)}, u32[]{:S(2)}) collective-permute-start(bf16[8,3584]{1,0:T(8,128)(2,1)S(1)} %get-tuple-element.60), channel_id=1, source_target_pairs={{0,14},{2,12},{4,2},{6,0},{8,6},{10,4},{12,10},{14,8},{1,15},{3,13... | collective-permute-start | bytes 172040 | tf_op jit(solution)/shard_map/ppermute | solution.py:41
  106.4 0.9 collective-permute-done.36.rest_4_
  107.3 1.5 %collective-permute-done.37.rest_5_ = bf16[8,3584]{1,0:T(8,128)(2,1)S(1)} collective-permute-done((bf16[8,3584]{1,0:T(8,128)(2,1)S(1)}, bf16[8,3584]{1,0:T(8,128)(2,1)S(1)}, u32[]{:S(2)}, u32[]{:S(2)}) %collective-permute-start.37) | collective-permute-done | bytes 57376 | tf_op jit(solution)/shard_map/ppermute | solution.py:41
  108.9 1.1 %collective-permute-done.39.rest_7_ = bf16[8,3584]{1,0:T(8,128)(2,1)S(1)} collective-permute-done((bf16[8,3584]{1,0:T(8,128)(2,1)S(1)}, bf16[8,3584]{1,0:T(8,128)(2,1)S(1)}, u32[]{:S(2)}, u32[]{:S(2)}) %collective-permute-start.39) | collective-permute-done | bytes 57376 | tf_op jit(solution)/shard_map/ppermute | solution.py:41
  110.0 0.7 finish.1
  (49 shorter events, 1.6 us)
Async XLA Ops:
  0.0 12.8 %copy-start = (bf16[7168,160]{0,1:T(8,128)(2,1)S(1)}, bf16[7168,160]{0,1:T(8,128)(2,1)}, u32[]{:S(2)}) copy-start(bf16[7168,160]{0,1:T(8,128)(2,1)} %param.21) | copy-start | bytes 6881284
  1.7 1.9 %copy-start.4 = (bf16[8,384,512]{2,1,0:T(8,128)(2,1)S(1)}, bf16[8,384,512]{2,1,0:T(8,128)(2,1)}, u32[]{:S(2)}) copy-start(bf16[8,384,512]{2,1,0:T(8,128)(2,1)} %cache_ref.1) | copy-start | bytes 9437188
  3.6 0.9 copy-start.5
  4.5 0.9 copy-start.6
  5.4 0.7 copy-start.8
  6.1 0.7 copy-start.9
  12.9 1.6 %copy-start.1 = (bf16[7168,160]{0,1:T(8,128)(2,1)S(1)}, bf16[7168,160]{0,1:T(8,128)(2,1)}, u32[]{:S(2)}) copy-start(bf16[7168,160]{0,1:T(8,128)(2,1)} %param.22) | copy-start | bytes 6881284
  16.8 70.7 %collective-permute-start.29 = (bf16[8,320,512]{2,1,0:T(8,128)(2,1)}, bf16[8,320,512]{2,1,0:T(8,128)(2,1)S(1)}, u32[]{:S(2)}, u32[]{:S(2)}) collective-permute-start(bf16[8,320,512]{2,1,0:T(8,128)(2,1)} %get-tuple-element.48), channel_id=1, source_target_pairs={{0,1},{1,0},{2,3},{3,2},{4,5},{5,4},{6,7},{7,6},{8,9},{9,8},{10,11... | collective-permute-start | bytes 7864328 | tf_op jit(solution)/shard_map/ppermute | solution.py:62
  17.3 26.3 %collective-permute-start.5 = (bf16[8,4096]{1,0:T(8,128)(2,1)S(1)}, bf16[8,4096]{1,0:T(8,128)(2,1)S(1)}, u32[]{:S(2)}, u32[]{:S(2)}) collective-permute-start(bf16[8,4096]{1,0:T(8,128)(2,1)S(1)} %get-tuple-element.33.refs_0_), channel_id=1, source_target_pairs={{0,12},{2,14},{4,0},{6,2},{8,4},{10,6},{12,8},{14,10},{1,13},{3,15... | collective-permute-start | bytes 196616 | tf_op jit(solution)/shard_map/ppermute | solution.py:41
  21.9 23.0 %collective-permute-start.3 = (bf16[8,4096]{1,0:T(8,128)(2,1)S(1)}, bf16[8,4096]{1,0:T(8,128)(2,1)S(1)}, u32[]{:S(2)}, u32[]{:S(2)}) collective-permute-start(bf16[8,4096]{1,0:T(8,128)(2,1)S(1)} %get-tuple-element.33.refs_0_), channel_id=1, source_target_pairs={{0,8},{2,10},{4,12},{6,14},{8,0},{10,2},{12,4},{14,6},{1,9},{3,11}... | collective-permute-start | bytes 196616 | tf_op jit(solution)/shard_map/ppermute | solution.py:41
  21.9 3.7 %collective-permute-start.14 = (bf16[8,640]{1,0:T(8,128)(2,1)S(1)}, bf16[8,640]{1,0:T(8,128)(2,1)S(1)}, u32[]{:S(2)}, u32[]{:S(2)}) collective-permute-start(bf16[8,640]{1,0:T(8,128)(2,1)S(1)} %get-tuple-element.36), channel_id=1, source_target_pairs={{0,2},{2,0},{4,6},{6,4},{8,10},{10,8},{12,14},{14,12},{1,3},{3,1},... | collective-permute-start | bytes 30728 | tf_op jit(solution)/shard_map/ppermute | solution.py:41
  23.4 5.5 %collective-permute-start.15 = (bf16[8,640]{1,0:T(8,128)(2,1)S(1)}, bf16[8,640]{1,0:T(8,128)(2,1)S(1)}, u32[]{:S(2)}, u32[]{:S(2)}) collective-permute-start(bf16[8,640]{1,0:T(8,128)(2,1)S(1)} %get-tuple-element.37), channel_id=1, source_target_pairs={{0,4},{2,6},{4,8},{6,10},{8,12},{10,14},{12,0},{14,2},{1,5},{3,7},... | collective-permute-start | bytes 30728 | tf_op jit(solution)/shard_map/ppermute | solution.py:41
  25.6 6.4 %collective-permute-start.16 = (bf16[8,640]{1,0:T(8,128)(2,1)S(1)}, bf16[8,640]{1,0:T(8,128)(2,1)S(1)}, u32[]{:S(2)}, u32[]{:S(2)}) collective-permute-start(bf16[8,640]{1,0:T(8,128)(2,1)S(1)} %get-tuple-element.38), channel_id=1, source_target_pairs={{0,6},{2,4},{4,10},{6,8},{8,14},{10,12},{12,2},{14,0},{1,7},{3,5},... | collective-permute-start | bytes 30728 | tf_op jit(solution)/shard_map/ppermute | solution.py:41
  28.9 5.1 %collective-permute-start.17 = (bf16[8,640]{1,0:T(8,128)(2,1)S(1)}, bf16[8,640]{1,0:T(8,128)(2,1)S(1)}, u32[]{:S(2)}, u32[]{:S(2)}) collective-permute-start(bf16[8,640]{1,0:T(8,128)(2,1)S(1)} %get-tuple-element.39), channel_id=1, source_target_pairs={{0,8},{2,10},{4,12},{6,14},{8,0},{10,2},{12,4},{14,6},{1,9},{3,11}... | collective-permute-start | bytes 30728 | tf_op jit(solution)/shard_map/ppermute | solution.py:41
  32.0 5.5 %collective-permute-start.18 = (bf16[8,640]{1,0:T(8,128)(2,1)S(1)}, bf16[8,640]{1,0:T(8,128)(2,1)S(1)}, u32[]{:S(2)}, u32[]{:S(2)}) collective-permute-start(bf16[8,640]{1,0:T(8,128)(2,1)S(1)} %get-tuple-element.40), channel_id=1, source_target_pairs={{0,10},{2,8},{4,14},{6,12},{8,2},{10,0},{12,6},{14,4},{1,11},{3,9}... | collective-permute-start | bytes 30728 | tf_op jit(solution)/shard_map/ppermute | solution.py:41
  34.0 4.0 %collective-permute-start.19 = (bf16[8,640]{1,0:T(8,128)(2,1)S(1)}, bf16[8,640]{1,0:T(8,128)(2,1)S(1)}, u32[]{:S(2)}, u32[]{:S(2)}) collective-permute-start(bf16[8,640]{1,0:T(8,128)(2,1)S(1)} %get-tuple-element.41), channel_id=1, source_target_pairs={{0,12},{2,14},{4,0},{6,2},{8,4},{10,6},{12,8},{14,10},{1,13},{3,15... | collective-permute-start | bytes 30728 | tf_op jit(solution)/shard_map/ppermute | solution.py:41
  37.5 4.6 %collective-permute-start.20 = (bf16[8,640]{1,0:T(8,128)(2,1)S(1)}, bf16[8,640]{1,0:T(8,128)(2,1)S(1)}, u32[]{:S(2)}, u32[]{:S(2)}) collective-permute-start(bf16[8,640]{1,0:T(8,128)(2,1)S(1)} %get-tuple-element.42), channel_id=1, source_target_pairs={{0,14},{2,12},{4,2},{6,0},{8,6},{10,4},{12,10},{14,8},{1,15},{3,13... | collective-permute-start | bytes 30728 | tf_op jit(solution)/shard_map/ppermute | solution.py:41
  38.0 6.9 %collective-permute-start.1 = (bf16[8,4096]{1,0:T(8,128)(2,1)S(1)}, bf16[8,4096]{1,0:T(8,128)(2,1)S(1)}, u32[]{:S(2)}, u32[]{:S(2)}) collective-permute-start(bf16[8,4096]{1,0:T(8,128)(2,1)S(1)} %get-tuple-element.33.refs_0_), channel_id=1, source_target_pairs={{0,4},{2,6},{4,8},{6,10},{8,12},{10,14},{12,0},{14,2},{1,5},{3,7},... | collective-permute-start | bytes 196616 | tf_op jit(solution)/shard_map/ppermute | solution.py:41
  42.1 4.3 %collective-permute-start = (bf16[8,4096]{1,0:T(8,128)(2,1)S(1)}, bf16[8,4096]{1,0:T(8,128)(2,1)S(1)}, u32[]{:S(2)}, u32[]{:S(2)}) collective-permute-start(bf16[8,4096]{1,0:T(8,128)(2,1)S(1)} %get-tuple-element.33.refs_0_), channel_id=1, source_target_pairs={{0,2},{2,0},{4,6},{6,4},{8,10},{10,8},{12,14},{14,12},{1,3},{3,1},... | collective-permute-start | bytes 196616 | tf_op jit(solution)/shard_map/ppermute | solution.py:41
  43.6 4.3 %collective-permute-start.12 = (bf16[8,4096]{1,0:T(8,128)(2,1)S(1)}, bf16[8,4096]{1,0:T(8,128)(2,1)S(1)}, u32[]{:S(2)}, u32[]{:S(2)}) collective-permute-start(bf16[8,4096]{1,0:T(8,128)(2,1)S(1)} %get-tuple-element.34.refs_0_), channel_id=1, source_target_pairs={{0,12},{2,14},{4,0},{6,2},{8,4},{10,6},{12,8},{14,10},{1,13},{3,15... | collective-permute-start | bytes 196616 | tf_op jit(solution)/shard_map/ppermute | solution.py:41
  45.0 47.8 %collective-permute-start.32 = (bf16[160,3584]{1,0:T(8,128)(2,1)S(1)}, bf16[160,3584]{1,0:T(8,128)(2,1)S(1)}, u32[]{:S(2)}, u32[]{:S(2)}) collective-permute-start(bf16[160,3584]{1,0:T(8,128)(2,1)S(1)} %get-tuple-element.52), channel_id=1, source_target_pairs={{0,1},{1,0},{2,3},{3,2},{4,5},{5,4},{6,7},{7,6},{8,9},{9,8},{10,11... | collective-permute-start | bytes 3440648 | tf_op jit(solution)/shard_map/ppermute | solution.py:62
  45.0 8.2 %collective-permute-start.10 = (bf16[8,4096]{1,0:T(8,128)(2,1)S(1)}, bf16[8,4096]{1,0:T(8,128)(2,1)S(1)}, u32[]{:S(2)}, u32[]{:S(2)}) collective-permute-start(bf16[8,4096]{1,0:T(8,128)(2,1)S(1)} %get-tuple-element.34.refs_0_), channel_id=1, source_target_pairs={{0,8},{2,10},{4,12},{6,14},{8,0},{10,2},{12,4},{14,6},{1,9},{3,11}... | collective-permute-start | bytes 196616 | tf_op jit(solution)/shard_map/ppermute | solution.py:41
  46.3 6.9 %collective-permute-start.8 = (bf16[8,4096]{1,0:T(8,128)(2,1)S(1)}, bf16[8,4096]{1,0:T(8,128)(2,1)S(1)}, u32[]{:S(2)}, u32[]{:S(2)}) collective-permute-start(bf16[8,4096]{1,0:T(8,128)(2,1)S(1)} %get-tuple-element.34.refs_0_), channel_id=1, source_target_pairs={{0,4},{2,6},{4,8},{6,10},{8,12},{10,14},{12,0},{14,2},{1,5},{3,7},... | collective-permute-start | bytes 196616 | tf_op jit(solution)/shard_map/ppermute | solution.py:41
  47.8 7.4 %collective-permute-start.7 = (bf16[8,4096]{1,0:T(8,128)(2,1)S(1)}, bf16[8,4096]{1,0:T(8,128)(2,1)S(1)}, u32[]{:S(2)}, u32[]{:S(2)}) collective-permute-start(bf16[8,4096]{1,0:T(8,128)(2,1)S(1)} %get-tuple-element.34.refs_0_), channel_id=1, source_target_pairs={{0,2},{2,0},{4,6},{6,4},{8,10},{10,8},{12,14},{14,12},{1,3},{3,1},... | collective-permute-start | bytes 196616 | tf_op jit(solution)/shard_map/ppermute | solution.py:41
  53.2 5.0 %collective-permute-start.13 = (bf16[8,4096]{1,0:T(8,128)(2,1)S(1)}, bf16[8,4096]{1,0:T(8,128)(2,1)S(1)}, u32[]{:S(2)}, u32[]{:S(2)}) collective-permute-start(bf16[8,4096]{1,0:T(8,128)(2,1)S(1)} %collective-permute-done.12.refs_6_), channel_id=1, source_target_pairs={{0,2},{2,0},{4,6},{6,4},{8,10},{10,8},{12,14},{14,12},{1,3},{3,1},... | collective-permute-start | bytes 196616 | tf_op jit(solution)/shard_map/ppermute | solution.py:41
  53.2 6.4 %collective-permute-start.11 = (bf16[8,4096]{1,0:T(8,128)(2,1)S(1)}, bf16[8,4096]{1,0:T(8,128)(2,1)S(1)}, u32[]{:S(2)}, u32[]{:S(2)}) collective-permute-start(bf16[8,4096]{1,0:T(8,128)(2,1)S(1)} %collective-permute-done.10.refs_4_), channel_id=1, source_target_pairs={{0,2},{2,0},{4,6},{6,4},{8,10},{10,8},{12,14},{14,12},{1,3},{3,1},... | collective-permute-start | bytes 196616 | tf_op jit(solution)/shard_map/ppermute | solution.py:41
  55.2 5.7 %collective-permute-start.9 = (bf16[8,4096]{1,0:T(8,128)(2,1)S(1)}, bf16[8,4096]{1,0:T(8,128)(2,1)S(1)}, u32[]{:S(2)}, u32[]{:S(2)}) collective-permute-start(bf16[8,4096]{1,0:T(8,128)(2,1)S(1)} %collective-permute-done.8.refs_2_), channel_id=1, source_target_pairs={{0,2},{2,0},{4,6},{6,4},{8,10},{10,8},{12,14},{14,12},{1,3},{3,1},... | collective-permute-start | bytes 196616 | tf_op jit(solution)/shard_map/ppermute | solution.py:41
  58.2 8.1 %collective-permute-start.6 = (bf16[8,4096]{1,0:T(8,128)(2,1)S(1)}, bf16[8,4096]{1,0:T(8,128)(2,1)S(1)}, u32[]{:S(2)}, u32[]{:S(2)}) collective-permute-start(bf16[8,4096]{1,0:T(8,128)(2,1)S(1)} %collective-permute-done.5.refs_6_), channel_id=1, source_target_pairs={{0,2},{2,0},{4,6},{6,4},{8,10},{10,8},{12,14},{14,12},{1,3},{3,1},... | collective-permute-start | bytes 196616 | tf_op jit(solution)/shard_map/ppermute | solution.py:41
  59.6 6.7 %collective-permute-start.4 = (bf16[8,4096]{1,0:T(8,128)(2,1)S(1)}, bf16[8,4096]{1,0:T(8,128)(2,1)S(1)}, u32[]{:S(2)}, u32[]{:S(2)}) collective-permute-start(bf16[8,4096]{1,0:T(8,128)(2,1)S(1)} %collective-permute-done.3.refs_4_), channel_id=1, source_target_pairs={{0,2},{2,0},{4,6},{6,4},{8,10},{10,8},{12,14},{14,12},{1,3},{3,1},... | collective-permute-start | bytes 196616 | tf_op jit(solution)/shard_map/ppermute | solution.py:41
  61.0 5.3 %collective-permute-start.2 = (bf16[8,4096]{1,0:T(8,128)(2,1)S(1)}, bf16[8,4096]{1,0:T(8,128)(2,1)S(1)}, u32[]{:S(2)}, u32[]{:S(2)}) collective-permute-start(bf16[8,4096]{1,0:T(8,128)(2,1)S(1)} %collective-permute-done.1.refs_2_), channel_id=1, source_target_pairs={{0,2},{2,0},{4,6},{6,4},{8,10},{10,8},{12,14},{14,12},{1,3},{3,1},... | collective-permute-start | bytes 196616 | tf_op jit(solution)/shard_map/ppermute | solution.py:41
  66.3 22.6 %copy-start.2 = (bf16[7168,160]{0,1:T(8,128)(2,1)S(1)}, bf16[7168,160]{0,1:T(8,128)(2,1)}, u32[]{:S(2)}) copy-start(bf16[7168,160]{0,1:T(8,128)(2,1)} %param.22) | copy-start | bytes 6881284
  66.3 22.6 %copy-start.7 = (f32[7168]{0:T(1024)S(1)}, f32[7168]{0:T(1024)}, u32[]{:S(2)}) copy-start(f32[7168]{0:T(1024)} %param.18) | copy-start | bytes 86020
  71.3 1.4 %collective-permute-start.21 = (f32[64,512]{1,0:T(8,128)S(1)}, f32[64,512]{1,0:T(8,128)S(1)}, u32[]{:S(2)}, u32[]{:S(2)}) collective-permute-start(f32[64,512]{1,0:T(8,128)S(1)} %get-tuple-element.44), channel_id=1, source_target_pairs={{0,1},{1,0},{2,3},{3,2},{4,5},{5,4},{6,7},{7,6},{8,9},{9,8},{10,11... | collective-permute-start | bytes 393224 | tf_op jit(solution)/shard_map/ppermute | solution.py:62
  72.7 4.3 %collective-permute-start.27 = (bf16[64,512]{1,0:T(8,128)(2,1)S(1)}, bf16[64,512]{1,0:T(8,128)(2,1)S(1)}, u32[]{:S(2)}, u32[]{:S(2)}) collective-permute-start(bf16[64,512]{1,0:T(8,128)(2,1)S(1)} %add_convert_fusion.refs_0_), channel_id=1, source_target_pairs={{0,12},{2,14},{4,0},{6,2},{8,4},{10,6},{12,8},{14,10},{1,13},{3,15... | collective-permute-start | bytes 196616 | tf_op jit(solution)/shard_map/ppermute | solution.py:41
  73.6 7.6 %collective-permute-start.25 = (bf16[64,512]{1,0:T(8,128)(2,1)S(1)}, bf16[64,512]{1,0:T(8,128)(2,1)S(1)}, u32[]{:S(2)}, u32[]{:S(2)}) collective-permute-start(bf16[64,512]{1,0:T(8,128)(2,1)S(1)} %add_convert_fusion.refs_0_), channel_id=1, source_target_pairs={{0,8},{2,10},{4,12},{6,14},{8,0},{10,2},{12,4},{14,6},{1,9},{3,11}... | collective-permute-start | bytes 196616 | tf_op jit(solution)/shard_map/ppermute | solution.py:41
  73.6 8.9 %collective-permute-start.23 = (bf16[64,512]{1,0:T(8,128)(2,1)S(1)}, bf16[64,512]{1,0:T(8,128)(2,1)S(1)}, u32[]{:S(2)}, u32[]{:S(2)}) collective-permute-start(bf16[64,512]{1,0:T(8,128)(2,1)S(1)} %add_convert_fusion.refs_0_), channel_id=1, source_target_pairs={{0,4},{2,6},{4,8},{6,10},{8,12},{10,14},{12,0},{14,2},{1,5},{3,7},... | collective-permute-start | bytes 196616 | tf_op jit(solution)/shard_map/ppermute | solution.py:41
  77.0 6.2 %collective-permute-start.22 = (bf16[64,512]{1,0:T(8,128)(2,1)S(1)}, bf16[64,512]{1,0:T(8,128)(2,1)S(1)}, u32[]{:S(2)}, u32[]{:S(2)}) collective-permute-start(bf16[64,512]{1,0:T(8,128)(2,1)S(1)} %add_convert_fusion.refs_0_), channel_id=1, source_target_pairs={{0,2},{2,0},{4,6},{6,4},{8,10},{10,8},{12,14},{14,12},{1,3},{3,1},... | collective-permute-start | bytes 196616 | tf_op jit(solution)/shard_map/ppermute | solution.py:41
  81.2 4.3 %collective-permute-start.28 = (bf16[64,512]{1,0:T(8,128)(2,1)S(1)}, bf16[64,512]{1,0:T(8,128)(2,1)S(1)}, u32[]{:S(2)}, u32[]{:S(2)}) collective-permute-start(bf16[64,512]{1,0:T(8,128)(2,1)S(1)} %collective-permute-done.27.refs_6_), channel_id=1, source_target_pairs={{0,2},{2,0},{4,6},{6,4},{8,10},{10,8},{12,14},{14,12},{1,3},{3,1},... | collective-permute-start | bytes 196616 | tf_op jit(solution)/shard_map/ppermute | solution.py:41
  82.5 4.3 %collective-permute-start.26 = (bf16[64,512]{1,0:T(8,128)(2,1)S(1)}, bf16[64,512]{1,0:T(8,128)(2,1)S(1)}, u32[]{:S(2)}, u32[]{:S(2)}) collective-permute-start(bf16[64,512]{1,0:T(8,128)(2,1)S(1)} %collective-permute-done.25.refs_4_), channel_id=1, source_target_pairs={{0,2},{2,0},{4,6},{6,4},{8,10},{10,8},{12,14},{14,12},{1,3},{3,1},... | collective-permute-start | bytes 196616 | tf_op jit(solution)/shard_map/ppermute | solution.py:41
  83.2 4.3 %collective-permute-start.24 = (bf16[64,512]{1,0:T(8,128)(2,1)S(1)}, bf16[64,512]{1,0:T(8,128)(2,1)S(1)}, u32[]{:S(2)}, u32[]{:S(2)}) collective-permute-start(bf16[64,512]{1,0:T(8,128)(2,1)S(1)} %collective-permute-done.23.refs_2_), channel_id=1, source_target_pairs={{0,2},{2,0},{4,6},{6,4},{8,10},{10,8},{12,14},{14,12},{1,3},{3,1},... | collective-permute-start | bytes 196616 | tf_op jit(solution)/shard_map/ppermute | solution.py:41
  87.5 1.5 %copy-start.10 = (bf16[8,320,512]{2,1,0:T(8,128)(2,1)}, bf16[8,320,512]{2,1,0:T(8,128)(2,1)S(1)}, u32[]{:S(2)}) copy-start(bf16[8,320,512]{2,1,0:T(8,128)(2,1)S(1)} %collective-permute-done.29.refs_11_) | copy-start | bytes 7864324
  89.0 5.4 %copy-start.3 = (bf16[160,7168]{1,0:T(8,128)(2,1)S(1)}, bf16[160,7168]{1,0:T(8,128)(2,1)}, u32[]{:S(2)}) copy-start(bf16[160,7168]{1,0:T(8,128)(2,1)} %down_ref.2) | copy-start | bytes 6881284
  92.7 1.7 %collective-permute-start.31 = (f32[5,64,256]{2,1,0:T(8,128)S(1)}, f32[5,64,256]{2,1,0:T(8,128)S(1)}, u32[]{:S(2)}, u32[]{:S(2)}) collective-permute-start(f32[5,64,256]{2,1,0:T(8,128)S(1)} %get-tuple-element.50.sums_ref), channel_id=1, source_target_pairs={{0,1},{1,0},{2,3},{3,2},{4,5},{5,4},{6,7},{7,6},{8,9},{9,8},{10,11... | collective-permute-start | bytes 983048 | tf_op jit(solution)/shard_map/ppermute | solution.py:62
  95.1 6.7 %collective-permute-start.33 = (bf16[8,3584]{1,0:T(8,128)(2,1)S(1)}, bf16[8,3584]{1,0:T(8,128)(2,1)S(1)}, u32[]{:S(2)}, u32[]{:S(2)}) collective-permute-start(bf16[8,3584]{1,0:T(8,128)(2,1)S(1)} %get-tuple-element.54), channel_id=1, source_target_pairs={{0,2},{2,0},{4,6},{6,4},{8,10},{10,8},{12,14},{14,12},{1,3},{3,1},... | collective-permute-start | bytes 172040 | tf_op jit(solution)/shard_map/ppermute | solution.py:41
  96.5 7.8 %collective-permute-start.34 = (bf16[8,3584]{1,0:T(8,128)(2,1)S(1)}, bf16[8,3584]{1,0:T(8,128)(2,1)S(1)}, u32[]{:S(2)}, u32[]{:S(2)}) collective-permute-start(bf16[8,3584]{1,0:T(8,128)(2,1)S(1)} %get-tuple-element.55), channel_id=1, source_target_pairs={{0,4},{2,6},{4,8},{6,10},{8,12},{10,14},{12,0},{14,2},{1,5},{3,7},... | collective-permute-start | bytes 172040 | tf_op jit(solution)/shard_map/ppermute | solution.py:41
  96.5 4.6 %collective-permute-start.30 = (bf16[8,2048]{1,0:T(8,128)(2,1)S(1)}, bf16[8,2048]{1,0:T(8,128)(2,1)S(1)}, u32[]{:S(2)}, u32[]{:S(2)}) collective-permute-start(bf16[8,2048]{1,0:T(8,128)(2,1)S(1)} %get-tuple-element.61), channel_id=1, source_target_pairs={{0,1},{1,0},{2,3},{3,2},{4,5},{5,4},{6,7},{7,6},{8,9},{9,8},{10,11... | collective-permute-start | bytes 98312 | tf_op jit(solution)/shard_map/ppermute | solution.py:62
  96.6 9.8 %collective-permute-start.35 = (bf16[8,3584]{1,0:T(8,128)(2,1)S(1)}, bf16[8,3584]{1,0:T(8,128)(2,1)S(1)}, u32[]{:S(2)}, u32[]{:S(2)}) collective-permute-start(bf16[8,3584]{1,0:T(8,128)(2,1)S(1)} %get-tuple-element.56), channel_id=1, source_target_pairs={{0,6},{2,4},{4,10},{6,8},{8,14},{10,12},{12,2},{14,0},{1,7},{3,5},... | collective-permute-start | bytes 172040 | tf_op jit(solution)/shard_map/ppermute | solution.py:41
  98.0 9.3 %collective-permute-start.36 = (bf16[8,3584]{1,0:T(8,128)(2,1)S(1)}, bf16[8,3584]{1,0:T(8,128)(2,1)S(1)}, u32[]{:S(2)}, u32[]{:S(2)}) collective-permute-start(bf16[8,3584]{1,0:T(8,128)(2,1)S(1)} %get-tuple-element.57), channel_id=1, source_target_pairs={{0,8},{2,10},{4,12},{6,14},{8,0},{10,2},{12,4},{14,6},{1,9},{3,11}... | collective-permute-start | bytes 172040 | tf_op jit(solution)/shard_map/ppermute | solution.py:41
  101.1 7.8 %collective-permute-start.37 = (bf16[8,3584]{1,0:T(8,128)(2,1)S(1)}, bf16[8,3584]{1,0:T(8,128)(2,1)S(1)}, u32[]{:S(2)}, u32[]{:S(2)}) collective-permute-start(bf16[8,3584]{1,0:T(8,128)(2,1)S(1)} %get-tuple-element.58), channel_id=1, source_target_pairs={{0,10},{2,8},{4,14},{6,12},{8,2},{10,0},{12,6},{14,4},{1,11},{3,9}... | collective-permute-start | bytes 172040 | tf_op jit(solution)/shard_map/ppermute | solution.py:41
  101.9 7.0 %collective-permute-start.38 = (bf16[8,3584]{1,0:T(8,128)(2,1)S(1)}, bf16[8,3584]{1,0:T(8,128)(2,1)S(1)}, u32[]{:S(2)}, u32[]{:S(2)}) collective-permute-start(bf16[8,3584]{1,0:T(8,128)(2,1)S(1)} %get-tuple-element.59), channel_id=1, source_target_pairs={{0,12},{2,14},{4,0},{6,2},{8,4},{10,6},{12,8},{14,10},{1,13},{3,15... | collective-permute-start | bytes 172040 | tf_op jit(solution)/shard_map/ppermute | solution.py:41
  104.3 5.7 %collective-permute-start.39 = (bf16[8,3584]{1,0:T(8,128)(2,1)S(1)}, bf16[8,3584]{1,0:T(8,128)(2,1)S(1)}, u32[]{:S(2)}, u32[]{:S(2)}) collective-permute-start(bf16[8,3584]{1,0:T(8,128)(2,1)S(1)} %get-tuple-element.60), channel_id=1, source_target_pairs={{0,14},{2,12},{4,2},{6,0},{8,6},{10,4},{12,10},{14,8},{1,15},{3,13... | collective-permute-start | bytes 172040 | tf_op jit(solution)/shard_map/ppermute | solution.py:41

commit v3 on v2

v3 whole, which is shorter than its diff:
```python
import functools

import jax
import jax.numpy as jnp
from jax import lax
from jax.experimental import pallas as pl
from jax.experimental.pallas import tpu as pltpu
from jax.sharding import PartitionSpec as P

HD = 256
TOPK = 3
EXPERTS = 4
CAP = 8
LANES = 128


def params(mebibytes):
    return pltpu.CompilerParams(vmem_limit_bytes=mebibytes * 1024 * 1024)


def vmem():
    return pl.BlockSpec(memory_space=pltpu.VMEM)


def anywhere():
    return pl.BlockSpec(memory_space=pl.ANY)


def shape_of(shape, dtype):
    return jax.ShapeDtypeStruct(shape, dtype)


class Grid:
    def __init__(self, ep_size, x_size):
        self.ep, self.x, self.z = ep_size, x_size, ep_size // x_size
        self.steps = [(s, u) for s in range(self.z) for u in range(x_size)]

    def send(self, arr, s, u):
        pairs = [
            (z * self.x + x, (z + s) % self.z * self.x + (x + u) % self.x)
            for z in range(self.z)
            for x in range(self.x)
        ]
        return lax.ppermute(arr, "ep", pairs)

    def spread(self, own):
        got = {(0, 0): own[0]}
        for s in range(1, self.z):
            got[s, 0] = self.send(own[s], s, 0)
        for s in range(self.z):
            for u in range(1, self.x):
                got[s, u] = self.send(got[s, 0], 0, u)
        return [got[step] for step in self.steps]

    def source(self, step):
        me = lax.axis_index("ep")
        z = lax.rem(me // self.x - step[0] + self.z, self.z)
        return z * self.x + lax.rem(lax.rem(me, self.x) - step[1] + self.x, self.x)

    def target(self, step):
        return self.source((-step[0] % self.z, -step[1] % self.x))


def swap(arr):
    return lax.ppermute(arr, "tp", [(0, 1), (1, 0)])


def nt_dot(a, b):
    return lax.dot_general(a, b, (((1,), (1,)), ((), ())), preferred_element_type=jnp.float32)


def in_hbm():
    return pl.BlockSpec(memory_space=pltpu.HBM)


def attention(
    grid,
    piece,
    cols,
    queries,
    new_kv,
    cache,
    lengths,
    residual,
    route_ids,
    route_weights,
    gate_t,
    up_t,
    w_down,
):
    rows, width = queries.shape
    heads = width // HD
    ctx = cache.shape[1]
    tall = rows * heads
    note = piece + LANES
    scaling = HD ** (-0.5)
    units, features = gate_t.shape
    out_width = features // 2
    down_blocks = out_width // piece
    packed_rows = (2 * grid.ep + down_blocks) * units

    def kernel(*refs):
        sources, rest = refs[:7], refs[7:]
        gate_ref, up_ref, down_ref, rest = rest[0], rest[1], rest[2], rest[3:]
        out_refs, pack_ref, rest = rest[: grid.z], rest[grid.z], rest[grid.z + 1 :]
        q_ref, kv_ref, res_ref, ids_ref, wts_ref, len_ref, kept, score, sems, row_sems, pack_sems = rest
        cache_ref = sources[6]
        copies = [
            pltpu.make_async_copy(src, dst, sems.at[i])
            for i, (src, dst) in enumerate(
                zip(sources[:6], (q_ref, kv_ref, res_ref, ids_ref, wts_ref, len_ref))
            )
        ]
        row_copies = [
            pltpu.make_async_copy(cache_ref.at[r], kept.at[r], row_sems.at[r]) for r in range(rows)
        ]
        other = 1 - lax.axis_index("tp")
        blocks = []
        for j in range(grid.ep):
            begin = pl.multiple_of(j * cols + other * (cols - piece), LANES)
            blocks += [ref.at[:, pl.ds(begin, piece)] for ref in (gate_ref, up_ref)]
        for b in range(down_blocks):
            begin = pl.multiple_of(other * out_width + b * piece, LANES)
            blocks.append(down_ref.at[:, pl.ds(begin, piece)])
        packs = [
            pltpu.make_async_copy(block, pack_ref.at[pl.ds(i * units, units), :], pack_sems.at[i])
            for i, block in enumerate(blocks)
        ]
        for copy in copies[:2] + row_copies + copies[2:] + packs:
            copy.start()

        copies[0].wait()
        copies[1].wait()
        q = q_ref[...].astype(jnp.float32)
        stacked = jnp.concatenate([q[:, h * HD : (h + 1) * HD] for h in range(heads)], axis=0)
        narrow = stacked.astype(jnp.bfloat16)
        new_kv_f = kv_ref[...].astype(jnp.float32)
        new_k = jnp.concatenate([new_kv_f[:, :HD]] * heads, axis=0)
        new_v = jnp.concatenate([new_kv_f[:, HD:]] * heads, axis=0)
        own = jnp.sum(stacked * new_k, axis=1, keepdims=True) * scaling
        row_of = lax.rem(lax.broadcasted_iota(jnp.int32, (tall, 1), 0), rows)
        row_wide = lax.rem(lax.broadcasted_iota(jnp.int32, (tall, ctx), 0), rows)
        for r in range(rows):
            row_copies[r].wait()
            part = nt_dot(narrow, kept[r, :, :HD])
            score[...] = jnp.where(row_wide == r, part, score[...]) if r else part

        for copy in copies[2:]:
            copy.wait()
        lane = lax.broadcasted_iota(jnp.int32, (rows, LANES), 1)
        square = (rows, rows)
        diagonal = lax.broadcasted_iota(jnp.int32, square, 0) == lax.broadcasted_iota(jnp.int32, square, 1)
        skip = lax.axis_index("tp") * (cols - piece)
        for s, u in grid.steps:
            to = grid.target((s, u))
            begin = pl.multiple_of(to * cols + skip, LANES)
            at = width + u * note
            out_refs[s][:, at : at + piece] = res_ref[:, pl.ds(begin, piece)]
            chosen = ids_ref[...] == to * EXPERTS // grid.ep
            across = jnp.sum(jnp.where(chosen, wts_ref[...], 0.0), axis=0, keepdims=True)
            weight = jnp.sum(
                jnp.where(diagonal, jnp.broadcast_to(across, square), 0.0), axis=1, keepdims=True
            )
            high = weight.astype(jnp.bfloat16).astype(jnp.float32)
            middle = (weight - high).astype(jnp.bfloat16).astype(jnp.float32)
            low = weight - high - middle
            tile = jnp.where(lane == 0, high, 0.0)
            tile = jnp.where(lane == 1, middle, tile)
            tile = jnp.where(lane == 2, low, tile)
            out_refs[s][:, at + piece : at + note] = tile.astype(jnp.bfloat16)

        length = jnp.zeros((tall, 1), jnp.int32)
        for r in range(rows):
            length = jnp.where(row_of == r, len_ref[r], length)
        place = lax.broadcasted_iota(jnp.int32, (tall, ctx), 1)
        scores = jnp.where(place < length, score[...] * scaling, -jnp.inf)
        peak = jnp.maximum(jnp.max(scores, axis=1, keepdims=True), own)
        exps = jnp.exp(scores - peak)
        own_exp = jnp.exp(own - peak)
        denominator = jnp.sum(exps, axis=1, keepdims=True) + own_exp
        prob = exps / denominator
        own_prob = (own_exp / denominator).astype(jnp.bfloat16).astype(jnp.float32)
        total = own_prob * new_v
        for r in range(rows):
            only = jnp.where(row_wide == r, prob, 0.0).astype(jnp.bfloat16)
            total = total + jnp.dot(only, kept[r, :, HD:], preferred_element_type=jnp.float32)
        for h in range(heads):
            value = total[h * rows : (h + 1) * rows].astype(jnp.bfloat16)
            for ref in out_refs:
                ref[:, h * HD : (h + 1) * HD] = value
        for copy in packs:
            copy.wait()

    return pl.pallas_call(
        kernel,
        name="attention",
        out_shape=[shape_of((rows, width + grid.x * note), jnp.bfloat16)] * grid.z
        + [shape_of((packed_rows, piece), jnp.bfloat16)],
        in_specs=[in_hbm()] * 10,
        out_specs=[vmem()] * grid.z + [in_hbm()],
        scratch_shapes=[
            pltpu.VMEM(queries.shape, jnp.bfloat16),
            pltpu.VMEM(new_kv.shape, jnp.bfloat16),
            pltpu.VMEM(residual.shape, jnp.bfloat16),
            pltpu.VMEM(route_ids.shape, jnp.int32),
            pltpu.VMEM(route_weights.shape, jnp.float32),
            pltpu.SMEM(lengths.shape, jnp.int32),
            pltpu.VMEM(cache.shape, jnp.bfloat16),
            pltpu.VMEM((tall, ctx), jnp.float32),
            pltpu.SemaphoreType.DMA((6,)),
            pltpu.SemaphoreType.DMA((rows,)),
            pltpu.SemaphoreType.DMA((2 * grid.ep + down_blocks,)),
        ],
        compiler_params=params(60),
    )(
        queries,
        new_kv,
        residual,
        route_ids,
        route_weights,
        lengths,
        cache,
        gate_t,
        up_t,
        w_down,
    )


def project(grid, piece, chunks, w_out):
    rows = chunks[0].shape[0]
    depth, cols = w_out.shape
    count = len(chunks)
    tall = rows * count
    blocks = 8
    block = depth // blocks
    note = piece + LANES

    def kernel(*refs):
        chunk_refs, rest = refs[:count], refs[count:]
        w_ref, ours_ref, theirs_ref, weight_ref, stacked, total = rest
        k = pl.program_id(0)

        @pl.when(k == 0)
        def _():
            both = jnp.concatenate([ref[:, :depth] for ref in chunk_refs], axis=0)
            for i in range(blocks):
                stacked[i] = both[:, i * block : (i + 1) * block]

        product = jnp.dot(stacked[k], w_ref[...], preferred_element_type=jnp.float32)

        @pl.when(k == 0)
        def _():
            total[...] = product

        @pl.when(k > 0)
        def _():
            total[...] += product

        @pl.when(k == blocks - 1)
        def _():
            core = lax.axis_index("tp")
            mine = pl.multiple_of(core * (cols - piece), LANES)
            other = pl.multiple_of((1 - core) * (cols - piece), LANES)
            for i, (s, u) in enumerate(grid.steps):
                here = pl.ds(pl.multiple_of(grid.source((s, u)) * rows, rows), rows)
                at = depth + u * note
                beside = chunk_refs[i][:, at : at + note].astype(jnp.float32)
                block_rows = slice(i * rows, (i + 1) * rows)
                ours_ref[here, :] = total[block_rows, pl.ds(mine, piece)] + beside[:, :piece]
                theirs_ref[here, :] = total[block_rows, pl.ds(other, piece)]
                weight_ref[here, :] = jnp.broadcast_to(
                    jnp.sum(beside[:, piece:], axis=1, keepdims=True), (rows, LANES)
                )

    def whole(arr):
        return pl.BlockSpec(arr.shape, lambda k: (0, 0))

    outs = [shape_of((tall, piece), jnp.float32)] * 2 + [shape_of((tall, LANES), jnp.float32)]
    return pl.pallas_call(
        kernel,
        name="project",
        grid=(blocks,),
        out_shape=outs,
        in_specs=[whole(c) for c in chunks] + [pl.BlockSpec((block, cols), lambda k: (k, 0))],
        out_specs=[whole(o) for o in outs],
        scratch_shapes=[
            pltpu.VMEM((blocks, tall, block), jnp.bfloat16),
            pltpu.VMEM((tall, cols), jnp.float32),
        ],
        cost_estimate=pl.CostEstimate(
            flops=2 * tall * depth * cols,
            bytes_accessed=2 * depth * cols + 2 * tall * depth + 8 * tall * piece,
            transcendentals=0,
        ),
        compiler_params=params(48),
    )(*chunks, w_out)


def gate_up(grid, piece, cols, rows, pieces, gain, gate_t, up_t, other):
    tall = pieces[0].shape[0]
    units = gate_t.shape[0]
    count = grid.ep
    dup = 2 * piece - cols
    per_half = count // 2
    sums_width = 4 * units + LANES
    extra = -(-per_half * piece // sums_width)

    def kernel(*refs):
        piece_refs, rest = refs[:count], refs[count:]
        gain_ref, gate_ref, up_ref, other_ref, sums_ref, home_ref, held, home = rest
        home[1] = jnp.zeros((rows, extra * sums_width), jnp.float32)
        core = lax.axis_index("tp")
        me = lax.axis_index("ep")
        fresh = lax.broadcasted_iota(jnp.int32, (tall, piece), 1) >= core * dup
        square = jnp.zeros((tall, 1), jnp.float32)
        own_gate = jnp.zeros((units, tall), jnp.float32)
        own_up = jnp.zeros((units, tall), jnp.float32)
        far = jnp.zeros((2 * units, tall), jnp.float32)
        for i, step in enumerate(grid.steps):
            j = grid.source(step)
            lanes = pl.ds(pl.multiple_of(j * cols + core * (cols - piece), LANES), piece)
            stream = piece_refs[i][...].astype(jnp.float32)
            held[...] = stream
            mine = held[pl.ds(pl.multiple_of(me * rows, rows), rows), :]
            side = lax.rem(j // per_half + core, 2)
            at = pl.multiple_of(lax.rem(j, per_half) * piece, LANES)
            home[side, :, pl.ds(at, piece)] = mine
            stream = jnp.where(fresh, stream, 0.0)
            square = square + jnp.sum(stream * stream, axis=1, keepdims=True)
            scaled = (stream * gain_ref[:, lanes]).astype(jnp.bfloat16)
            own_gate = own_gate + nt_dot(gate_ref[:, lanes], scaled)
            own_up = own_up + nt_dot(up_ref[:, lanes], scaled)
            block = pl.ds(pl.multiple_of(j * 2 * units, 2 * units), 2 * units)
            far = far + nt_dot(other_ref[block, :], scaled)
        sums_ref[:tall, : 4 * units] = jnp.concatenate([own_gate, own_up, far], axis=0).T
        sums_ref[:tall, 4 * units :] = jnp.broadcast_to(square, (tall, LANES))
        for b in range(extra):
            at = tall + b * rows
            sums_ref[at : at + rows, :] = home[1, :, b * sums_width : (b + 1) * sums_width]
        home_ref[...] = home[0, :, : per_half * piece]

    return pl.pallas_call(
        kernel,
        name="gate_up",
        out_shape=[
            shape_of((tall + extra * rows, sums_width), jnp.float32),
            shape_of((rows, per_half * piece), jnp.float32),
        ],
        in_specs=[vmem()] * (count + 4),
        out_specs=[vmem()] * 2,
        scratch_shapes=[
            pltpu.VMEM((tall, piece), jnp.float32),
            pltpu.VMEM((2, rows, extra * sums_width), jnp.float32),
        ],
        compiler_params=params(8),
    )(*pieces, gain, gate_t, up_t, other)


def down(grid, piece, rows, sums, far_sums, weight, w_down, far_weights):
    tall = weight.shape[0]
    units, width = w_down.shape
    out_width = width // 2
    count = grid.ep

    def kernel(sums_ref, far_ref, weight_ref, down_ref, packed_ref, *rest):
        out_refs, total, down_half, sem = rest[:count], rest[count], rest[count + 1], rest[count + 2]
        begin = pl.multiple_of(lax.axis_index("tp") * out_width, LANES)
        copy = pltpu.make_async_copy(down_ref.at[:, pl.ds(begin, out_width)], down_half, sem)
        copy.start()
        square = (
            sums_ref[:tall, 4 * units : 4 * units + 1] + far_ref[:tall, 4 * units : 4 * units + 1]
        )
        scale = lax.rsqrt(square / width + 1e-06)

        def hidden(a, b):
            both = (
                sums_ref[:tall, a * units : (a + 2) * units]
                + far_ref[:tall, b * units : (b + 2) * units]
            )
            gate, up = both[:, :units] * scale, both[:, units:] * scale
            return (gate / (1.0 + jnp.exp(-gate)) * up).astype(jnp.bfloat16)

        near, far = hidden(0, 2), hidden(2, 0)
        copy.wait()
        for b in range(out_width // piece):
            span = slice(b * piece, (b + 1) * piece)
            block = slice((2 * count + b) * units, (2 * count + b + 1) * units)
            value = jnp.dot(near, down_half[:, span], preferred_element_type=jnp.float32)
            value = value + jnp.dot(far, packed_ref[block, :], preferred_element_type=jnp.float32)
            total[:, span] = value * weight_ref[:, :1]
        for i, step in enumerate(grid.steps):
            there = pl.ds(pl.multiple_of(grid.target(step) * rows, rows), rows)
            out_refs[i][...] = total[there, :].astype(out_refs[i].dtype)

    return pl.pallas_call(
        kernel,
        name="down",
        out_shape=[
            shape_of((rows, out_width), jnp.bfloat16 if i else jnp.float32) for i in range(count)
        ],
        in_specs=[vmem()] * 3 + [pl.BlockSpec(memory_space=pl.ANY), vmem()],
        out_specs=[vmem()] * count,
        scratch_shapes=[
            pltpu.VMEM((tall, out_width), jnp.float32),
            pltpu.VMEM((units, out_width), jnp.bfloat16),
            pltpu.SemaphoreType.DMA(()),
        ],
        compiler_params=params(8),
    )(sums, far_sums, weight, w_down, far_weights)


def finish(piece, cols, near, far_sums, parts):
    rows, out_width = parts[0].shape
    extra = -(-near.shape[1] // far_sums.shape[1])
    top = far_sums.shape[0] - extra * rows
    dup = 2 * piece - cols

    def kernel(near_ref, far_ref, *rest):
        part_refs, out_ref = rest[:-1], rest[-1]
        first = lax.axis_index("tp") == 0
        far = jnp.concatenate(
            [far_ref[top + b * rows : top + (b + 1) * rows, :] for b in range(extra)], axis=1
        )
        for c in range(out_width // cols):
            span = slice(c * piece, (c + 1) * piece)
            a, b = near_ref[:, span], far[:, span]
            low = jnp.where(first, a, b)
            high = jnp.where(first, b, a)[:, dup:]
            value = jnp.concatenate([low, high], axis=1)
            for ref in part_refs:
                value = value + ref[:, c * cols : (c + 1) * cols].astype(jnp.float32)
            out_ref[:, c * cols : (c + 1) * cols] = value.astype(jnp.bfloat16)

    return pl.pallas_call(
        kernel,
        name="finish",
        out_shape=shape_of((rows, out_width), jnp.bfloat16),
        in_specs=[vmem()] * (2 + len(parts)),
        out_specs=vmem(),
        compiler_params=params(4),
    )(near, far_sums, *parts)


def tuned_body(
    grid,
    residual,
    queries,
    new_kv,
    cache,
    lengths,
    w_out,
    gain,
    route_ids,
    route_weights,
    w_gate,
    w_up,
    w_down,
):
    rows, width = residual.shape
    cols = w_out.shape[1]
    piece = -(-cols // (2 * LANES)) * LANES
    gate_t, up_t = w_gate.T, w_up.T
    *outgoing, packed = attention(
        grid,
        piece,
        cols,
        queries,
        new_kv,
        cache,
        lengths,
        residual,
        route_ids.T,
        route_weights.T,
        gate_t,
        up_t,
        w_down,
    )
    chunks = grid.spread(outgoing)
    packed, *_ = lax.optimization_barrier((packed, *chunks))
    far_weights = swap(packed)
    ours, theirs, weight = project(grid, piece, chunks, w_out)
    stream = (ours + swap(theirs)).astype(jnp.bfloat16)
    stream, far_weights = lax.optimization_barrier((stream, far_weights))
    pieces = grid.spread([stream] * grid.z)
    sums, home = gate_up(
        grid, piece, cols, rows, pieces, gain.reshape(1, width), gate_t, up_t, far_weights
    )
    far_sums = swap(sums)
    parts = down(grid, piece, rows, sums, far_sums, weight, w_down, far_weights)
    shares = [grid.send(p, s, u) if s or u else p for p, (s, u) in zip(parts, grid.steps)]
    return finish(piece, cols, home, far_sums, shares)


def general_body(
    residual,
    queries,
    new_kv,
    cache,
    lengths,
    w_out,
    gain,
    route_ids,
    route_weights,
    w_gate,
    w_up,
    w_down,
):
    row_count = queries.shape[0]
    head_count = queries.shape[1] // HD
    scaling = HD ** (-0.5)
    query_heads = queries.reshape(row_count, head_count, HD)
    key_rows = cache[:, :, :HD]
    value_rows = cache[:, :, HD:]
    scores = (
        jnp.einsum("rhd,rpd->rhp", query_heads, key_rows, preferred_element_type=jnp.float32)
        * scaling
    )
    usable = jnp.arange(cache.shape[1], dtype=jnp.int32)[None, :] < lengths[:, None]
    scores = jnp.where(usable[:, None, :], scores, -jnp.inf)
    own_score = (
        jnp.einsum("rhd,rd->rh", query_heads, new_kv[:, :HD], preferred_element_type=jnp.float32)
        * scaling
    )
    peak_score = jnp.maximum(jnp.max(scores, axis=2), own_score)
    cache_weight = jnp.exp(scores - peak_score[:, :, None])
    own_weight = jnp.exp(own_score - peak_score)
    denominator = jnp.sum(cache_weight, axis=2) + own_weight
    probabilities = (cache_weight / denominator[:, :, None]).astype(jnp.bfloat16)
    own_prob = (own_weight / denominator).astype(jnp.bfloat16)
    context = jnp.einsum(
        "rhp,rpd->rhd", probabilities, value_rows, preferred_element_type=jnp.float32
    )
    context = context + own_prob.astype(jnp.float32)[:, :, None] * new_kv[:, None, HD:].astype(
        jnp.float32
    )
    context = context.astype(jnp.bfloat16).reshape(row_count, head_count * HD)
    attn_cols = jnp.dot(
        lax.all_gather(context, "ep", axis=0, tiled=True), w_out, preferred_element_type=jnp.float32
    )
    attn_rows = lax.all_to_all(attn_cols, "ep", split_axis=0, concat_axis=1, tiled=True)
    attention = lax.psum(attn_rows, "tp")
    stream = residual.astype(jnp.float32) + attention
    mean_square = jnp.mean(stream * stream, axis=1, keepdims=True)
    normed = (stream * lax.rsqrt(mean_square + 1e-06) * gain[None, :]).astype(jnp.bfloat16)
    width = normed.shape[1]
    ep_size = lax.axis_size("ep")
    members = ep_size // EXPERTS
    slot_count = EXPERTS * CAP
    flat_ids = route_ids.reshape(-1)
    one_hot = (flat_ids[:, None] == jnp.arange(EXPERTS, dtype=jnp.int32)[None, :]).astype(jnp.int32)
    earlier = jnp.cumsum(one_hot, axis=0) - one_hot
    slot_index = jnp.sum(earlier * one_hot, axis=1)
    target = (flat_ids * CAP + slot_index).reshape(row_count, TOPK)
    placed = (target[:, :, None] == jnp.arange(slot_count, dtype=jnp.int32)[None, None, :]).astype(
        jnp.float32
    )
    chosen = jnp.sum(placed, axis=1).reshape(row_count, EXPERTS, CAP).astype(jnp.bfloat16)
    mixing = jnp.sum(placed * route_weights[:, :, None], axis=1).reshape(row_count, EXPERTS, CAP)
    outgoing = jnp.einsum("rec,rd->ecd", chosen, normed, preferred_element_type=jnp.float32).astype(
        jnp.bfloat16
    )
    outgoing = jnp.broadcast_to(outgoing[:, None], (EXPERTS, members, CAP, width)).reshape(
        ep_size * CAP, width
    )
    arrived = lax.all_to_all(outgoing, "ep", split_axis=0, concat_axis=0, tiled=True)
    gate_act = jnp.dot(arrived, w_gate, preferred_element_type=jnp.float32)
    up_act = jnp.dot(arrived, w_up, preferred_element_type=jnp.float32)
    hidden = (jax.nn.silu(gate_act) * up_act).astype(jnp.bfloat16)
    partial_value = jnp.dot(hidden, w_down, preferred_element_type=jnp.float32)
    halves = lax.psum_scatter(partial_value, "tp", scatter_dimension=1, tiled=True)
    returned = lax.all_to_all(halves, "ep", split_axis=0, concat_axis=0, tiled=True)
    returned = returned.reshape(EXPERTS, members, CAP, returned.shape[1])
    mixed = jnp.einsum("rec,egcw->rw", mixing, returned, precision=lax.Precision.HIGHEST)
    tp_start = lax.axis_index("tp") * mixed.shape[1]
    stream_part = lax.dynamic_slice_in_dim(stream, tp_start, mixed.shape[1], 1)
    return (stream_part + mixed).astype(jnp.bfloat16)


def body(*args):
    ep_size, cols, heads_width = lax.axis_size("ep"), args[5].shape[1], args[5].shape[0]
    if ep_size == 8 and lax.axis_size("tp") == 2 and cols % LANES == 0 and heads_width % (8 * HD) == 0:
        return tuned_body(Grid(ep_size, 2), *args)
    return general_body(*args)


def solution(mesh):
    placed = (
        P(("grp", "ep"), None),
        P(("grp", "ep"), "tp"),
        P(("grp", "ep"), None),
        P(("grp", "ep"), None, None),
        P(("grp", "ep")),
        P("tp", "ep"),
        P(),
        P(("grp", "ep"), None),
        P(("grp", "ep"), None),
        P(None, ("ep", "tp")),
        P(None, ("ep", "tp")),
        P(("ep", "tp"), None),
    )
    return jax.shard_map(
        body, mesh=mesh, in_specs=placed, out_specs=P(("grp", "ep"), "tp"), check_vma=False
    )
```

time: 111 us -> 189 us (1.70)
  Pallas kernels: 23.1 us -> 129 us
  starting transfers between devices: 43.7 us -> 33.5 us
  local copies, waits for them, and re-layouts: 9.85 us -> 1.08 us
  waiting for transfers between devices: 33.8 us -> 25.3 us
    pallas_call x1, Pallas kernels: 6.13 us -> 116 us  [attention(): pl.pallas_call(kernel, name='attention', out_shape=[shape_of((rows, width...]
    ppermute x35 -> x21, starting transfers between devices: 43 us -> 33.3 us  [send(): return lax.ppermute(arr, 'ep', pairs)]
    unnamed x24 -> x10, local copies, waits for them, and re-layouts: 9.84 us -> 1.08 us
    ppermute x35 -> x21, waiting for transfers between devices: 30.8 us -> 22.4 us  [send(): return lax.ppermute(arr, 'ep', pairs)]
    pallas_call x4 -> x2, Pallas kernels: 15.5 us -> 11.1 us  [the longest x1 9.39 us: project(): pl.pallas_call(kernel, name='project', grid=(blocks,), out_shape=outs, in...]
  transfers between devices with their start and end apart: 40 -> 24, of which waited for: 21 -> 12; matrix products, arithmetic and copies ran while one was open for 0% -> 0% of each run, Pallas kernels for 12% -> 5%
where the time goes in v3:
time: 189 us
  Pallas kernels  129 us (68%)
  starting transfers between devices  33.5 us (18%)
  waiting for transfers between devices  25.3 us (13%)
    pallas_call x1, Pallas kernels, attention(): pl.pallas_call(kernel, name='attention', out_shape=[shape_of((rows, width...  116 us
    ppermute x21, starting transfers between devices, send(): return lax.ppermute(arr, 'ep', pairs)  33.3 us
    ppermute x21, waiting for transfers between devices, send(): return lax.ppermute(arr, 'ep', pairs)  22.4 us
    pallas_call x1, Pallas kernels, project(): pl.pallas_call(kernel, name='project', grid=(blocks,), out_shape=outs, in...  9.39 us
  transfers between devices with their start and end apart: 24, of which 12 were waited for; matrix products, arithmetic and copies ran while one was open for 0% of the time, Pallas kernels for 5%

profile of v3, /device:TPU:0, one launch (start us, length us, event | category | flops | bytes accessed | tf_op | source)
XLA Modules:
  0.0 189.0 jit_solution(9128577819818027152)
XLA Ops:
  0.0 116.4 %attention.1 = (bf16[8,9472]{1,0:T(8,128)(2,1)}, bf16[8,9472]{1,0:T(8,128)(2,1)}, bf16[8,9472]{1,0:T(8,128)(2,1)}, bf16[8,9472]{1,0:T(8,128)(2,1)}, bf16[3680,512]{1,0:T(8,128)(2,1)}) custom-call(bf16[8,8192]{1,0:T(8,128)(2,1)} %refs_0_.1, bf16[8,512]{1,0:T(8,128)(2,1)} %refs_1_.1, bf16[8,7168]{1,0:T(8,128)(2,1)} %refs_2_.1, s32[3,8]{1,0:T(4,128)} %bitcast.10, ...), custom_call_target="tpu_custom_call" | custom-call | tf_op jit(solution)/shard_map/attention/pallas_call | solution.py:194
  116.4 3.1 %collective-permute-start.1 = (bf16[8,9472]{1,0:T(8,128)(2,1)}, bf16[8,9472]{1,0:T(8,128)(2,1)S(1)}, u32[]{:S(2)}, u32[]{:S(2)}) collective-permute-start(bf16[8,9472]{1,0:T(8,128)(2,1)} %get-tuple-element.27), channel_id=1, source_target_pairs={{0,4},{2,6},{4,8},{6,10},{8,12},{10,14},{12,0},{14,2},{1,5},{3,7},... | collective-permute-start | bytes 454664 | tf_op jit(solution)/shard_map/ppermute | solution.py:44
  119.5 2.6 %collective-permute-start.3 = (bf16[8,9472]{1,0:T(8,128)(2,1)}, bf16[8,9472]{1,0:T(8,128)(2,1)S(1)}, u32[]{:S(2)}, u32[]{:S(2)}) collective-permute-start(bf16[8,9472]{1,0:T(8,128)(2,1)} %get-tuple-element.28), channel_id=1, source_target_pairs={{0,8},{2,10},{4,12},{6,14},{8,0},{10,2},{12,4},{14,6},{1,9},{3,11}... | collective-permute-start | bytes 454664 | tf_op jit(solution)/shard_map/ppermute | solution.py:44
  122.1 1.3 collective-permute-start.5
  123.5 1.5 collective-permute-start
  125.0 1.7 collective-permute-done.1.refs_2_
  126.6 1.7 collective-permute-start.2
  128.4 3.9 %collective-permute-done.3.refs_4_ = bf16[8,9472]{1,0:T(8,128)(2,1)S(1)} collective-permute-done((bf16[8,9472]{1,0:T(8,128)(2,1)}, bf16[8,9472]{1,0:T(8,128)(2,1)S(1)}, u32[]{:S(2)}, u32[]{:S(2)}) %collective-permute-start.3) | collective-permute-done | bytes 151584 | tf_op jit(solution)/shard_map/ppermute | solution.py:44
  132.3 1.5 collective-permute-start.4
  133.8 0.0 collective-permute-done.5.refs_6_
  133.8 0.5 collective-permute-start.6
  134.3 0.0 collective-permute-done.refs_1_
  134.3 0.0 collective-permute-done.2.refs_3_
  134.3 4.8 %collective-permute-done.4.refs_5_ = bf16[8,9472]{1,0:T(8,128)(2,1)S(1)} collective-permute-done((bf16[8,9472]{1,0:T(8,128)(2,1)S(1)}, bf16[8,9472]{1,0:T(8,128)(2,1)S(1)}, u32[]{:S(2)}, u32[]{:S(2)}) %collective-permute-start.4) | collective-permute-done | bytes 151584 | tf_op jit(solution)/shard_map/ppermute | solution.py:44
  139.1 2.2 %collective-permute-done.6.refs_7_ = bf16[8,9472]{1,0:T(8,128)(2,1)S(1)} collective-permute-done((bf16[8,9472]{1,0:T(8,128)(2,1)S(1)}, bf16[8,9472]{1,0:T(8,128)(2,1)S(1)}, u32[]{:S(2)}, u32[]{:S(2)}) %collective-permute-start.6) | collective-permute-done | bytes 151584 | tf_op jit(solution)/shard_map/ppermute | solution.py:44
  141.3 0.0 copy-start
  141.3 0.0 copy-start.1
  141.3 0.0 collective-permute-start.8
  141.3 0.0 copy-start.3
  141.3 1.1 copy-done.3
  142.4 0.0 copy-start.4
  142.4 9.4 %project.1 = (f32[64,512]{1,0:T(8,128)S(1)}, f32[64,512]{1,0:T(8,128)S(1)}, f32[64,128]{1,0:T(8,128)S(1)}) custom-call(bf16[8,9472]{1,0:T(8,128)(2,1)S(1)} %copy-done.3, bf16[8,9472]{1,0:T(8,128)(2,1)S(1)} %collective-permute-done.refs_1_, bf16[8,9472]{1,0:T(8,128)(2,1)S(1)} %collective-permute-done.1.refs_2_, ...), custom_call_target="tpu_custom_call" | custom-call | flops 939524096 | bytes 15990784 | tf_op jit(solution)/shard_map/project/pallas_call | solution.py:279
  151.8 0.1 collective-permute-start.7
  151.9 1.3 collective-permute-done.7
  153.2 0.0 collective-permute-done.8.refs_11_.packed_ref
  153.2 3.9 %collective-permute-start.14 = (bf16[64,512]{1,0:T(8,128)(2,1)S(1)}, bf16[64,512]{1,0:T(8,128)(2,1)S(1)}, u32[]{:S(2)}, u32[]{:S(2)}) collective-permute-start(bf16[64,512]{1,0:T(8,128)(2,1)S(1)} %add_convert_fusion.refs_0_), channel_id=1, source_target_pairs={{0,12},{2,14},{4,0},{6,2},{8,4},{10,6},{12,8},{14,10},{1,13},{3,15... | collective-permute-start | bytes 196616 | tf_op jit(solution)/shard_map/ppermute | solution.py:44
  157.1 0.3 collective-permute-start.12
  157.4 0.8 collective-permute-start.10
  158.1 1.5 collective-permute-start.9
  159.6 0.0 collective-permute-done.14.refs_6_
  159.6 1.4 collective-permute-start.15
  161.1 2.9 %collective-permute-done.12.refs_4_ = bf16[64,512]{1,0:T(8,128)(2,1)S(1)} collective-permute-done((bf16[64,512]{1,0:T(8,128)(2,1)S(1)}, bf16[64,512]{1,0:T(8,128)(2,1)S(1)}, u32[]{:S(2)}, u32[]{:S(2)}) %collective-permute-start.12) | collective-permute-done | bytes 65568 | tf_op jit(solution)/shard_map/ppermute | solution.py:44
  164.0 1.5 collective-permute-start.13
  165.5 0.0 collective-permute-done.10.refs_2_
  165.5 0.5 collective-permute-start.11
  166.0 0.0 collective-permute-done.9.refs_1_
  166.0 0.0 collective-permute-done.15.refs_7_
  166.0 2.8 %collective-permute-done.13.refs_5_ = bf16[64,512]{1,0:T(8,128)(2,1)S(1)} collective-permute-done((bf16[64,512]{1,0:T(8,128)(2,1)S(1)}, bf16[64,512]{1,0:T(8,128)(2,1)S(1)}, u32[]{:S(2)}, u32[]{:S(2)}) %collective-permute-start.13) | collective-permute-done | bytes 65568 | tf_op jit(solution)/shard_map/ppermute | solution.py:44
  168.8 1.0 collective-permute-done.11.refs_3_
  169.7 0.0 copy-done
  169.7 0.0 copy-done.1
  169.7 0.0 copy-done.4
  169.7 0.0 copy-start.2
  169.8 1.7 gate_up.1
  171.4 0.1 collective-permute-start.16
  171.5 1.5 collective-permute-done.16.far_ref
  173.0 0.0 copy-done.2
  173.0 0.9 down.1
  173.9 1.1 collective-permute-start.17
  175.0 0.0 collective-permute-start.18
  175.0 1.3 collective-permute-start.19
  176.3 3.5 %collective-permute-start.20 = (bf16[8,3584]{1,0:T(8,128)(2,1)S(1)}, bf16[8,3584]{1,0:T(8,128)(2,1)S(1)}, u32[]{:S(2)}, u32[]{:S(2)}) collective-permute-start(bf16[8,3584]{1,0:T(8,128)(2,1)S(1)} %get-tuple-element.43), channel_id=1, source_target_pairs={{0,8},{2,10},{4,12},{6,14},{8,0},{10,2},{12,4},{14,6},{1,9},{3,11}... | collective-permute-start | bytes 172040 | tf_op jit(solution)/shard_map/ppermute | solution.py:44
  179.8 0.5 collective-permute-start.21
  180.3 0.0 collective-permute-done.17.rest_1_
  180.3 2.4 %collective-permute-start.22 = (bf16[8,3584]{1,0:T(8,128)(2,1)S(1)}, bf16[8,3584]{1,0:T(8,128)(2,1)S(1)}, u32[]{:S(2)}, u32[]{:S(2)}) collective-permute-start(bf16[8,3584]{1,0:T(8,128)(2,1)S(1)} %get-tuple-element.45), channel_id=1, source_target_pairs={{0,12},{2,14},{4,0},{6,2},{8,4},{10,6},{12,8},{14,10},{1,13},{3,15... | collective-permute-start | bytes 172040 | tf_op jit(solution)/shard_map/ppermute | solution.py:44
  182.7 0.0 collective-permute-done.18.rest_2_
  182.7 2.4 %collective-permute-start.23 = (bf16[8,3584]{1,0:T(8,128)(2,1)S(1)}, bf16[8,3584]{1,0:T(8,128)(2,1)S(1)}, u32[]{:S(2)}, u32[]{:S(2)}) collective-permute-start(bf16[8,3584]{1,0:T(8,128)(2,1)S(1)} %get-tuple-element.46), channel_id=1, source_target_pairs={{0,14},{2,12},{4,2},{6,0},{8,6},{10,4},{12,10},{14,8},{1,15},{3,13... | collective-permute-start | bytes 172040 | tf_op jit(solution)/shard_map/ppermute | solution.py:44
  185.1 0.0 collective-permute-done.19.rest_3_
  185.1 0.4 collective-permute-done.20.rest_4_
  185.5 1.7 collective-permute-done.21.rest_5_
  187.2 0.0 collective-permute-done.22.rest_6_
  187.2 1.1 collective-permute-done.23.rest_7_
  188.3 0.7 finish.1
  (1 shorter events, 0.0 us)
Async XLA Ops:
  116.4 10.2 %collective-permute-start.1 = (bf16[8,9472]{1,0:T(8,128)(2,1)}, bf16[8,9472]{1,0:T(8,128)(2,1)S(1)}, u32[]{:S(2)}, u32[]{:S(2)}) collective-permute-start(bf16[8,9472]{1,0:T(8,128)(2,1)} %get-tuple-element.27), channel_id=1, source_target_pairs={{0,4},{2,6},{4,8},{6,10},{8,12},{10,14},{12,0},{14,2},{1,5},{3,7},... | collective-permute-start | bytes 454664 | tf_op jit(solution)/shard_map/ppermute | solution.py:44
  119.5 12.8 %collective-permute-start.3 = (bf16[8,9472]{1,0:T(8,128)(2,1)}, bf16[8,9472]{1,0:T(8,128)(2,1)S(1)}, u32[]{:S(2)}, u32[]{:S(2)}) collective-permute-start(bf16[8,9472]{1,0:T(8,128)(2,1)} %get-tuple-element.28), channel_id=1, source_target_pairs={{0,8},{2,10},{4,12},{6,14},{8,0},{10,2},{12,4},{14,6},{1,9},{3,11}... | collective-permute-start | bytes 454664 | tf_op jit(solution)/shard_map/ppermute | solution.py:44
  122.1 11.7 %collective-permute-start.5 = (bf16[8,9472]{1,0:T(8,128)(2,1)}, bf16[8,9472]{1,0:T(8,128)(2,1)S(1)}, u32[]{:S(2)}, u32[]{:S(2)}) collective-permute-start(bf16[8,9472]{1,0:T(8,128)(2,1)} %get-tuple-element.29), channel_id=1, source_target_pairs={{0,12},{2,14},{4,0},{6,2},{8,4},{10,6},{12,8},{14,10},{1,13},{3,15... | collective-permute-start | bytes 454664 | tf_op jit(solution)/shard_map/ppermute | solution.py:44
  123.5 10.9 %collective-permute-start = (bf16[8,9472]{1,0:T(8,128)(2,1)}, bf16[8,9472]{1,0:T(8,128)(2,1)S(1)}, u32[]{:S(2)}, u32[]{:S(2)}) collective-permute-start(bf16[8,9472]{1,0:T(8,128)(2,1)} %get-tuple-element.26.refs_0_), channel_id=1, source_target_pairs={{0,2},{2,0},{4,6},{6,4},{8,10},{10,8},{12,14},{14,12},{1,3},{3,1},... | collective-permute-start | bytes 454664 | tf_op jit(solution)/shard_map/ppermute | solution.py:44
  126.6 7.7 %collective-permute-start.2 = (bf16[8,9472]{1,0:T(8,128)(2,1)S(1)}, bf16[8,9472]{1,0:T(8,128)(2,1)S(1)}, u32[]{:S(2)}, u32[]{:S(2)}) collective-permute-start(bf16[8,9472]{1,0:T(8,128)(2,1)S(1)} %collective-permute-done.1.refs_2_), channel_id=1, source_target_pairs={{0,2},{2,0},{4,6},{6,4},{8,10},{10,8},{12,14},{14,12},{1,3},{3,1},... | collective-permute-start | bytes 454664 | tf_op jit(solution)/shard_map/ppermute | solution.py:44
  132.3 6.8 %collective-permute-start.4 = (bf16[8,9472]{1,0:T(8,128)(2,1)S(1)}, bf16[8,9472]{1,0:T(8,128)(2,1)S(1)}, u32[]{:S(2)}, u32[]{:S(2)}) collective-permute-start(bf16[8,9472]{1,0:T(8,128)(2,1)S(1)} %collective-permute-done.3.refs_4_), channel_id=1, source_target_pairs={{0,2},{2,0},{4,6},{6,4},{8,10},{10,8},{12,14},{14,12},{1,3},{3,1},... | collective-permute-start | bytes 454664 | tf_op jit(solution)/shard_map/ppermute | solution.py:44
  133.8 7.5 %collective-permute-start.6 = (bf16[8,9472]{1,0:T(8,128)(2,1)S(1)}, bf16[8,9472]{1,0:T(8,128)(2,1)S(1)}, u32[]{:S(2)}, u32[]{:S(2)}) collective-permute-start(bf16[8,9472]{1,0:T(8,128)(2,1)S(1)} %collective-permute-done.5.refs_6_), channel_id=1, source_target_pairs={{0,2},{2,0},{4,6},{6,4},{8,10},{10,8},{12,14},{14,12},{1,3},{3,1},... | collective-permute-start | bytes 454664 | tf_op jit(solution)/shard_map/ppermute | solution.py:44
  141.3 28.4 %copy-start = (bf16[7168,160]{0,1:T(8,128)(2,1)S(1)}, bf16[7168,160]{0,1:T(8,128)(2,1)}, u32[]{:S(2)}) copy-start(bf16[7168,160]{0,1:T(8,128)(2,1)} %param.21) | copy-start | bytes 6881284
  141.3 28.4 %copy-start.1 = (bf16[7168,160]{0,1:T(8,128)(2,1)S(1)}, bf16[7168,160]{0,1:T(8,128)(2,1)}, u32[]{:S(2)}) copy-start(bf16[7168,160]{0,1:T(8,128)(2,1)} %param.22) | copy-start | bytes 6881284
  141.3 11.9 %collective-permute-start.8 = (bf16[3680,512]{1,0:T(8,128)(2,1)}, bf16[3680,512]{1,0:T(8,128)(2,1)S(1)}, u32[]{:S(2)}, u32[]{:S(2)}) collective-permute-start(bf16[3680,512]{1,0:T(8,128)(2,1)} %get-tuple-element.33), channel_id=1, source_target_pairs={{0,1},{1,0},{2,3},{3,2},{4,5},{5,4},{6,7},{7,6},{8,9},{9,8},{10,11... | collective-permute-start | bytes 11304968 | tf_op jit(solution)/shard_map/ppermute | solution.py:65
  141.3 1.1 copy-start.3
  142.4 27.4 %copy-start.4 = (f32[7168]{0:T(1024)S(1)}, f32[7168]{0:T(1024)}, u32[]{:S(2)}) copy-start(f32[7168]{0:T(1024)} %param.18) | copy-start | bytes 86020
  151.8 1.4 collective-permute-start.7
  153.2 6.4 %collective-permute-start.14 = (bf16[64,512]{1,0:T(8,128)(2,1)S(1)}, bf16[64,512]{1,0:T(8,128)(2,1)S(1)}, u32[]{:S(2)}, u32[]{:S(2)}) collective-permute-start(bf16[64,512]{1,0:T(8,128)(2,1)S(1)} %add_convert_fusion.refs_0_), channel_id=1, source_target_pairs={{0,12},{2,14},{4,0},{6,2},{8,4},{10,6},{12,8},{14,10},{1,13},{3,15... | collective-permute-start | bytes 196616 | tf_op jit(solution)/shard_map/ppermute | solution.py:44
  157.1 6.9 %collective-permute-start.12 = (bf16[64,512]{1,0:T(8,128)(2,1)S(1)}, bf16[64,512]{1,0:T(8,128)(2,1)S(1)}, u32[]{:S(2)}, u32[]{:S(2)}) collective-permute-start(bf16[64,512]{1,0:T(8,128)(2,1)S(1)} %add_convert_fusion.refs_0_), channel_id=1, source_target_pairs={{0,8},{2,10},{4,12},{6,14},{8,0},{10,2},{12,4},{14,6},{1,9},{3,11}... | collective-permute-start | bytes 196616 | tf_op jit(solution)/shard_map/ppermute | solution.py:44
  157.4 8.1 %collective-permute-start.10 = (bf16[64,512]{1,0:T(8,128)(2,1)S(1)}, bf16[64,512]{1,0:T(8,128)(2,1)S(1)}, u32[]{:S(2)}, u32[]{:S(2)}) collective-permute-start(bf16[64,512]{1,0:T(8,128)(2,1)S(1)} %add_convert_fusion.refs_0_), channel_id=1, source_target_pairs={{0,4},{2,6},{4,8},{6,10},{8,12},{10,14},{12,0},{14,2},{1,5},{3,7},... | collective-permute-start | bytes 196616 | tf_op jit(solution)/shard_map/ppermute | solution.py:44
  158.1 7.9 %collective-permute-start.9 = (bf16[64,512]{1,0:T(8,128)(2,1)S(1)}, bf16[64,512]{1,0:T(8,128)(2,1)S(1)}, u32[]{:S(2)}, u32[]{:S(2)}) collective-permute-start(bf16[64,512]{1,0:T(8,128)(2,1)S(1)} %add_convert_fusion.refs_0_), channel_id=1, source_target_pairs={{0,2},{2,0},{4,6},{6,4},{8,10},{10,8},{12,14},{14,12},{1,3},{3,1},... | collective-permute-start | bytes 196616 | tf_op jit(solution)/shard_map/ppermute | solution.py:44
  159.6 6.4 %collective-permute-start.15 = (bf16[64,512]{1,0:T(8,128)(2,1)S(1)}, bf16[64,512]{1,0:T(8,128)(2,1)S(1)}, u32[]{:S(2)}, u32[]{:S(2)}) collective-permute-start(bf16[64,512]{1,0:T(8,128)(2,1)S(1)} %collective-permute-done.14.refs_6_), channel_id=1, source_target_pairs={{0,2},{2,0},{4,6},{6,4},{8,10},{10,8},{12,14},{14,12},{1,3},{3,1},... | collective-permute-start | bytes 196616 | tf_op jit(solution)/shard_map/ppermute | solution.py:44
  164.0 4.8 %collective-permute-start.13 = (bf16[64,512]{1,0:T(8,128)(2,1)S(1)}, bf16[64,512]{1,0:T(8,128)(2,1)S(1)}, u32[]{:S(2)}, u32[]{:S(2)}) collective-permute-start(bf16[64,512]{1,0:T(8,128)(2,1)S(1)} %collective-permute-done.12.refs_4_), channel_id=1, source_target_pairs={{0,2},{2,0},{4,6},{6,4},{8,10},{10,8},{12,14},{14,12},{1,3},{3,1},... | collective-permute-start | bytes 196616 | tf_op jit(solution)/shard_map/ppermute | solution.py:44
  165.5 4.3 %collective-permute-start.11 = (bf16[64,512]{1,0:T(8,128)(2,1)S(1)}, bf16[64,512]{1,0:T(8,128)(2,1)S(1)}, u32[]{:S(2)}, u32[]{:S(2)}) collective-permute-start(bf16[64,512]{1,0:T(8,128)(2,1)S(1)} %collective-permute-done.10.refs_2_), channel_id=1, source_target_pairs={{0,2},{2,0},{4,6},{6,4},{8,10},{10,8},{12,14},{14,12},{1,3},{3,1},... | collective-permute-start | bytes 196616 | tf_op jit(solution)/shard_map/ppermute | solution.py:44
  169.7 3.3 %copy-start.2 = (bf16[160,7168]{1,0:T(8,128)(2,1)S(1)}, bf16[160,7168]{1,0:T(8,128)(2,1)}, u32[]{:S(2)}) copy-start(bf16[160,7168]{1,0:T(8,128)(2,1)} %down_ref.1) | copy-start | bytes 6881284
  171.4 1.6 collective-permute-start.16
  173.9 6.4 %collective-permute-start.17 = (bf16[8,3584]{1,0:T(8,128)(2,1)S(1)}, bf16[8,3584]{1,0:T(8,128)(2,1)S(1)}, u32[]{:S(2)}, u32[]{:S(2)}) collective-permute-start(bf16[8,3584]{1,0:T(8,128)(2,1)S(1)} %get-tuple-element.40), channel_id=1, source_target_pairs={{0,2},{2,0},{4,6},{6,4},{8,10},{10,8},{12,14},{14,12},{1,3},{3,1},... | collective-permute-start | bytes 172040 | tf_op jit(solution)/shard_map/ppermute | solution.py:44
  175.0 7.7 %collective-permute-start.18 = (bf16[8,3584]{1,0:T(8,128)(2,1)S(1)}, bf16[8,3584]{1,0:T(8,128)(2,1)S(1)}, u32[]{:S(2)}, u32[]{:S(2)}) collective-permute-start(bf16[8,3584]{1,0:T(8,128)(2,1)S(1)} %get-tuple-element.41), channel_id=1, source_target_pairs={{0,4},{2,6},{4,8},{6,10},{8,12},{10,14},{12,0},{14,2},{1,5},{3,7},... | collective-permute-start | bytes 172040 | tf_op jit(solution)/shard_map/ppermute | solution.py:44
  175.0 10.1 %collective-permute-start.19 = (bf16[8,3584]{1,0:T(8,128)(2,1)S(1)}, bf16[8,3584]{1,0:T(8,128)(2,1)S(1)}, u32[]{:S(2)}, u32[]{:S(2)}) collective-permute-start(bf16[8,3584]{1,0:T(8,128)(2,1)S(1)} %get-tuple-element.42), channel_id=1, source_target_pairs={{0,6},{2,4},{4,10},{6,8},{8,14},{10,12},{12,2},{14,0},{1,7},{3,5},... | collective-permute-start | bytes 172040 | tf_op jit(solution)/shard_map/ppermute | solution.py:44
  176.3 9.2 %collective-permute-start.20 = (bf16[8,3584]{1,0:T(8,128)(2,1)S(1)}, bf16[8,3584]{1,0:T(8,128)(2,1)S(1)}, u32[]{:S(2)}, u32[]{:S(2)}) collective-permute-start(bf16[8,3584]{1,0:T(8,128)(2,1)S(1)} %get-tuple-element.43), channel_id=1, source_target_pairs={{0,8},{2,10},{4,12},{6,14},{8,0},{10,2},{12,4},{14,6},{1,9},{3,11}... | collective-permute-start | bytes 172040 | tf_op jit(solution)/shard_map/ppermute | solution.py:44
  179.8 7.3 %collective-permute-start.21 = (bf16[8,3584]{1,0:T(8,128)(2,1)S(1)}, bf16[8,3584]{1,0:T(8,128)(2,1)S(1)}, u32[]{:S(2)}, u32[]{:S(2)}) collective-permute-start(bf16[8,3584]{1,0:T(8,128)(2,1)S(1)} %get-tuple-element.44), channel_id=1, source_target_pairs={{0,10},{2,8},{4,14},{6,12},{8,2},{10,0},{12,6},{14,4},{1,11},{3,9}... | collective-permute-start | bytes 172040 | tf_op jit(solution)/shard_map/ppermute | solution.py:44
  180.3 6.9 %collective-permute-start.22 = (bf16[8,3584]{1,0:T(8,128)(2,1)S(1)}, bf16[8,3584]{1,0:T(8,128)(2,1)S(1)}, u32[]{:S(2)}, u32[]{:S(2)}) collective-permute-start(bf16[8,3584]{1,0:T(8,128)(2,1)S(1)} %get-tuple-element.45), channel_id=1, source_target_pairs={{0,12},{2,14},{4,0},{6,2},{8,4},{10,6},{12,8},{14,10},{1,13},{3,15... | collective-permute-start | bytes 172040 | tf_op jit(solution)/shard_map/ppermute | solution.py:44
  182.7 5.6 %collective-permute-start.23 = (bf16[8,3584]{1,0:T(8,128)(2,1)S(1)}, bf16[8,3584]{1,0:T(8,128)(2,1)S(1)}, u32[]{:S(2)}, u32[]{:S(2)}) collective-permute-start(bf16[8,3584]{1,0:T(8,128)(2,1)S(1)} %get-tuple-element.46), channel_id=1, source_target_pairs={{0,14},{2,12},{4,2},{6,0},{8,6},{10,4},{12,10},{14,8},{1,15},{3,13... | collective-permute-start | bytes 172040 | tf_op jit(solution)/shard_map/ppermute | solution.py:44

commit v4 on v3

--- a/solution.py
+++ b/solution.py
@@ -43,11 +43,15 @@
         ]
         return lax.ppermute(arr, "ep", pairs)
 
-    def spread(self, own):
+    def spread(self, own, spaced=False):
         got = {(0, 0): own[0]}
-        for s in range(1, self.z):
-            got[s, 0] = self.send(own[s], s, 0)
-        for s in range(self.z):
+        near_first = sorted(range(self.z), key=lambda s: min(s, self.z - s))
+        for s in near_first:
+            block = own[s]
+            if spaced and min(s, self.z - s) > 1:
+                block, *_ = lax.optimization_barrier((block, got[1, 0], got[0, self.x - 1]))
+            if s:
+                got[s, 0] = self.send(block, s, 0)
             for u in range(1, self.x):
                 got[s, u] = self.send(got[s, 0], 0, u)
         return [got[step] for step in self.steps]
@@ -103,7 +107,7 @@
         sources, rest = refs[:7], refs[7:]
         gate_ref, up_ref, down_ref, rest = rest[0], rest[1], rest[2], rest[3:]
         out_refs, pack_ref, rest = rest[: grid.z], rest[grid.z], rest[grid.z + 1 :]
-        q_ref, kv_ref, res_ref, ids_ref, wts_ref, len_ref, kept, score, sems, row_sems, pack_sems = rest
+        q_ref, kv_ref, res_ref, ids_ref, wts_ref, len_ref, kept, score, packed, sems, row_sems, pack_sems = rest
         cache_ref = sources[6]
         copies = [
             pltpu.make_async_copy(src, dst, sems.at[i])
@@ -123,9 +127,10 @@
             begin = pl.multiple_of(other * out_width + b * piece, LANES)
             blocks.append(down_ref.at[:, pl.ds(begin, piece)])
         packs = [
-            pltpu.make_async_copy(block, pack_ref.at[pl.ds(i * units, units), :], pack_sems.at[i])
+            pltpu.make_async_copy(block, packed.at[pl.ds(i * units, units), :], pack_sems.at[i])
             for i, block in enumerate(blocks)
         ]
+        pack_out = pltpu.make_async_copy(packed, pack_ref, pack_sems.at[len(blocks)])
         for copy in copies[:2] + row_copies + copies[2:] + packs:
             copy.start()
 
@@ -145,8 +150,9 @@
             part = nt_dot(narrow, kept[r, :, :HD])
             score[...] = jnp.where(row_wide == r, part, score[...]) if r else part
 
-        for copy in copies[2:]:
+        for copy in copies[2:] + packs:
             copy.wait()
+        pack_out.start()
         lane = lax.broadcasted_iota(jnp.int32, (rows, LANES), 1)
         square = (rows, rows)
         diagonal = lax.broadcasted_iota(jnp.int32, square, 0) == lax.broadcasted_iota(jnp.int32, square, 1)
@@ -188,8 +194,7 @@
             value = total[h * rows : (h + 1) * rows].astype(jnp.bfloat16)
             for ref in out_refs:
                 ref[:, h * HD : (h + 1) * HD] = value
-        for copy in packs:
-            copy.wait()
+        pack_out.wait()
 
     return pl.pallas_call(
         kernel,
@@ -207,9 +212,10 @@
             pltpu.SMEM(lengths.shape, jnp.int32),
             pltpu.VMEM(cache.shape, jnp.bfloat16),
             pltpu.VMEM((tall, ctx), jnp.float32),
+            pltpu.VMEM((packed_rows, piece), jnp.bfloat16),
             pltpu.SemaphoreType.DMA((6,)),
             pltpu.SemaphoreType.DMA((rows,)),
-            pltpu.SemaphoreType.DMA((2 * grid.ep + down_blocks,)),
+            pltpu.SemaphoreType.DMA((2 * grid.ep + down_blocks + 1,)),
         ],
         compiler_params=params(60),
     )(
@@ -475,7 +481,7 @@
         up_t,
         w_down,
     )
-    chunks = grid.spread(outgoing)
+    chunks = grid.spread(outgoing, spaced=True)
     packed, *_ = lax.optimization_barrier((packed, *chunks))
     far_weights = swap(packed)
     ours, theirs, weight = project(grid, piece, chunks, w_out)

time: 189 us -> 78.8 us (0.42)
  Pallas kernels: 129 us -> 20.4 us
    pallas_call x1, Pallas kernels: 116 us -> 7.76 us  [attention(): pl.pallas_call(kernel, name='attention', out_shape=[shape_of((rows, width...]
  transfers between devices with their start and end apart: 24 -> 24, of which waited for: 12 -> 11; matrix products, arithmetic and copies ran while one was open for 0% -> 0% of each run, Pallas kernels for 5% -> 12%
where the time goes in v4:
time: 78.8 us; the launch traced here: 78.6 us
  starting transfers between devices  33.4 us (42%)
  waiting for transfers between devices  23.7 us (30%)
  Pallas kernels  20.4 us (26%)
  local copies, waits for them, and re-layouts  1.08 us (1%)
    ppermute x21, starting transfers between devices, send(): return lax.ppermute(arr, 'ep', pairs)  33.2 us
    ppermute x21, waiting for transfers between devices, send(): return lax.ppermute(arr, 'ep', pairs)  20.8 us
    pallas_call x1, Pallas kernels, project(): pl.pallas_call(kernel, name='project', grid=(blocks,), out_shape=outs, in...  9.39 us
    pallas_call x1, Pallas kernels, attention(): pl.pallas_call(kernel, name='attention', out_shape=[shape_of((rows, width...  7.76 us
    ppermute x3, waiting for transfers between devices, swap(): return lax.ppermute(arr, 'tp', [(0, 1), (1, 0)])  2.87 us
    pallas_call x1, Pallas kernels, gate_up(): pl.pallas_call(kernel, name='gate_up', out_shape=[shape_of((tall + extra...  1.68 us
  transfers between devices with their start and end apart: 24, of which 11 were waited for; matrix products, arithmetic and copies ran while one was open for 0% of the time, Pallas kernels for 12%

profile of v4, /device:TPU:0, one launch (start us, length us, event | category | flops | bytes accessed | tf_op | source)
XLA Modules:
  0.0 78.6 jit_solution(12786732283916616655)
XLA Ops:
  0.0 7.8 %attention.1 = (bf16[8,9472]{1,0:T(8,128)(2,1)}, bf16[8,9472]{1,0:T(8,128)(2,1)}, bf16[8,9472]{1,0:T(8,128)(2,1)}, bf16[8,9472]{1,0:T(8,128)(2,1)}, bf16[3680,512]{1,0:T(8,128)(2,1)}) custom-call(bf16[8,8192]{1,0:T(8,128)(2,1)} %refs_0_.1, bf16[8,512]{1,0:T(8,128)(2,1)} %refs_1_.1, bf16[8,7168]{1,0:T(8,128)(2,1)} %refs_2_.1, s32[3,8]{1,0:T(4,128)} %bitcast.10, ...), custom_call_target="tpu_custom_call" | custom-call | tf_op jit(solution)/shard_map/attention/pallas_call | solution.py:199
  7.8 3.1 %collective-permute-start.1 = (bf16[8,9472]{1,0:T(8,128)(2,1)}, bf16[8,9472]{1,0:T(8,128)(2,1)S(1)}, u32[]{:S(2)}, u32[]{:S(2)}) collective-permute-start(bf16[8,9472]{1,0:T(8,128)(2,1)} %get-tuple-element.28), channel_id=1, source_target_pairs={{0,4},{2,6},{4,8},{6,10},{8,12},{10,14},{12,0},{14,2},{1,5},{3,7},... | collective-permute-start | bytes 454664 | tf_op jit(solution)/shard_map/ppermute | solution.py:44
  10.8 1.5 %collective-permute-start = (bf16[8,9472]{1,0:T(8,128)(2,1)}, bf16[8,9472]{1,0:T(8,128)(2,1)S(1)}, u32[]{:S(2)}, u32[]{:S(2)}) collective-permute-start(bf16[8,9472]{1,0:T(8,128)(2,1)} %get-tuple-element.27.refs_0_), channel_id=1, source_target_pairs={{0,2},{2,0},{4,6},{6,4},{8,10},{10,8},{12,14},{14,12},{1,3},{3,1},... | collective-permute-start | bytes 454664 | tf_op jit(solution)/shard_map/ppermute | solution.py:44
  12.3 2.2 %collective-permute-start.5 = (bf16[8,9472]{1,0:T(8,128)(2,1)}, bf16[8,9472]{1,0:T(8,128)(2,1)S(1)}, u32[]{:S(2)}, u32[]{:S(2)}) collective-permute-start(bf16[8,9472]{1,0:T(8,128)(2,1)} %get-tuple-element.31), channel_id=1, source_target_pairs={{0,12},{2,14},{4,0},{6,2},{8,4},{10,6},{12,8},{14,10},{1,13},{3,15... | collective-permute-start | bytes 454664 | tf_op jit(solution)/shard_map/ppermute | solution.py:44
  14.6 2.9 %collective-permute-done.1.refs_2_ = bf16[8,9472]{1,0:T(8,128)(2,1)S(1)} collective-permute-done((bf16[8,9472]{1,0:T(8,128)(2,1)}, bf16[8,9472]{1,0:T(8,128)(2,1)S(1)}, u32[]{:S(2)}, u32[]{:S(2)}) %collective-permute-start.1) | collective-permute-done | bytes 151584 | tf_op jit(solution)/shard_map/ppermute | solution.py:44
  17.5 0.0 collective-permute-done.refs_1_
  17.5 1.5 %collective-permute-start.3 = (bf16[8,9472]{1,0:T(8,128)(2,1)}, bf16[8,9472]{1,0:T(8,128)(2,1)S(1)}, u32[]{:S(2)}, u32[]{:S(2)}) collective-permute-start(bf16[8,9472]{1,0:T(8,128)(2,1)} %get-tuple-element.30), channel_id=1, source_target_pairs={{0,8},{2,10},{4,12},{6,14},{8,0},{10,2},{12,4},{14,6},{1,9},{3,11}... | collective-permute-start | bytes 454664 | tf_op jit(solution)/shard_map/ppermute | solution.py:44
  19.0 3.4 %collective-permute-start.2 = (bf16[8,9472]{1,0:T(8,128)(2,1)S(1)}, bf16[8,9472]{1,0:T(8,128)(2,1)S(1)}, u32[]{:S(2)}, u32[]{:S(2)}) collective-permute-start(bf16[8,9472]{1,0:T(8,128)(2,1)S(1)} %collective-permute-done.1.refs_2_), channel_id=1, source_target_pairs={{0,2},{2,0},{4,6},{6,4},{8,10},{10,8},{12,14},{14,12},{1,3},{3,1},... | collective-permute-start | bytes 454664 | tf_op jit(solution)/shard_map/ppermute | solution.py:44
  22.5 0.0 collective-permute-done.5.refs_6_
  22.5 0.0 collective-permute-start.6
  22.5 4.2 %collective-permute-done.3.refs_4_ = bf16[8,9472]{1,0:T(8,128)(2,1)S(1)} collective-permute-done((bf16[8,9472]{1,0:T(8,128)(2,1)}, bf16[8,9472]{1,0:T(8,128)(2,1)S(1)}, u32[]{:S(2)}, u32[]{:S(2)}) %collective-permute-start.3) | collective-permute-done | bytes 151584 | tf_op jit(solution)/shard_map/ppermute | solution.py:44
  26.8 1.5 %collective-permute-start.4 = (bf16[8,9472]{1,0:T(8,128)(2,1)S(1)}, bf16[8,9472]{1,0:T(8,128)(2,1)S(1)}, u32[]{:S(2)}, u32[]{:S(2)}) collective-permute-start(bf16[8,9472]{1,0:T(8,128)(2,1)S(1)} %collective-permute-done.3.refs_4_), channel_id=1, source_target_pairs={{0,2},{2,0},{4,6},{6,4},{8,10},{10,8},{12,14},{14,12},{1,3},{3,1},... | collective-permute-start | bytes 454664 | tf_op jit(solution)/shard_map/ppermute | solution.py:44
  28.2 0.0 collective-permute-done.2.refs_3_
  28.3 0.0 collective-permute-done.6.refs_7_
  28.3 4.1 %collective-permute-done.4.refs_5_ = bf16[8,9472]{1,0:T(8,128)(2,1)S(1)} collective-permute-done((bf16[8,9472]{1,0:T(8,128)(2,1)S(1)}, bf16[8,9472]{1,0:T(8,128)(2,1)S(1)}, u32[]{:S(2)}, u32[]{:S(2)}) %collective-permute-start.4) | collective-permute-done | bytes 151584 | tf_op jit(solution)/shard_map/ppermute | solution.py:44
  32.3 0.0 copy-start
  32.3 0.0 copy-start.1
  32.3 0.0 collective-permute-start.8
  32.3 0.0 copy-start.3
  32.3 1.1 %copy-done.3 = bf16[8,9472]{1,0:T(8,128)(2,1)S(1)} copy-done((bf16[8,9472]{1,0:T(8,128)(2,1)S(1)}, bf16[8,9472]{1,0:T(8,128)(2,1)}, u32[]{:S(2)}) %copy-start.3) | copy-done | bytes 151576
  33.4 0.0 copy-start.4
  33.4 9.4 %project.1 = (f32[64,512]{1,0:T(8,128)S(1)}, f32[64,512]{1,0:T(8,128)S(1)}, f32[64,128]{1,0:T(8,128)S(1)}) custom-call(bf16[8,9472]{1,0:T(8,128)(2,1)S(1)} %copy-done.3, bf16[8,9472]{1,0:T(8,128)(2,1)S(1)} %collective-permute-done.refs_1_, bf16[8,9472]{1,0:T(8,128)(2,1)S(1)} %collective-permute-done.1.refs_2_, ...), custom_call_target="tpu_custom_call" | custom-call | flops 939524096 | bytes 15990784 | tf_op jit(solution)/shard_map/project/pallas_call | solution.py:285
  42.8 0.1 collective-permute-start.7
  42.9 1.3 %collective-permute-done.7 = f32[64,512]{1,0:T(8,128)S(1)} collective-permute-done((f32[64,512]{1,0:T(8,128)S(1)}, f32[64,512]{1,0:T(8,128)S(1)}, u32[]{:S(2)}, u32[]{:S(2)}) %collective-permute-start.7) | collective-permute-done | bytes 131104 | tf_op jit(solution)/shard_map/ppermute | solution.py:69
  44.2 0.0 collective-permute-done.8.refs_11_.packed_ref
  44.2 2.2 %collective-permute-start.14 = (bf16[64,512]{1,0:T(8,128)(2,1)S(1)}, bf16[64,512]{1,0:T(8,128)(2,1)S(1)}, u32[]{:S(2)}, u32[]{:S(2)}) collective-permute-start(bf16[64,512]{1,0:T(8,128)(2,1)S(1)} %add_convert_fusion.refs_0_), channel_id=1, source_target_pairs={{0,12},{2,14},{4,0},{6,2},{8,4},{10,6},{12,8},{14,10},{1,13},{3,15... | collective-permute-start | bytes 196616 | tf_op jit(solution)/shard_map/ppermute | solution.py:44
  46.4 0.0 collective-permute-start.12
  46.5 0.6 collective-permute-start.10
  47.1 2.0 %collective-permute-start.9 = (bf16[64,512]{1,0:T(8,128)(2,1)S(1)}, bf16[64,512]{1,0:T(8,128)(2,1)S(1)}, u32[]{:S(2)}, u32[]{:S(2)}) collective-permute-start(bf16[64,512]{1,0:T(8,128)(2,1)S(1)} %add_convert_fusion.refs_0_), channel_id=1, source_target_pairs={{0,2},{2,0},{4,6},{6,4},{8,10},{10,8},{12,14},{14,12},{1,3},{3,1},... | collective-permute-start | bytes 196616 | tf_op jit(solution)/shard_map/ppermute | solution.py:44
  49.1 0.0 collective-permute-done.14.refs_6_
  49.1 1.9 %collective-permute-start.15 = (bf16[64,512]{1,0:T(8,128)(2,1)S(1)}, bf16[64,512]{1,0:T(8,128)(2,1)S(1)}, u32[]{:S(2)}, u32[]{:S(2)}) collective-permute-start(bf16[64,512]{1,0:T(8,128)(2,1)S(1)} %collective-permute-done.14.refs_6_), channel_id=1, source_target_pairs={{0,2},{2,0},{4,6},{6,4},{8,10},{10,8},{12,14},{14,12},{1,3},{3,1},... | collective-permute-start | bytes 196616 | tf_op jit(solution)/shard_map/ppermute | solution.py:44
  51.0 2.4 %collective-permute-done.12.refs_4_ = bf16[64,512]{1,0:T(8,128)(2,1)S(1)} collective-permute-done((bf16[64,512]{1,0:T(8,128)(2,1)S(1)}, bf16[64,512]{1,0:T(8,128)(2,1)S(1)}, u32[]{:S(2)}, u32[]{:S(2)}) %collective-permute-start.12) | collective-permute-done | bytes 65568 | tf_op jit(solution)/shard_map/ppermute | solution.py:44
  53.3 1.7 %collective-permute-start.13 = (bf16[64,512]{1,0:T(8,128)(2,1)S(1)}, bf16[64,512]{1,0:T(8,128)(2,1)S(1)}, u32[]{:S(2)}, u32[]{:S(2)}) collective-permute-start(bf16[64,512]{1,0:T(8,128)(2,1)S(1)} %collective-permute-done.12.refs_4_), channel_id=1, source_target_pairs={{0,2},{2,0},{4,6},{6,4},{8,10},{10,8},{12,14},{14,12},{1,3},{3,1},... | collective-permute-start | bytes 196616 | tf_op jit(solution)/shard_map/ppermute | solution.py:44
  55.1 0.0 collective-permute-done.10.refs_2_
  55.1 0.3 collective-permute-start.11
  55.4 0.0 collective-permute-done.9.refs_1_
  55.4 0.0 collective-permute-done.15.refs_7_
  55.4 2.8 %collective-permute-done.13.refs_5_ = bf16[64,512]{1,0:T(8,128)(2,1)S(1)} collective-permute-done((bf16[64,512]{1,0:T(8,128)(2,1)S(1)}, bf16[64,512]{1,0:T(8,128)(2,1)S(1)}, u32[]{:S(2)}, u32[]{:S(2)}) %collective-permute-start.13) | collective-permute-done | bytes 65568 | tf_op jit(solution)/shard_map/ppermute | solution.py:44
  58.2 1.2 %collective-permute-done.11.refs_3_ = bf16[64,512]{1,0:T(8,128)(2,1)S(1)} collective-permute-done((bf16[64,512]{1,0:T(8,128)(2,1)S(1)}, bf16[64,512]{1,0:T(8,128)(2,1)S(1)}, u32[]{:S(2)}, u32[]{:S(2)}) %collective-permute-start.11) | collective-permute-done | bytes 65568 | tf_op jit(solution)/shard_map/ppermute | solution.py:44
  59.4 0.0 copy-done
  59.4 0.0 copy-done.1
  59.4 0.0 copy-done.4
  59.4 0.0 copy-start.2
  59.4 1.7 %gate_up.1 = (f32[88,768]{1,0:T(8,128)S(1)}, f32[8,2048]{1,0:T(8,128)S(1)}) custom-call(bf16[64,512]{1,0:T(8,128)(2,1)S(1)} %add_convert_fusion.refs_0_, bf16[64,512]{1,0:T(8,128)(2,1)S(1)} %collective-permute-done.9.refs_1_, bf16[64,512]{1,0:T(8,128)(2,1)S(1)} %collective-permute-done.10.refs_2_, bf16[64,512]{1,0:T(8,128)(2,1)S(1)} %collective-permute-done.11.refs_3_, ...), custom_call_target="tpu_custom_call" | custom-call | tf_op jit(solution)/shard_map/gate_up/pallas_call | solution.py:348
  61.1 0.1 collective-permute-start.16
  61.1 1.5 %collective-permute-done.16.far_ref = f32[88,768]{1,0:T(8,128)S(1)} collective-permute-done((f32[88,768]{1,0:T(8,128)S(1)}, f32[88,768]{1,0:T(8,128)S(1)}, u32[]{:S(2)}, u32[]{:S(2)}) %collective-permute-start.16) | collective-permute-done | bytes 270368 | tf_op jit(solution)/shard_map/ppermute | solution.py:69
  62.7 0.0 copy-done.2
  62.7 0.9 %down.1 = (f32[8,3584]{1,0:T(8,128)S(1)}, bf16[8,3584]{1,0:T(8,128)(2,1)S(1)}, bf16[8,3584]{1,0:T(8,128)(2,1)S(1)}, bf16[8,3584]{1,0:T(8,128)(2,1)S(1)}, bf16[8,...) custom-call(f32[88,768]{1,0:T(8,128)S(1)} %get-tuple-element.39.sums, ...), custom_call_target="tpu_custom_call" | custom-call | tf_op jit(solution)/shard_map/down/pallas_call | solution.py:401
  63.6 0.8 %collective-permute-start.17 = (bf16[8,3584]{1,0:T(8,128)(2,1)S(1)}, bf16[8,3584]{1,0:T(8,128)(2,1)S(1)}, u32[]{:S(2)}, u32[]{:S(2)}) collective-permute-start(bf16[8,3584]{1,0:T(8,128)(2,1)S(1)} %get-tuple-element.42), channel_id=1, source_target_pairs={{0,2},{2,0},{4,6},{6,4},{8,10},{10,8},{12,14},{14,12},{1,3},{3,1},... | collective-permute-start | bytes 172040 | tf_op jit(solution)/shard_map/ppermute | solution.py:44
  64.4 0.0 collective-permute-start.18
  64.4 1.8 %collective-permute-start.19 = (bf16[8,3584]{1,0:T(8,128)(2,1)S(1)}, bf16[8,3584]{1,0:T(8,128)(2,1)S(1)}, u32[]{:S(2)}, u32[]{:S(2)}) collective-permute-start(bf16[8,3584]{1,0:T(8,128)(2,1)S(1)} %get-tuple-element.44), channel_id=1, source_target_pairs={{0,6},{2,4},{4,10},{6,8},{8,14},{10,12},{12,2},{14,0},{1,7},{3,5},... | collective-permute-start | bytes 172040 | tf_op jit(solution)/shard_map/ppermute | solution.py:44
  66.2 3.3 %collective-permute-start.20 = (bf16[8,3584]{1,0:T(8,128)(2,1)S(1)}, bf16[8,3584]{1,0:T(8,128)(2,1)S(1)}, u32[]{:S(2)}, u32[]{:S(2)}) collective-permute-start(bf16[8,3584]{1,0:T(8,128)(2,1)S(1)} %get-tuple-element.45), channel_id=1, source_target_pairs={{0,8},{2,10},{4,12},{6,14},{8,0},{10,2},{12,4},{14,6},{1,9},{3,11}... | collective-permute-start | bytes 172040 | tf_op jit(solution)/shard_map/ppermute | solution.py:44
  69.5 0.4 collective-permute-start.21
  69.9 0.0 collective-permute-done.17.rest_1_
  69.9 2.1 %collective-permute-start.22 = (bf16[8,3584]{1,0:T(8,128)(2,1)S(1)}, bf16[8,3584]{1,0:T(8,128)(2,1)S(1)}, u32[]{:S(2)}, u32[]{:S(2)}) collective-permute-start(bf16[8,3584]{1,0:T(8,128)(2,1)S(1)} %get-tuple-element.47), channel_id=1, source_target_pairs={{0,12},{2,14},{4,0},{6,2},{8,4},{10,6},{12,8},{14,10},{1,13},{3,15... | collective-permute-start | bytes 172040 | tf_op jit(solution)/shard_map/ppermute | solution.py:44
  72.0 0.0 collective-permute-done.18.rest_2_
  72.0 2.7 %collective-permute-start.23 = (bf16[8,3584]{1,0:T(8,128)(2,1)S(1)}, bf16[8,3584]{1,0:T(8,128)(2,1)S(1)}, u32[]{:S(2)}, u32[]{:S(2)}) collective-permute-start(bf16[8,3584]{1,0:T(8,128)(2,1)S(1)} %get-tuple-element.48), channel_id=1, source_target_pairs={{0,14},{2,12},{4,2},{6,0},{8,6},{10,4},{12,10},{14,8},{1,15},{3,13... | collective-permute-start | bytes 172040 | tf_op jit(solution)/shard_map/ppermute | solution.py:44
  74.8 0.0 collective-permute-done.19.rest_3_
  74.8 0.2 collective-permute-done.20.rest_4_
  75.0 1.8 %collective-permute-done.21.rest_5_ = bf16[8,3584]{1,0:T(8,128)(2,1)S(1)} collective-permute-done((bf16[8,3584]{1,0:T(8,128)(2,1)S(1)}, bf16[8,3584]{1,0:T(8,128)(2,1)S(1)}, u32[]{:S(2)}, u32[]{:S(2)}) %collective-permute-start.21) | collective-permute-done | bytes 57376 | tf_op jit(solution)/shard_map/ppermute | solution.py:44
  76.8 0.0 collective-permute-done.22.rest_6_
  76.8 1.1 %collective-permute-done.23.rest_7_ = bf16[8,3584]{1,0:T(8,128)(2,1)S(1)} collective-permute-done((bf16[8,3584]{1,0:T(8,128)(2,1)S(1)}, bf16[8,3584]{1,0:T(8,128)(2,1)S(1)}, u32[]{:S(2)}, u32[]{:S(2)}) %collective-permute-start.23) | collective-permute-done | bytes 57376 | tf_op jit(solution)/shard_map/ppermute | solution.py:44
  77.9 0.7 finish.1
  (1 shorter events, 0.0 us)
Async XLA Ops:
  7.8 9.8 %collective-permute-start.1 = (bf16[8,9472]{1,0:T(8,128)(2,1)}, bf16[8,9472]{1,0:T(8,128)(2,1)S(1)}, u32[]{:S(2)}, u32[]{:S(2)}) collective-permute-start(bf16[8,9472]{1,0:T(8,128)(2,1)} %get-tuple-element.28), channel_id=1, source_target_pairs={{0,4},{2,6},{4,8},{6,10},{8,12},{10,14},{12,0},{14,2},{1,5},{3,7},... | collective-permute-start | bytes 454664 | tf_op jit(solution)/shard_map/ppermute | solution.py:44
  10.8 6.7 %collective-permute-start = (bf16[8,9472]{1,0:T(8,128)(2,1)}, bf16[8,9472]{1,0:T(8,128)(2,1)S(1)}, u32[]{:S(2)}, u32[]{:S(2)}) collective-permute-start(bf16[8,9472]{1,0:T(8,128)(2,1)} %get-tuple-element.27.refs_0_), channel_id=1, source_target_pairs={{0,2},{2,0},{4,6},{6,4},{8,10},{10,8},{12,14},{14,12},{1,3},{3,1},... | collective-permute-start | bytes 454664 | tf_op jit(solution)/shard_map/ppermute | solution.py:44
  12.3 10.2 %collective-permute-start.5 = (bf16[8,9472]{1,0:T(8,128)(2,1)}, bf16[8,9472]{1,0:T(8,128)(2,1)S(1)}, u32[]{:S(2)}, u32[]{:S(2)}) collective-permute-start(bf16[8,9472]{1,0:T(8,128)(2,1)} %get-tuple-element.31), channel_id=1, source_target_pairs={{0,12},{2,14},{4,0},{6,2},{8,4},{10,6},{12,8},{14,10},{1,13},{3,15... | collective-permute-start | bytes 454664 | tf_op jit(solution)/shard_map/ppermute | solution.py:44
  17.5 9.2 %collective-permute-start.3 = (bf16[8,9472]{1,0:T(8,128)(2,1)}, bf16[8,9472]{1,0:T(8,128)(2,1)S(1)}, u32[]{:S(2)}, u32[]{:S(2)}) collective-permute-start(bf16[8,9472]{1,0:T(8,128)(2,1)} %get-tuple-element.30), channel_id=1, source_target_pairs={{0,8},{2,10},{4,12},{6,14},{8,0},{10,2},{12,4},{14,6},{1,9},{3,11}... | collective-permute-start | bytes 454664 | tf_op jit(solution)/shard_map/ppermute | solution.py:44
  19.0 9.2 %collective-permute-start.2 = (bf16[8,9472]{1,0:T(8,128)(2,1)S(1)}, bf16[8,9472]{1,0:T(8,128)(2,1)S(1)}, u32[]{:S(2)}, u32[]{:S(2)}) collective-permute-start(bf16[8,9472]{1,0:T(8,128)(2,1)S(1)} %collective-permute-done.1.refs_2_), channel_id=1, source_target_pairs={{0,2},{2,0},{4,6},{6,4},{8,10},{10,8},{12,14},{14,12},{1,3},{3,1},... | collective-permute-start | bytes 454664 | tf_op jit(solution)/shard_map/ppermute | solution.py:44
  22.5 5.8 %collective-permute-start.6 = (bf16[8,9472]{1,0:T(8,128)(2,1)S(1)}, bf16[8,9472]{1,0:T(8,128)(2,1)S(1)}, u32[]{:S(2)}, u32[]{:S(2)}) collective-permute-start(bf16[8,9472]{1,0:T(8,128)(2,1)S(1)} %collective-permute-done.5.refs_6_), channel_id=1, source_target_pairs={{0,2},{2,0},{4,6},{6,4},{8,10},{10,8},{12,14},{14,12},{1,3},{3,1},... | collective-permute-start | bytes 454664 | tf_op jit(solution)/shard_map/ppermute | solution.py:44
  26.8 5.6 %collective-permute-start.4 = (bf16[8,9472]{1,0:T(8,128)(2,1)S(1)}, bf16[8,9472]{1,0:T(8,128)(2,1)S(1)}, u32[]{:S(2)}, u32[]{:S(2)}) collective-permute-start(bf16[8,9472]{1,0:T(8,128)(2,1)S(1)} %collective-permute-done.3.refs_4_), channel_id=1, source_target_pairs={{0,2},{2,0},{4,6},{6,4},{8,10},{10,8},{12,14},{14,12},{1,3},{3,1},... | collective-permute-start | bytes 454664 | tf_op jit(solution)/shard_map/ppermute | solution.py:44
  32.3 27.0 %copy-start = (bf16[7168,160]{0,1:T(8,128)(2,1)S(1)}, bf16[7168,160]{0,1:T(8,128)(2,1)}, u32[]{:S(2)}) copy-start(bf16[7168,160]{0,1:T(8,128)(2,1)} %param.21) | copy-start | bytes 6881284
  32.3 27.0 %copy-start.1 = (bf16[7168,160]{0,1:T(8,128)(2,1)S(1)}, bf16[7168,160]{0,1:T(8,128)(2,1)}, u32[]{:S(2)}) copy-start(bf16[7168,160]{0,1:T(8,128)(2,1)} %param.22) | copy-start | bytes 6881284
  32.3 11.9 %collective-permute-start.8 = (bf16[3680,512]{1,0:T(8,128)(2,1)}, bf16[3680,512]{1,0:T(8,128)(2,1)S(1)}, u32[]{:S(2)}, u32[]{:S(2)}) collective-permute-start(bf16[3680,512]{1,0:T(8,128)(2,1)} %get-tuple-element.35), channel_id=1, source_target_pairs={{0,1},{1,0},{2,3},{3,2},{4,5},{5,4},{6,7},{7,6},{8,9},{9,8},{10,11... | collective-permute-start | bytes 11304968 | tf_op jit(solution)/shard_map/ppermute | solution.py:69
  32.3 1.1 %copy-start.3 = (bf16[8,9472]{1,0:T(8,128)(2,1)S(1)}, bf16[8,9472]{1,0:T(8,128)(2,1)}, u32[]{:S(2)}) copy-start(bf16[8,9472]{1,0:T(8,128)(2,1)} %get-tuple-element.27.refs_0_) | copy-start | bytes 454660
  33.4 26.0 %copy-start.4 = (f32[7168]{0:T(1024)S(1)}, f32[7168]{0:T(1024)}, u32[]{:S(2)}) copy-start(f32[7168]{0:T(1024)} %param.18) | copy-start | bytes 86020
  42.8 1.4 %collective-permute-start.7 = (f32[64,512]{1,0:T(8,128)S(1)}, f32[64,512]{1,0:T(8,128)S(1)}, u32[]{:S(2)}, u32[]{:S(2)}) collective-permute-start(f32[64,512]{1,0:T(8,128)S(1)} %get-tuple-element.33), channel_id=1, source_target_pairs={{0,1},{1,0},{2,3},{3,2},{4,5},{5,4},{6,7},{7,6},{8,9},{9,8},{10,11... | collective-permute-start | bytes 393224 | tf_op jit(solution)/shard_map/ppermute | solution.py:69
  44.2 4.9 %collective-permute-start.14 = (bf16[64,512]{1,0:T(8,128)(2,1)S(1)}, bf16[64,512]{1,0:T(8,128)(2,1)S(1)}, u32[]{:S(2)}, u32[]{:S(2)}) collective-permute-start(bf16[64,512]{1,0:T(8,128)(2,1)S(1)} %add_convert_fusion.refs_0_), channel_id=1, source_target_pairs={{0,12},{2,14},{4,0},{6,2},{8,4},{10,6},{12,8},{14,10},{1,13},{3,15... | collective-permute-start | bytes 196616 | tf_op jit(solution)/shard_map/ppermute | solution.py:44
  46.4 6.9 %collective-permute-start.12 = (bf16[64,512]{1,0:T(8,128)(2,1)S(1)}, bf16[64,512]{1,0:T(8,128)(2,1)S(1)}, u32[]{:S(2)}, u32[]{:S(2)}) collective-permute-start(bf16[64,512]{1,0:T(8,128)(2,1)S(1)} %add_convert_fusion.refs_0_), channel_id=1, source_target_pairs={{0,8},{2,10},{4,12},{6,14},{8,0},{10,2},{12,4},{14,6},{1,9},{3,11}... | collective-permute-start | bytes 196616 | tf_op jit(solution)/shard_map/ppermute | solution.py:44
  46.5 8.6 %collective-permute-start.10 = (bf16[64,512]{1,0:T(8,128)(2,1)S(1)}, bf16[64,512]{1,0:T(8,128)(2,1)S(1)}, u32[]{:S(2)}, u32[]{:S(2)}) collective-permute-start(bf16[64,512]{1,0:T(8,128)(2,1)S(1)} %add_convert_fusion.refs_0_), channel_id=1, source_target_pairs={{0,4},{2,6},{4,8},{6,10},{8,12},{10,14},{12,0},{14,2},{1,5},{3,7},... | collective-permute-start | bytes 196616 | tf_op jit(solution)/shard_map/ppermute | solution.py:44
  47.1 8.3 %collective-permute-start.9 = (bf16[64,512]{1,0:T(8,128)(2,1)S(1)}, bf16[64,512]{1,0:T(8,128)(2,1)S(1)}, u32[]{:S(2)}, u32[]{:S(2)}) collective-permute-start(bf16[64,512]{1,0:T(8,128)(2,1)S(1)} %add_convert_fusion.refs_0_), channel_id=1, source_target_pairs={{0,2},{2,0},{4,6},{6,4},{8,10},{10,8},{12,14},{14,12},{1,3},{3,1},... | collective-permute-start | bytes 196616 | tf_op jit(solution)/shard_map/ppermute | solution.py:44
  49.1 6.3 %collective-permute-start.15 = (bf16[64,512]{1,0:T(8,128)(2,1)S(1)}, bf16[64,512]{1,0:T(8,128)(2,1)S(1)}, u32[]{:S(2)}, u32[]{:S(2)}) collective-permute-start(bf16[64,512]{1,0:T(8,128)(2,1)S(1)} %collective-permute-done.14.refs_6_), channel_id=1, source_target_pairs={{0,2},{2,0},{4,6},{6,4},{8,10},{10,8},{12,14},{14,12},{1,3},{3,1},... | collective-permute-start | bytes 196616 | tf_op jit(solution)/shard_map/ppermute | solution.py:44
  53.3 4.8 %collective-permute-start.13 = (bf16[64,512]{1,0:T(8,128)(2,1)S(1)}, bf16[64,512]{1,0:T(8,128)(2,1)S(1)}, u32[]{:S(2)}, u32[]{:S(2)}) collective-permute-start(bf16[64,512]{1,0:T(8,128)(2,1)S(1)} %collective-permute-done.12.refs_4_), channel_id=1, source_target_pairs={{0,2},{2,0},{4,6},{6,4},{8,10},{10,8},{12,14},{14,12},{1,3},{3,1},... | collective-permute-start | bytes 196616 | tf_op jit(solution)/shard_map/ppermute | solution.py:44
  55.1 4.3 %collective-permute-start.11 = (bf16[64,512]{1,0:T(8,128)(2,1)S(1)}, bf16[64,512]{1,0:T(8,128)(2,1)S(1)}, u32[]{:S(2)}, u32[]{:S(2)}) collective-permute-start(bf16[64,512]{1,0:T(8,128)(2,1)S(1)} %collective-permute-done.10.refs_2_), channel_id=1, source_target_pairs={{0,2},{2,0},{4,6},{6,4},{8,10},{10,8},{12,14},{14,12},{1,3},{3,1},... | collective-permute-start | bytes 196616 | tf_op jit(solution)/shard_map/ppermute | solution.py:44
  59.4 3.3 %copy-start.2 = (bf16[160,7168]{1,0:T(8,128)(2,1)S(1)}, bf16[160,7168]{1,0:T(8,128)(2,1)}, u32[]{:S(2)}) copy-start(bf16[160,7168]{1,0:T(8,128)(2,1)} %down_ref.1) | copy-start | bytes 6881284
  61.1 1.6 %collective-permute-start.16 = (f32[88,768]{1,0:T(8,128)S(1)}, f32[88,768]{1,0:T(8,128)S(1)}, u32[]{:S(2)}, u32[]{:S(2)}) collective-permute-start(f32[88,768]{1,0:T(8,128)S(1)} %get-tuple-element.39.sums_ref), channel_id=1, source_target_pairs={{0,1},{1,0},{2,3},{3,2},{4,5},{5,4},{6,7},{7,6},{8,9},{9,8},{10,11... | collective-permute-start | bytes 811016 | tf_op jit(solution)/shard_map/ppermute | solution.py:69
  63.6 6.4 %collective-permute-start.17 = (bf16[8,3584]{1,0:T(8,128)(2,1)S(1)}, bf16[8,3584]{1,0:T(8,128)(2,1)S(1)}, u32[]{:S(2)}, u32[]{:S(2)}) collective-permute-start(bf16[8,3584]{1,0:T(8,128)(2,1)S(1)} %get-tuple-element.42), channel_id=1, source_target_pairs={{0,2},{2,0},{4,6},{6,4},{8,10},{10,8},{12,14},{14,12},{1,3},{3,1},... | collective-permute-start | bytes 172040 | tf_op jit(solution)/shard_map/ppermute | solution.py:44
  64.4 7.7 %collective-permute-start.18 = (bf16[8,3584]{1,0:T(8,128)(2,1)S(1)}, bf16[8,3584]{1,0:T(8,128)(2,1)S(1)}, u32[]{:S(2)}, u32[]{:S(2)}) collective-permute-start(bf16[8,3584]{1,0:T(8,128)(2,1)S(1)} %get-tuple-element.43), channel_id=1, source_target_pairs={{0,4},{2,6},{4,8},{6,10},{8,12},{10,14},{12,0},{14,2},{1,5},{3,7},... | collective-permute-start | bytes 172040 | tf_op jit(solution)/shard_map/ppermute | solution.py:44
  64.4 10.4 %collective-permute-start.19 = (bf16[8,3584]{1,0:T(8,128)(2,1)S(1)}, bf16[8,3584]{1,0:T(8,128)(2,1)S(1)}, u32[]{:S(2)}, u32[]{:S(2)}) collective-permute-start(bf16[8,3584]{1,0:T(8,128)(2,1)S(1)} %get-tuple-element.44), channel_id=1, source_target_pairs={{0,6},{2,4},{4,10},{6,8},{8,14},{10,12},{12,2},{14,0},{1,7},{3,5},... | collective-permute-start | bytes 172040 | tf_op jit(solution)/shard_map/ppermute | solution.py:44
  66.2 8.7 %collective-permute-start.20 = (bf16[8,3584]{1,0:T(8,128)(2,1)S(1)}, bf16[8,3584]{1,0:T(8,128)(2,1)S(1)}, u32[]{:S(2)}, u32[]{:S(2)}) collective-permute-start(bf16[8,3584]{1,0:T(8,128)(2,1)S(1)} %get-tuple-element.45), channel_id=1, source_target_pairs={{0,8},{2,10},{4,12},{6,14},{8,0},{10,2},{12,4},{14,6},{1,9},{3,11}... | collective-permute-start | bytes 172040 | tf_op jit(solution)/shard_map/ppermute | solution.py:44
  69.5 7.3 %collective-permute-start.21 = (bf16[8,3584]{1,0:T(8,128)(2,1)S(1)}, bf16[8,3584]{1,0:T(8,128)(2,1)S(1)}, u32[]{:S(2)}, u32[]{:S(2)}) collective-permute-start(bf16[8,3584]{1,0:T(8,128)(2,1)S(1)} %get-tuple-element.46), channel_id=1, source_target_pairs={{0,10},{2,8},{4,14},{6,12},{8,2},{10,0},{12,6},{14,4},{1,11},{3,9}... | collective-permute-start | bytes 172040 | tf_op jit(solution)/shard_map/ppermute | solution.py:44
  69.9 6.9 %collective-permute-start.22 = (bf16[8,3584]{1,0:T(8,128)(2,1)S(1)}, bf16[8,3584]{1,0:T(8,128)(2,1)S(1)}, u32[]{:S(2)}, u32[]{:S(2)}) collective-permute-start(bf16[8,3584]{1,0:T(8,128)(2,1)S(1)} %get-tuple-element.47), channel_id=1, source_target_pairs={{0,12},{2,14},{4,0},{6,2},{8,4},{10,6},{12,8},{14,10},{1,13},{3,15... | collective-permute-start | bytes 172040 | tf_op jit(solution)/shard_map/ppermute | solution.py:44
  72.0 5.9 %collective-permute-start.23 = (bf16[8,3584]{1,0:T(8,128)(2,1)S(1)}, bf16[8,3584]{1,0:T(8,128)(2,1)S(1)}, u32[]{:S(2)}, u32[]{:S(2)}) collective-permute-start(bf16[8,3584]{1,0:T(8,128)(2,1)S(1)} %get-tuple-element.48), channel_id=1, source_target_pairs={{0,14},{2,12},{4,2},{6,0},{8,6},{10,4},{12,10},{14,8},{1,15},{3,13... | collective-permute-start | bytes 172040 | tf_op jit(solution)/shard_map/ppermute | solution.py:44

commit v5 on v4

--- a/solution.py
+++ b/solution.py
@@ -43,18 +43,30 @@
         ]
         return lax.ppermute(arr, "ep", pairs)
 
-    def spread(self, own, spaced=False):
+    def near(self, own):
         got = {(0, 0): own[0]}
-        near_first = sorted(range(self.z), key=lambda s: min(s, self.z - s))
-        for s in near_first:
-            block = own[s]
-            if spaced and min(s, self.z - s) > 1:
-                block, *_ = lax.optimization_barrier((block, got[1, 0], got[0, self.x - 1]))
-            if s:
-                got[s, 0] = self.send(block, s, 0)
-            for u in range(1, self.x):
+        for s in range(1, self.z):
+            if min(s, self.z - s) == 1:
+                got[s, 0] = self.send(own[s], s, 0)
+        for u in range(1, self.x):
+            got[0, u] = self.send(own[0], 0, u)
+        return got
+
+    def far(self, own, got):
+        for s in range(1, self.z):
+            if (s, 0) not in got:
+                got[s, 0] = self.send(own[s], s, 0)
+
+    def forward(self, got):
+        for s, u in self.steps:
+            if (s, u) not in got:
                 got[s, u] = self.send(got[s, 0], 0, u)
         return [got[step] for step in self.steps]
+
+    def spread(self, own):
+        got = self.near([own] * self.z)
+        self.far([own] * self.z, got)
+        return self.forward(got)
 
     def source(self, step):
         me = lax.axis_index("ep")
@@ -95,7 +107,8 @@
     rows, width = queries.shape
     heads = width // HD
     ctx = cache.shape[1]
-    tall = rows * heads
+    parts = HD // LANES
+    half = width // 2
     note = piece + LANES
     scaling = HD ** (-0.5)
     units, features = gate_t.shape
@@ -106,8 +119,8 @@
     def kernel(*refs):
         sources, rest = refs[:7], refs[7:]
         gate_ref, up_ref, down_ref, rest = rest[0], rest[1], rest[2], rest[3:]
-        out_refs, pack_ref, rest = rest[: grid.z], rest[grid.z], rest[grid.z + 1 :]
-        q_ref, kv_ref, res_ref, ids_ref, wts_ref, len_ref, kept, score, packed, sems, row_sems, pack_sems = rest
+        lead_refs, tail_ref, pack_ref, rest = rest[: grid.z], rest[grid.z], rest[grid.z + 1], rest[grid.z + 2 :]
+        q_ref, kv_ref, res_ref, ids_ref, wts_ref, len_ref, kept, turned, packed, sems, row_sems, pack_sems = rest
         cache_ref = sources[6]
         copies = [
             pltpu.make_async_copy(src, dst, sems.at[i])
@@ -136,19 +149,20 @@
 
         copies[0].wait()
         copies[1].wait()
-        q = q_ref[...].astype(jnp.float32)
-        stacked = jnp.concatenate([q[:, h * HD : (h + 1) * HD] for h in range(heads)], axis=0)
-        narrow = stacked.astype(jnp.bfloat16)
-        new_kv_f = kv_ref[...].astype(jnp.float32)
-        new_k = jnp.concatenate([new_kv_f[:, :HD]] * heads, axis=0)
-        new_v = jnp.concatenate([new_kv_f[:, HD:]] * heads, axis=0)
-        own = jnp.sum(stacked * new_k, axis=1, keepdims=True) * scaling
-        row_of = lax.rem(lax.broadcasted_iota(jnp.int32, (tall, 1), 0), rows)
-        row_wide = lax.rem(lax.broadcasted_iota(jnp.int32, (tall, ctx), 0), rows)
+        for h in range(heads):
+            for c in range(parts):
+                at = h * HD + c * LANES
+                turned[c, h * rows : (h + 1) * rows, :] = q_ref[:, at : at + LANES].astype(jnp.float32)
+        new_k = kv_ref[:, :HD].astype(jnp.float32)
+        new_v = kv_ref[:, HD:].astype(jnp.float32)
+        scores, owns = [], []
         for r in range(rows):
+            q = jnp.concatenate(
+                [turned[c, pl.ds(r, heads, stride=rows), :] for c in range(parts)], axis=1
+            )
+            owns.append(jnp.sum(q * new_k[r : r + 1], axis=1, keepdims=True) * scaling)
             row_copies[r].wait()
-            part = nt_dot(narrow, kept[r, :, :HD])
-            score[...] = jnp.where(row_wide == r, part, score[...]) if r else part
+            scores.append(nt_dot(q.astype(jnp.bfloat16), kept[r, :, :HD]) * scaling)
 
         for copy in copies[2:] + packs:
             copy.wait()
@@ -160,8 +174,8 @@
         for s, u in grid.steps:
             to = grid.target((s, u))
             begin = pl.multiple_of(to * cols + skip, LANES)
-            at = width + u * note
-            out_refs[s][:, at : at + piece] = res_ref[:, pl.ds(begin, piece)]
+            at = half + u * note
+            lead_refs[s][:, at : at + piece] = res_ref[:, pl.ds(begin, piece)]
             chosen = ids_ref[...] == to * EXPERTS // grid.ep
             across = jnp.sum(jnp.where(chosen, wts_ref[...], 0.0), axis=0, keepdims=True)
             weight = jnp.sum(
@@ -173,36 +187,39 @@
             tile = jnp.where(lane == 0, high, 0.0)
             tile = jnp.where(lane == 1, middle, tile)
             tile = jnp.where(lane == 2, low, tile)
-            out_refs[s][:, at + piece : at + note] = tile.astype(jnp.bfloat16)
-
-        length = jnp.zeros((tall, 1), jnp.int32)
+            lead_refs[s][:, at + piece : at + note] = tile.astype(jnp.bfloat16)
+
+        place = lax.broadcasted_iota(jnp.int32, (heads, ctx), 1)
+        probs, own_probs = [], []
         for r in range(rows):
-            length = jnp.where(row_of == r, len_ref[r], length)
-        place = lax.broadcasted_iota(jnp.int32, (tall, ctx), 1)
-        scores = jnp.where(place < length, score[...] * scaling, -jnp.inf)
-        peak = jnp.maximum(jnp.max(scores, axis=1, keepdims=True), own)
-        exps = jnp.exp(scores - peak)
-        own_exp = jnp.exp(own - peak)
-        denominator = jnp.sum(exps, axis=1, keepdims=True) + own_exp
-        prob = exps / denominator
-        own_prob = (own_exp / denominator).astype(jnp.bfloat16).astype(jnp.float32)
-        total = own_prob * new_v
+            score = jnp.where(place < len_ref[r], scores[r], -jnp.inf)
+            peak = jnp.maximum(jnp.max(score, axis=1, keepdims=True), owns[r])
+            exps = jnp.exp(score - peak)
+            own_exp = jnp.exp(owns[r] - peak)
+            denominator = jnp.sum(exps, axis=1, keepdims=True) + own_exp
+            probs.append((exps / denominator).astype(jnp.bfloat16))
+            own_probs.append((own_exp / denominator).astype(jnp.bfloat16).astype(jnp.float32))
         for r in range(rows):
-            only = jnp.where(row_wide == r, prob, 0.0).astype(jnp.bfloat16)
-            total = total + jnp.dot(only, kept[r, :, HD:], preferred_element_type=jnp.float32)
+            mixed = jnp.dot(probs[r], kept[r, :, HD:], preferred_element_type=jnp.float32)
+            mixed = mixed + own_probs[r] * new_v[r : r + 1]
+            for c in range(parts):
+                turned[c, r * heads : (r + 1) * heads, :] = mixed[:, c * LANES : (c + 1) * LANES]
         for h in range(heads):
-            value = total[h * rows : (h + 1) * rows].astype(jnp.bfloat16)
-            for ref in out_refs:
-                ref[:, h * HD : (h + 1) * HD] = value
+            part, at = divmod(h, heads // 2)
+            for c in range(parts):
+                value = turned[c, pl.ds(h, rows, stride=heads), :].astype(jnp.bfloat16)
+                begin = at * HD + c * LANES
+                for ref in (tail_ref,) if part else lead_refs:
+                    ref[:, begin : begin + LANES] = value
         pack_out.wait()
 
     return pl.pallas_call(
         kernel,
         name="attention",
-        out_shape=[shape_of((rows, width + grid.x * note), jnp.bfloat16)] * grid.z
-        + [shape_of((packed_rows, piece), jnp.bfloat16)],
+        out_shape=[shape_of((rows, half + grid.x * note), jnp.bfloat16)] * grid.z
+        + [shape_of((rows, half), jnp.bfloat16), shape_of((packed_rows, piece), jnp.bfloat16)],
         in_specs=[in_hbm()] * 10,
-        out_specs=[vmem()] * grid.z + [in_hbm()],
+        out_specs=[vmem()] * (grid.z + 1) + [in_hbm()],
         scratch_shapes=[
             pltpu.VMEM(queries.shape, jnp.bfloat16),
             pltpu.VMEM(new_kv.shape, jnp.bfloat16),
@@ -211,7 +228,7 @@
             pltpu.VMEM(route_weights.shape, jnp.float32),
             pltpu.SMEM(lengths.shape, jnp.int32),
             pltpu.VMEM(cache.shape, jnp.bfloat16),
-            pltpu.VMEM((tall, ctx), jnp.float32),
+            pltpu.VMEM((parts, rows * heads, LANES), jnp.float32),
             pltpu.VMEM((packed_rows, piece), jnp.bfloat16),
             pltpu.SemaphoreType.DMA((6,)),
             pltpu.SemaphoreType.DMA((rows,)),
@@ -232,18 +249,23 @@
     )
 
 
-def project(grid, piece, chunks, w_out):
+def project(grid, piece, chunks, w_out, before=None):
     rows = chunks[0].shape[0]
-    depth, cols = w_out.shape
+    depth, cols = w_out.shape[0] // 2, w_out.shape[1]
     count = len(chunks)
     tall = rows * count
-    blocks = 8
+    blocks = 4
     block = depth // blocks
+    last = before is not None
     note = piece + LANES
 
     def kernel(*refs):
         chunk_refs, rest = refs[:count], refs[count:]
-        w_ref, ours_ref, theirs_ref, weight_ref, stacked, total = rest
+        w_ref, rest = rest[0], rest[1:]
+        if last:
+            before_ref, base_ref, ours_ref, theirs_ref, stacked, total = rest
+        else:
+            out_ref, base_ref, weight_ref, stacked, total = rest
         k = pl.program_id(0)
 
         @pl.when(k == 0)
@@ -256,7 +278,7 @@
 
         @pl.when(k == 0)
         def _():
-            total[...] = product
+            total[...] = product + before_ref[...] if last else product
 
         @pl.when(k > 0)
         def _():
@@ -267,39 +289,52 @@
             core = lax.axis_index("tp")
             mine = pl.multiple_of(core * (cols - piece), LANES)
             other = pl.multiple_of((1 - core) * (cols - piece), LANES)
+            if not last:
+                out_ref[...] = total[...]
             for i, (s, u) in enumerate(grid.steps):
                 here = pl.ds(pl.multiple_of(grid.source((s, u)) * rows, rows), rows)
-                at = depth + u * note
-                beside = chunk_refs[i][:, at : at + note].astype(jnp.float32)
                 block_rows = slice(i * rows, (i + 1) * rows)
-                ours_ref[here, :] = total[block_rows, pl.ds(mine, piece)] + beside[:, :piece]
-                theirs_ref[here, :] = total[block_rows, pl.ds(other, piece)]
-                weight_ref[here, :] = jnp.broadcast_to(
-                    jnp.sum(beside[:, piece:], axis=1, keepdims=True), (rows, LANES)
-                )
+                if last:
+                    ours_ref[here, :] = total[block_rows, pl.ds(mine, piece)] + base_ref[here, :]
+                    theirs_ref[here, :] = total[block_rows, pl.ds(other, piece)]
+                else:
+                    at = depth + u * note
+                    beside = chunk_refs[i][:, at : at + note].astype(jnp.float32)
+                    base_ref[here, :] = beside[:, :piece]
+                    weight_ref[here, :] = jnp.broadcast_to(
+                        jnp.sum(beside[:, piece:], axis=1, keepdims=True), (rows, LANES)
+                    )
 
     def whole(arr):
         return pl.BlockSpec(arr.shape, lambda k: (0, 0))
 
-    outs = [shape_of((tall, piece), jnp.float32)] * 2 + [shape_of((tall, LANES), jnp.float32)]
+    pieces = shape_of((tall, piece), jnp.float32)
+    if last:
+        outs = [pieces] * 2
+    else:
+        outs = [shape_of((tall, cols), jnp.float32), pieces, shape_of((tall, LANES), jnp.float32)]
+    extra = list(before) if last else []
+    first_block = blocks if last else 0
     return pl.pallas_call(
         kernel,
         name="project",
         grid=(blocks,),
         out_shape=outs,
-        in_specs=[whole(c) for c in chunks] + [pl.BlockSpec((block, cols), lambda k: (k, 0))],
+        in_specs=[whole(c) for c in chunks]
+        + [pl.BlockSpec((block, cols), lambda k: (first_block + k, 0))]
+        + [whole(e) for e in extra],
         out_specs=[whole(o) for o in outs],
         scratch_shapes=[
             pltpu.VMEM((blocks, tall, block), jnp.bfloat16),
             pltpu.VMEM((tall, cols), jnp.float32),
         ],
         cost_estimate=pl.CostEstimate(
-            flops=2 * tall * depth * cols,
-            bytes_accessed=2 * depth * cols + 2 * tall * depth + 8 * tall * piece,
+            flops=8 * tall * depth * cols,
+            bytes_accessed=4 * depth * cols,
             transcendentals=0,
         ),
         compiler_params=params(48),
-    )(*chunks, w_out)
+    )(*chunks, w_out, *extra)
 
 
 def gate_up(grid, piece, cols, rows, pieces, gain, gate_t, up_t, other):
@@ -466,7 +501,7 @@
     cols = w_out.shape[1]
     piece = -(-cols // (2 * LANES)) * LANES
     gate_t, up_t = w_gate.T, w_up.T
-    *outgoing, packed = attention(
+    *lead, tail, packed = attention(
         grid,
         piece,
         cols,
@@ -481,13 +516,28 @@
         up_t,
         w_down,
     )
-    chunks = grid.spread(outgoing, spaced=True)
-    packed, *_ = lax.optimization_barrier((packed, *chunks))
+    first = grid.near(lead)
+    arrived = (first[1, 0], first[0, grid.x - 1])
+    *lead, tail, _, _ = lax.optimization_barrier((*lead, tail, *arrived))
+    grid.far(lead, first)
+    tails = [tail] * grid.z
+    second = grid.near(tails)
+    for s in range(2, grid.z - 1):
+        first[s, 0], second = lax.optimization_barrier((first[s, 0], second))
+    first_chunks = grid.forward(first)
+    *tails, _, _ = lax.optimization_barrier((*tails, second[1, 0], second[0, grid.x - 1]))
+    grid.far(tails, second)
+    far_blocks = [second[s, 0] for s in range(2, grid.z - 1)]
+    packed, first_chunks, far_blocks = lax.optimization_barrier((packed, first_chunks, far_blocks))
+    for s, block in zip(range(2, grid.z - 1), far_blocks):
+        second[s, 0] = block
+    second_chunks = grid.forward(second)
     far_weights = swap(packed)
-    ours, theirs, weight = project(grid, piece, chunks, w_out)
+    before, base, weight = project(grid, piece, first_chunks, w_out)
+    ours, theirs = project(grid, piece, second_chunks, w_out, (before, base))
     stream = (ours + swap(theirs)).astype(jnp.bfloat16)
     stream, far_weights = lax.optimization_barrier((stream, far_weights))
-    pieces = grid.spread([stream] * grid.z)
+    pieces = grid.spread(stream)
     sums, home = gate_up(
         grid, piece, cols, rows, pieces, gain.reshape(1, width), gate_t, up_t, far_weights
     )

time: 78.8 us -> 81.2 us (1.030)
  starting transfers between devices: 33.4 us -> 38.4 us
  waiting for transfers between devices: 23.7 us -> 21.6 us
    ppermute x21 -> x28, starting transfers between devices: 33.2 us -> 38.3 us  [send(): return lax.ppermute(arr, 'ep', pairs)]
    ppermute x21 -> x28, waiting for transfers between devices: 20.8 us -> 18.8 us  [send(): return lax.ppermute(arr, 'ep', pairs)]
    pallas_call x1, Pallas kernels: 7.76 us -> 6.74 us  [attention(): pl.pallas_call(kernel, name='attention', out_shape=[shape_of((rows, half...]
    pallas_call x1 -> x2, Pallas kernels: 9.39 us -> 9.86 us  [project(): pl.pallas_call(kernel, name='project', grid=(blocks,), out_shape=outs, in...]
  transfers between devices with their start and end apart: 24 -> 31, of which waited for: 11 -> 14; matrix products, arithmetic and copies ran while one was open for 0% -> 0% of each run, Pallas kernels for 12% -> 12%
where the time goes in v5:
time: 81.2 us; the launch traced here: 81 us
  starting transfers between devices  38.4 us (47%)
  waiting for transfers between devices  21.6 us (27%)
  Pallas kernels  19.8 us (24%)
  local copies, waits for them, and re-layouts  0.92 us (1%)
    ppermute x28, starting transfers between devices, send(): return lax.ppermute(arr, 'ep', pairs)  38.3 us
    ppermute x28, waiting for transfers between devices, send(): return lax.ppermute(arr, 'ep', pairs)  18.8 us
    pallas_call x2, Pallas kernels, project(): pl.pallas_call(kernel, name='project', grid=(blocks,), out_shape=outs, in...  9.86 us
    pallas_call x1, Pallas kernels, attention(): pl.pallas_call(kernel, name='attention', out_shape=[shape_of((rows, half...  6.74 us
    ppermute x3, waiting for transfers between devices, swap(): return lax.ppermute(arr, 'tp', [(0, 1), (1, 0)])  2.87 us
    pallas_call x1, Pallas kernels, gate_up(): pl.pallas_call(kernel, name='gate_up', out_shape=[shape_of((tall + extra...  1.66 us
  transfers between devices with their start and end apart: 31, of which 14 were waited for; matrix products, arithmetic and copies ran while one was open for 0% of the time, Pallas kernels for 12%

profile of v5, /device:TPU:0, one launch (start us, length us, event | category | flops | bytes accessed | tf_op | source)
XLA Modules:
  0.0 81.0 jit_solution(1651201568051290276)
XLA Ops:
  0.0 6.7 %attention.1 = (bf16[8,5376]{1,0:T(8,128)(2,1)}, bf16[8,5376]{1,0:T(8,128)(2,1)}, bf16[8,5376]{1,0:T(8,128)(2,1)}, bf16[8,5376]{1,0:T(8,128)(2,1)}, bf16[8,4096]{1,0:T(8,128)(2,1)}, /*index=5*/bf16[3680,512]{1,0:T(8,128)(2,1)}) custom-call(bf16[8,8192]{1,0:T(8,128)(2,1)} %refs_0_.1, bf16[8,512]{1,0:T(8,128)(2,1)} %refs_1_.1, bf16[8,7168]{1,0:T(8,128)(2,1)} %refs_2_.1, ...), custom_call_target="tpu_custom_call" | custom-call | tf_op jit(solution)/shard_map/attention/pallas_call | solution.py:216
  6.7 3.1 %collective-permute-start = (bf16[8,5376]{1,0:T(8,128)(2,1)}, bf16[8,5376]{1,0:T(8,128)(2,1)S(1)}, u32[]{:S(2)}, u32[]{:S(2)}) collective-permute-start(bf16[8,5376]{1,0:T(8,128)(2,1)} %get-tuple-element.47), channel_id=1, source_target_pairs={{0,4},{2,6},{4,8},{6,10},{8,12},{10,14},{12,0},{14,2},{1,5},{3,7},... | collective-permute-start | bytes 258056 | tf_op jit(solution)/shard_map/ppermute | solution.py:44
  9.8 1.5 %collective-permute-start.1 = (bf16[8,5376]{1,0:T(8,128)(2,1)}, bf16[8,5376]{1,0:T(8,128)(2,1)S(1)}, u32[]{:S(2)}, u32[]{:S(2)}) collective-permute-start(bf16[8,5376]{1,0:T(8,128)(2,1)} %get-tuple-element.61.refs_0_), channel_id=1, source_target_pairs={{0,2},{2,0},{4,6},{6,4},{8,10},{10,8},{12,14},{14,12},{1,3},{3,1},... | collective-permute-start | bytes 258056 | tf_op jit(solution)/shard_map/ppermute | solution.py:44
  11.3 2.2 %collective-permute-start.9 = (bf16[8,5376]{1,0:T(8,128)(2,1)}, bf16[8,5376]{1,0:T(8,128)(2,1)S(1)}, u32[]{:S(2)}, u32[]{:S(2)}) collective-permute-start(bf16[8,5376]{1,0:T(8,128)(2,1)} %get-tuple-element.49), channel_id=1, source_target_pairs={{0,12},{2,14},{4,0},{6,2},{8,4},{10,6},{12,8},{14,10},{1,13},{3,15... | collective-permute-start | bytes 258056 | tf_op jit(solution)/shard_map/ppermute | solution.py:44
  13.6 1.1 %collective-permute-done.refs_2_ = bf16[8,5376]{1,0:T(8,128)(2,1)S(1)} collective-permute-done((bf16[8,5376]{1,0:T(8,128)(2,1)}, bf16[8,5376]{1,0:T(8,128)(2,1)S(1)}, u32[]{:S(2)}, u32[]{:S(2)}) %collective-permute-start) | collective-permute-done | bytes 86048 | tf_op jit(solution)/shard_map/ppermute | solution.py:44
  14.7 0.0 collective-permute-done.1.refs_1_
  14.7 2.4 %collective-permute-start.2 = (bf16[8,5376]{1,0:T(8,128)(2,1)}, bf16[8,5376]{1,0:T(8,128)(2,1)S(1)}, u32[]{:S(2)}, u32[]{:S(2)}) collective-permute-start(bf16[8,5376]{1,0:T(8,128)(2,1)} %get-tuple-element.51), channel_id=1, source_target_pairs={{0,8},{2,10},{4,12},{6,14},{8,0},{10,2},{12,4},{14,6},{1,9},{3,11}... | collective-permute-start | bytes 258056 | tf_op jit(solution)/shard_map/ppermute | solution.py:44
  17.1 1.3 %collective-permute-start.5 = (bf16[8,4096]{1,0:T(8,128)(2,1)}, bf16[8,4096]{1,0:T(8,128)(2,1)S(1)}, u32[]{:S(2)}, u32[]{:S(2)}) collective-permute-start(bf16[8,4096]{1,0:T(8,128)(2,1)} %get-tuple-element.58.refs_0_), channel_id=1, source_target_pairs={{0,12},{2,14},{4,0},{6,2},{8,4},{10,6},{12,8},{14,10},{1,13},{3,15... | collective-permute-start | bytes 196616 | tf_op jit(solution)/shard_map/ppermute | solution.py:44
  18.5 0.7 collective-permute-start.4
  19.1 1.5 %collective-permute-start.3 = (bf16[8,4096]{1,0:T(8,128)(2,1)}, bf16[8,4096]{1,0:T(8,128)(2,1)S(1)}, u32[]{:S(2)}, u32[]{:S(2)}) collective-permute-start(bf16[8,4096]{1,0:T(8,128)(2,1)} %get-tuple-element.58.refs_0_), channel_id=1, source_target_pairs={{0,2},{2,0},{4,6},{6,4},{8,10},{10,8},{12,14},{14,12},{1,3},{3,1},... | collective-permute-start | bytes 196616 | tf_op jit(solution)/shard_map/ppermute | solution.py:44
  20.6 0.5 collective-permute-start.7
  21.2 1.6 %collective-permute-done.5.refs_6_ = bf16[8,4096]{1,0:T(8,128)(2,1)S(1)} collective-permute-done((bf16[8,4096]{1,0:T(8,128)(2,1)}, bf16[8,4096]{1,0:T(8,128)(2,1)S(1)}, u32[]{:S(2)}, u32[]{:S(2)}) %collective-permute-start.5) | collective-permute-done | bytes 65568 | tf_op jit(solution)/shard_map/ppermute | solution.py:44
  22.8 1.5 %collective-permute-start.10 = (bf16[8,5376]{1,0:T(8,128)(2,1)S(1)}, bf16[8,5376]{1,0:T(8,128)(2,1)S(1)}, u32[]{:S(2)}, u32[]{:S(2)}) collective-permute-start(bf16[8,5376]{1,0:T(8,128)(2,1)S(1)} %collective-permute-done.9.refs_6_), channel_id=1, source_target_pairs={{0,2},{2,0},{4,6},{6,4},{8,10},{10,8},{12,14},{14,12},{1,3},{3,1},... | collective-permute-start | bytes 258056 | tf_op jit(solution)/shard_map/ppermute | solution.py:44
  24.3 0.5 collective-permute-done.4.refs_2_
  24.7 0.0 collective-permute-done.3.refs_1_
  24.7 0.0 collective-permute-done.2.refs_4_
  24.7 1.5 %collective-permute-start.8 = (bf16[8,5376]{1,0:T(8,128)(2,1)S(1)}, bf16[8,5376]{1,0:T(8,128)(2,1)S(1)}, u32[]{:S(2)}, u32[]{:S(2)}) collective-permute-start(bf16[8,5376]{1,0:T(8,128)(2,1)S(1)} %collective-permute-done.2.refs_4_), channel_id=1, source_target_pairs={{0,2},{2,0},{4,6},{6,4},{8,10},{10,8},{12,14},{14,12},{1,3},{3,1},... | collective-permute-start | bytes 258056 | tf_op jit(solution)/shard_map/ppermute | solution.py:44
  26.2 0.2 collective-permute-start.11
  26.4 0.0 collective-permute-done.7.refs_3_
  26.4 0.8 %collective-permute-done.10.refs_7_ = bf16[8,5376]{1,0:T(8,128)(2,1)S(1)} collective-permute-done((bf16[8,5376]{1,0:T(8,128)(2,1)S(1)}, bf16[8,5376]{1,0:T(8,128)(2,1)S(1)}, u32[]{:S(2)}, u32[]{:S(2)}) %collective-permute-start.10) | collective-permute-done | bytes 86048 | tf_op jit(solution)/shard_map/ppermute | solution.py:44
  27.3 4.7 %collective-permute-done.11.refs_4_ = bf16[8,4096]{1,0:T(8,128)(2,1)S(1)} collective-permute-done((bf16[8,4096]{1,0:T(8,128)(2,1)}, bf16[8,4096]{1,0:T(8,128)(2,1)S(1)}, u32[]{:S(2)}, u32[]{:S(2)}) %collective-permute-start.11) | collective-permute-done | bytes 65568 | tf_op jit(solution)/shard_map/ppermute | solution.py:44
  32.0 0.0 collective-permute-done.8.refs_5_
  32.0 0.8 collective-permute-start.6
  32.8 1.2 %collective-permute-start.13 = (bf16[8,4096]{1,0:T(8,128)(2,1)S(1)}, bf16[8,4096]{1,0:T(8,128)(2,1)S(1)}, u32[]{:S(2)}, u32[]{:S(2)}) collective-permute-start(bf16[8,4096]{1,0:T(8,128)(2,1)S(1)} %collective-permute-done.5.refs_6_), channel_id=1, source_target_pairs={{0,2},{2,0},{4,6},{6,4},{8,10},{10,8},{12,14},{14,12},{1,3},{3,1},... | collective-permute-start | bytes 196616 | tf_op jit(solution)/shard_map/ppermute | solution.py:44
  34.0 0.8 collective-permute-start.12
  34.8 0.9 %copy-done.3 = bf16[8,5376]{1,0:T(8,128)(2,1)S(1)} copy-done((bf16[8,5376]{1,0:T(8,128)(2,1)S(1)}, bf16[8,5376]{1,0:T(8,128)(2,1)}, u32[]{:S(2)}) %copy-start.3) | copy-done | bytes 86040
  35.7 4.8 %project.2 = (f32[64,896]{1,0:T(8,128)S(1)}, f32[64,512]{1,0:T(8,128)S(1)}, f32[64,128]{1,0:T(8,128)S(1)}) custom-call(bf16[8,5376]{1,0:T(8,128)(2,1)S(1)} %copy-done.3, bf16[8,5376]{1,0:T(8,128)(2,1)S(1)} %collective-permute-done.1.refs_1_, bf16[8,5376]{1,0:T(8,128)(2,1)S(1)} %collective-permute-done.refs_2_, ...), custom_call_target="tpu_custom_call" | custom-call | flops 1879048192 | bytes 14680064 | tf_op jit(solution)/shard_map/project/pallas_call | solution.py:318
  40.5 0.0 collective-permute-done.12.refs_5_
  40.5 0.0 copy-start
  40.5 0.0 copy-start.1
  40.5 0.0 copy-start.5
  40.5 5.1 %project.3 = (f32[64,512]{1,0:T(8,128)S(1)}, f32[64,512]{1,0:T(8,128)S(1)}) custom-call(bf16[8,4096]{1,0:T(8,128)(2,1)S(1)} %copy-done.4, bf16[8,4096]{1,0:T(8,128)(2,1)S(1)} %collective-permute-done.3.refs_1_, bf16[8,4096]{1,0:T(8,128)(2,1)S(1)} %collective-permute-done.4.refs_2_, bf16[8,4096]{1,0:T(8,128)(2,1)S(1)} %collective-permute-done.6.refs_3_, ...), custom_call_target="tpu_custom_call" | custom-call | flops 1879048192 | bytes 14680064 | tf_op jit(solution)/shard_map/project/pallas_call | solution.py:318
  45.6 0.1 collective-permute-start.14
  45.7 1.3 %collective-permute-done.14 = f32[64,512]{1,0:T(8,128)S(1)} collective-permute-done((f32[64,512]{1,0:T(8,128)S(1)}, f32[64,512]{1,0:T(8,128)S(1)}, u32[]{:S(2)}, u32[]{:S(2)}) %collective-permute-start.14) | collective-permute-done | bytes 131104 | tf_op jit(solution)/shard_map/ppermute | solution.py:81
  47.1 1.8 %collective-permute-start.21 = (bf16[64,512]{1,0:T(8,128)(2,1)S(1)}, bf16[64,512]{1,0:T(8,128)(2,1)S(1)}, u32[]{:S(2)}, u32[]{:S(2)}) collective-permute-start(bf16[64,512]{1,0:T(8,128)(2,1)S(1)} %add_convert_fusion.refs_0_), channel_id=1, source_target_pairs={{0,12},{2,14},{4,0},{6,2},{8,4},{10,6},{12,8},{14,10},{1,13},{3,15... | collective-permute-start | bytes 196616 | tf_op jit(solution)/shard_map/ppermute | solution.py:44
  48.9 0.6 collective-permute-start.17
  49.6 1.7 %collective-permute-start.16 = (bf16[64,512]{1,0:T(8,128)(2,1)S(1)}, bf16[64,512]{1,0:T(8,128)(2,1)S(1)}, u32[]{:S(2)}, u32[]{:S(2)}) collective-permute-start(bf16[64,512]{1,0:T(8,128)(2,1)S(1)} %add_convert_fusion.refs_0_), channel_id=1, source_target_pairs={{0,2},{2,0},{4,6},{6,4},{8,10},{10,8},{12,14},{14,12},{1,3},{3,1},... | collective-permute-start | bytes 196616 | tf_op jit(solution)/shard_map/ppermute | solution.py:44
  51.2 0.2 collective-permute-done.21.refs_6_
  51.4 1.7 %collective-permute-start.22 = (bf16[64,512]{1,0:T(8,128)(2,1)S(1)}, bf16[64,512]{1,0:T(8,128)(2,1)S(1)}, u32[]{:S(2)}, u32[]{:S(2)}) collective-permute-start(bf16[64,512]{1,0:T(8,128)(2,1)S(1)} %collective-permute-done.21.refs_6_), channel_id=1, source_target_pairs={{0,2},{2,0},{4,6},{6,4},{8,10},{10,8},{12,14},{14,12},{1,3},{3,1},... | collective-permute-start | bytes 196616 | tf_op jit(solution)/shard_map/ppermute | solution.py:44
  53.1 3.1 %collective-permute-done.19.refs_4_ = bf16[64,512]{1,0:T(8,128)(2,1)S(1)} collective-permute-done((bf16[64,512]{1,0:T(8,128)(2,1)S(1)}, bf16[64,512]{1,0:T(8,128)(2,1)S(1)}, u32[]{:S(2)}, u32[]{:S(2)}) %collective-permute-start.19) | collective-permute-done | bytes 65568 | tf_op jit(solution)/shard_map/ppermute | solution.py:44
  56.2 1.3 %collective-permute-start.20 = (bf16[64,512]{1,0:T(8,128)(2,1)S(1)}, bf16[64,512]{1,0:T(8,128)(2,1)S(1)}, u32[]{:S(2)}, u32[]{:S(2)}) collective-permute-start(bf16[64,512]{1,0:T(8,128)(2,1)S(1)} %collective-permute-done.19.refs_4_), channel_id=1, source_target_pairs={{0,2},{2,0},{4,6},{6,4},{8,10},{10,8},{12,14},{14,12},{1,3},{3,1},... | collective-permute-start | bytes 196616 | tf_op jit(solution)/shard_map/ppermute | solution.py:44
  57.5 0.0 collective-permute-done.17.refs_2_
  57.5 0.7 collective-permute-start.18
  58.2 0.0 collective-permute-done.16.refs_1_
  58.2 2.6 %collective-permute-done.20.refs_5_ = bf16[64,512]{1,0:T(8,128)(2,1)S(1)} collective-permute-done((bf16[64,512]{1,0:T(8,128)(2,1)S(1)}, bf16[64,512]{1,0:T(8,128)(2,1)S(1)}, u32[]{:S(2)}, u32[]{:S(2)}) %collective-permute-start.20) | collective-permute-done | bytes 65568 | tf_op jit(solution)/shard_map/ppermute | solution.py:44
  60.8 0.9 %collective-permute-done.18.refs_3_ = bf16[64,512]{1,0:T(8,128)(2,1)S(1)} collective-permute-done((bf16[64,512]{1,0:T(8,128)(2,1)S(1)}, bf16[64,512]{1,0:T(8,128)(2,1)S(1)}, u32[]{:S(2)}, u32[]{:S(2)}) %collective-permute-start.18) | collective-permute-done | bytes 65568 | tf_op jit(solution)/shard_map/ppermute | solution.py:44
  61.7 0.0 copy-start.2
  61.7 1.7 %gate_up.1 = (f32[88,768]{1,0:T(8,128)S(1)}, f32[8,2048]{1,0:T(8,128)S(1)}) custom-call(bf16[64,512]{1,0:T(8,128)(2,1)S(1)} %add_convert_fusion.refs_0_, bf16[64,512]{1,0:T(8,128)(2,1)S(1)} %collective-permute-done.16.refs_1_, bf16[64,512]{1,0:T(8,128)(2,1)S(1)} %collective-permute-done.17.refs_2_, bf16[64,512]{1,0:T(8,128)(2,1)S(1)} %collective-permute-done.18.refs_3_, ...), custom_call_target="tpu_custom_call" | custom-call | tf_op jit(solution)/shard_map/gate_up/pallas_call | solution.py:383
  63.4 0.1 collective-permute-start.23
  63.5 1.5 %collective-permute-done.23.far_ref = f32[88,768]{1,0:T(8,128)S(1)} collective-permute-done((f32[88,768]{1,0:T(8,128)S(1)}, f32[88,768]{1,0:T(8,128)S(1)}, u32[]{:S(2)}, u32[]{:S(2)}) %collective-permute-start.23) | collective-permute-done | bytes 270368 | tf_op jit(solution)/shard_map/ppermute | solution.py:81
  65.0 0.9 %down.1 = (f32[8,3584]{1,0:T(8,128)S(1)}, bf16[8,3584]{1,0:T(8,128)(2,1)S(1)}, bf16[8,3584]{1,0:T(8,128)(2,1)S(1)}, bf16[8,3584]{1,0:T(8,128)(2,1)S(1)}, bf16[8,...) custom-call(f32[88,768]{1,0:T(8,128)S(1)} %get-tuple-element.77.sums, ...), custom_call_target="tpu_custom_call" | custom-call | tf_op jit(solution)/shard_map/down/pallas_call | solution.py:436
  65.9 0.8 %collective-permute-start.24 = (bf16[8,3584]{1,0:T(8,128)(2,1)S(1)}, bf16[8,3584]{1,0:T(8,128)(2,1)S(1)}, u32[]{:S(2)}, u32[]{:S(2)}) collective-permute-start(bf16[8,3584]{1,0:T(8,128)(2,1)S(1)} %get-tuple-element.80), channel_id=1, source_target_pairs={{0,2},{2,0},{4,6},{6,4},{8,10},{10,8},{12,14},{14,12},{1,3},{3,1},... | collective-permute-start | bytes 172040 | tf_op jit(solution)/shard_map/ppermute | solution.py:44
  66.8 0.0 collective-permute-start.25
  66.8 1.6 %collective-permute-start.26 = (bf16[8,3584]{1,0:T(8,128)(2,1)S(1)}, bf16[8,3584]{1,0:T(8,128)(2,1)S(1)}, u32[]{:S(2)}, u32[]{:S(2)}) collective-permute-start(bf16[8,3584]{1,0:T(8,128)(2,1)S(1)} %get-tuple-element.82), channel_id=1, source_target_pairs={{0,6},{2,4},{4,10},{6,8},{8,14},{10,12},{12,2},{14,0},{1,7},{3,5},... | collective-permute-start | bytes 172040 | tf_op jit(solution)/shard_map/ppermute | solution.py:44
  68.3 3.5 %collective-permute-start.27 = (bf16[8,3584]{1,0:T(8,128)(2,1)S(1)}, bf16[8,3584]{1,0:T(8,128)(2,1)S(1)}, u32[]{:S(2)}, u32[]{:S(2)}) collective-permute-start(bf16[8,3584]{1,0:T(8,128)(2,1)S(1)} %get-tuple-element.83), channel_id=1, source_target_pairs={{0,8},{2,10},{4,12},{6,14},{8,0},{10,2},{12,4},{14,6},{1,9},{3,11}... | collective-permute-start | bytes 172040 | tf_op jit(solution)/shard_map/ppermute | solution.py:44
  71.8 0.2 collective-permute-start.28
  72.1 2.4 %collective-permute-start.29 = (bf16[8,3584]{1,0:T(8,128)(2,1)S(1)}, bf16[8,3584]{1,0:T(8,128)(2,1)S(1)}, u32[]{:S(2)}, u32[]{:S(2)}) collective-permute-start(bf16[8,3584]{1,0:T(8,128)(2,1)S(1)} %get-tuple-element.85), channel_id=1, source_target_pairs={{0,12},{2,14},{4,0},{6,2},{8,4},{10,6},{12,8},{14,10},{1,13},{3,15... | collective-permute-start | bytes 172040 | tf_op jit(solution)/shard_map/ppermute | solution.py:44
  74.4 0.0 collective-permute-done.25.rest_2_
  74.4 2.7 %collective-permute-start.30 = (bf16[8,3584]{1,0:T(8,128)(2,1)S(1)}, bf16[8,3584]{1,0:T(8,128)(2,1)S(1)}, u32[]{:S(2)}, u32[]{:S(2)}) collective-permute-start(bf16[8,3584]{1,0:T(8,128)(2,1)S(1)} %get-tuple-element.86), channel_id=1, source_target_pairs={{0,14},{2,12},{4,2},{6,0},{8,6},{10,4},{12,10},{14,8},{1,15},{3,13... | collective-permute-start | bytes 172040 | tf_op jit(solution)/shard_map/ppermute | solution.py:44
  77.1 0.0 collective-permute-done.26.rest_3_
  77.1 0.2 collective-permute-done.27.rest_4_
  77.3 1.8 %collective-permute-done.28.rest_5_ = bf16[8,3584]{1,0:T(8,128)(2,1)S(1)} collective-permute-done((bf16[8,3584]{1,0:T(8,128)(2,1)S(1)}, bf16[8,3584]{1,0:T(8,128)(2,1)S(1)}, u32[]{:S(2)}, u32[]{:S(2)}) %collective-permute-start.28) | collective-permute-done | bytes 57376 | tf_op jit(solution)/shard_map/ppermute | solution.py:44
  79.2 1.1 %collective-permute-done.30.rest_7_ = bf16[8,3584]{1,0:T(8,128)(2,1)S(1)} collective-permute-done((bf16[8,3584]{1,0:T(8,128)(2,1)S(1)}, bf16[8,3584]{1,0:T(8,128)(2,1)S(1)}, u32[]{:S(2)}, u32[]{:S(2)}) %collective-permute-start.30) | collective-permute-done | bytes 57376 | tf_op jit(solution)/shard_map/ppermute | solution.py:44
  80.3 0.7 finish.1
  (17 shorter events, 0.1 us)
Async XLA Ops:
  6.7 7.9 %collective-permute-start = (bf16[8,5376]{1,0:T(8,128)(2,1)}, bf16[8,5376]{1,0:T(8,128)(2,1)S(1)}, u32[]{:S(2)}, u32[]{:S(2)}) collective-permute-start(bf16[8,5376]{1,0:T(8,128)(2,1)} %get-tuple-element.47), channel_id=1, source_target_pairs={{0,4},{2,6},{4,8},{6,10},{8,12},{10,14},{12,0},{14,2},{1,5},{3,7},... | collective-permute-start | bytes 258056 | tf_op jit(solution)/shard_map/ppermute | solution.py:44
  9.8 4.9 %collective-permute-start.1 = (bf16[8,5376]{1,0:T(8,128)(2,1)}, bf16[8,5376]{1,0:T(8,128)(2,1)S(1)}, u32[]{:S(2)}, u32[]{:S(2)}) collective-permute-start(bf16[8,5376]{1,0:T(8,128)(2,1)} %get-tuple-element.61.refs_0_), channel_id=1, source_target_pairs={{0,2},{2,0},{4,6},{6,4},{8,10},{10,8},{12,14},{14,12},{1,3},{3,1},... | collective-permute-start | bytes 258056 | tf_op jit(solution)/shard_map/ppermute | solution.py:44
  11.3 9.3 %collective-permute-start.9 = (bf16[8,5376]{1,0:T(8,128)(2,1)}, bf16[8,5376]{1,0:T(8,128)(2,1)S(1)}, u32[]{:S(2)}, u32[]{:S(2)}) collective-permute-start(bf16[8,5376]{1,0:T(8,128)(2,1)} %get-tuple-element.49), channel_id=1, source_target_pairs={{0,12},{2,14},{4,0},{6,2},{8,4},{10,6},{12,8},{14,10},{1,13},{3,15... | collective-permute-start | bytes 258056 | tf_op jit(solution)/shard_map/ppermute | solution.py:44
  14.7 10.0 %collective-permute-start.2 = (bf16[8,5376]{1,0:T(8,128)(2,1)}, bf16[8,5376]{1,0:T(8,128)(2,1)S(1)}, u32[]{:S(2)}, u32[]{:S(2)}) collective-permute-start(bf16[8,5376]{1,0:T(8,128)(2,1)} %get-tuple-element.51), channel_id=1, source_target_pairs={{0,8},{2,10},{4,12},{6,14},{8,0},{10,2},{12,4},{14,6},{1,9},{3,11}... | collective-permute-start | bytes 258056 | tf_op jit(solution)/shard_map/ppermute | solution.py:44
  17.1 5.7 %collective-permute-start.5 = (bf16[8,4096]{1,0:T(8,128)(2,1)}, bf16[8,4096]{1,0:T(8,128)(2,1)S(1)}, u32[]{:S(2)}, u32[]{:S(2)}) collective-permute-start(bf16[8,4096]{1,0:T(8,128)(2,1)} %get-tuple-element.58.refs_0_), channel_id=1, source_target_pairs={{0,12},{2,14},{4,0},{6,2},{8,4},{10,6},{12,8},{14,10},{1,13},{3,15... | collective-permute-start | bytes 196616 | tf_op jit(solution)/shard_map/ppermute | solution.py:44
  18.5 6.3 %collective-permute-start.4 = (bf16[8,4096]{1,0:T(8,128)(2,1)}, bf16[8,4096]{1,0:T(8,128)(2,1)S(1)}, u32[]{:S(2)}, u32[]{:S(2)}) collective-permute-start(bf16[8,4096]{1,0:T(8,128)(2,1)} %get-tuple-element.58.refs_0_), channel_id=1, source_target_pairs={{0,4},{2,6},{4,8},{6,10},{8,12},{10,14},{12,0},{14,2},{1,5},{3,7},... | collective-permute-start | bytes 196616 | tf_op jit(solution)/shard_map/ppermute | solution.py:44
  19.1 5.6 %collective-permute-start.3 = (bf16[8,4096]{1,0:T(8,128)(2,1)}, bf16[8,4096]{1,0:T(8,128)(2,1)S(1)}, u32[]{:S(2)}, u32[]{:S(2)}) collective-permute-start(bf16[8,4096]{1,0:T(8,128)(2,1)} %get-tuple-element.58.refs_0_), channel_id=1, source_target_pairs={{0,2},{2,0},{4,6},{6,4},{8,10},{10,8},{12,14},{14,12},{1,3},{3,1},... | collective-permute-start | bytes 196616 | tf_op jit(solution)/shard_map/ppermute | solution.py:44
  20.6 5.8 %collective-permute-start.7 = (bf16[8,5376]{1,0:T(8,128)(2,1)S(1)}, bf16[8,5376]{1,0:T(8,128)(2,1)S(1)}, u32[]{:S(2)}, u32[]{:S(2)}) collective-permute-start(bf16[8,5376]{1,0:T(8,128)(2,1)S(1)} %collective-permute-done.refs_2_), channel_id=1, source_target_pairs={{0,2},{2,0},{4,6},{6,4},{8,10},{10,8},{12,14},{14,12},{1,3},{3,1},... | collective-permute-start | bytes 258056 | tf_op jit(solution)/shard_map/ppermute | solution.py:44
  22.8 4.5 %collective-permute-start.10 = (bf16[8,5376]{1,0:T(8,128)(2,1)S(1)}, bf16[8,5376]{1,0:T(8,128)(2,1)S(1)}, u32[]{:S(2)}, u32[]{:S(2)}) collective-permute-start(bf16[8,5376]{1,0:T(8,128)(2,1)S(1)} %collective-permute-done.9.refs_6_), channel_id=1, source_target_pairs={{0,2},{2,0},{4,6},{6,4},{8,10},{10,8},{12,14},{14,12},{1,3},{3,1},... | collective-permute-start | bytes 258056 | tf_op jit(solution)/shard_map/ppermute | solution.py:44
  24.7 7.2 %collective-permute-start.8 = (bf16[8,5376]{1,0:T(8,128)(2,1)S(1)}, bf16[8,5376]{1,0:T(8,128)(2,1)S(1)}, u32[]{:S(2)}, u32[]{:S(2)}) collective-permute-start(bf16[8,5376]{1,0:T(8,128)(2,1)S(1)} %collective-permute-done.2.refs_4_), channel_id=1, source_target_pairs={{0,2},{2,0},{4,6},{6,4},{8,10},{10,8},{12,14},{14,12},{1,3},{3,1},... | collective-permute-start | bytes 258056 | tf_op jit(solution)/shard_map/ppermute | solution.py:44
  26.2 5.7 %collective-permute-start.11 = (bf16[8,4096]{1,0:T(8,128)(2,1)}, bf16[8,4096]{1,0:T(8,128)(2,1)S(1)}, u32[]{:S(2)}, u32[]{:S(2)}) collective-permute-start(bf16[8,4096]{1,0:T(8,128)(2,1)} %get-tuple-element.58.refs_0_), channel_id=1, source_target_pairs={{0,8},{2,10},{4,12},{6,14},{8,0},{10,2},{12,4},{14,6},{1,9},{3,11}... | collective-permute-start | bytes 196616 | tf_op jit(solution)/shard_map/ppermute | solution.py:44
  32.0 15.1 %collective-permute-start.15 = (bf16[3680,512]{1,0:T(8,128)(2,1)}, bf16[3680,512]{1,0:T(8,128)(2,1)S(1)}, u32[]{:S(2)}, u32[]{:S(2)}) collective-permute-start(bf16[3680,512]{1,0:T(8,128)(2,1)} %get-tuple-element.73), channel_id=1, source_target_pairs={{0,1},{1,0},{2,3},{3,2},{4,5},{5,4},{6,7},{7,6},{8,9},{9,8},{10,11... | collective-permute-start | bytes 11304968 | tf_op jit(solution)/shard_map/ppermute | solution.py:81
  32.0 8.5 %collective-permute-start.6 = (bf16[8,4096]{1,0:T(8,128)(2,1)S(1)}, bf16[8,4096]{1,0:T(8,128)(2,1)S(1)}, u32[]{:S(2)}, u32[]{:S(2)}) collective-permute-start(bf16[8,4096]{1,0:T(8,128)(2,1)S(1)} %collective-permute-done.4.refs_2_), channel_id=1, source_target_pairs={{0,2},{2,0},{4,6},{6,4},{8,10},{10,8},{12,14},{14,12},{1,3},{3,1},... | collective-permute-start | bytes 196616 | tf_op jit(solution)/shard_map/ppermute | solution.py:44
  32.8 7.7 %collective-permute-start.13 = (bf16[8,4096]{1,0:T(8,128)(2,1)S(1)}, bf16[8,4096]{1,0:T(8,128)(2,1)S(1)}, u32[]{:S(2)}, u32[]{:S(2)}) collective-permute-start(bf16[8,4096]{1,0:T(8,128)(2,1)S(1)} %collective-permute-done.5.refs_6_), channel_id=1, source_target_pairs={{0,2},{2,0},{4,6},{6,4},{8,10},{10,8},{12,14},{14,12},{1,3},{3,1},... | collective-permute-start | bytes 196616 | tf_op jit(solution)/shard_map/ppermute | solution.py:44
  34.0 6.5 %collective-permute-start.12 = (bf16[8,4096]{1,0:T(8,128)(2,1)S(1)}, bf16[8,4096]{1,0:T(8,128)(2,1)S(1)}, u32[]{:S(2)}, u32[]{:S(2)}) collective-permute-start(bf16[8,4096]{1,0:T(8,128)(2,1)S(1)} %collective-permute-done.11.refs_4_), channel_id=1, source_target_pairs={{0,2},{2,0},{4,6},{6,4},{8,10},{10,8},{12,14},{14,12},{1,3},{3,1},... | collective-permute-start | bytes 196616 | tf_op jit(solution)/shard_map/ppermute | solution.py:44
  34.8 0.9 %copy-start.3 = (bf16[8,5376]{1,0:T(8,128)(2,1)S(1)}, bf16[8,5376]{1,0:T(8,128)(2,1)}, u32[]{:S(2)}) copy-start(bf16[8,5376]{1,0:T(8,128)(2,1)} %get-tuple-element.61.refs_0_) | copy-start | bytes 258052
  35.7 4.8 %copy-start.4 = (bf16[8,4096]{1,0:T(8,128)(2,1)S(1)}, bf16[8,4096]{1,0:T(8,128)(2,1)}, u32[]{:S(2)}) copy-start(bf16[8,4096]{1,0:T(8,128)(2,1)} %get-tuple-element.58.refs_0_) | copy-start | bytes 196612
  40.5 21.2 %copy-start = (bf16[7168,160]{0,1:T(8,128)(2,1)S(1)}, bf16[7168,160]{0,1:T(8,128)(2,1)}, u32[]{:S(2)}) copy-start(bf16[7168,160]{0,1:T(8,128)(2,1)} %param.21) | copy-start | bytes 6881284
  40.5 21.2 %copy-start.1 = (bf16[7168,160]{0,1:T(8,128)(2,1)S(1)}, bf16[7168,160]{0,1:T(8,128)(2,1)}, u32[]{:S(2)}) copy-start(bf16[7168,160]{0,1:T(8,128)(2,1)} %param.22) | copy-start | bytes 6881284
  40.5 21.2 %copy-start.5 = (f32[7168]{0:T(1024)S(1)}, f32[7168]{0:T(1024)}, u32[]{:S(2)}) copy-start(f32[7168]{0:T(1024)} %param.18) | copy-start | bytes 86020
  45.6 1.4 %collective-permute-start.14 = (f32[64,512]{1,0:T(8,128)S(1)}, f32[64,512]{1,0:T(8,128)S(1)}, u32[]{:S(2)}, u32[]{:S(2)}) collective-permute-start(f32[64,512]{1,0:T(8,128)S(1)} %get-tuple-element.72), channel_id=1, source_target_pairs={{0,1},{1,0},{2,3},{3,2},{4,5},{5,4},{6,7},{7,6},{8,9},{9,8},{10,11... | collective-permute-start | bytes 393224 | tf_op jit(solution)/shard_map/ppermute | solution.py:81
  47.1 4.3 %collective-permute-start.21 = (bf16[64,512]{1,0:T(8,128)(2,1)S(1)}, bf16[64,512]{1,0:T(8,128)(2,1)S(1)}, u32[]{:S(2)}, u32[]{:S(2)}) collective-permute-start(bf16[64,512]{1,0:T(8,128)(2,1)S(1)} %add_convert_fusion.refs_0_), channel_id=1, source_target_pairs={{0,12},{2,14},{4,0},{6,2},{8,4},{10,6},{12,8},{14,10},{1,13},{3,15... | collective-permute-start | bytes 196616 | tf_op jit(solution)/shard_map/ppermute | solution.py:44
  48.9 7.3 %collective-permute-start.19 = (bf16[64,512]{1,0:T(8,128)(2,1)S(1)}, bf16[64,512]{1,0:T(8,128)(2,1)S(1)}, u32[]{:S(2)}, u32[]{:S(2)}) collective-permute-start(bf16[64,512]{1,0:T(8,128)(2,1)S(1)} %add_convert_fusion.refs_0_), channel_id=1, source_target_pairs={{0,8},{2,10},{4,12},{6,14},{8,0},{10,2},{12,4},{14,6},{1,9},{3,11}... | collective-permute-start | bytes 196616 | tf_op jit(solution)/shard_map/ppermute | solution.py:44
  48.9 8.5 %collective-permute-start.17 = (bf16[64,512]{1,0:T(8,128)(2,1)S(1)}, bf16[64,512]{1,0:T(8,128)(2,1)S(1)}, u32[]{:S(2)}, u32[]{:S(2)}) collective-permute-start(bf16[64,512]{1,0:T(8,128)(2,1)S(1)} %add_convert_fusion.refs_0_), channel_id=1, source_target_pairs={{0,4},{2,6},{4,8},{6,10},{8,12},{10,14},{12,0},{14,2},{1,5},{3,7},... | collective-permute-start | bytes 196616 | tf_op jit(solution)/shard_map/ppermute | solution.py:44
  49.6 8.7 %collective-permute-start.16 = (bf16[64,512]{1,0:T(8,128)(2,1)S(1)}, bf16[64,512]{1,0:T(8,128)(2,1)S(1)}, u32[]{:S(2)}, u32[]{:S(2)}) collective-permute-start(bf16[64,512]{1,0:T(8,128)(2,1)S(1)} %add_convert_fusion.refs_0_), channel_id=1, source_target_pairs={{0,2},{2,0},{4,6},{6,4},{8,10},{10,8},{12,14},{14,12},{1,3},{3,1},... | collective-permute-start | bytes 196616 | tf_op jit(solution)/shard_map/ppermute | solution.py:44
  51.4 6.8 %collective-permute-start.22 = (bf16[64,512]{1,0:T(8,128)(2,1)S(1)}, bf16[64,512]{1,0:T(8,128)(2,1)S(1)}, u32[]{:S(2)}, u32[]{:S(2)}) collective-permute-start(bf16[64,512]{1,0:T(8,128)(2,1)S(1)} %collective-permute-done.21.refs_6_), channel_id=1, source_target_pairs={{0,2},{2,0},{4,6},{6,4},{8,10},{10,8},{12,14},{14,12},{1,3},{3,1},... | collective-permute-start | bytes 196616 | tf_op jit(solution)/shard_map/ppermute | solution.py:44
  56.2 4.7 %collective-permute-start.20 = (bf16[64,512]{1,0:T(8,128)(2,1)S(1)}, bf16[64,512]{1,0:T(8,128)(2,1)S(1)}, u32[]{:S(2)}, u32[]{:S(2)}) collective-permute-start(bf16[64,512]{1,0:T(8,128)(2,1)S(1)} %collective-permute-done.19.refs_4_), channel_id=1, source_target_pairs={{0,2},{2,0},{4,6},{6,4},{8,10},{10,8},{12,14},{14,12},{1,3},{3,1},... | collective-permute-start | bytes 196616 | tf_op jit(solution)/shard_map/ppermute | solution.py:44
  57.5 4.3 %collective-permute-start.18 = (bf16[64,512]{1,0:T(8,128)(2,1)S(1)}, bf16[64,512]{1,0:T(8,128)(2,1)S(1)}, u32[]{:S(2)}, u32[]{:S(2)}) collective-permute-start(bf16[64,512]{1,0:T(8,128)(2,1)S(1)} %collective-permute-done.17.refs_2_), channel_id=1, source_target_pairs={{0,2},{2,0},{4,6},{6,4},{8,10},{10,8},{12,14},{14,12},{1,3},{3,1},... | collective-permute-start | bytes 196616 | tf_op jit(solution)/shard_map/ppermute | solution.py:44
  61.7 3.3 %copy-start.2 = (bf16[160,7168]{1,0:T(8,128)(2,1)S(1)}, bf16[160,7168]{1,0:T(8,128)(2,1)}, u32[]{:S(2)}) copy-start(bf16[160,7168]{1,0:T(8,128)(2,1)} %down_ref.1) | copy-start | bytes 6881284
  63.4 1.6 %collective-permute-start.23 = (f32[88,768]{1,0:T(8,128)S(1)}, f32[88,768]{1,0:T(8,128)S(1)}, u32[]{:S(2)}, u32[]{:S(2)}) collective-permute-start(f32[88,768]{1,0:T(8,128)S(1)} %get-tuple-element.77.sums_ref), channel_id=1, source_target_pairs={{0,1},{1,0},{2,3},{3,2},{4,5},{5,4},{6,7},{7,6},{8,9},{9,8},{10,11... | collective-permute-start | bytes 811016 | tf_op jit(solution)/shard_map/ppermute | solution.py:81
  65.9 6.1 %collective-permute-start.24 = (bf16[8,3584]{1,0:T(8,128)(2,1)S(1)}, bf16[8,3584]{1,0:T(8,128)(2,1)S(1)}, u32[]{:S(2)}, u32[]{:S(2)}) collective-permute-start(bf16[8,3584]{1,0:T(8,128)(2,1)S(1)} %get-tuple-element.80), channel_id=1, source_target_pairs={{0,2},{2,0},{4,6},{6,4},{8,10},{10,8},{12,14},{14,12},{1,3},{3,1},... | collective-permute-start | bytes 172040 | tf_op jit(solution)/shard_map/ppermute | solution.py:44
  66.8 7.7 %collective-permute-start.25 = (bf16[8,3584]{1,0:T(8,128)(2,1)S(1)}, bf16[8,3584]{1,0:T(8,128)(2,1)S(1)}, u32[]{:S(2)}, u32[]{:S(2)}) collective-permute-start(bf16[8,3584]{1,0:T(8,128)(2,1)S(1)} %get-tuple-element.81), channel_id=1, source_target_pairs={{0,4},{2,6},{4,8},{6,10},{8,12},{10,14},{12,0},{14,2},{1,5},{3,7},... | collective-permute-start | bytes 172040 | tf_op jit(solution)/shard_map/ppermute | solution.py:44
  66.8 10.4 %collective-permute-start.26 = (bf16[8,3584]{1,0:T(8,128)(2,1)S(1)}, bf16[8,3584]{1,0:T(8,128)(2,1)S(1)}, u32[]{:S(2)}, u32[]{:S(2)}) collective-permute-start(bf16[8,3584]{1,0:T(8,128)(2,1)S(1)} %get-tuple-element.82), channel_id=1, source_target_pairs={{0,6},{2,4},{4,10},{6,8},{8,14},{10,12},{12,2},{14,0},{1,7},{3,5},... | collective-permute-start | bytes 172040 | tf_op jit(solution)/shard_map/ppermute | solution.py:44
  68.3 9.0 %collective-permute-start.27 = (bf16[8,3584]{1,0:T(8,128)(2,1)S(1)}, bf16[8,3584]{1,0:T(8,128)(2,1)S(1)}, u32[]{:S(2)}, u32[]{:S(2)}) collective-permute-start(bf16[8,3584]{1,0:T(8,128)(2,1)S(1)} %get-tuple-element.83), channel_id=1, source_target_pairs={{0,8},{2,10},{4,12},{6,14},{8,0},{10,2},{12,4},{14,6},{1,9},{3,11}... | collective-permute-start | bytes 172040 | tf_op jit(solution)/shard_map/ppermute | solution.py:44
  71.8 7.3 %collective-permute-start.28 = (bf16[8,3584]{1,0:T(8,128)(2,1)S(1)}, bf16[8,3584]{1,0:T(8,128)(2,1)S(1)}, u32[]{:S(2)}, u32[]{:S(2)}) collective-permute-start(bf16[8,3584]{1,0:T(8,128)(2,1)S(1)} %get-tuple-element.84), channel_id=1, source_target_pairs={{0,10},{2,8},{4,14},{6,12},{8,2},{10,0},{12,6},{14,4},{1,11},{3,9}... | collective-permute-start | bytes 172040 | tf_op jit(solution)/shard_map/ppermute | solution.py:44
  72.1 7.1 %collective-permute-start.29 = (bf16[8,3584]{1,0:T(8,128)(2,1)S(1)}, bf16[8,3584]{1,0:T(8,128)(2,1)S(1)}, u32[]{:S(2)}, u32[]{:S(2)}) collective-permute-start(bf16[8,3584]{1,0:T(8,128)(2,1)S(1)} %get-tuple-element.85), channel_id=1, source_target_pairs={{0,12},{2,14},{4,0},{6,2},{8,4},{10,6},{12,8},{14,10},{1,13},{3,15... | collective-permute-start | bytes 172040 | tf_op jit(solution)/shard_map/ppermute | solution.py:44
  74.4 5.9 %collective-permute-start.30 = (bf16[8,3584]{1,0:T(8,128)(2,1)S(1)}, bf16[8,3584]{1,0:T(8,128)(2,1)S(1)}, u32[]{:S(2)}, u32[]{:S(2)}) collective-permute-start(bf16[8,3584]{1,0:T(8,128)(2,1)S(1)} %get-tuple-element.86), channel_id=1, source_target_pairs={{0,14},{2,12},{4,2},{6,0},{8,6},{10,4},{12,10},{14,8},{1,15},{3,13... | collective-permute-start | bytes 172040 | tf_op jit(solution)/shard_map/ppermute | solution.py:44

commit v6 on v4

--- a/solution.py
+++ b/solution.py
@@ -31,38 +31,54 @@
 
 
 class Grid:
-    def __init__(self, ep_size, x_size):
-        self.ep, self.x, self.z = ep_size, x_size, ep_size // x_size
-        self.steps = [(s, u) for s in range(self.z) for u in range(x_size)]
+    def __init__(self, ep_size):
+        self.ep, self.x, self.z = ep_size, ep_size // 4, 4
+        self.steps = [(s, u) for s in range(self.z) for u in range(self.x)]
 
     def send(self, arr, s, u):
         pairs = [
-            (z * self.x + x, (z + s) % self.z * self.x + (x + u) % self.x)
+            (z * self.x + x, (z ^ s) * self.x + (x + u) % self.x)
             for z in range(self.z)
             for x in range(self.x)
         ]
         return lax.ppermute(arr, "ep", pairs)
 
-    def spread(self, own, spaced=False):
-        got = {(0, 0): own[0]}
-        near_first = sorted(range(self.z), key=lambda s: min(s, self.z - s))
-        for s in near_first:
-            block = own[s]
-            if spaced and min(s, self.z - s) > 1:
-                block, *_ = lax.optimization_barrier((block, got[1, 0], got[0, self.x - 1]))
-            if s:
-                got[s, 0] = self.send(block, s, 0)
-            for u in range(1, self.x):
+    def carried(self, step):
+        s, u = step
+        return (s, u) if s < 3 else (2, self.x + u)
+
+    def block_sizes(self):
+        return [self.x, self.x, 2 * self.x]
+
+    def spread(self, blocks):
+        got = {(0, 0): blocks[0]}
+        got[2, 0] = self.send(blocks[2], 2, 0)
+        got[1, 0] = self.send(blocks[1], 1, 0)
+        for u in range(1, self.x):
+            got[0, u] = self.send(got[0, 0], 0, u)
+        leaving, *_ = lax.optimization_barrier((got[2, 0], got[1, 0], got[0, self.x - 1]))
+        last = self.send(leaving, 1, 0)
+        for u in range(1, self.x):
+            got[1, u] = self.send(got[1, 0], 0, u)
+        got[3, 0], *_ = lax.optimization_barrier((last, got[1, self.x - 1]))
+        return self.forward(got)
+
+    def spread_at_once(self, own):
+        return self.forward({(s, 0): self.send(own, s, 0) if s else own for s in range(self.z)})
+
+    def forward(self, got):
+        for s, u in self.steps:
+            if (s, u) not in got:
                 got[s, u] = self.send(got[s, 0], 0, u)
         return [got[step] for step in self.steps]
 
     def source(self, step):
         me = lax.axis_index("ep")
-        z = lax.rem(me // self.x - step[0] + self.z, self.z)
+        z = (me // self.x) ^ step[0]
         return z * self.x + lax.rem(lax.rem(me, self.x) - step[1] + self.x, self.x)
 
     def target(self, step):
-        return self.source((-step[0] % self.z, -step[1] % self.x))
+        return self.source((step[0], -step[1] % self.x))
 
 
 def swap(arr):
@@ -95,7 +111,8 @@
     rows, width = queries.shape
     heads = width // HD
     ctx = cache.shape[1]
-    tall = rows * heads
+    parts = HD // LANES
+    sizes = grid.block_sizes()
     note = piece + LANES
     scaling = HD ** (-0.5)
     units, features = gate_t.shape
@@ -106,8 +123,8 @@
     def kernel(*refs):
         sources, rest = refs[:7], refs[7:]
         gate_ref, up_ref, down_ref, rest = rest[0], rest[1], rest[2], rest[3:]
-        out_refs, pack_ref, rest = rest[: grid.z], rest[grid.z], rest[grid.z + 1 :]
-        q_ref, kv_ref, res_ref, ids_ref, wts_ref, len_ref, kept, score, packed, sems, row_sems, pack_sems = rest
+        out_refs, pack_ref, rest = rest[: len(sizes)], rest[len(sizes)], rest[len(sizes) + 1 :]
+        q_ref, kv_ref, res_ref, ids_ref, wts_ref, len_ref, kept, turned, packed, sems, row_sems, pack_sems = rest
         cache_ref = sources[6]
         copies = [
             pltpu.make_async_copy(src, dst, sems.at[i])
@@ -136,19 +153,20 @@
 
         copies[0].wait()
         copies[1].wait()
-        q = q_ref[...].astype(jnp.float32)
-        stacked = jnp.concatenate([q[:, h * HD : (h + 1) * HD] for h in range(heads)], axis=0)
-        narrow = stacked.astype(jnp.bfloat16)
-        new_kv_f = kv_ref[...].astype(jnp.float32)
-        new_k = jnp.concatenate([new_kv_f[:, :HD]] * heads, axis=0)
-        new_v = jnp.concatenate([new_kv_f[:, HD:]] * heads, axis=0)
-        own = jnp.sum(stacked * new_k, axis=1, keepdims=True) * scaling
-        row_of = lax.rem(lax.broadcasted_iota(jnp.int32, (tall, 1), 0), rows)
-        row_wide = lax.rem(lax.broadcasted_iota(jnp.int32, (tall, ctx), 0), rows)
+        for h in range(heads):
+            for c in range(parts):
+                at = h * HD + c * LANES
+                turned[c, h * rows : (h + 1) * rows, :] = q_ref[:, at : at + LANES].astype(jnp.float32)
+        new_k = kv_ref[:, :HD].astype(jnp.float32)
+        new_v = kv_ref[:, HD:].astype(jnp.float32)
+        scores, owns = [], []
         for r in range(rows):
+            q = jnp.concatenate(
+                [turned[c, pl.ds(r, heads, stride=rows), :] for c in range(parts)], axis=1
+            )
+            owns.append(jnp.sum(q * new_k[r : r + 1], axis=1, keepdims=True) * scaling)
             row_copies[r].wait()
-            part = nt_dot(narrow, kept[r, :, :HD])
-            score[...] = jnp.where(row_wide == r, part, score[...]) if r else part
+            scores.append(nt_dot(q.astype(jnp.bfloat16), kept[r, :, :HD]) * scaling)
 
         for copy in copies[2:] + packs:
             copy.wait()
@@ -160,8 +178,9 @@
         for s, u in grid.steps:
             to = grid.target((s, u))
             begin = pl.multiple_of(to * cols + skip, LANES)
-            at = width + u * note
-            out_refs[s][:, at : at + piece] = res_ref[:, pl.ds(begin, piece)]
+            block, place_in = grid.carried((s, u))
+            at = width + place_in * note
+            out_refs[block][:, at : at + piece] = res_ref[:, pl.ds(begin, piece)]
             chosen = ids_ref[...] == to * EXPERTS // grid.ep
             across = jnp.sum(jnp.where(chosen, wts_ref[...], 0.0), axis=0, keepdims=True)
             weight = jnp.sum(
@@ -173,36 +192,38 @@
             tile = jnp.where(lane == 0, high, 0.0)
             tile = jnp.where(lane == 1, middle, tile)
             tile = jnp.where(lane == 2, low, tile)
-            out_refs[s][:, at + piece : at + note] = tile.astype(jnp.bfloat16)
-
-        length = jnp.zeros((tall, 1), jnp.int32)
+            out_refs[block][:, at + piece : at + note] = tile.astype(jnp.bfloat16)
+
+        place = lax.broadcasted_iota(jnp.int32, (heads, ctx), 1)
+        probs, own_probs = [], []
         for r in range(rows):
-            length = jnp.where(row_of == r, len_ref[r], length)
-        place = lax.broadcasted_iota(jnp.int32, (tall, ctx), 1)
-        scores = jnp.where(place < length, score[...] * scaling, -jnp.inf)
-        peak = jnp.maximum(jnp.max(scores, axis=1, keepdims=True), own)
-        exps = jnp.exp(scores - peak)
-        own_exp = jnp.exp(own - peak)
-        denominator = jnp.sum(exps, axis=1, keepdims=True) + own_exp
-        prob = exps / denominator
-        own_prob = (own_exp / denominator).astype(jnp.bfloat16).astype(jnp.float32)
-        total = own_prob * new_v
+            score = jnp.where(place < len_ref[r], scores[r], -jnp.inf)
+            peak = jnp.maximum(jnp.max(score, axis=1, keepdims=True), owns[r])
+            exps = jnp.exp(score - peak)
+            own_exp = jnp.exp(owns[r] - peak)
+            denominator = jnp.sum(exps, axis=1, keepdims=True) + own_exp
+            probs.append((exps / denominator).astype(jnp.bfloat16))
+            own_probs.append((own_exp / denominator).astype(jnp.bfloat16).astype(jnp.float32))
         for r in range(rows):
-            only = jnp.where(row_wide == r, prob, 0.0).astype(jnp.bfloat16)
-            total = total + jnp.dot(only, kept[r, :, HD:], preferred_element_type=jnp.float32)
+            mixed = jnp.dot(probs[r], kept[r, :, HD:], preferred_element_type=jnp.float32)
+            mixed = mixed + own_probs[r] * new_v[r : r + 1]
+            for c in range(parts):
+                turned[c, r * heads : (r + 1) * heads, :] = mixed[:, c * LANES : (c + 1) * LANES]
         for h in range(heads):
-            value = total[h * rows : (h + 1) * rows].astype(jnp.bfloat16)
-            for ref in out_refs:
-                ref[:, h * HD : (h + 1) * HD] = value
+            for c in range(parts):
+                value = turned[c, pl.ds(h, rows, stride=heads), :].astype(jnp.bfloat16)
+                begin = h * HD + c * LANES
+                for ref in out_refs:
+                    ref[:, begin : begin + LANES] = value
         pack_out.wait()
 
     return pl.pallas_call(
         kernel,
         name="attention",
-        out_shape=[shape_of((rows, width + grid.x * note), jnp.bfloat16)] * grid.z
+        out_shape=[shape_of((rows, width + size * note), jnp.bfloat16) for size in sizes]
         + [shape_of((packed_rows, piece), jnp.bfloat16)],
         in_specs=[in_hbm()] * 10,
-        out_specs=[vmem()] * grid.z + [in_hbm()],
+        out_specs=[vmem()] * len(sizes) + [in_hbm()],
         scratch_shapes=[
             pltpu.VMEM(queries.shape, jnp.bfloat16),
             pltpu.VMEM(new_kv.shape, jnp.bfloat16),
@@ -211,7 +232,7 @@
             pltpu.VMEM(route_weights.shape, jnp.float32),
             pltpu.SMEM(lengths.shape, jnp.int32),
             pltpu.VMEM(cache.shape, jnp.bfloat16),
-            pltpu.VMEM((tall, ctx), jnp.float32),
+            pltpu.VMEM((parts, rows * heads, LANES), jnp.float32),
             pltpu.VMEM((packed_rows, piece), jnp.bfloat16),
             pltpu.SemaphoreType.DMA((6,)),
             pltpu.SemaphoreType.DMA((rows,)),
@@ -269,7 +290,7 @@
             other = pl.multiple_of((1 - core) * (cols - piece), LANES)
             for i, (s, u) in enumerate(grid.steps):
                 here = pl.ds(pl.multiple_of(grid.source((s, u)) * rows, rows), rows)
-                at = depth + u * note
+                at = depth + grid.carried((s, u))[1] * note
                 beside = chunk_refs[i][:, at : at + note].astype(jnp.float32)
                 block_rows = slice(i * rows, (i + 1) * rows)
                 ours_ref[here, :] = total[block_rows, pl.ds(mine, piece)] + beside[:, :piece]
@@ -481,19 +502,20 @@
         up_t,
         w_down,
     )
-    chunks = grid.spread(outgoing, spaced=True)
+    chunks = grid.spread(outgoing)
     packed, *_ = lax.optimization_barrier((packed, *chunks))
     far_weights = swap(packed)
     ours, theirs, weight = project(grid, piece, chunks, w_out)
     stream = (ours + swap(theirs)).astype(jnp.bfloat16)
     stream, far_weights = lax.optimization_barrier((stream, far_weights))
-    pieces = grid.spread([stream] * grid.z)
+    pieces = grid.spread_at_once(stream)
     sums, home = gate_up(
         grid, piece, cols, rows, pieces, gain.reshape(1, width), gate_t, up_t, far_weights
     )
     far_sums = swap(sums)
     parts = down(grid, piece, rows, sums, far_sums, weight, w_down, far_weights)
-    shares = [grid.send(p, s, u) if s or u else p for p, (s, u) in zip(parts, grid.steps)]
+    order = sorted(range(grid.ep), key=lambda i: (grid.steps[i] == (0, 0), -grid.steps[i][0]))
+    shares = [grid.send(parts[i], *grid.steps[i]) if any(grid.steps[i]) else parts[i] for i in order]
     return finish(piece, cols, home, far_sums, shares)
 
 
@@ -585,7 +607,7 @@
 def body(*args):
     ep_size, cols, heads_width = lax.axis_size("ep"), args[5].shape[1], args[5].shape[0]
     if ep_size == 8 and lax.axis_size("tp") == 2 and cols % LANES == 0 and heads_width % (8 * HD) == 0:
-        return tuned_body(Grid(ep_size, 2), *args)
+        return tuned_body(Grid(ep_size), *args)
     return general_body(*args)
 
 

time: 78.8 us -> 80.9 us (1.027)
  waiting for transfers between devices: 23.7 us -> 27.3 us
  Pallas kernels: 20.4 us -> 19.3 us
    ppermute x21, waiting for transfers between devices: 20.8 us -> 24.5 us  [send(): return lax.ppermute(arr, 'ep', pairs)]
    pallas_call x1, Pallas kernels: 7.76 us -> 6.72 us  [attention(): pl.pallas_call(kernel, name='attention', out_shape=[shape_of((rows, width...]
  transfers between devices with their start and end apart: 24 -> 24, of which waited for: 11 -> 15; matrix products, arithmetic and copies ran while one was open for 0% -> 0% of each run, Pallas kernels for 12% -> 12%
where the time goes in v6:
time: 80.9 us; the launch traced here: 80.7 us
  starting transfers between devices  32.8 us (41%)
  waiting for transfers between devices  27.3 us (34%)
  Pallas kernels  19.3 us (24%)
  local copies, waits for them, and re-layouts  1.08 us (1%)
    ppermute x21, starting transfers between devices, send(): return lax.ppermute(arr, 'ep', pairs)  32.7 us
    ppermute x21, waiting for transfers between devices, send(): return lax.ppermute(arr, 'ep', pairs)  24.5 us
    pallas_call x1, Pallas kernels, project(): pl.pallas_call(kernel, name='project', grid=(blocks,), out_shape=outs, in...  9.38 us
    pallas_call x1, Pallas kernels, attention(): pl.pallas_call(kernel, name='attention', out_shape=[shape_of((rows, width...  6.72 us
    ppermute x3, waiting for transfers between devices, swap(): return lax.ppermute(arr, 'tp', [(0, 1), (1, 0)])  2.87 us
    pallas_call x1, Pallas kernels, gate_up(): pl.pallas_call(kernel, name='gate_up', out_shape=[shape_of((tall + extra...  1.67 us
  transfers between devices with their start and end apart: 24, of which 15 were waited for; matrix products, arithmetic and copies ran while one was open for 0% of the time, Pallas kernels for 12%

profile of v6, /device:TPU:0, one launch (start us, length us, event | category | flops | bytes accessed | tf_op | source)
XLA Modules:
  0.0 80.7 jit_solution(15780743507710974551)
XLA Ops:
  0.0 6.7 %attention.1 = (bf16[8,9472]{1,0:T(8,128)(2,1)}, bf16[8,9472]{1,0:T(8,128)(2,1)}, bf16[8,10752]{1,0:T(8,128)(2,1)}, bf16[3680,512]{1,0:T(8,128)(2,1)}) custom-call(bf16[8,8192]{1,0:T(8,128)(2,1)} %refs_0_.1, bf16[8,512]{1,0:T(8,128)(2,1)} %refs_1_.1, bf16[8,7168]{1,0:T(8,128)(2,1)} %refs_2_.1, s32[3,8]{1,0:T(4,128)} %bitcast.10, f32[3,8]{1,0:T(4,128)} %bitcast.11, ...), custom_call_target="tpu_custom_call" | custom-call | tf_op jit(solution)/shard_map/attention/pallas_call | solution.py:220
  6.7 4.1 %collective-permute-start.3 = (bf16[8,10752]{1,0:T(8,128)(2,1)}, bf16[8,10752]{1,0:T(8,128)(2,1)S(1)}, u32[]{:S(2)}, u32[]{:S(2)}) collective-permute-start(bf16[8,10752]{1,0:T(8,128)(2,1)} %get-tuple-element.29), channel_id=1, source_target_pairs={{0,8},{2,10},{4,12},{6,14},{8,0},{10,2},{12,4},{14,6},{1,9},{3,11}... | collective-permute-start | bytes 516104 | tf_op jit(solution)/shard_map/ppermute | solution.py:44
  10.8 1.6 %collective-permute-start.1 = (bf16[8,9472]{1,0:T(8,128)(2,1)}, bf16[8,9472]{1,0:T(8,128)(2,1)S(1)}, u32[]{:S(2)}, u32[]{:S(2)}) collective-permute-start(bf16[8,9472]{1,0:T(8,128)(2,1)} %get-tuple-element.28), channel_id=1, source_target_pairs={{0,4},{2,6},{4,0},{6,2},{8,12},{10,14},{12,8},{14,10},{1,5},{3,7},... | collective-permute-start | bytes 454664 | tf_op jit(solution)/shard_map/ppermute | solution.py:44
  12.4 1.5 %collective-permute-start = (bf16[8,9472]{1,0:T(8,128)(2,1)}, bf16[8,9472]{1,0:T(8,128)(2,1)S(1)}, u32[]{:S(2)}, u32[]{:S(2)}) collective-permute-start(bf16[8,9472]{1,0:T(8,128)(2,1)} %get-tuple-element.27.refs_0_), channel_id=1, source_target_pairs={{0,2},{2,0},{4,6},{6,4},{8,10},{10,8},{12,14},{14,12},{1,3},{3,1},... | collective-permute-start | bytes 454664 | tf_op jit(solution)/shard_map/ppermute | solution.py:44
  13.9 4.2 %collective-permute-done.1.refs_2_ = bf16[8,9472]{1,0:T(8,128)(2,1)S(1)} collective-permute-done((bf16[8,9472]{1,0:T(8,128)(2,1)}, bf16[8,9472]{1,0:T(8,128)(2,1)S(1)}, u32[]{:S(2)}, u32[]{:S(2)}) %collective-permute-start.1) | collective-permute-done | bytes 151584 | tf_op jit(solution)/shard_map/ppermute | solution.py:44
  18.1 0.0 collective-permute-done.refs_1_
  18.1 1.0 %collective-permute-done.3.refs_4_ = bf16[8,10752]{1,0:T(8,128)(2,1)S(1)} collective-permute-done((bf16[8,10752]{1,0:T(8,128)(2,1)}, bf16[8,10752]{1,0:T(8,128)(2,1)S(1)}, u32[]{:S(2)}, u32[]{:S(2)}) %collective-permute-start.3) | collective-permute-done | bytes 172064 | tf_op jit(solution)/shard_map/ppermute | solution.py:44
  19.1 1.4 %collective-permute-start.5 = (bf16[8,10752]{1,0:T(8,128)(2,1)S(1)}, bf16[8,10752]{1,0:T(8,128)(2,1)S(1)}, u32[]{:S(2)}, u32[]{:S(2)}) collective-permute-start(bf16[8,10752]{1,0:T(8,128)(2,1)S(1)} %collective-permute-done.3.refs_4_), channel_id=1, source_target_pairs={{0,4},{2,6},{4,0},{6,2},{8,12},{10,14},{12,8},{14,10},{1,5},{3,7},... | collective-permute-start | bytes 516104 | tf_op jit(solution)/shard_map/ppermute | solution.py:44
  20.5 1.5 %collective-permute-start.2 = (bf16[8,9472]{1,0:T(8,128)(2,1)S(1)}, bf16[8,9472]{1,0:T(8,128)(2,1)S(1)}, u32[]{:S(2)}, u32[]{:S(2)}) collective-permute-start(bf16[8,9472]{1,0:T(8,128)(2,1)S(1)} %collective-permute-done.1.refs_2_), channel_id=1, source_target_pairs={{0,2},{2,0},{4,6},{6,4},{8,10},{10,8},{12,14},{14,12},{1,3},{3,1},... | collective-permute-start | bytes 454664 | tf_op jit(solution)/shard_map/ppermute | solution.py:44
  21.9 0.5 collective-permute-start.4
  22.5 4.8 %collective-permute-done.2.refs_3_ = bf16[8,9472]{1,0:T(8,128)(2,1)S(1)} collective-permute-done((bf16[8,9472]{1,0:T(8,128)(2,1)S(1)}, bf16[8,9472]{1,0:T(8,128)(2,1)S(1)}, u32[]{:S(2)}, u32[]{:S(2)}) %collective-permute-start.2) | collective-permute-done | bytes 151584 | tf_op jit(solution)/shard_map/ppermute | solution.py:44
  27.3 0.0 collective-permute-done.5.refs_6_
  27.3 1.5 %collective-permute-start.6 = (bf16[8,10752]{1,0:T(8,128)(2,1)S(1)}, bf16[8,10752]{1,0:T(8,128)(2,1)S(1)}, u32[]{:S(2)}, u32[]{:S(2)}) collective-permute-start(bf16[8,10752]{1,0:T(8,128)(2,1)S(1)} %collective-permute-done.5.refs_6_), channel_id=1, source_target_pairs={{0,2},{2,0},{4,6},{6,4},{8,10},{10,8},{12,14},{14,12},{1,3},{3,1},... | collective-permute-start | bytes 516104 | tf_op jit(solution)/shard_map/ppermute | solution.py:44
  28.8 2.2 %collective-permute-done.4.refs_5_ = bf16[8,10752]{1,0:T(8,128)(2,1)S(1)} collective-permute-done((bf16[8,10752]{1,0:T(8,128)(2,1)S(1)}, bf16[8,10752]{1,0:T(8,128)(2,1)S(1)}, u32[]{:S(2)}, u32[]{:S(2)}) %collective-permute-start.4) | collective-permute-done | bytes 172064 | tf_op jit(solution)/shard_map/ppermute | solution.py:44
  31.0 1.9 %collective-permute-done.6.refs_7_ = bf16[8,10752]{1,0:T(8,128)(2,1)S(1)} collective-permute-done((bf16[8,10752]{1,0:T(8,128)(2,1)S(1)}, bf16[8,10752]{1,0:T(8,128)(2,1)S(1)}, u32[]{:S(2)}, u32[]{:S(2)}) %collective-permute-start.6) | collective-permute-done | bytes 172064 | tf_op jit(solution)/shard_map/ppermute | solution.py:44
  32.9 0.0 copy-start
  32.9 0.0 copy-start.1
  32.9 0.0 collective-permute-start.8
  32.9 0.0 copy-start.3
  32.9 1.1 %copy-done.3 = bf16[8,9472]{1,0:T(8,128)(2,1)S(1)} copy-done((bf16[8,9472]{1,0:T(8,128)(2,1)S(1)}, bf16[8,9472]{1,0:T(8,128)(2,1)}, u32[]{:S(2)}) %copy-start.3) | copy-done | bytes 151576
  34.0 0.0 copy-start.4
  34.0 9.4 %project.1 = (f32[64,512]{1,0:T(8,128)S(1)}, f32[64,512]{1,0:T(8,128)S(1)}, f32[64,128]{1,0:T(8,128)S(1)}) custom-call(bf16[8,9472]{1,0:T(8,128)(2,1)S(1)} %copy-done.3, bf16[8,9472]{1,0:T(8,128)(2,1)S(1)} %collective-permute-done.refs_1_, bf16[8,9472]{1,0:T(8,128)(2,1)S(1)} %collective-permute-done.1.refs_2_, ...), custom_call_target="tpu_custom_call" | custom-call | flops 939524096 | bytes 15990784 | tf_op jit(solution)/shard_map/project/pallas_call | solution.py:306
  43.3 0.1 collective-permute-start.7
  43.4 1.3 %collective-permute-done.7 = f32[64,512]{1,0:T(8,128)S(1)} collective-permute-done((f32[64,512]{1,0:T(8,128)S(1)}, f32[64,512]{1,0:T(8,128)S(1)}, u32[]{:S(2)}, u32[]{:S(2)}) %collective-permute-start.7) | collective-permute-done | bytes 131104 | tf_op jit(solution)/shard_map/ppermute | solution.py:85
  44.8 0.0 collective-permute-done.8.refs_11_.packed_ref
  44.8 3.1 %collective-permute-start.14 = (bf16[64,512]{1,0:T(8,128)(2,1)S(1)}, bf16[64,512]{1,0:T(8,128)(2,1)S(1)}, u32[]{:S(2)}, u32[]{:S(2)}) collective-permute-start(bf16[64,512]{1,0:T(8,128)(2,1)S(1)} %add_convert_fusion.refs_0_), channel_id=1, source_target_pairs={{0,12},{2,14},{4,8},{6,10},{8,4},{10,6},{12,0},{14,2},{1,13},{3,15... | collective-permute-start | bytes 196616 | tf_op jit(solution)/shard_map/ppermute | solution.py:44
  47.8 0.4 collective-permute-start.12
  48.2 1.0 %collective-permute-start.10 = (bf16[64,512]{1,0:T(8,128)(2,1)S(1)}, bf16[64,512]{1,0:T(8,128)(2,1)S(1)}, u32[]{:S(2)}, u32[]{:S(2)}) collective-permute-start(bf16[64,512]{1,0:T(8,128)(2,1)S(1)} %add_convert_fusion.refs_0_), channel_id=1, source_target_pairs={{0,4},{2,6},{4,0},{6,2},{8,12},{10,14},{12,8},{14,10},{1,5},{3,7},... | collective-permute-start | bytes 196616 | tf_op jit(solution)/shard_map/ppermute | solution.py:44
  49.2 1.5 %collective-permute-start.9 = (bf16[64,512]{1,0:T(8,128)(2,1)S(1)}, bf16[64,512]{1,0:T(8,128)(2,1)S(1)}, u32[]{:S(2)}, u32[]{:S(2)}) collective-permute-start(bf16[64,512]{1,0:T(8,128)(2,1)S(1)} %add_convert_fusion.refs_0_), channel_id=1, source_target_pairs={{0,2},{2,0},{4,6},{6,4},{8,10},{10,8},{12,14},{14,12},{1,3},{3,1},... | collective-permute-start | bytes 196616 | tf_op jit(solution)/shard_map/ppermute | solution.py:44
  50.7 0.3 collective-permute-done.14.refs_6_
  51.0 1.5 %collective-permute-start.15 = (bf16[64,512]{1,0:T(8,128)(2,1)S(1)}, bf16[64,512]{1,0:T(8,128)(2,1)S(1)}, u32[]{:S(2)}, u32[]{:S(2)}) collective-permute-start(bf16[64,512]{1,0:T(8,128)(2,1)S(1)} %collective-permute-done.14.refs_6_), channel_id=1, source_target_pairs={{0,2},{2,0},{4,6},{6,4},{8,10},{10,8},{12,14},{14,12},{1,3},{3,1},... | collective-permute-start | bytes 196616 | tf_op jit(solution)/shard_map/ppermute | solution.py:44
  52.5 2.3 %collective-permute-done.12.refs_4_ = bf16[64,512]{1,0:T(8,128)(2,1)S(1)} collective-permute-done((bf16[64,512]{1,0:T(8,128)(2,1)S(1)}, bf16[64,512]{1,0:T(8,128)(2,1)S(1)}, u32[]{:S(2)}, u32[]{:S(2)}) %collective-permute-start.12) | collective-permute-done | bytes 65568 | tf_op jit(solution)/shard_map/ppermute | solution.py:44
  54.7 1.5 %collective-permute-start.13 = (bf16[64,512]{1,0:T(8,128)(2,1)S(1)}, bf16[64,512]{1,0:T(8,128)(2,1)S(1)}, u32[]{:S(2)}, u32[]{:S(2)}) collective-permute-start(bf16[64,512]{1,0:T(8,128)(2,1)S(1)} %collective-permute-done.12.refs_4_), channel_id=1, source_target_pairs={{0,2},{2,0},{4,6},{6,4},{8,10},{10,8},{12,14},{14,12},{1,3},{3,1},... | collective-permute-start | bytes 196616 | tf_op jit(solution)/shard_map/ppermute | solution.py:44
  56.2 0.0 collective-permute-done.10.refs_2_
  56.2 0.5 collective-permute-start.11
  56.8 0.0 collective-permute-done.9.refs_1_
  56.8 0.0 collective-permute-done.15.refs_7_
  56.8 2.9 %collective-permute-done.13.refs_5_ = bf16[64,512]{1,0:T(8,128)(2,1)S(1)} collective-permute-done((bf16[64,512]{1,0:T(8,128)(2,1)S(1)}, bf16[64,512]{1,0:T(8,128)(2,1)S(1)}, u32[]{:S(2)}, u32[]{:S(2)}) %collective-permute-start.13) | collective-permute-done | bytes 65568 | tf_op jit(solution)/shard_map/ppermute | solution.py:44
  59.6 0.9 %collective-permute-done.11.refs_3_ = bf16[64,512]{1,0:T(8,128)(2,1)S(1)} collective-permute-done((bf16[64,512]{1,0:T(8,128)(2,1)S(1)}, bf16[64,512]{1,0:T(8,128)(2,1)S(1)}, u32[]{:S(2)}, u32[]{:S(2)}) %collective-permute-start.11) | collective-permute-done | bytes 65568 | tf_op jit(solution)/shard_map/ppermute | solution.py:44
  60.5 0.0 copy-done
  60.5 0.0 copy-done.1
  60.5 0.0 copy-done.4
  60.5 0.0 copy-start.2
  60.5 1.7 %gate_up.1 = (f32[88,768]{1,0:T(8,128)S(1)}, f32[8,2048]{1,0:T(8,128)S(1)}) custom-call(bf16[64,512]{1,0:T(8,128)(2,1)S(1)} %add_convert_fusion.refs_0_, bf16[64,512]{1,0:T(8,128)(2,1)S(1)} %collective-permute-done.9.refs_1_, bf16[64,512]{1,0:T(8,128)(2,1)S(1)} %collective-permute-done.10.refs_2_, bf16[64,512]{1,0:T(8,128)(2,1)S(1)} %collective-permute-done.11.refs_3_, ...), custom_call_target="tpu_custom_call" | custom-call | tf_op jit(solution)/shard_map/gate_up/pallas_call | solution.py:369
  62.2 0.1 collective-permute-start.16
  62.3 1.5 %collective-permute-done.16.far_ref = f32[88,768]{1,0:T(8,128)S(1)} collective-permute-done((f32[88,768]{1,0:T(8,128)S(1)}, f32[88,768]{1,0:T(8,128)S(1)}, u32[]{:S(2)}, u32[]{:S(2)}) %collective-permute-start.16) | collective-permute-done | bytes 270368 | tf_op jit(solution)/shard_map/ppermute | solution.py:85
  63.8 0.0 copy-done.2
  63.8 0.9 %down.1 = (f32[8,3584]{1,0:T(8,128)S(1)}, bf16[8,3584]{1,0:T(8,128)(2,1)S(1)}, bf16[8,3584]{1,0:T(8,128)(2,1)S(1)}, bf16[8,3584]{1,0:T(8,128)(2,1)S(1)}, bf16[8,...) custom-call(f32[88,768]{1,0:T(8,128)S(1)} %get-tuple-element.39.sums, ...), custom_call_target="tpu_custom_call" | custom-call | tf_op jit(solution)/shard_map/down/pallas_call | solution.py:422
  64.7 2.7 %collective-permute-start.17 = (bf16[8,3584]{1,0:T(8,128)(2,1)S(1)}, bf16[8,3584]{1,0:T(8,128)(2,1)S(1)}, u32[]{:S(2)}, u32[]{:S(2)}) collective-permute-start(bf16[8,3584]{1,0:T(8,128)(2,1)S(1)} %get-tuple-element.41), channel_id=1, source_target_pairs={{0,12},{2,14},{4,8},{6,10},{8,4},{10,6},{12,0},{14,2},{1,13},{3,15... | collective-permute-start | bytes 172040 | tf_op jit(solution)/shard_map/ppermute | solution.py:44
  67.4 1.6 %collective-permute-start.18 = (bf16[8,3584]{1,0:T(8,128)(2,1)S(1)}, bf16[8,3584]{1,0:T(8,128)(2,1)S(1)}, u32[]{:S(2)}, u32[]{:S(2)}) collective-permute-start(bf16[8,3584]{1,0:T(8,128)(2,1)S(1)} %get-tuple-element.42), channel_id=1, source_target_pairs={{0,14},{2,12},{4,10},{6,8},{8,6},{10,4},{12,2},{14,0},{1,15},{3,13... | collective-permute-start | bytes 172040 | tf_op jit(solution)/shard_map/ppermute | solution.py:44
  68.9 0.3 collective-permute-start.19
  69.2 3.2 %collective-permute-start.20 = (bf16[8,3584]{1,0:T(8,128)(2,1)S(1)}, bf16[8,3584]{1,0:T(8,128)(2,1)S(1)}, u32[]{:S(2)}, u32[]{:S(2)}) collective-permute-start(bf16[8,3584]{1,0:T(8,128)(2,1)S(1)} %get-tuple-element.44), channel_id=1, source_target_pairs={{0,10},{2,8},{4,14},{6,12},{8,2},{10,0},{12,6},{14,4},{1,11},{3,9}... | collective-permute-start | bytes 172040 | tf_op jit(solution)/shard_map/ppermute | solution.py:44
  72.4 0.3 collective-permute-start.21
  72.7 0.0 collective-permute-done.17.rest_0_
  72.7 2.1 %collective-permute-start.22 = (bf16[8,3584]{1,0:T(8,128)(2,1)S(1)}, bf16[8,3584]{1,0:T(8,128)(2,1)S(1)}, u32[]{:S(2)}, u32[]{:S(2)}) collective-permute-start(bf16[8,3584]{1,0:T(8,128)(2,1)S(1)} %get-tuple-element.46), channel_id=1, source_target_pairs={{0,6},{2,4},{4,2},{6,0},{8,14},{10,12},{12,10},{14,8},{1,7},{3,5},... | collective-permute-start | bytes 172040 | tf_op jit(solution)/shard_map/ppermute | solution.py:44
  74.8 0.0 collective-permute-done.18.rest_1_
  74.8 1.1 %collective-permute-start.23 = (bf16[8,3584]{1,0:T(8,128)(2,1)S(1)}, bf16[8,3584]{1,0:T(8,128)(2,1)S(1)}, u32[]{:S(2)}, u32[]{:S(2)}) collective-permute-start(bf16[8,3584]{1,0:T(8,128)(2,1)S(1)} %get-tuple-element.47), channel_id=1, source_target_pairs={{0,2},{2,0},{4,6},{6,4},{8,10},{10,8},{12,14},{14,12},{1,3},{3,1},... | collective-permute-start | bytes 172040 | tf_op jit(solution)/shard_map/ppermute | solution.py:44
  75.9 0.3 collective-permute-done.19.rest_2_
  76.2 2.6 %collective-permute-done.20.rest_3_ = bf16[8,3584]{1,0:T(8,128)(2,1)S(1)} collective-permute-done((bf16[8,3584]{1,0:T(8,128)(2,1)S(1)}, bf16[8,3584]{1,0:T(8,128)(2,1)S(1)}, u32[]{:S(2)}, u32[]{:S(2)}) %collective-permute-start.20) | collective-permute-done | bytes 57376 | tf_op jit(solution)/shard_map/ppermute | solution.py:44
  78.8 0.0 collective-permute-done.21.rest_4_
  78.8 0.6 collective-permute-done.22.rest_5_
  79.5 0.5 collective-permute-done.23.rest_6_
  80.0 0.7 finish.1
  (1 shorter events, 0.0 us)
Async XLA Ops:
  6.7 12.4 %collective-permute-start.3 = (bf16[8,10752]{1,0:T(8,128)(2,1)}, bf16[8,10752]{1,0:T(8,128)(2,1)S(1)}, u32[]{:S(2)}, u32[]{:S(2)}) collective-permute-start(bf16[8,10752]{1,0:T(8,128)(2,1)} %get-tuple-element.29), channel_id=1, source_target_pairs={{0,8},{2,10},{4,12},{6,14},{8,0},{10,2},{12,4},{14,6},{1,9},{3,11}... | collective-permute-start | bytes 516104 | tf_op jit(solution)/shard_map/ppermute | solution.py:44
  10.8 7.2 %collective-permute-start.1 = (bf16[8,9472]{1,0:T(8,128)(2,1)}, bf16[8,9472]{1,0:T(8,128)(2,1)S(1)}, u32[]{:S(2)}, u32[]{:S(2)}) collective-permute-start(bf16[8,9472]{1,0:T(8,128)(2,1)} %get-tuple-element.28), channel_id=1, source_target_pairs={{0,4},{2,6},{4,0},{6,2},{8,12},{10,14},{12,8},{14,10},{1,5},{3,7},... | collective-permute-start | bytes 454664 | tf_op jit(solution)/shard_map/ppermute | solution.py:44
  12.4 5.7 %collective-permute-start = (bf16[8,9472]{1,0:T(8,128)(2,1)}, bf16[8,9472]{1,0:T(8,128)(2,1)S(1)}, u32[]{:S(2)}, u32[]{:S(2)}) collective-permute-start(bf16[8,9472]{1,0:T(8,128)(2,1)} %get-tuple-element.27.refs_0_), channel_id=1, source_target_pairs={{0,2},{2,0},{4,6},{6,4},{8,10},{10,8},{12,14},{14,12},{1,3},{3,1},... | collective-permute-start | bytes 454664 | tf_op jit(solution)/shard_map/ppermute | solution.py:44
  19.1 8.2 %collective-permute-start.5 = (bf16[8,10752]{1,0:T(8,128)(2,1)S(1)}, bf16[8,10752]{1,0:T(8,128)(2,1)S(1)}, u32[]{:S(2)}, u32[]{:S(2)}) collective-permute-start(bf16[8,10752]{1,0:T(8,128)(2,1)S(1)} %collective-permute-done.3.refs_4_), channel_id=1, source_target_pairs={{0,4},{2,6},{4,0},{6,2},{8,12},{10,14},{12,8},{14,10},{1,5},{3,7},... | collective-permute-start | bytes 516104 | tf_op jit(solution)/shard_map/ppermute | solution.py:44
  20.5 6.9 %collective-permute-start.2 = (bf16[8,9472]{1,0:T(8,128)(2,1)S(1)}, bf16[8,9472]{1,0:T(8,128)(2,1)S(1)}, u32[]{:S(2)}, u32[]{:S(2)}) collective-permute-start(bf16[8,9472]{1,0:T(8,128)(2,1)S(1)} %collective-permute-done.1.refs_2_), channel_id=1, source_target_pairs={{0,2},{2,0},{4,6},{6,4},{8,10},{10,8},{12,14},{14,12},{1,3},{3,1},... | collective-permute-start | bytes 454664 | tf_op jit(solution)/shard_map/ppermute | solution.py:44
  21.9 9.1 %collective-permute-start.4 = (bf16[8,10752]{1,0:T(8,128)(2,1)S(1)}, bf16[8,10752]{1,0:T(8,128)(2,1)S(1)}, u32[]{:S(2)}, u32[]{:S(2)}) collective-permute-start(bf16[8,10752]{1,0:T(8,128)(2,1)S(1)} %collective-permute-done.3.refs_4_), channel_id=1, source_target_pairs={{0,2},{2,0},{4,6},{6,4},{8,10},{10,8},{12,14},{14,12},{1,3},{3,1},... | collective-permute-start | bytes 516104 | tf_op jit(solution)/shard_map/ppermute | solution.py:44
  27.3 5.5 %collective-permute-start.6 = (bf16[8,10752]{1,0:T(8,128)(2,1)S(1)}, bf16[8,10752]{1,0:T(8,128)(2,1)S(1)}, u32[]{:S(2)}, u32[]{:S(2)}) collective-permute-start(bf16[8,10752]{1,0:T(8,128)(2,1)S(1)} %collective-permute-done.5.refs_6_), channel_id=1, source_target_pairs={{0,2},{2,0},{4,6},{6,4},{8,10},{10,8},{12,14},{14,12},{1,3},{3,1},... | collective-permute-start | bytes 516104 | tf_op jit(solution)/shard_map/ppermute | solution.py:44
  32.9 27.6 %copy-start = (bf16[7168,160]{0,1:T(8,128)(2,1)S(1)}, bf16[7168,160]{0,1:T(8,128)(2,1)}, u32[]{:S(2)}) copy-start(bf16[7168,160]{0,1:T(8,128)(2,1)} %param.21) | copy-start | bytes 6881284
  32.9 27.6 %copy-start.1 = (bf16[7168,160]{0,1:T(8,128)(2,1)S(1)}, bf16[7168,160]{0,1:T(8,128)(2,1)}, u32[]{:S(2)}) copy-start(bf16[7168,160]{0,1:T(8,128)(2,1)} %param.22) | copy-start | bytes 6881284
  32.9 11.9 %collective-permute-start.8 = (bf16[3680,512]{1,0:T(8,128)(2,1)}, bf16[3680,512]{1,0:T(8,128)(2,1)S(1)}, u32[]{:S(2)}, u32[]{:S(2)}) collective-permute-start(bf16[3680,512]{1,0:T(8,128)(2,1)} %get-tuple-element.35), channel_id=1, source_target_pairs={{0,1},{1,0},{2,3},{3,2},{4,5},{5,4},{6,7},{7,6},{8,9},{9,8},{10,11... | collective-permute-start | bytes 11304968 | tf_op jit(solution)/shard_map/ppermute | solution.py:85
  32.9 1.1 %copy-start.3 = (bf16[8,9472]{1,0:T(8,128)(2,1)S(1)}, bf16[8,9472]{1,0:T(8,128)(2,1)}, u32[]{:S(2)}) copy-start(bf16[8,9472]{1,0:T(8,128)(2,1)} %get-tuple-element.27.refs_0_) | copy-start | bytes 454660
  34.0 26.6 %copy-start.4 = (f32[7168]{0:T(1024)S(1)}, f32[7168]{0:T(1024)}, u32[]{:S(2)}) copy-start(f32[7168]{0:T(1024)} %param.18) | copy-start | bytes 86020
  43.3 1.4 %collective-permute-start.7 = (f32[64,512]{1,0:T(8,128)S(1)}, f32[64,512]{1,0:T(8,128)S(1)}, u32[]{:S(2)}, u32[]{:S(2)}) collective-permute-start(f32[64,512]{1,0:T(8,128)S(1)} %get-tuple-element.33), channel_id=1, source_target_pairs={{0,1},{1,0},{2,3},{3,2},{4,5},{5,4},{6,7},{7,6},{8,9},{9,8},{10,11... | collective-permute-start | bytes 393224 | tf_op jit(solution)/shard_map/ppermute | solution.py:85
  44.8 6.2 %collective-permute-start.14 = (bf16[64,512]{1,0:T(8,128)(2,1)S(1)}, bf16[64,512]{1,0:T(8,128)(2,1)S(1)}, u32[]{:S(2)}, u32[]{:S(2)}) collective-permute-start(bf16[64,512]{1,0:T(8,128)(2,1)S(1)} %add_convert_fusion.refs_0_), channel_id=1, source_target_pairs={{0,12},{2,14},{4,8},{6,10},{8,4},{10,6},{12,0},{14,2},{1,13},{3,15... | collective-permute-start | bytes 196616 | tf_op jit(solution)/shard_map/ppermute | solution.py:44
  47.8 6.9 %collective-permute-start.12 = (bf16[64,512]{1,0:T(8,128)(2,1)S(1)}, bf16[64,512]{1,0:T(8,128)(2,1)S(1)}, u32[]{:S(2)}, u32[]{:S(2)}) collective-permute-start(bf16[64,512]{1,0:T(8,128)(2,1)S(1)} %add_convert_fusion.refs_0_), channel_id=1, source_target_pairs={{0,8},{2,10},{4,12},{6,14},{8,0},{10,2},{12,4},{14,6},{1,9},{3,11}... | collective-permute-start | bytes 196616 | tf_op jit(solution)/shard_map/ppermute | solution.py:44
  48.2 8.0 %collective-permute-start.10 = (bf16[64,512]{1,0:T(8,128)(2,1)S(1)}, bf16[64,512]{1,0:T(8,128)(2,1)S(1)}, u32[]{:S(2)}, u32[]{:S(2)}) collective-permute-start(bf16[64,512]{1,0:T(8,128)(2,1)S(1)} %add_convert_fusion.refs_0_), channel_id=1, source_target_pairs={{0,4},{2,6},{4,0},{6,2},{8,12},{10,14},{12,8},{14,10},{1,5},{3,7},... | collective-permute-start | bytes 196616 | tf_op jit(solution)/shard_map/ppermute | solution.py:44
  49.2 7.5 %collective-permute-start.9 = (bf16[64,512]{1,0:T(8,128)(2,1)S(1)}, bf16[64,512]{1,0:T(8,128)(2,1)S(1)}, u32[]{:S(2)}, u32[]{:S(2)}) collective-permute-start(bf16[64,512]{1,0:T(8,128)(2,1)S(1)} %add_convert_fusion.refs_0_), channel_id=1, source_target_pairs={{0,2},{2,0},{4,6},{6,4},{8,10},{10,8},{12,14},{14,12},{1,3},{3,1},... | collective-permute-start | bytes 196616 | tf_op jit(solution)/shard_map/ppermute | solution.py:44
  51.0 5.8 %collective-permute-start.15 = (bf16[64,512]{1,0:T(8,128)(2,1)S(1)}, bf16[64,512]{1,0:T(8,128)(2,1)S(1)}, u32[]{:S(2)}, u32[]{:S(2)}) collective-permute-start(bf16[64,512]{1,0:T(8,128)(2,1)S(1)} %collective-permute-done.14.refs_6_), channel_id=1, source_target_pairs={{0,2},{2,0},{4,6},{6,4},{8,10},{10,8},{12,14},{14,12},{1,3},{3,1},... | collective-permute-start | bytes 196616 | tf_op jit(solution)/shard_map/ppermute | solution.py:44
  54.7 4.9 %collective-permute-start.13 = (bf16[64,512]{1,0:T(8,128)(2,1)S(1)}, bf16[64,512]{1,0:T(8,128)(2,1)S(1)}, u32[]{:S(2)}, u32[]{:S(2)}) collective-permute-start(bf16[64,512]{1,0:T(8,128)(2,1)S(1)} %collective-permute-done.12.refs_4_), channel_id=1, source_target_pairs={{0,2},{2,0},{4,6},{6,4},{8,10},{10,8},{12,14},{14,12},{1,3},{3,1},... | collective-permute-start | bytes 196616 | tf_op jit(solution)/shard_map/ppermute | solution.py:44
  56.2 4.3 %collective-permute-start.11 = (bf16[64,512]{1,0:T(8,128)(2,1)S(1)}, bf16[64,512]{1,0:T(8,128)(2,1)S(1)}, u32[]{:S(2)}, u32[]{:S(2)}) collective-permute-start(bf16[64,512]{1,0:T(8,128)(2,1)S(1)} %collective-permute-done.10.refs_2_), channel_id=1, source_target_pairs={{0,2},{2,0},{4,6},{6,4},{8,10},{10,8},{12,14},{14,12},{1,3},{3,1},... | collective-permute-start | bytes 196616 | tf_op jit(solution)/shard_map/ppermute | solution.py:44
  60.5 3.3 %copy-start.2 = (bf16[160,7168]{1,0:T(8,128)(2,1)S(1)}, bf16[160,7168]{1,0:T(8,128)(2,1)}, u32[]{:S(2)}) copy-start(bf16[160,7168]{1,0:T(8,128)(2,1)} %down_ref.1) | copy-start | bytes 6881284
  62.2 1.6 %collective-permute-start.16 = (f32[88,768]{1,0:T(8,128)S(1)}, f32[88,768]{1,0:T(8,128)S(1)}, u32[]{:S(2)}, u32[]{:S(2)}) collective-permute-start(f32[88,768]{1,0:T(8,128)S(1)} %get-tuple-element.39.sums_ref), channel_id=1, source_target_pairs={{0,1},{1,0},{2,3},{3,2},{4,5},{5,4},{6,7},{7,6},{8,9},{9,8},{10,11... | collective-permute-start | bytes 811016 | tf_op jit(solution)/shard_map/ppermute | solution.py:85
  64.7 8.0 %collective-permute-start.17 = (bf16[8,3584]{1,0:T(8,128)(2,1)S(1)}, bf16[8,3584]{1,0:T(8,128)(2,1)S(1)}, u32[]{:S(2)}, u32[]{:S(2)}) collective-permute-start(bf16[8,3584]{1,0:T(8,128)(2,1)S(1)} %get-tuple-element.41), channel_id=1, source_target_pairs={{0,12},{2,14},{4,8},{6,10},{8,4},{10,6},{12,0},{14,2},{1,13},{3,15... | collective-permute-start | bytes 172040 | tf_op jit(solution)/shard_map/ppermute | solution.py:44
  67.4 7.4 %collective-permute-start.18 = (bf16[8,3584]{1,0:T(8,128)(2,1)S(1)}, bf16[8,3584]{1,0:T(8,128)(2,1)S(1)}, u32[]{:S(2)}, u32[]{:S(2)}) collective-permute-start(bf16[8,3584]{1,0:T(8,128)(2,1)S(1)} %get-tuple-element.42), channel_id=1, source_target_pairs={{0,14},{2,12},{4,10},{6,8},{8,6},{10,4},{12,2},{14,0},{1,15},{3,13... | collective-permute-start | bytes 172040 | tf_op jit(solution)/shard_map/ppermute | solution.py:44
  68.9 7.3 %collective-permute-start.19 = (bf16[8,3584]{1,0:T(8,128)(2,1)S(1)}, bf16[8,3584]{1,0:T(8,128)(2,1)S(1)}, u32[]{:S(2)}, u32[]{:S(2)}) collective-permute-start(bf16[8,3584]{1,0:T(8,128)(2,1)S(1)} %get-tuple-element.43), channel_id=1, source_target_pairs={{0,8},{2,10},{4,12},{6,14},{8,0},{10,2},{12,4},{14,6},{1,9},{3,11}... | collective-permute-start | bytes 172040 | tf_op jit(solution)/shard_map/ppermute | solution.py:44
  69.2 9.6 %collective-permute-start.20 = (bf16[8,3584]{1,0:T(8,128)(2,1)S(1)}, bf16[8,3584]{1,0:T(8,128)(2,1)S(1)}, u32[]{:S(2)}, u32[]{:S(2)}) collective-permute-start(bf16[8,3584]{1,0:T(8,128)(2,1)S(1)} %get-tuple-element.44), channel_id=1, source_target_pairs={{0,10},{2,8},{4,14},{6,12},{8,2},{10,0},{12,6},{14,4},{1,11},{3,9}... | collective-permute-start | bytes 172040 | tf_op jit(solution)/shard_map/ppermute | solution.py:44
  72.4 6.4 %collective-permute-start.21 = (bf16[8,3584]{1,0:T(8,128)(2,1)S(1)}, bf16[8,3584]{1,0:T(8,128)(2,1)S(1)}, u32[]{:S(2)}, u32[]{:S(2)}) collective-permute-start(bf16[8,3584]{1,0:T(8,128)(2,1)S(1)} %get-tuple-element.45), channel_id=1, source_target_pairs={{0,4},{2,6},{4,0},{6,2},{8,12},{10,14},{12,8},{14,10},{1,5},{3,7},... | collective-permute-start | bytes 172040 | tf_op jit(solution)/shard_map/ppermute | solution.py:44
  72.7 6.8 %collective-permute-start.22 = (bf16[8,3584]{1,0:T(8,128)(2,1)S(1)}, bf16[8,3584]{1,0:T(8,128)(2,1)S(1)}, u32[]{:S(2)}, u32[]{:S(2)}) collective-permute-start(bf16[8,3584]{1,0:T(8,128)(2,1)S(1)} %get-tuple-element.46), channel_id=1, source_target_pairs={{0,6},{2,4},{4,2},{6,0},{8,14},{10,12},{12,10},{14,8},{1,7},{3,5},... | collective-permute-start | bytes 172040 | tf_op jit(solution)/shard_map/ppermute | solution.py:44
  74.8 5.2 %collective-permute-start.23 = (bf16[8,3584]{1,0:T(8,128)(2,1)S(1)}, bf16[8,3584]{1,0:T(8,128)(2,1)S(1)}, u32[]{:S(2)}, u32[]{:S(2)}) collective-permute-start(bf16[8,3584]{1,0:T(8,128)(2,1)S(1)} %get-tuple-element.47), channel_id=1, source_target_pairs={{0,2},{2,0},{4,6},{6,4},{8,10},{10,8},{12,14},{14,12},{1,3},{3,1},... | collective-permute-start | bytes 172040 | tf_op jit(solution)/shard_map/ppermute | solution.py:44

commit v7 on v6

--- a/solution.py
+++ b/solution.py
@@ -37,48 +37,39 @@
 
     def send(self, arr, s, u):
         pairs = [
-            (z * self.x + x, (z ^ s) * self.x + (x + u) % self.x)
+            (z * self.x + x, (z + s) % self.z * self.x + (x + u) % self.x)
             for z in range(self.z)
             for x in range(self.x)
         ]
         return lax.ppermute(arr, "ep", pairs)
 
-    def carried(self, step):
-        s, u = step
-        return (s, u) if s < 3 else (2, self.x + u)
-
-    def block_sizes(self):
-        return [self.x, self.x, 2 * self.x]
-
-    def spread(self, blocks):
-        got = {(0, 0): blocks[0]}
-        got[2, 0] = self.send(blocks[2], 2, 0)
-        got[1, 0] = self.send(blocks[1], 1, 0)
+    def along_x(self, got, s):
         for u in range(1, self.x):
-            got[0, u] = self.send(got[0, 0], 0, u)
-        leaving, *_ = lax.optimization_barrier((got[2, 0], got[1, 0], got[0, self.x - 1]))
-        last = self.send(leaving, 1, 0)
-        for u in range(1, self.x):
-            got[1, u] = self.send(got[1, 0], 0, u)
-        got[3, 0], *_ = lax.optimization_barrier((last, got[1, self.x - 1]))
-        return self.forward(got)
-
-    def spread_at_once(self, own):
-        return self.forward({(s, 0): self.send(own, s, 0) if s else own for s in range(self.z)})
-
-    def forward(self, got):
-        for s, u in self.steps:
-            if (s, u) not in got:
-                got[s, u] = self.send(got[s, 0], 0, u)
+            got[s, u] = self.send(got[s, 0], 0, u)
+
+    def spread(self, own, spaced):
+        got = {(0, 0): own[0]}
+        got[1, 0] = self.send(own[1], 1, 0)
+        got[3, 0] = self.send(own[3], 3, 0)
+        self.along_x(got, 0)
+        far = own[2]
+        if spaced:
+            far, *_ = lax.optimization_barrier((far, got[1, 0], got[0, self.x - 1]))
+        got[2, 0] = self.send(far, 2, 0)
+        self.along_x(got, 1)
+        self.along_x(got, 3)
+        if not spaced:
+            got[2, 0], *_ = lax.optimization_barrier((got[2, 0], got[1, self.x - 1]))
+        self.along_x(got, 2)
         return [got[step] for step in self.steps]
 
     def source(self, step):
         me = lax.axis_index("ep")
-        z = (me // self.x) ^ step[0]
+        z = lax.rem(me // self.x - step[0] + self.z, self.z)
         return z * self.x + lax.rem(lax.rem(me, self.x) - step[1] + self.x, self.x)
 
     def target(self, step):
-        return self.source((step[0], -step[1] % self.x))
+        return self.source((-step[0] % self.z, -step[1] % self.x))
 
 
 def swap(arr):
@@ -112,7 +103,7 @@
     heads = width // HD
     ctx = cache.shape[1]
     parts = HD // LANES
-    sizes = grid.block_sizes()
+    sizes = [grid.x] * grid.z
     note = piece + LANES
     scaling = HD ** (-0.5)
     units, features = gate_t.shape
@@ -178,9 +169,8 @@
         for s, u in grid.steps:
             to = grid.target((s, u))
             begin = pl.multiple_of(to * cols + skip, LANES)
-            block, place_in = grid.carried((s, u))
-            at = width + place_in * note
-            out_refs[block][:, at : at + piece] = res_ref[:, pl.ds(begin, piece)]
+            at = width + u * note
+            out_refs[s][:, at : at + piece] = res_ref[:, pl.ds(begin, piece)]
             chosen = ids_ref[...] == to * EXPERTS // grid.ep
             across = jnp.sum(jnp.where(chosen, wts_ref[...], 0.0), axis=0, keepdims=True)
             weight = jnp.sum(
@@ -192,7 +182,7 @@
             tile = jnp.where(lane == 0, high, 0.0)
             tile = jnp.where(lane == 1, middle, tile)
             tile = jnp.where(lane == 2, low, tile)
-            out_refs[block][:, at + piece : at + note] = tile.astype(jnp.bfloat16)
+            out_refs[s][:, at + piece : at + note] = tile.astype(jnp.bfloat16)
 
         place = lax.broadcasted_iota(jnp.int32, (heads, ctx), 1)
         probs, own_probs = [], []
@@ -290,7 +280,7 @@
             other = pl.multiple_of((1 - core) * (cols - piece), LANES)
             for i, (s, u) in enumerate(grid.steps):
                 here = pl.ds(pl.multiple_of(grid.source((s, u)) * rows, rows), rows)
-                at = depth + grid.carried((s, u))[1] * note
+                at = depth + u * note
                 beside = chunk_refs[i][:, at : at + note].astype(jnp.float32)
                 block_rows = slice(i * rows, (i + 1) * rows)
                 ours_ref[here, :] = total[block_rows, pl.ds(mine, piece)] + beside[:, :piece]
@@ -502,19 +492,19 @@
         up_t,
         w_down,
     )
-    chunks = grid.spread(outgoing)
+    chunks = grid.spread(outgoing, spaced=True)
     packed, *_ = lax.optimization_barrier((packed, *chunks))
     far_weights = swap(packed)
     ours, theirs, weight = project(grid, piece, chunks, w_out)
     stream = (ours + swap(theirs)).astype(jnp.bfloat16)
     stream, far_weights = lax.optimization_barrier((stream, far_weights))
-    pieces = grid.spread_at_once(stream)
+    pieces = grid.spread([stream] * grid.z, spaced=False)
     sums, home = gate_up(
         grid, piece, cols, rows, pieces, gain.reshape(1, width), gate_t, up_t, far_weights
     )
     far_sums = swap(sums)
     parts = down(grid, piece, rows, sums, far_sums, weight, w_down, far_weights)
-    order = sorted(range(grid.ep), key=lambda i: (grid.steps[i] == (0, 0), -grid.steps[i][0]))
+    order = sorted(range(grid.ep), key=lambda i: (grid.steps[i][0] == 0, grid.steps[i][0] != 2))
     shares = [grid.send(parts[i], *grid.steps[i]) if any(grid.steps[i]) else parts[i] for i in order]
     return finish(piece, cols, home, far_sums, shares)
 

time: 80.9 us -> 78 us (0.964)
  waiting for transfers between devices: 27.3 us -> 24.7 us
    ppermute x21, waiting for transfers between devices: 24.5 us -> 21.8 us  [send(): return lax.ppermute(arr, 'ep', pairs)]
  transfers between devices with their start and end apart: 24 -> 24, of which waited for: 15 -> 14; matrix products, arithmetic and copies ran while one was open for 0% -> 0% of each run, Pallas kernels for 12% -> 12%
where the time goes in v7:
time: 78 us; the launch traced here: 77.8 us
  starting transfers between devices  32.5 us (42%)
  waiting for transfers between devices  24.7 us (32%)
  Pallas kernels  19.4 us (25%)
  local copies, waits for them, and re-layouts  1.08 us (1%)
    ppermute x21, starting transfers between devices, send(): return lax.ppermute(arr, 'ep', pairs)  32.4 us
    ppermute x21, waiting for transfers between devices, send(): return lax.ppermute(arr, 'ep', pairs)  21.8 us
    pallas_call x1, Pallas kernels, project(): pl.pallas_call(kernel, name='project', grid=(blocks,), out_shape=outs, in...  9.39 us
    pallas_call x1, Pallas kernels, attention(): pl.pallas_call(kernel, name='attention', out_shape=[shape_of((rows, width...  6.79 us
    ppermute x3, waiting for transfers between devices, swap(): return lax.ppermute(arr, 'tp', [(0, 1), (1, 0)])  2.87 us
    pallas_call x1, Pallas kernels, gate_up(): pl.pallas_call(kernel, name='gate_up', out_shape=[shape_of((tall + extra...  1.68 us
  transfers between devices with their start and end apart: 24, of which 14 were waited for; matrix products, arithmetic and copies ran while one was open for 0% of the time, Pallas kernels for 12%

profile of v7, /device:TPU:0, one launch (start us, length us, event | category | flops | bytes accessed | tf_op | source)
XLA Modules:
  0.0 77.8 jit_solution(1082134212914444967)
XLA Ops:
  0.0 6.8 %attention.1 = (bf16[8,9472]{1,0:T(8,128)(2,1)}, bf16[8,9472]{1,0:T(8,128)(2,1)}, bf16[8,9472]{1,0:T(8,128)(2,1)}, bf16[8,9472]{1,0:T(8,128)(2,1)}, bf16[3680,512]{1,0:T(8,128)(2,1)}) custom-call(bf16[8,8192]{1,0:T(8,128)(2,1)} %refs_0_.1, bf16[8,512]{1,0:T(8,128)(2,1)} %refs_1_.1, bf16[8,7168]{1,0:T(8,128)(2,1)} %refs_2_.1, s32[3,8]{1,0:T(4,128)} %bitcast.10, ...), custom_call_target="tpu_custom_call" | custom-call | tf_op jit(solution)/shard_map/attention/pallas_call | solution.py:210
  6.8 3.1 %collective-permute-start.1 = (bf16[8,9472]{1,0:T(8,128)(2,1)}, bf16[8,9472]{1,0:T(8,128)(2,1)S(1)}, u32[]{:S(2)}, u32[]{:S(2)}) collective-permute-start(bf16[8,9472]{1,0:T(8,128)(2,1)} %get-tuple-element.29), channel_id=1, source_target_pairs={{0,4},{2,6},{4,8},{6,10},{8,12},{10,14},{12,0},{14,2},{1,5},{3,7},... | collective-permute-start | bytes 454664 | tf_op jit(solution)/shard_map/ppermute | solution.py:44
  9.9 1.5 %collective-permute-start = (bf16[8,9472]{1,0:T(8,128)(2,1)}, bf16[8,9472]{1,0:T(8,128)(2,1)S(1)}, u32[]{:S(2)}, u32[]{:S(2)}) collective-permute-start(bf16[8,9472]{1,0:T(8,128)(2,1)} %get-tuple-element.28.refs_0_), channel_id=1, source_target_pairs={{0,2},{2,0},{4,6},{6,4},{8,10},{10,8},{12,14},{14,12},{1,3},{3,1},... | collective-permute-start | bytes 454664 | tf_op jit(solution)/shard_map/ppermute | solution.py:44
  11.4 2.2 %collective-permute-start.5 = (bf16[8,9472]{1,0:T(8,128)(2,1)}, bf16[8,9472]{1,0:T(8,128)(2,1)S(1)}, u32[]{:S(2)}, u32[]{:S(2)}) collective-permute-start(bf16[8,9472]{1,0:T(8,128)(2,1)} %get-tuple-element.32), channel_id=1, source_target_pairs={{0,12},{2,14},{4,0},{6,2},{8,4},{10,6},{12,8},{14,10},{1,13},{3,15... | collective-permute-start | bytes 454664 | tf_op jit(solution)/shard_map/ppermute | solution.py:44
  13.6 2.9 %collective-permute-done.1.refs_2_ = bf16[8,9472]{1,0:T(8,128)(2,1)S(1)} collective-permute-done((bf16[8,9472]{1,0:T(8,128)(2,1)}, bf16[8,9472]{1,0:T(8,128)(2,1)S(1)}, u32[]{:S(2)}, u32[]{:S(2)}) %collective-permute-start.1) | collective-permute-done | bytes 151584 | tf_op jit(solution)/shard_map/ppermute | solution.py:44
  16.6 0.0 collective-permute-done.refs_1_
  16.6 1.5 %collective-permute-start.3 = (bf16[8,9472]{1,0:T(8,128)(2,1)}, bf16[8,9472]{1,0:T(8,128)(2,1)S(1)}, u32[]{:S(2)}, u32[]{:S(2)}) collective-permute-start(bf16[8,9472]{1,0:T(8,128)(2,1)} %get-tuple-element.31), channel_id=1, source_target_pairs={{0,8},{2,10},{4,12},{6,14},{8,0},{10,2},{12,4},{14,6},{1,9},{3,11}... | collective-permute-start | bytes 454664 | tf_op jit(solution)/shard_map/ppermute | solution.py:44
  18.1 3.4 %collective-permute-start.2 = (bf16[8,9472]{1,0:T(8,128)(2,1)S(1)}, bf16[8,9472]{1,0:T(8,128)(2,1)S(1)}, u32[]{:S(2)}, u32[]{:S(2)}) collective-permute-start(bf16[8,9472]{1,0:T(8,128)(2,1)S(1)} %collective-permute-done.1.refs_2_), channel_id=1, source_target_pairs={{0,2},{2,0},{4,6},{6,4},{8,10},{10,8},{12,14},{14,12},{1,3},{3,1},... | collective-permute-start | bytes 454664 | tf_op jit(solution)/shard_map/ppermute | solution.py:44
  21.5 0.0 collective-permute-done.5.refs_6_
  21.5 0.0 collective-permute-start.6
  21.6 4.2 %collective-permute-done.3.refs_4_ = bf16[8,9472]{1,0:T(8,128)(2,1)S(1)} collective-permute-done((bf16[8,9472]{1,0:T(8,128)(2,1)}, bf16[8,9472]{1,0:T(8,128)(2,1)S(1)}, u32[]{:S(2)}, u32[]{:S(2)}) %collective-permute-start.3) | collective-permute-done | bytes 151584 | tf_op jit(solution)/shard_map/ppermute | solution.py:44
  25.8 1.5 %collective-permute-start.4 = (bf16[8,9472]{1,0:T(8,128)(2,1)S(1)}, bf16[8,9472]{1,0:T(8,128)(2,1)S(1)}, u32[]{:S(2)}, u32[]{:S(2)}) collective-permute-start(bf16[8,9472]{1,0:T(8,128)(2,1)S(1)} %collective-permute-done.3.refs_4_), channel_id=1, source_target_pairs={{0,2},{2,0},{4,6},{6,4},{8,10},{10,8},{12,14},{14,12},{1,3},{3,1},... | collective-permute-start | bytes 454664 | tf_op jit(solution)/shard_map/ppermute | solution.py:44
  27.3 0.0 collective-permute-done.2.refs_3_
  27.3 0.0 collective-permute-done.6.refs_7_
  27.3 4.1 %collective-permute-done.4.refs_5_ = bf16[8,9472]{1,0:T(8,128)(2,1)S(1)} collective-permute-done((bf16[8,9472]{1,0:T(8,128)(2,1)S(1)}, bf16[8,9472]{1,0:T(8,128)(2,1)S(1)}, u32[]{:S(2)}, u32[]{:S(2)}) %collective-permute-start.4) | collective-permute-done | bytes 151584 | tf_op jit(solution)/shard_map/ppermute | solution.py:44
  31.4 0.0 copy-start
  31.4 0.0 copy-start.1
  31.4 0.0 collective-permute-start.8
  31.4 0.0 copy-start.3
  31.4 1.1 %copy-done.3 = bf16[8,9472]{1,0:T(8,128)(2,1)S(1)} copy-done((bf16[8,9472]{1,0:T(8,128)(2,1)S(1)}, bf16[8,9472]{1,0:T(8,128)(2,1)}, u32[]{:S(2)}) %copy-start.3) | copy-done | bytes 151576
  32.4 0.0 copy-start.4
  32.4 9.4 %project.1 = (f32[64,512]{1,0:T(8,128)S(1)}, f32[64,512]{1,0:T(8,128)S(1)}, f32[64,128]{1,0:T(8,128)S(1)}) custom-call(bf16[8,9472]{1,0:T(8,128)(2,1)S(1)} %copy-done.3, bf16[8,9472]{1,0:T(8,128)(2,1)S(1)} %collective-permute-done.refs_1_, bf16[8,9472]{1,0:T(8,128)(2,1)S(1)} %collective-permute-done.1.refs_2_, ...), custom_call_target="tpu_custom_call" | custom-call | flops 939524096 | bytes 15990784 | tf_op jit(solution)/shard_map/project/pallas_call | solution.py:296
  41.8 0.1 collective-permute-start.7
  41.9 1.3 %collective-permute-done.7 = f32[64,512]{1,0:T(8,128)S(1)} collective-permute-done((f32[64,512]{1,0:T(8,128)S(1)}, f32[64,512]{1,0:T(8,128)S(1)}, u32[]{:S(2)}, u32[]{:S(2)}) %collective-permute-start.7) | collective-permute-done | bytes 131104 | tf_op jit(solution)/shard_map/ppermute | solution.py:76
  43.3 0.0 collective-permute-done.8.refs_11_.packed_ref
  43.3 0.7 collective-permute-start.10
  44.0 3.1 %collective-permute-start.14 = (bf16[64,512]{1,0:T(8,128)(2,1)S(1)}, bf16[64,512]{1,0:T(8,128)(2,1)S(1)}, u32[]{:S(2)}, u32[]{:S(2)}) collective-permute-start(bf16[64,512]{1,0:T(8,128)(2,1)S(1)} %add_convert_fusion.refs_0_), channel_id=1, source_target_pairs={{0,12},{2,14},{4,0},{6,2},{8,4},{10,6},{12,8},{14,10},{1,13},{3,15... | collective-permute-start | bytes 196616 | tf_op jit(solution)/shard_map/ppermute | solution.py:44
  47.2 0.0 collective-permute-start.12
  47.2 2.9 %collective-permute-done.10.refs_2_ = bf16[64,512]{1,0:T(8,128)(2,1)S(1)} collective-permute-done((bf16[64,512]{1,0:T(8,128)(2,1)S(1)}, bf16[64,512]{1,0:T(8,128)(2,1)S(1)}, u32[]{:S(2)}, u32[]{:S(2)}) %collective-permute-start.10) | collective-permute-done | bytes 65568 | tf_op jit(solution)/shard_map/ppermute | solution.py:44
  50.1 1.0 %collective-permute-start.11 = (bf16[64,512]{1,0:T(8,128)(2,1)S(1)}, bf16[64,512]{1,0:T(8,128)(2,1)S(1)}, u32[]{:S(2)}, u32[]{:S(2)}) collective-permute-start(bf16[64,512]{1,0:T(8,128)(2,1)S(1)} %collective-permute-done.10.refs_2_), channel_id=1, source_target_pairs={{0,2},{2,0},{4,6},{6,4},{8,10},{10,8},{12,14},{14,12},{1,3},{3,1},... | collective-permute-start | bytes 196616 | tf_op jit(solution)/shard_map/ppermute | solution.py:44
  51.0 1.0 %collective-permute-start.9 = (bf16[64,512]{1,0:T(8,128)(2,1)S(1)}, bf16[64,512]{1,0:T(8,128)(2,1)S(1)}, u32[]{:S(2)}, u32[]{:S(2)}) collective-permute-start(bf16[64,512]{1,0:T(8,128)(2,1)S(1)} %add_convert_fusion.refs_0_), channel_id=1, source_target_pairs={{0,2},{2,0},{4,6},{6,4},{8,10},{10,8},{12,14},{14,12},{1,3},{3,1},... | collective-permute-start | bytes 196616 | tf_op jit(solution)/shard_map/ppermute | solution.py:44
  52.1 0.0 collective-permute-done.14.refs_6_
  52.1 1.0 %collective-permute-start.15 = (bf16[64,512]{1,0:T(8,128)(2,1)S(1)}, bf16[64,512]{1,0:T(8,128)(2,1)S(1)}, u32[]{:S(2)}, u32[]{:S(2)}) collective-permute-start(bf16[64,512]{1,0:T(8,128)(2,1)S(1)} %collective-permute-done.14.refs_6_), channel_id=1, source_target_pairs={{0,2},{2,0},{4,6},{6,4},{8,10},{10,8},{12,14},{14,12},{1,3},{3,1},... | collective-permute-start | bytes 196616 | tf_op jit(solution)/shard_map/ppermute | solution.py:44
  53.1 0.0 collective-permute-done.12.refs_4_
  53.1 1.3 %collective-permute-done.11.refs_3_ = bf16[64,512]{1,0:T(8,128)(2,1)S(1)} collective-permute-done((bf16[64,512]{1,0:T(8,128)(2,1)S(1)}, bf16[64,512]{1,0:T(8,128)(2,1)S(1)}, u32[]{:S(2)}, u32[]{:S(2)}) %collective-permute-start.11) | collective-permute-done | bytes 65568 | tf_op jit(solution)/shard_map/ppermute | solution.py:44
  54.3 1.0 %collective-permute-start.13 = (bf16[64,512]{1,0:T(8,128)(2,1)S(1)}, bf16[64,512]{1,0:T(8,128)(2,1)S(1)}, u32[]{:S(2)}, u32[]{:S(2)}) collective-permute-start(bf16[64,512]{1,0:T(8,128)(2,1)S(1)} %collective-permute-done.12.refs_4_), channel_id=1, source_target_pairs={{0,2},{2,0},{4,6},{6,4},{8,10},{10,8},{12,14},{14,12},{1,3},{3,1},... | collective-permute-start | bytes 196616 | tf_op jit(solution)/shard_map/ppermute | solution.py:44
  55.3 0.4 collective-permute-done.9.refs_1_
  55.7 1.1 %collective-permute-done.15.refs_7_ = bf16[64,512]{1,0:T(8,128)(2,1)S(1)} collective-permute-done((bf16[64,512]{1,0:T(8,128)(2,1)S(1)}, bf16[64,512]{1,0:T(8,128)(2,1)S(1)}, u32[]{:S(2)}, u32[]{:S(2)}) %collective-permute-start.15) | collective-permute-done | bytes 65568 | tf_op jit(solution)/shard_map/ppermute | solution.py:44
  56.7 1.9 %collective-permute-done.13.refs_5_ = bf16[64,512]{1,0:T(8,128)(2,1)S(1)} collective-permute-done((bf16[64,512]{1,0:T(8,128)(2,1)S(1)}, bf16[64,512]{1,0:T(8,128)(2,1)S(1)}, u32[]{:S(2)}, u32[]{:S(2)}) %collective-permute-start.13) | collective-permute-done | bytes 65568 | tf_op jit(solution)/shard_map/ppermute | solution.py:44
  58.6 0.0 copy-done
  58.6 0.0 copy-done.1
  58.6 0.0 copy-done.4
  58.6 0.0 copy-start.2
  58.6 1.7 %gate_up.1 = (f32[88,768]{1,0:T(8,128)S(1)}, f32[8,2048]{1,0:T(8,128)S(1)}) custom-call(bf16[64,512]{1,0:T(8,128)(2,1)S(1)} %add_convert_fusion.refs_0_, bf16[64,512]{1,0:T(8,128)(2,1)S(1)} %collective-permute-done.9.refs_1_, bf16[64,512]{1,0:T(8,128)(2,1)S(1)} %collective-permute-done.10.refs_2_, bf16[64,512]{1,0:T(8,128)(2,1)S(1)} %collective-permute-done.11.refs_3_, ...), custom_call_target="tpu_custom_call" | custom-call | tf_op jit(solution)/shard_map/gate_up/pallas_call | solution.py:359
  60.3 0.1 collective-permute-start.16
  60.4 1.5 %collective-permute-done.16.far_ref = f32[88,768]{1,0:T(8,128)S(1)} collective-permute-done((f32[88,768]{1,0:T(8,128)S(1)}, f32[88,768]{1,0:T(8,128)S(1)}, u32[]{:S(2)}, u32[]{:S(2)}) %collective-permute-start.16) | collective-permute-done | bytes 270368 | tf_op jit(solution)/shard_map/ppermute | solution.py:76
  61.9 0.0 copy-done.2
  61.9 0.9 %down.1 = (f32[8,3584]{1,0:T(8,128)S(1)}, bf16[8,3584]{1,0:T(8,128)(2,1)S(1)}, bf16[8,3584]{1,0:T(8,128)(2,1)S(1)}, bf16[8,3584]{1,0:T(8,128)(2,1)S(1)}, bf16[8,...) custom-call(f32[88,768]{1,0:T(8,128)S(1)} %get-tuple-element.41.sums, ...), custom_call_target="tpu_custom_call" | custom-call | tf_op jit(solution)/shard_map/down/pallas_call | solution.py:412
  62.8 0.6 collective-permute-start.17
  63.4 2.8 %collective-permute-start.18 = (bf16[8,3584]{1,0:T(8,128)(2,1)S(1)}, bf16[8,3584]{1,0:T(8,128)(2,1)S(1)}, u32[]{:S(2)}, u32[]{:S(2)}) collective-permute-start(bf16[8,3584]{1,0:T(8,128)(2,1)S(1)} %get-tuple-element.44), channel_id=1, source_target_pairs={{0,10},{2,8},{4,14},{6,12},{8,2},{10,0},{12,6},{14,4},{1,11},{3,9}... | collective-permute-start | bytes 172040 | tf_op jit(solution)/shard_map/ppermute | solution.py:44
  66.2 0.0 collective-permute-start.19
  66.2 1.6 %collective-permute-start.20 = (bf16[8,3584]{1,0:T(8,128)(2,1)S(1)}, bf16[8,3584]{1,0:T(8,128)(2,1)S(1)}, u32[]{:S(2)}, u32[]{:S(2)}) collective-permute-start(bf16[8,3584]{1,0:T(8,128)(2,1)S(1)} %get-tuple-element.46), channel_id=1, source_target_pairs={{0,6},{2,4},{4,10},{6,8},{8,14},{10,12},{12,2},{14,0},{1,7},{3,5},... | collective-permute-start | bytes 172040 | tf_op jit(solution)/shard_map/ppermute | solution.py:44
  67.8 2.7 %collective-permute-start.21 = (bf16[8,3584]{1,0:T(8,128)(2,1)S(1)}, bf16[8,3584]{1,0:T(8,128)(2,1)S(1)}, u32[]{:S(2)}, u32[]{:S(2)}) collective-permute-start(bf16[8,3584]{1,0:T(8,128)(2,1)S(1)} %get-tuple-element.47), channel_id=1, source_target_pairs={{0,12},{2,14},{4,0},{6,2},{8,4},{10,6},{12,8},{14,10},{1,13},{3,15... | collective-permute-start | bytes 172040 | tf_op jit(solution)/shard_map/ppermute | solution.py:44
  70.5 0.0 collective-permute-done.17.rest_0_
  70.5 2.4 %collective-permute-start.22 = (bf16[8,3584]{1,0:T(8,128)(2,1)S(1)}, bf16[8,3584]{1,0:T(8,128)(2,1)S(1)}, u32[]{:S(2)}, u32[]{:S(2)}) collective-permute-start(bf16[8,3584]{1,0:T(8,128)(2,1)S(1)} %get-tuple-element.48), channel_id=1, source_target_pairs={{0,14},{2,12},{4,2},{6,0},{8,6},{10,4},{12,10},{14,8},{1,15},{3,13... | collective-permute-start | bytes 172040 | tf_op jit(solution)/shard_map/ppermute | solution.py:44
  73.0 0.0 collective-permute-done.18.rest_1_
  73.0 1.1 %collective-permute-start.23 = (bf16[8,3584]{1,0:T(8,128)(2,1)S(1)}, bf16[8,3584]{1,0:T(8,128)(2,1)S(1)}, u32[]{:S(2)}, u32[]{:S(2)}) collective-permute-start(bf16[8,3584]{1,0:T(8,128)(2,1)S(1)} %get-tuple-element.50), channel_id=1, source_target_pairs={{0,2},{2,0},{4,6},{6,4},{8,10},{10,8},{12,14},{14,12},{1,3},{3,1},... | collective-permute-start | bytes 172040 | tf_op jit(solution)/shard_map/ppermute | solution.py:44
  74.0 0.0 collective-permute-done.19.rest_2_
  74.0 0.1 collective-permute-done.20.rest_3_
  74.1 0.1 collective-permute-done.21.rest_4_
  74.2 1.5 %collective-permute-done.22.rest_5_ = bf16[8,3584]{1,0:T(8,128)(2,1)S(1)} collective-permute-done((bf16[8,3584]{1,0:T(8,128)(2,1)S(1)}, bf16[8,3584]{1,0:T(8,128)(2,1)S(1)}, u32[]{:S(2)}, u32[]{:S(2)}) %collective-permute-start.22) | collective-permute-done | bytes 57376 | tf_op jit(solution)/shard_map/ppermute | solution.py:44
  75.8 1.4 %collective-permute-done.23.rest_7_ = bf16[8,3584]{1,0:T(8,128)(2,1)S(1)} collective-permute-done((bf16[8,3584]{1,0:T(8,128)(2,1)S(1)}, bf16[8,3584]{1,0:T(8,128)(2,1)S(1)}, u32[]{:S(2)}, u32[]{:S(2)}) %collective-permute-start.23) | collective-permute-done | bytes 57376 | tf_op jit(solution)/shard_map/ppermute | solution.py:44
  77.1 0.7 finish.1
  (1 shorter events, 0.0 us)
Async XLA Ops:
  6.8 9.8 %collective-permute-start.1 = (bf16[8,9472]{1,0:T(8,128)(2,1)}, bf16[8,9472]{1,0:T(8,128)(2,1)S(1)}, u32[]{:S(2)}, u32[]{:S(2)}) collective-permute-start(bf16[8,9472]{1,0:T(8,128)(2,1)} %get-tuple-element.29), channel_id=1, source_target_pairs={{0,4},{2,6},{4,8},{6,10},{8,12},{10,14},{12,0},{14,2},{1,5},{3,7},... | collective-permute-start | bytes 454664 | tf_op jit(solution)/shard_map/ppermute | solution.py:44
  9.9 6.7 %collective-permute-start = (bf16[8,9472]{1,0:T(8,128)(2,1)}, bf16[8,9472]{1,0:T(8,128)(2,1)S(1)}, u32[]{:S(2)}, u32[]{:S(2)}) collective-permute-start(bf16[8,9472]{1,0:T(8,128)(2,1)} %get-tuple-element.28.refs_0_), channel_id=1, source_target_pairs={{0,2},{2,0},{4,6},{6,4},{8,10},{10,8},{12,14},{14,12},{1,3},{3,1},... | collective-permute-start | bytes 454664 | tf_op jit(solution)/shard_map/ppermute | solution.py:44
  11.4 10.2 %collective-permute-start.5 = (bf16[8,9472]{1,0:T(8,128)(2,1)}, bf16[8,9472]{1,0:T(8,128)(2,1)S(1)}, u32[]{:S(2)}, u32[]{:S(2)}) collective-permute-start(bf16[8,9472]{1,0:T(8,128)(2,1)} %get-tuple-element.32), channel_id=1, source_target_pairs={{0,12},{2,14},{4,0},{6,2},{8,4},{10,6},{12,8},{14,10},{1,13},{3,15... | collective-permute-start | bytes 454664 | tf_op jit(solution)/shard_map/ppermute | solution.py:44
  16.6 9.2 %collective-permute-start.3 = (bf16[8,9472]{1,0:T(8,128)(2,1)}, bf16[8,9472]{1,0:T(8,128)(2,1)S(1)}, u32[]{:S(2)}, u32[]{:S(2)}) collective-permute-start(bf16[8,9472]{1,0:T(8,128)(2,1)} %get-tuple-element.31), channel_id=1, source_target_pairs={{0,8},{2,10},{4,12},{6,14},{8,0},{10,2},{12,4},{14,6},{1,9},{3,11}... | collective-permute-start | bytes 454664 | tf_op jit(solution)/shard_map/ppermute | solution.py:44
  18.1 9.2 %collective-permute-start.2 = (bf16[8,9472]{1,0:T(8,128)(2,1)S(1)}, bf16[8,9472]{1,0:T(8,128)(2,1)S(1)}, u32[]{:S(2)}, u32[]{:S(2)}) collective-permute-start(bf16[8,9472]{1,0:T(8,128)(2,1)S(1)} %collective-permute-done.1.refs_2_), channel_id=1, source_target_pairs={{0,2},{2,0},{4,6},{6,4},{8,10},{10,8},{12,14},{14,12},{1,3},{3,1},... | collective-permute-start | bytes 454664 | tf_op jit(solution)/shard_map/ppermute | solution.py:44
  21.5 5.8 %collective-permute-start.6 = (bf16[8,9472]{1,0:T(8,128)(2,1)S(1)}, bf16[8,9472]{1,0:T(8,128)(2,1)S(1)}, u32[]{:S(2)}, u32[]{:S(2)}) collective-permute-start(bf16[8,9472]{1,0:T(8,128)(2,1)S(1)} %collective-permute-done.5.refs_6_), channel_id=1, source_target_pairs={{0,2},{2,0},{4,6},{6,4},{8,10},{10,8},{12,14},{14,12},{1,3},{3,1},... | collective-permute-start | bytes 454664 | tf_op jit(solution)/shard_map/ppermute | solution.py:44
  25.8 5.6 %collective-permute-start.4 = (bf16[8,9472]{1,0:T(8,128)(2,1)S(1)}, bf16[8,9472]{1,0:T(8,128)(2,1)S(1)}, u32[]{:S(2)}, u32[]{:S(2)}) collective-permute-start(bf16[8,9472]{1,0:T(8,128)(2,1)S(1)} %collective-permute-done.3.refs_4_), channel_id=1, source_target_pairs={{0,2},{2,0},{4,6},{6,4},{8,10},{10,8},{12,14},{14,12},{1,3},{3,1},... | collective-permute-start | bytes 454664 | tf_op jit(solution)/shard_map/ppermute | solution.py:44
  31.4 27.2 %copy-start = (bf16[7168,160]{0,1:T(8,128)(2,1)S(1)}, bf16[7168,160]{0,1:T(8,128)(2,1)}, u32[]{:S(2)}) copy-start(bf16[7168,160]{0,1:T(8,128)(2,1)} %param.21) | copy-start | bytes 6881284
  31.4 27.2 %copy-start.1 = (bf16[7168,160]{0,1:T(8,128)(2,1)S(1)}, bf16[7168,160]{0,1:T(8,128)(2,1)}, u32[]{:S(2)}) copy-start(bf16[7168,160]{0,1:T(8,128)(2,1)} %param.22) | copy-start | bytes 6881284
  31.4 11.9 %collective-permute-start.8 = (bf16[3680,512]{1,0:T(8,128)(2,1)}, bf16[3680,512]{1,0:T(8,128)(2,1)S(1)}, u32[]{:S(2)}, u32[]{:S(2)}) collective-permute-start(bf16[3680,512]{1,0:T(8,128)(2,1)} %get-tuple-element.36), channel_id=1, source_target_pairs={{0,1},{1,0},{2,3},{3,2},{4,5},{5,4},{6,7},{7,6},{8,9},{9,8},{10,11... | collective-permute-start | bytes 11304968 | tf_op jit(solution)/shard_map/ppermute | solution.py:76
  31.4 1.1 %copy-start.3 = (bf16[8,9472]{1,0:T(8,128)(2,1)S(1)}, bf16[8,9472]{1,0:T(8,128)(2,1)}, u32[]{:S(2)}) copy-start(bf16[8,9472]{1,0:T(8,128)(2,1)} %get-tuple-element.28.refs_0_) | copy-start | bytes 454660
  32.4 26.2 %copy-start.4 = (f32[7168]{0:T(1024)S(1)}, f32[7168]{0:T(1024)}, u32[]{:S(2)}) copy-start(f32[7168]{0:T(1024)} %param.18) | copy-start | bytes 86020
  41.8 1.4 %collective-permute-start.7 = (f32[64,512]{1,0:T(8,128)S(1)}, f32[64,512]{1,0:T(8,128)S(1)}, u32[]{:S(2)}, u32[]{:S(2)}) collective-permute-start(f32[64,512]{1,0:T(8,128)S(1)} %get-tuple-element.34), channel_id=1, source_target_pairs={{0,1},{1,0},{2,3},{3,2},{4,5},{5,4},{6,7},{7,6},{8,9},{9,8},{10,11... | collective-permute-start | bytes 393224 | tf_op jit(solution)/shard_map/ppermute | solution.py:76
  43.3 6.8 %collective-permute-start.10 = (bf16[64,512]{1,0:T(8,128)(2,1)S(1)}, bf16[64,512]{1,0:T(8,128)(2,1)S(1)}, u32[]{:S(2)}, u32[]{:S(2)}) collective-permute-start(bf16[64,512]{1,0:T(8,128)(2,1)S(1)} %add_convert_fusion.refs_0_), channel_id=1, source_target_pairs={{0,4},{2,6},{4,8},{6,10},{8,12},{10,14},{12,0},{14,2},{1,5},{3,7},... | collective-permute-start | bytes 196616 | tf_op jit(solution)/shard_map/ppermute | solution.py:44
  44.0 8.1 %collective-permute-start.14 = (bf16[64,512]{1,0:T(8,128)(2,1)S(1)}, bf16[64,512]{1,0:T(8,128)(2,1)S(1)}, u32[]{:S(2)}, u32[]{:S(2)}) collective-permute-start(bf16[64,512]{1,0:T(8,128)(2,1)S(1)} %add_convert_fusion.refs_0_), channel_id=1, source_target_pairs={{0,12},{2,14},{4,0},{6,2},{8,4},{10,6},{12,8},{14,10},{1,13},{3,15... | collective-permute-start | bytes 196616 | tf_op jit(solution)/shard_map/ppermute | solution.py:44
  47.2 5.9 %collective-permute-start.12 = (bf16[64,512]{1,0:T(8,128)(2,1)S(1)}, bf16[64,512]{1,0:T(8,128)(2,1)S(1)}, u32[]{:S(2)}, u32[]{:S(2)}) collective-permute-start(bf16[64,512]{1,0:T(8,128)(2,1)S(1)} %add_convert_fusion.refs_0_), channel_id=1, source_target_pairs={{0,8},{2,10},{4,12},{6,14},{8,0},{10,2},{12,4},{14,6},{1,9},{3,11}... | collective-permute-start | bytes 196616 | tf_op jit(solution)/shard_map/ppermute | solution.py:44
  50.1 4.3 %collective-permute-start.11 = (bf16[64,512]{1,0:T(8,128)(2,1)S(1)}, bf16[64,512]{1,0:T(8,128)(2,1)S(1)}, u32[]{:S(2)}, u32[]{:S(2)}) collective-permute-start(bf16[64,512]{1,0:T(8,128)(2,1)S(1)} %collective-permute-done.10.refs_2_), channel_id=1, source_target_pairs={{0,2},{2,0},{4,6},{6,4},{8,10},{10,8},{12,14},{14,12},{1,3},{3,1},... | collective-permute-start | bytes 196616 | tf_op jit(solution)/shard_map/ppermute | solution.py:44
  51.0 4.6 %collective-permute-start.9 = (bf16[64,512]{1,0:T(8,128)(2,1)S(1)}, bf16[64,512]{1,0:T(8,128)(2,1)S(1)}, u32[]{:S(2)}, u32[]{:S(2)}) collective-permute-start(bf16[64,512]{1,0:T(8,128)(2,1)S(1)} %add_convert_fusion.refs_0_), channel_id=1, source_target_pairs={{0,2},{2,0},{4,6},{6,4},{8,10},{10,8},{12,14},{14,12},{1,3},{3,1},... | collective-permute-start | bytes 196616 | tf_op jit(solution)/shard_map/ppermute | solution.py:44
  52.1 4.6 %collective-permute-start.15 = (bf16[64,512]{1,0:T(8,128)(2,1)S(1)}, bf16[64,512]{1,0:T(8,128)(2,1)S(1)}, u32[]{:S(2)}, u32[]{:S(2)}) collective-permute-start(bf16[64,512]{1,0:T(8,128)(2,1)S(1)} %collective-permute-done.14.refs_6_), channel_id=1, source_target_pairs={{0,2},{2,0},{4,6},{6,4},{8,10},{10,8},{12,14},{14,12},{1,3},{3,1},... | collective-permute-start | bytes 196616 | tf_op jit(solution)/shard_map/ppermute | solution.py:44
  54.3 4.3 %collective-permute-start.13 = (bf16[64,512]{1,0:T(8,128)(2,1)S(1)}, bf16[64,512]{1,0:T(8,128)(2,1)S(1)}, u32[]{:S(2)}, u32[]{:S(2)}) collective-permute-start(bf16[64,512]{1,0:T(8,128)(2,1)S(1)} %collective-permute-done.12.refs_4_), channel_id=1, source_target_pairs={{0,2},{2,0},{4,6},{6,4},{8,10},{10,8},{12,14},{14,12},{1,3},{3,1},... | collective-permute-start | bytes 196616 | tf_op jit(solution)/shard_map/ppermute | solution.py:44
  58.6 3.3 %copy-start.2 = (bf16[160,7168]{1,0:T(8,128)(2,1)S(1)}, bf16[160,7168]{1,0:T(8,128)(2,1)}, u32[]{:S(2)}) copy-start(bf16[160,7168]{1,0:T(8,128)(2,1)} %down_ref.1) | copy-start | bytes 6881284
  60.3 1.6 %collective-permute-start.16 = (f32[88,768]{1,0:T(8,128)S(1)}, f32[88,768]{1,0:T(8,128)S(1)}, u32[]{:S(2)}, u32[]{:S(2)}) collective-permute-start(f32[88,768]{1,0:T(8,128)S(1)} %get-tuple-element.41.sums_ref), channel_id=1, source_target_pairs={{0,1},{1,0},{2,3},{3,2},{4,5},{5,4},{6,7},{7,6},{8,9},{9,8},{10,11... | collective-permute-start | bytes 811016 | tf_op jit(solution)/shard_map/ppermute | solution.py:76
  62.8 7.7 %collective-permute-start.17 = (bf16[8,3584]{1,0:T(8,128)(2,1)S(1)}, bf16[8,3584]{1,0:T(8,128)(2,1)S(1)}, u32[]{:S(2)}, u32[]{:S(2)}) collective-permute-start(bf16[8,3584]{1,0:T(8,128)(2,1)S(1)} %get-tuple-element.43), channel_id=1, source_target_pairs={{0,8},{2,10},{4,12},{6,14},{8,0},{10,2},{12,4},{14,6},{1,9},{3,11}... | collective-permute-start | bytes 172040 | tf_op jit(solution)/shard_map/ppermute | solution.py:44
  63.4 9.5 %collective-permute-start.18 = (bf16[8,3584]{1,0:T(8,128)(2,1)S(1)}, bf16[8,3584]{1,0:T(8,128)(2,1)S(1)}, u32[]{:S(2)}, u32[]{:S(2)}) collective-permute-start(bf16[8,3584]{1,0:T(8,128)(2,1)S(1)} %get-tuple-element.44), channel_id=1, source_target_pairs={{0,10},{2,8},{4,14},{6,12},{8,2},{10,0},{12,6},{14,4},{1,11},{3,9}... | collective-permute-start | bytes 172040 | tf_op jit(solution)/shard_map/ppermute | solution.py:44
  66.2 7.8 %collective-permute-start.19 = (bf16[8,3584]{1,0:T(8,128)(2,1)S(1)}, bf16[8,3584]{1,0:T(8,128)(2,1)S(1)}, u32[]{:S(2)}, u32[]{:S(2)}) collective-permute-start(bf16[8,3584]{1,0:T(8,128)(2,1)S(1)} %get-tuple-element.45), channel_id=1, source_target_pairs={{0,4},{2,6},{4,8},{6,10},{8,12},{10,14},{12,0},{14,2},{1,5},{3,7},... | collective-permute-start | bytes 172040 | tf_op jit(solution)/shard_map/ppermute | solution.py:44
  66.2 7.9 %collective-permute-start.20 = (bf16[8,3584]{1,0:T(8,128)(2,1)S(1)}, bf16[8,3584]{1,0:T(8,128)(2,1)S(1)}, u32[]{:S(2)}, u32[]{:S(2)}) collective-permute-start(bf16[8,3584]{1,0:T(8,128)(2,1)S(1)} %get-tuple-element.46), channel_id=1, source_target_pairs={{0,6},{2,4},{4,10},{6,8},{8,14},{10,12},{12,2},{14,0},{1,7},{3,5},... | collective-permute-start | bytes 172040 | tf_op jit(solution)/shard_map/ppermute | solution.py:44
  67.8 6.4 %collective-permute-start.21 = (bf16[8,3584]{1,0:T(8,128)(2,1)S(1)}, bf16[8,3584]{1,0:T(8,128)(2,1)S(1)}, u32[]{:S(2)}, u32[]{:S(2)}) collective-permute-start(bf16[8,3584]{1,0:T(8,128)(2,1)S(1)} %get-tuple-element.47), channel_id=1, source_target_pairs={{0,12},{2,14},{4,0},{6,2},{8,4},{10,6},{12,8},{14,10},{1,13},{3,15... | collective-permute-start | bytes 172040 | tf_op jit(solution)/shard_map/ppermute | solution.py:44
  70.5 5.2 %collective-permute-start.22 = (bf16[8,3584]{1,0:T(8,128)(2,1)S(1)}, bf16[8,3584]{1,0:T(8,128)(2,1)S(1)}, u32[]{:S(2)}, u32[]{:S(2)}) collective-permute-start(bf16[8,3584]{1,0:T(8,128)(2,1)S(1)} %get-tuple-element.48), channel_id=1, source_target_pairs={{0,14},{2,12},{4,2},{6,0},{8,6},{10,4},{12,10},{14,8},{1,15},{3,13... | collective-permute-start | bytes 172040 | tf_op jit(solution)/shard_map/ppermute | solution.py:44
  73.0 4.2 %collective-permute-start.23 = (bf16[8,3584]{1,0:T(8,128)(2,1)S(1)}, bf16[8,3584]{1,0:T(8,128)(2,1)S(1)}, u32[]{:S(2)}, u32[]{:S(2)}) collective-permute-start(bf16[8,3584]{1,0:T(8,128)(2,1)S(1)} %get-tuple-element.50), channel_id=1, source_target_pairs={{0,2},{2,0},{4,6},{6,4},{8,10},{10,8},{12,14},{14,12},{1,3},{3,1},... | collective-permute-start | bytes 172040 | tf_op jit(solution)/shard_map/ppermute | solution.py:44

commit v8 on v7

--- a/solution.py
+++ b/solution.py
@@ -37,7 +37,7 @@
 
     def send(self, arr, s, u):
         pairs = [
-            (z * self.x + x, (z + s) % self.z * self.x + (x + u) % self.x)
+            (z * self.x + x, (z ^ s) * self.x + (x + u) % self.x)
             for z in range(self.z)
             for x in range(self.x)
         ]
@@ -65,11 +65,11 @@
 
     def source(self, step):
         me = lax.axis_index("ep")
-        z = lax.rem(me // self.x - step[0] + self.z, self.z)
+        z = (me // self.x) ^ step[0]
         return z * self.x + lax.rem(lax.rem(me, self.x) - step[1] + self.x, self.x)
 
     def target(self, step):
-        return self.source((-step[0] % self.z, -step[1] % self.x))
+        return self.source((step[0], -step[1] % self.x))
 
 
 def swap(arr):
@@ -504,7 +504,7 @@
     )
     far_sums = swap(sums)
     parts = down(grid, piece, rows, sums, far_sums, weight, w_down, far_weights)
-    order = sorted(range(grid.ep), key=lambda i: (grid.steps[i][0] == 0, grid.steps[i][0] != 2))
+    order = sorted(range(grid.ep), key=lambda i: (grid.steps[i] == (0, 0), -grid.steps[i][0]))
     shares = [grid.send(parts[i], *grid.steps[i]) if any(grid.steps[i]) else parts[i] for i in order]
     return finish(piece, cols, home, far_sums, shares)
 

time: 78 us -> 78.8 us (1.010)
  waiting for transfers between devices: 24.7 us -> 26.4 us
  starting transfers between devices: 32.5 us -> 31.7 us
    ppermute x21, waiting for transfers between devices: 21.8 us -> 23.5 us  [send(): return lax.ppermute(arr, 'ep', pairs)]
    ppermute x21, starting transfers between devices: 32.4 us -> 31.5 us  [send(): return lax.ppermute(arr, 'ep', pairs)]
  transfers between devices with their start and end apart: 24 -> 24, of which waited for: 14 -> 16; matrix products, arithmetic and copies ran while one was open for 0% -> 0% of each run, Pallas kernels for 12% -> 12%
where the time goes in v8:
time: 78.8 us; the launch traced here: 78.6 us
  starting transfers between devices  31.7 us (40%)
  waiting for transfers between devices  26.4 us (34%)
  Pallas kernels  19.4 us (25%)
  local copies, waits for them, and re-layouts  1.08 us (1%)
    ppermute x21, starting transfers between devices, send(): return lax.ppermute(arr, 'ep', pairs)  31.5 us
    ppermute x21, waiting for transfers between devices, send(): return lax.ppermute(arr, 'ep', pairs)  23.5 us
    pallas_call x1, Pallas kernels, project(): pl.pallas_call(kernel, name='project', grid=(blocks,), out_shape=outs, in...  9.39 us
    pallas_call x1, Pallas kernels, attention(): pl.pallas_call(kernel, name='attention', out_shape=[shape_of((rows, width...  6.79 us
    ppermute x3, waiting for transfers between devices, swap(): return lax.ppermute(arr, 'tp', [(0, 1), (1, 0)])  2.87 us
    pallas_call x1, Pallas kernels, gate_up(): pl.pallas_call(kernel, name='gate_up', out_shape=[shape_of((tall + extra...  1.67 us
  transfers between devices with their start and end apart: 24, of which 16 were waited for; matrix products, arithmetic and copies ran while one was open for 0% of the time, Pallas kernels for 12%

profile of v8, /device:TPU:0, one launch (start us, length us, event | category | flops | bytes accessed | tf_op | source)
XLA Modules:
  0.0 78.6 jit_solution(12056575193683731250)
XLA Ops:
  0.0 6.8 %attention.1 = (bf16[8,9472]{1,0:T(8,128)(2,1)}, bf16[8,9472]{1,0:T(8,128)(2,1)}, bf16[8,9472]{1,0:T(8,128)(2,1)}, bf16[8,9472]{1,0:T(8,128)(2,1)}, bf16[3680,512]{1,0:T(8,128)(2,1)}) custom-call(bf16[8,8192]{1,0:T(8,128)(2,1)} %refs_0_.1, bf16[8,512]{1,0:T(8,128)(2,1)} %refs_1_.1, bf16[8,7168]{1,0:T(8,128)(2,1)} %refs_2_.1, s32[3,8]{1,0:T(4,128)} %bitcast.10, ...), custom_call_target="tpu_custom_call" | custom-call | tf_op jit(solution)/shard_map/attention/pallas_call | solution.py:210
  6.8 3.1 %collective-permute-start.1 = (bf16[8,9472]{1,0:T(8,128)(2,1)}, bf16[8,9472]{1,0:T(8,128)(2,1)S(1)}, u32[]{:S(2)}, u32[]{:S(2)}) collective-permute-start(bf16[8,9472]{1,0:T(8,128)(2,1)} %get-tuple-element.29), channel_id=1, source_target_pairs={{0,4},{2,6},{4,0},{6,2},{8,12},{10,14},{12,8},{14,10},{1,5},{3,7},... | collective-permute-start | bytes 454664 | tf_op jit(solution)/shard_map/ppermute | solution.py:44
  9.9 1.5 %collective-permute-start = (bf16[8,9472]{1,0:T(8,128)(2,1)}, bf16[8,9472]{1,0:T(8,128)(2,1)S(1)}, u32[]{:S(2)}, u32[]{:S(2)}) collective-permute-start(bf16[8,9472]{1,0:T(8,128)(2,1)} %get-tuple-element.28.refs_0_), channel_id=1, source_target_pairs={{0,2},{2,0},{4,6},{6,4},{8,10},{10,8},{12,14},{14,12},{1,3},{3,1},... | collective-permute-start | bytes 454664 | tf_op jit(solution)/shard_map/ppermute | solution.py:44
  11.4 2.5 %collective-permute-start.5 = (bf16[8,9472]{1,0:T(8,128)(2,1)}, bf16[8,9472]{1,0:T(8,128)(2,1)S(1)}, u32[]{:S(2)}, u32[]{:S(2)}) collective-permute-start(bf16[8,9472]{1,0:T(8,128)(2,1)} %get-tuple-element.32), channel_id=1, source_target_pairs={{0,12},{2,14},{4,8},{6,10},{8,4},{10,6},{12,0},{14,2},{1,13},{3,15... | collective-permute-start | bytes 454664 | tf_op jit(solution)/shard_map/ppermute | solution.py:44
  13.9 0.2 collective-permute-done.1.refs_2_
  14.0 1.5 %collective-permute-done.refs_1_ = bf16[8,9472]{1,0:T(8,128)(2,1)S(1)} collective-permute-done((bf16[8,9472]{1,0:T(8,128)(2,1)}, bf16[8,9472]{1,0:T(8,128)(2,1)S(1)}, u32[]{:S(2)}, u32[]{:S(2)}) %collective-permute-start) | collective-permute-done | bytes 151584 | tf_op jit(solution)/shard_map/ppermute | solution.py:44
  15.5 2.6 %collective-permute-start.3 = (bf16[8,9472]{1,0:T(8,128)(2,1)}, bf16[8,9472]{1,0:T(8,128)(2,1)S(1)}, u32[]{:S(2)}, u32[]{:S(2)}) collective-permute-start(bf16[8,9472]{1,0:T(8,128)(2,1)} %get-tuple-element.31), channel_id=1, source_target_pairs={{0,8},{2,10},{4,12},{6,14},{8,0},{10,2},{12,4},{14,6},{1,9},{3,11}... | collective-permute-start | bytes 454664 | tf_op jit(solution)/shard_map/ppermute | solution.py:44
  18.1 1.5 %collective-permute-start.2 = (bf16[8,9472]{1,0:T(8,128)(2,1)S(1)}, bf16[8,9472]{1,0:T(8,128)(2,1)S(1)}, u32[]{:S(2)}, u32[]{:S(2)}) collective-permute-start(bf16[8,9472]{1,0:T(8,128)(2,1)S(1)} %collective-permute-done.1.refs_2_), channel_id=1, source_target_pairs={{0,2},{2,0},{4,6},{6,4},{8,10},{10,8},{12,14},{14,12},{1,3},{3,1},... | collective-permute-start | bytes 454664 | tf_op jit(solution)/shard_map/ppermute | solution.py:44
  19.6 0.9 %collective-permute-done.5.refs_6_ = bf16[8,9472]{1,0:T(8,128)(2,1)S(1)} collective-permute-done((bf16[8,9472]{1,0:T(8,128)(2,1)}, bf16[8,9472]{1,0:T(8,128)(2,1)S(1)}, u32[]{:S(2)}, u32[]{:S(2)}) %collective-permute-start.5) | collective-permute-done | bytes 151584 | tf_op jit(solution)/shard_map/ppermute | solution.py:44
  20.5 1.7 %collective-permute-start.6 = (bf16[8,9472]{1,0:T(8,128)(2,1)S(1)}, bf16[8,9472]{1,0:T(8,128)(2,1)S(1)}, u32[]{:S(2)}, u32[]{:S(2)}) collective-permute-start(bf16[8,9472]{1,0:T(8,128)(2,1)S(1)} %collective-permute-done.5.refs_6_), channel_id=1, source_target_pairs={{0,2},{2,0},{4,6},{6,4},{8,10},{10,8},{12,14},{14,12},{1,3},{3,1},... | collective-permute-start | bytes 454664 | tf_op jit(solution)/shard_map/ppermute | solution.py:44
  22.2 5.1 %collective-permute-done.3.refs_4_ = bf16[8,9472]{1,0:T(8,128)(2,1)S(1)} collective-permute-done((bf16[8,9472]{1,0:T(8,128)(2,1)}, bf16[8,9472]{1,0:T(8,128)(2,1)S(1)}, u32[]{:S(2)}, u32[]{:S(2)}) %collective-permute-start.3) | collective-permute-done | bytes 151584 | tf_op jit(solution)/shard_map/ppermute | solution.py:44
  27.3 0.5 collective-permute-start.4
  27.8 0.0 collective-permute-done.2.refs_3_
  27.8 0.0 collective-permute-done.6.refs_7_
  27.8 4.6 %collective-permute-done.4.refs_5_ = bf16[8,9472]{1,0:T(8,128)(2,1)S(1)} collective-permute-done((bf16[8,9472]{1,0:T(8,128)(2,1)S(1)}, bf16[8,9472]{1,0:T(8,128)(2,1)S(1)}, u32[]{:S(2)}, u32[]{:S(2)}) %collective-permute-start.4) | collective-permute-done | bytes 151584 | tf_op jit(solution)/shard_map/ppermute | solution.py:44
  32.5 0.0 copy-start
  32.5 0.0 copy-start.1
  32.5 0.0 collective-permute-start.8
  32.5 0.0 copy-start.3
  32.5 1.1 %copy-done.3 = bf16[8,9472]{1,0:T(8,128)(2,1)S(1)} copy-done((bf16[8,9472]{1,0:T(8,128)(2,1)S(1)}, bf16[8,9472]{1,0:T(8,128)(2,1)}, u32[]{:S(2)}) %copy-start.3) | copy-done | bytes 151576
  33.6 0.0 copy-start.4
  33.6 9.4 %project.1 = (f32[64,512]{1,0:T(8,128)S(1)}, f32[64,512]{1,0:T(8,128)S(1)}, f32[64,128]{1,0:T(8,128)S(1)}) custom-call(bf16[8,9472]{1,0:T(8,128)(2,1)S(1)} %copy-done.3, bf16[8,9472]{1,0:T(8,128)(2,1)S(1)} %collective-permute-done.refs_1_, bf16[8,9472]{1,0:T(8,128)(2,1)S(1)} %collective-permute-done.1.refs_2_, ...), custom_call_target="tpu_custom_call" | custom-call | flops 939524096 | bytes 15990784 | tf_op jit(solution)/shard_map/project/pallas_call | solution.py:296
  42.9 0.1 collective-permute-start.7
  43.0 1.3 %collective-permute-done.7 = f32[64,512]{1,0:T(8,128)S(1)} collective-permute-done((f32[64,512]{1,0:T(8,128)S(1)}, f32[64,512]{1,0:T(8,128)S(1)}, u32[]{:S(2)}, u32[]{:S(2)}) %collective-permute-start.7) | collective-permute-done | bytes 131104 | tf_op jit(solution)/shard_map/ppermute | solution.py:76
  44.4 0.0 collective-permute-done.8.refs_11_.packed_ref
  44.4 1.4 %collective-permute-start.10 = (bf16[64,512]{1,0:T(8,128)(2,1)S(1)}, bf16[64,512]{1,0:T(8,128)(2,1)S(1)}, u32[]{:S(2)}, u32[]{:S(2)}) collective-permute-start(bf16[64,512]{1,0:T(8,128)(2,1)S(1)} %add_convert_fusion.refs_0_), channel_id=1, source_target_pairs={{0,4},{2,6},{4,0},{6,2},{8,12},{10,14},{12,8},{14,10},{1,5},{3,7},... | collective-permute-start | bytes 196616 | tf_op jit(solution)/shard_map/ppermute | solution.py:44
  45.8 1.7 %collective-permute-start.14 = (bf16[64,512]{1,0:T(8,128)(2,1)S(1)}, bf16[64,512]{1,0:T(8,128)(2,1)S(1)}, u32[]{:S(2)}, u32[]{:S(2)}) collective-permute-start(bf16[64,512]{1,0:T(8,128)(2,1)S(1)} %add_convert_fusion.refs_0_), channel_id=1, source_target_pairs={{0,12},{2,14},{4,8},{6,10},{8,4},{10,6},{12,0},{14,2},{1,13},{3,15... | collective-permute-start | bytes 196616 | tf_op jit(solution)/shard_map/ppermute | solution.py:44
  47.5 0.5 collective-permute-start.12
  47.9 0.8 collective-permute-done.10.refs_2_
  48.7 1.1 %collective-permute-start.11 = (bf16[64,512]{1,0:T(8,128)(2,1)S(1)}, bf16[64,512]{1,0:T(8,128)(2,1)S(1)}, u32[]{:S(2)}, u32[]{:S(2)}) collective-permute-start(bf16[64,512]{1,0:T(8,128)(2,1)S(1)} %collective-permute-done.10.refs_2_), channel_id=1, source_target_pairs={{0,2},{2,0},{4,6},{6,4},{8,10},{10,8},{12,14},{14,12},{1,3},{3,1},... | collective-permute-start | bytes 196616 | tf_op jit(solution)/shard_map/ppermute | solution.py:44
  49.8 0.9 %collective-permute-start.9 = (bf16[64,512]{1,0:T(8,128)(2,1)S(1)}, bf16[64,512]{1,0:T(8,128)(2,1)S(1)}, u32[]{:S(2)}, u32[]{:S(2)}) collective-permute-start(bf16[64,512]{1,0:T(8,128)(2,1)S(1)} %add_convert_fusion.refs_0_), channel_id=1, source_target_pairs={{0,2},{2,0},{4,6},{6,4},{8,10},{10,8},{12,14},{14,12},{1,3},{3,1},... | collective-permute-start | bytes 196616 | tf_op jit(solution)/shard_map/ppermute | solution.py:44
  50.7 1.5 %collective-permute-done.14.refs_6_ = bf16[64,512]{1,0:T(8,128)(2,1)S(1)} collective-permute-done((bf16[64,512]{1,0:T(8,128)(2,1)S(1)}, bf16[64,512]{1,0:T(8,128)(2,1)S(1)}, u32[]{:S(2)}, u32[]{:S(2)}) %collective-permute-start.14) | collective-permute-done | bytes 65568 | tf_op jit(solution)/shard_map/ppermute | solution.py:44
  52.3 0.4 collective-permute-start.15
  52.7 1.7 %collective-permute-done.12.refs_4_ = bf16[64,512]{1,0:T(8,128)(2,1)S(1)} collective-permute-done((bf16[64,512]{1,0:T(8,128)(2,1)S(1)}, bf16[64,512]{1,0:T(8,128)(2,1)S(1)}, u32[]{:S(2)}, u32[]{:S(2)}) %collective-permute-start.12) | collective-permute-done | bytes 65568 | tf_op jit(solution)/shard_map/ppermute | solution.py:44
  54.4 0.0 collective-permute-done.11.refs_3_
  54.4 1.0 %collective-permute-start.13 = (bf16[64,512]{1,0:T(8,128)(2,1)S(1)}, bf16[64,512]{1,0:T(8,128)(2,1)S(1)}, u32[]{:S(2)}, u32[]{:S(2)}) collective-permute-start(bf16[64,512]{1,0:T(8,128)(2,1)S(1)} %collective-permute-done.12.refs_4_), channel_id=1, source_target_pairs={{0,2},{2,0},{4,6},{6,4},{8,10},{10,8},{12,14},{14,12},{1,3},{3,1},... | collective-permute-start | bytes 196616 | tf_op jit(solution)/shard_map/ppermute | solution.py:44
  55.4 0.0 collective-permute-done.9.refs_1_
  55.4 1.2 %collective-permute-done.15.refs_7_ = bf16[64,512]{1,0:T(8,128)(2,1)S(1)} collective-permute-done((bf16[64,512]{1,0:T(8,128)(2,1)S(1)}, bf16[64,512]{1,0:T(8,128)(2,1)S(1)}, u32[]{:S(2)}, u32[]{:S(2)}) %collective-permute-start.15) | collective-permute-done | bytes 65568 | tf_op jit(solution)/shard_map/ppermute | solution.py:44
  56.6 2.1 %collective-permute-done.13.refs_5_ = bf16[64,512]{1,0:T(8,128)(2,1)S(1)} collective-permute-done((bf16[64,512]{1,0:T(8,128)(2,1)S(1)}, bf16[64,512]{1,0:T(8,128)(2,1)S(1)}, u32[]{:S(2)}, u32[]{:S(2)}) %collective-permute-start.13) | collective-permute-done | bytes 65568 | tf_op jit(solution)/shard_map/ppermute | solution.py:44
  58.7 0.0 copy-done
  58.7 0.0 copy-done.1
  58.7 0.0 copy-done.4
  58.7 0.0 copy-start.2
  58.7 1.7 %gate_up.1 = (f32[88,768]{1,0:T(8,128)S(1)}, f32[8,2048]{1,0:T(8,128)S(1)}) custom-call(bf16[64,512]{1,0:T(8,128)(2,1)S(1)} %add_convert_fusion.refs_0_, bf16[64,512]{1,0:T(8,128)(2,1)S(1)} %collective-permute-done.9.refs_1_, bf16[64,512]{1,0:T(8,128)(2,1)S(1)} %collective-permute-done.10.refs_2_, bf16[64,512]{1,0:T(8,128)(2,1)S(1)} %collective-permute-done.11.refs_3_, ...), custom_call_target="tpu_custom_call" | custom-call | tf_op jit(solution)/shard_map/gate_up/pallas_call | solution.py:359
  60.4 0.1 collective-permute-start.16
  60.4 1.5 %collective-permute-done.16.far_ref = f32[88,768]{1,0:T(8,128)S(1)} collective-permute-done((f32[88,768]{1,0:T(8,128)S(1)}, f32[88,768]{1,0:T(8,128)S(1)}, u32[]{:S(2)}, u32[]{:S(2)}) %collective-permute-start.16) | collective-permute-done | bytes 270368 | tf_op jit(solution)/shard_map/ppermute | solution.py:76
  62.0 0.0 copy-done.2
  62.0 0.9 %down.1 = (f32[8,3584]{1,0:T(8,128)S(1)}, bf16[8,3584]{1,0:T(8,128)(2,1)S(1)}, bf16[8,3584]{1,0:T(8,128)(2,1)S(1)}, bf16[8,3584]{1,0:T(8,128)(2,1)S(1)}, bf16[8,...) custom-call(f32[88,768]{1,0:T(8,128)S(1)} %get-tuple-element.41.sums, ...), custom_call_target="tpu_custom_call" | custom-call | tf_op jit(solution)/shard_map/down/pallas_call | solution.py:412
  62.9 2.5 %collective-permute-start.17 = (bf16[8,3584]{1,0:T(8,128)(2,1)S(1)}, bf16[8,3584]{1,0:T(8,128)(2,1)S(1)}, u32[]{:S(2)}, u32[]{:S(2)}) collective-permute-start(bf16[8,3584]{1,0:T(8,128)(2,1)S(1)} %get-tuple-element.43), channel_id=1, source_target_pairs={{0,12},{2,14},{4,8},{6,10},{8,4},{10,6},{12,0},{14,2},{1,13},{3,15... | collective-permute-start | bytes 172040 | tf_op jit(solution)/shard_map/ppermute | solution.py:44
  65.3 1.8 %collective-permute-start.18 = (bf16[8,3584]{1,0:T(8,128)(2,1)S(1)}, bf16[8,3584]{1,0:T(8,128)(2,1)S(1)}, u32[]{:S(2)}, u32[]{:S(2)}) collective-permute-start(bf16[8,3584]{1,0:T(8,128)(2,1)S(1)} %get-tuple-element.44), channel_id=1, source_target_pairs={{0,14},{2,12},{4,10},{6,8},{8,6},{10,4},{12,2},{14,0},{1,15},{3,13... | collective-permute-start | bytes 172040 | tf_op jit(solution)/shard_map/ppermute | solution.py:44
  67.1 0.0 collective-permute-start.19
  67.1 3.4 %collective-permute-start.20 = (bf16[8,3584]{1,0:T(8,128)(2,1)S(1)}, bf16[8,3584]{1,0:T(8,128)(2,1)S(1)}, u32[]{:S(2)}, u32[]{:S(2)}) collective-permute-start(bf16[8,3584]{1,0:T(8,128)(2,1)S(1)} %get-tuple-element.46), channel_id=1, source_target_pairs={{0,10},{2,8},{4,14},{6,12},{8,2},{10,0},{12,6},{14,4},{1,11},{3,9}... | collective-permute-start | bytes 172040 | tf_op jit(solution)/shard_map/ppermute | solution.py:44
  70.6 0.0 collective-permute-start.21
  70.6 0.0 collective-permute-done.17.rest_0_
  70.6 2.4 %collective-permute-start.22 = (bf16[8,3584]{1,0:T(8,128)(2,1)S(1)}, bf16[8,3584]{1,0:T(8,128)(2,1)S(1)}, u32[]{:S(2)}, u32[]{:S(2)}) collective-permute-start(bf16[8,3584]{1,0:T(8,128)(2,1)S(1)} %get-tuple-element.48), channel_id=1, source_target_pairs={{0,6},{2,4},{4,2},{6,0},{8,14},{10,12},{12,10},{14,8},{1,7},{3,5},... | collective-permute-start | bytes 172040 | tf_op jit(solution)/shard_map/ppermute | solution.py:44
  73.0 0.0 collective-permute-done.18.rest_1_
  73.0 1.1 %collective-permute-start.23 = (bf16[8,3584]{1,0:T(8,128)(2,1)S(1)}, bf16[8,3584]{1,0:T(8,128)(2,1)S(1)}, u32[]{:S(2)}, u32[]{:S(2)}) collective-permute-start(bf16[8,3584]{1,0:T(8,128)(2,1)S(1)} %get-tuple-element.49), channel_id=1, source_target_pairs={{0,2},{2,0},{4,6},{6,4},{8,10},{10,8},{12,14},{14,12},{1,3},{3,1},... | collective-permute-start | bytes 172040 | tf_op jit(solution)/shard_map/ppermute | solution.py:44
  74.1 0.3 collective-permute-done.19.rest_2_
  74.4 2.3 %collective-permute-done.20.rest_3_ = bf16[8,3584]{1,0:T(8,128)(2,1)S(1)} collective-permute-done((bf16[8,3584]{1,0:T(8,128)(2,1)S(1)}, bf16[8,3584]{1,0:T(8,128)(2,1)S(1)}, u32[]{:S(2)}, u32[]{:S(2)}) %collective-permute-start.20) | collective-permute-done | bytes 57376 | tf_op jit(solution)/shard_map/ppermute | solution.py:44
  76.7 0.0 collective-permute-done.21.rest_4_
  76.7 0.7 collective-permute-done.22.rest_5_
  77.4 0.5 collective-permute-done.23.rest_6_
  77.9 0.7 finish.1
  (1 shorter events, 0.0 us)
Async XLA Ops:
  6.8 7.2 %collective-permute-start.1 = (bf16[8,9472]{1,0:T(8,128)(2,1)}, bf16[8,9472]{1,0:T(8,128)(2,1)S(1)}, u32[]{:S(2)}, u32[]{:S(2)}) collective-permute-start(bf16[8,9472]{1,0:T(8,128)(2,1)} %get-tuple-element.29), channel_id=1, source_target_pairs={{0,4},{2,6},{4,0},{6,2},{8,12},{10,14},{12,8},{14,10},{1,5},{3,7},... | collective-permute-start | bytes 454664 | tf_op jit(solution)/shard_map/ppermute | solution.py:44
  9.9 5.6 %collective-permute-start = (bf16[8,9472]{1,0:T(8,128)(2,1)}, bf16[8,9472]{1,0:T(8,128)(2,1)S(1)}, u32[]{:S(2)}, u32[]{:S(2)}) collective-permute-start(bf16[8,9472]{1,0:T(8,128)(2,1)} %get-tuple-element.28.refs_0_), channel_id=1, source_target_pairs={{0,2},{2,0},{4,6},{6,4},{8,10},{10,8},{12,14},{14,12},{1,3},{3,1},... | collective-permute-start | bytes 454664 | tf_op jit(solution)/shard_map/ppermute | solution.py:44
  11.4 9.1 %collective-permute-start.5 = (bf16[8,9472]{1,0:T(8,128)(2,1)}, bf16[8,9472]{1,0:T(8,128)(2,1)S(1)}, u32[]{:S(2)}, u32[]{:S(2)}) collective-permute-start(bf16[8,9472]{1,0:T(8,128)(2,1)} %get-tuple-element.32), channel_id=1, source_target_pairs={{0,12},{2,14},{4,8},{6,10},{8,4},{10,6},{12,0},{14,2},{1,13},{3,15... | collective-permute-start | bytes 454664 | tf_op jit(solution)/shard_map/ppermute | solution.py:44
  15.5 11.8 %collective-permute-start.3 = (bf16[8,9472]{1,0:T(8,128)(2,1)}, bf16[8,9472]{1,0:T(8,128)(2,1)S(1)}, u32[]{:S(2)}, u32[]{:S(2)}) collective-permute-start(bf16[8,9472]{1,0:T(8,128)(2,1)} %get-tuple-element.31), channel_id=1, source_target_pairs={{0,8},{2,10},{4,12},{6,14},{8,0},{10,2},{12,4},{14,6},{1,9},{3,11}... | collective-permute-start | bytes 454664 | tf_op jit(solution)/shard_map/ppermute | solution.py:44
  18.1 9.7 %collective-permute-start.2 = (bf16[8,9472]{1,0:T(8,128)(2,1)S(1)}, bf16[8,9472]{1,0:T(8,128)(2,1)S(1)}, u32[]{:S(2)}, u32[]{:S(2)}) collective-permute-start(bf16[8,9472]{1,0:T(8,128)(2,1)S(1)} %collective-permute-done.1.refs_2_), channel_id=1, source_target_pairs={{0,2},{2,0},{4,6},{6,4},{8,10},{10,8},{12,14},{14,12},{1,3},{3,1},... | collective-permute-start | bytes 454664 | tf_op jit(solution)/shard_map/ppermute | solution.py:44
  20.5 7.3 %collective-permute-start.6 = (bf16[8,9472]{1,0:T(8,128)(2,1)S(1)}, bf16[8,9472]{1,0:T(8,128)(2,1)S(1)}, u32[]{:S(2)}, u32[]{:S(2)}) collective-permute-start(bf16[8,9472]{1,0:T(8,128)(2,1)S(1)} %collective-permute-done.5.refs_6_), channel_id=1, source_target_pairs={{0,2},{2,0},{4,6},{6,4},{8,10},{10,8},{12,14},{14,12},{1,3},{3,1},... | collective-permute-start | bytes 454664 | tf_op jit(solution)/shard_map/ppermute | solution.py:44
  27.3 5.2 %collective-permute-start.4 = (bf16[8,9472]{1,0:T(8,128)(2,1)S(1)}, bf16[8,9472]{1,0:T(8,128)(2,1)S(1)}, u32[]{:S(2)}, u32[]{:S(2)}) collective-permute-start(bf16[8,9472]{1,0:T(8,128)(2,1)S(1)} %collective-permute-done.3.refs_4_), channel_id=1, source_target_pairs={{0,2},{2,0},{4,6},{6,4},{8,10},{10,8},{12,14},{14,12},{1,3},{3,1},... | collective-permute-start | bytes 454664 | tf_op jit(solution)/shard_map/ppermute | solution.py:44
  32.5 26.2 %copy-start = (bf16[7168,160]{0,1:T(8,128)(2,1)S(1)}, bf16[7168,160]{0,1:T(8,128)(2,1)}, u32[]{:S(2)}) copy-start(bf16[7168,160]{0,1:T(8,128)(2,1)} %param.21) | copy-start | bytes 6881284
  32.5 26.2 %copy-start.1 = (bf16[7168,160]{0,1:T(8,128)(2,1)S(1)}, bf16[7168,160]{0,1:T(8,128)(2,1)}, u32[]{:S(2)}) copy-start(bf16[7168,160]{0,1:T(8,128)(2,1)} %param.22) | copy-start | bytes 6881284
  32.5 11.9 %collective-permute-start.8 = (bf16[3680,512]{1,0:T(8,128)(2,1)}, bf16[3680,512]{1,0:T(8,128)(2,1)S(1)}, u32[]{:S(2)}, u32[]{:S(2)}) collective-permute-start(bf16[3680,512]{1,0:T(8,128)(2,1)} %get-tuple-element.36), channel_id=1, source_target_pairs={{0,1},{1,0},{2,3},{3,2},{4,5},{5,4},{6,7},{7,6},{8,9},{9,8},{10,11... | collective-permute-start | bytes 11304968 | tf_op jit(solution)/shard_map/ppermute | solution.py:76
  32.5 1.1 %copy-start.3 = (bf16[8,9472]{1,0:T(8,128)(2,1)S(1)}, bf16[8,9472]{1,0:T(8,128)(2,1)}, u32[]{:S(2)}) copy-start(bf16[8,9472]{1,0:T(8,128)(2,1)} %get-tuple-element.28.refs_0_) | copy-start | bytes 454660
  33.6 25.1 %copy-start.4 = (f32[7168]{0:T(1024)S(1)}, f32[7168]{0:T(1024)}, u32[]{:S(2)}) copy-start(f32[7168]{0:T(1024)} %param.18) | copy-start | bytes 86020
  42.9 1.4 %collective-permute-start.7 = (f32[64,512]{1,0:T(8,128)S(1)}, f32[64,512]{1,0:T(8,128)S(1)}, u32[]{:S(2)}, u32[]{:S(2)}) collective-permute-start(f32[64,512]{1,0:T(8,128)S(1)} %get-tuple-element.34), channel_id=1, source_target_pairs={{0,1},{1,0},{2,3},{3,2},{4,5},{5,4},{6,7},{7,6},{8,9},{9,8},{10,11... | collective-permute-start | bytes 393224 | tf_op jit(solution)/shard_map/ppermute | solution.py:76
  44.4 4.3 %collective-permute-start.10 = (bf16[64,512]{1,0:T(8,128)(2,1)S(1)}, bf16[64,512]{1,0:T(8,128)(2,1)S(1)}, u32[]{:S(2)}, u32[]{:S(2)}) collective-permute-start(bf16[64,512]{1,0:T(8,128)(2,1)S(1)} %add_convert_fusion.refs_0_), channel_id=1, source_target_pairs={{0,4},{2,6},{4,0},{6,2},{8,12},{10,14},{12,8},{14,10},{1,5},{3,7},... | collective-permute-start | bytes 196616 | tf_op jit(solution)/shard_map/ppermute | solution.py:44
  45.8 6.5 %collective-permute-start.14 = (bf16[64,512]{1,0:T(8,128)(2,1)S(1)}, bf16[64,512]{1,0:T(8,128)(2,1)S(1)}, u32[]{:S(2)}, u32[]{:S(2)}) collective-permute-start(bf16[64,512]{1,0:T(8,128)(2,1)S(1)} %add_convert_fusion.refs_0_), channel_id=1, source_target_pairs={{0,12},{2,14},{4,8},{6,10},{8,4},{10,6},{12,0},{14,2},{1,13},{3,15... | collective-permute-start | bytes 196616 | tf_op jit(solution)/shard_map/ppermute | solution.py:44
  47.5 6.9 %collective-permute-start.12 = (bf16[64,512]{1,0:T(8,128)(2,1)S(1)}, bf16[64,512]{1,0:T(8,128)(2,1)S(1)}, u32[]{:S(2)}, u32[]{:S(2)}) collective-permute-start(bf16[64,512]{1,0:T(8,128)(2,1)S(1)} %add_convert_fusion.refs_0_), channel_id=1, source_target_pairs={{0,8},{2,10},{4,12},{6,14},{8,0},{10,2},{12,4},{14,6},{1,9},{3,11}... | collective-permute-start | bytes 196616 | tf_op jit(solution)/shard_map/ppermute | solution.py:44
  48.7 5.7 %collective-permute-start.11 = (bf16[64,512]{1,0:T(8,128)(2,1)S(1)}, bf16[64,512]{1,0:T(8,128)(2,1)S(1)}, u32[]{:S(2)}, u32[]{:S(2)}) collective-permute-start(bf16[64,512]{1,0:T(8,128)(2,1)S(1)} %collective-permute-done.10.refs_2_), channel_id=1, source_target_pairs={{0,2},{2,0},{4,6},{6,4},{8,10},{10,8},{12,14},{14,12},{1,3},{3,1},... | collective-permute-start | bytes 196616 | tf_op jit(solution)/shard_map/ppermute | solution.py:44
  49.8 5.5 %collective-permute-start.9 = (bf16[64,512]{1,0:T(8,128)(2,1)S(1)}, bf16[64,512]{1,0:T(8,128)(2,1)S(1)}, u32[]{:S(2)}, u32[]{:S(2)}) collective-permute-start(bf16[64,512]{1,0:T(8,128)(2,1)S(1)} %add_convert_fusion.refs_0_), channel_id=1, source_target_pairs={{0,2},{2,0},{4,6},{6,4},{8,10},{10,8},{12,14},{14,12},{1,3},{3,1},... | collective-permute-start | bytes 196616 | tf_op jit(solution)/shard_map/ppermute | solution.py:44
  52.3 4.3 %collective-permute-start.15 = (bf16[64,512]{1,0:T(8,128)(2,1)S(1)}, bf16[64,512]{1,0:T(8,128)(2,1)S(1)}, u32[]{:S(2)}, u32[]{:S(2)}) collective-permute-start(bf16[64,512]{1,0:T(8,128)(2,1)S(1)} %collective-permute-done.14.refs_6_), channel_id=1, source_target_pairs={{0,2},{2,0},{4,6},{6,4},{8,10},{10,8},{12,14},{14,12},{1,3},{3,1},... | collective-permute-start | bytes 196616 | tf_op jit(solution)/shard_map/ppermute | solution.py:44
  54.4 4.3 %collective-permute-start.13 = (bf16[64,512]{1,0:T(8,128)(2,1)S(1)}, bf16[64,512]{1,0:T(8,128)(2,1)S(1)}, u32[]{:S(2)}, u32[]{:S(2)}) collective-permute-start(bf16[64,512]{1,0:T(8,128)(2,1)S(1)} %collective-permute-done.12.refs_4_), channel_id=1, source_target_pairs={{0,2},{2,0},{4,6},{6,4},{8,10},{10,8},{12,14},{14,12},{1,3},{3,1},... | collective-permute-start | bytes 196616 | tf_op jit(solution)/shard_map/ppermute | solution.py:44
  58.7 3.3 %copy-start.2 = (bf16[160,7168]{1,0:T(8,128)(2,1)S(1)}, bf16[160,7168]{1,0:T(8,128)(2,1)}, u32[]{:S(2)}) copy-start(bf16[160,7168]{1,0:T(8,128)(2,1)} %down_ref.1) | copy-start | bytes 6881284
  60.4 1.6 %collective-permute-start.16 = (f32[88,768]{1,0:T(8,128)S(1)}, f32[88,768]{1,0:T(8,128)S(1)}, u32[]{:S(2)}, u32[]{:S(2)}) collective-permute-start(f32[88,768]{1,0:T(8,128)S(1)} %get-tuple-element.41.sums_ref), channel_id=1, source_target_pairs={{0,1},{1,0},{2,3},{3,2},{4,5},{5,4},{6,7},{7,6},{8,9},{9,8},{10,11... | collective-permute-start | bytes 811016 | tf_op jit(solution)/shard_map/ppermute | solution.py:76
  62.9 7.8 %collective-permute-start.17 = (bf16[8,3584]{1,0:T(8,128)(2,1)S(1)}, bf16[8,3584]{1,0:T(8,128)(2,1)S(1)}, u32[]{:S(2)}, u32[]{:S(2)}) collective-permute-start(bf16[8,3584]{1,0:T(8,128)(2,1)S(1)} %get-tuple-element.43), channel_id=1, source_target_pairs={{0,12},{2,14},{4,8},{6,10},{8,4},{10,6},{12,0},{14,2},{1,13},{3,15... | collective-permute-start | bytes 172040 | tf_op jit(solution)/shard_map/ppermute | solution.py:44
  65.3 7.7 %collective-permute-start.18 = (bf16[8,3584]{1,0:T(8,128)(2,1)S(1)}, bf16[8,3584]{1,0:T(8,128)(2,1)S(1)}, u32[]{:S(2)}, u32[]{:S(2)}) collective-permute-start(bf16[8,3584]{1,0:T(8,128)(2,1)S(1)} %get-tuple-element.44), channel_id=1, source_target_pairs={{0,14},{2,12},{4,10},{6,8},{8,6},{10,4},{12,2},{14,0},{1,15},{3,13... | collective-permute-start | bytes 172040 | tf_op jit(solution)/shard_map/ppermute | solution.py:44
  67.1 7.3 %collective-permute-start.19 = (bf16[8,3584]{1,0:T(8,128)(2,1)S(1)}, bf16[8,3584]{1,0:T(8,128)(2,1)S(1)}, u32[]{:S(2)}, u32[]{:S(2)}) collective-permute-start(bf16[8,3584]{1,0:T(8,128)(2,1)S(1)} %get-tuple-element.45), channel_id=1, source_target_pairs={{0,8},{2,10},{4,12},{6,14},{8,0},{10,2},{12,4},{14,6},{1,9},{3,11}... | collective-permute-start | bytes 172040 | tf_op jit(solution)/shard_map/ppermute | solution.py:44
  67.1 9.6 %collective-permute-start.20 = (bf16[8,3584]{1,0:T(8,128)(2,1)S(1)}, bf16[8,3584]{1,0:T(8,128)(2,1)S(1)}, u32[]{:S(2)}, u32[]{:S(2)}) collective-permute-start(bf16[8,3584]{1,0:T(8,128)(2,1)S(1)} %get-tuple-element.46), channel_id=1, source_target_pairs={{0,10},{2,8},{4,14},{6,12},{8,2},{10,0},{12,6},{14,4},{1,11},{3,9}... | collective-permute-start | bytes 172040 | tf_op jit(solution)/shard_map/ppermute | solution.py:44
  70.6 6.2 %collective-permute-start.21 = (bf16[8,3584]{1,0:T(8,128)(2,1)S(1)}, bf16[8,3584]{1,0:T(8,128)(2,1)S(1)}, u32[]{:S(2)}, u32[]{:S(2)}) collective-permute-start(bf16[8,3584]{1,0:T(8,128)(2,1)S(1)} %get-tuple-element.47), channel_id=1, source_target_pairs={{0,4},{2,6},{4,0},{6,2},{8,12},{10,14},{12,8},{14,10},{1,5},{3,7},... | collective-permute-start | bytes 172040 | tf_op jit(solution)/shard_map/ppermute | solution.py:44
  70.6 6.8 %collective-permute-start.22 = (bf16[8,3584]{1,0:T(8,128)(2,1)S(1)}, bf16[8,3584]{1,0:T(8,128)(2,1)S(1)}, u32[]{:S(2)}, u32[]{:S(2)}) collective-permute-start(bf16[8,3584]{1,0:T(8,128)(2,1)S(1)} %get-tuple-element.48), channel_id=1, source_target_pairs={{0,6},{2,4},{4,2},{6,0},{8,14},{10,12},{12,10},{14,8},{1,7},{3,5},... | collective-permute-start | bytes 172040 | tf_op jit(solution)/shard_map/ppermute | solution.py:44
  73.0 5.0 %collective-permute-start.23 = (bf16[8,3584]{1,0:T(8,128)(2,1)S(1)}, bf16[8,3584]{1,0:T(8,128)(2,1)S(1)}, u32[]{:S(2)}, u32[]{:S(2)}) collective-permute-start(bf16[8,3584]{1,0:T(8,128)(2,1)S(1)} %get-tuple-element.49), channel_id=1, source_target_pairs={{0,2},{2,0},{4,6},{6,4},{8,10},{10,8},{12,14},{14,12},{1,3},{3,1},... | collective-permute-start | bytes 172040 | tf_op jit(solution)/shard_map/ppermute | solution.py:44

commit v9 on v8

--- a/solution.py
+++ b/solution.py
@@ -31,13 +31,16 @@
 
 
 class Grid:
-    def __init__(self, ep_size):
-        self.ep, self.x, self.z = ep_size, ep_size // 4, 4
+    def __init__(self, ep_size, pairs):
+        self.ep, self.x, self.z, self.pairs = ep_size, ep_size // 4, 4, pairs
         self.steps = [(s, u) for s in range(self.z) for u in range(self.x)]
+
+    def along_z(self, z, s):
+        return z ^ s if self.pairs else (z + s) % self.z
 
     def send(self, arr, s, u):
         pairs = [
-            (z * self.x + x, (z ^ s) * self.x + (x + u) % self.x)
+            (z * self.x + x, self.along_z(z, s) * self.x + (x + u) % self.x)
             for z in range(self.z)
             for x in range(self.x)
         ]
@@ -65,11 +68,13 @@
 
     def source(self, step):
         me = lax.axis_index("ep")
-        z = (me // self.x) ^ step[0]
+        z = me // self.x
+        z = z ^ step[0] if self.pairs else lax.rem(z - step[0] + self.z, self.z)
         return z * self.x + lax.rem(lax.rem(me, self.x) - step[1] + self.x, self.x)
 
     def target(self, step):
-        return self.source((step[0], -step[1] % self.x))
+        s = step[0] if self.pairs else -step[0] % self.z
+        return self.source((s, -step[1] % self.x))
 
 
 def swap(arr):
@@ -139,7 +144,7 @@
             for i, block in enumerate(blocks)
         ]
         pack_out = pltpu.make_async_copy(packed, pack_ref, pack_sems.at[len(blocks)])
-        for copy in copies[:2] + row_copies + copies[2:] + packs:
+        for copy in copies[:2] + row_copies:
             copy.start()
 
         copies[0].wait()
@@ -148,6 +153,8 @@
             for c in range(parts):
                 at = h * HD + c * LANES
                 turned[c, h * rows : (h + 1) * rows, :] = q_ref[:, at : at + LANES].astype(jnp.float32)
+        for copy in copies[2:] + packs:
+            copy.start()
         new_k = kv_ref[:, :HD].astype(jnp.float32)
         new_v = kv_ref[:, HD:].astype(jnp.float32)
         scores, owns = [], []
@@ -159,9 +166,8 @@
             row_copies[r].wait()
             scores.append(nt_dot(q.astype(jnp.bfloat16), kept[r, :, :HD]) * scaling)
 
-        for copy in copies[2:] + packs:
+        for copy in copies[2:]:
             copy.wait()
-        pack_out.start()
         lane = lax.broadcasted_iota(jnp.int32, (rows, LANES), 1)
         square = (rows, rows)
         diagonal = lax.broadcasted_iota(jnp.int32, square, 0) == lax.broadcasted_iota(jnp.int32, square, 1)
@@ -194,6 +200,9 @@
             denominator = jnp.sum(exps, axis=1, keepdims=True) + own_exp
             probs.append((exps / denominator).astype(jnp.bfloat16))
             own_probs.append((own_exp / denominator).astype(jnp.bfloat16).astype(jnp.float32))
+        for copy in packs:
+            copy.wait()
+        pack_out.start()
         for r in range(rows):
             mixed = jnp.dot(probs[r], kept[r, :, HD:], preferred_element_type=jnp.float32)
             mixed = mixed + own_probs[r] * new_v[r : r + 1]
@@ -459,6 +468,7 @@
 
 
 def tuned_body(
+    ring,
     grid,
     residual,
     queries,
@@ -478,7 +488,7 @@
     piece = -(-cols // (2 * LANES)) * LANES
     gate_t, up_t = w_gate.T, w_up.T
     *outgoing, packed = attention(
-        grid,
+        ring,
         piece,
         cols,
         queries,
@@ -492,10 +502,10 @@
         up_t,
         w_down,
     )
-    chunks = grid.spread(outgoing, spaced=True)
+    chunks = ring.spread(outgoing, spaced=True)
     packed, *_ = lax.optimization_barrier((packed, *chunks))
     far_weights = swap(packed)
-    ours, theirs, weight = project(grid, piece, chunks, w_out)
+    ours, theirs, weight = project(ring, piece, chunks, w_out)
     stream = (ours + swap(theirs)).astype(jnp.bfloat16)
     stream, far_weights = lax.optimization_barrier((stream, far_weights))
     pieces = grid.spread([stream] * grid.z, spaced=False)
@@ -597,7 +607,7 @@
 def body(*args):
     ep_size, cols, heads_width = lax.axis_size("ep"), args[5].shape[1], args[5].shape[0]
     if ep_size == 8 and lax.axis_size("tp") == 2 and cols % LANES == 0 and heads_width % (8 * HD) == 0:
-        return tuned_body(Grid(ep_size), *args)
+        return tuned_body(Grid(ep_size, False), Grid(ep_size, True), *args)
     return general_body(*args)
 
 

time: 78.8 us -> 77.8 us (0.987)
  waiting for transfers between devices: 26.4 us -> 24.6 us
    ppermute x21, waiting for transfers between devices: 23.5 us -> 21.7 us  [send(): return lax.ppermute(arr, 'ep', pairs)]
  transfers between devices with their start and end apart: 24 -> 24, of which waited for: 16 -> 14; matrix products, arithmetic and copies ran while one was open for 0% -> 0% of each run, Pallas kernels for 12% -> 12%
where the time goes in v9:
time: 77.8 us; the launch traced here: 77.6 us
  starting transfers between devices  32.4 us (42%)
  waiting for transfers between devices  24.6 us (32%)
  Pallas kernels  19.4 us (25%)
  local copies, waits for them, and re-layouts  1.08 us (1%)
    ppermute x21, starting transfers between devices, send(): return lax.ppermute(arr, 'ep', pairs)  32.3 us
    ppermute x21, waiting for transfers between devices, send(): return lax.ppermute(arr, 'ep', pairs)  21.7 us
    pallas_call x1, Pallas kernels, project(): pl.pallas_call(kernel, name='project', grid=(blocks,), out_shape=outs, in...  9.39 us
    pallas_call x1, Pallas kernels, attention(): pl.pallas_call(kernel, name='attention', out_shape=[shape_of((rows, width...  6.82 us
    ppermute x3, waiting for transfers between devices, swap(): return lax.ppermute(arr, 'tp', [(0, 1), (1, 0)])  2.87 us
    pallas_call x1, Pallas kernels, gate_up(): pl.pallas_call(kernel, name='gate_up', out_shape=[shape_of((tall + extra...  1.65 us
  transfers between devices with their start and end apart: 24, of which 14 were waited for; matrix products, arithmetic and copies ran while one was open for 0% of the time, Pallas kernels for 12%

profile of v9, /device:TPU:0, one launch (start us, length us, event | category | flops | bytes accessed | tf_op | source)
XLA Modules:
  0.0 77.6 jit_solution(3812360299034207776)
XLA Ops:
  0.0 6.8 %attention.1 = (bf16[8,9472]{1,0:T(8,128)(2,1)}, bf16[8,9472]{1,0:T(8,128)(2,1)}, bf16[8,9472]{1,0:T(8,128)(2,1)}, bf16[8,9472]{1,0:T(8,128)(2,1)}, bf16[3680,512]{1,0:T(8,128)(2,1)}) custom-call(bf16[8,8192]{1,0:T(8,128)(2,1)} %refs_0_.1, bf16[8,512]{1,0:T(8,128)(2,1)} %refs_1_.1, bf16[8,7168]{1,0:T(8,128)(2,1)} %refs_2_.1, s32[3,8]{1,0:T(4,128)} %bitcast.10, ...), custom_call_target="tpu_custom_call" | custom-call | tf_op jit(solution)/shard_map/attention/pallas_call | solution.py:219
  6.8 3.1 %collective-permute-start.1 = (bf16[8,9472]{1,0:T(8,128)(2,1)}, bf16[8,9472]{1,0:T(8,128)(2,1)S(1)}, u32[]{:S(2)}, u32[]{:S(2)}) collective-permute-start(bf16[8,9472]{1,0:T(8,128)(2,1)} %get-tuple-element.29), channel_id=1, source_target_pairs={{0,4},{2,6},{4,8},{6,10},{8,12},{10,14},{12,0},{14,2},{1,5},{3,7},... | collective-permute-start | bytes 454664 | tf_op jit(solution)/shard_map/ppermute | solution.py:47
  9.9 1.5 %collective-permute-start = (bf16[8,9472]{1,0:T(8,128)(2,1)}, bf16[8,9472]{1,0:T(8,128)(2,1)S(1)}, u32[]{:S(2)}, u32[]{:S(2)}) collective-permute-start(bf16[8,9472]{1,0:T(8,128)(2,1)} %get-tuple-element.28.refs_0_), channel_id=1, source_target_pairs={{0,2},{2,0},{4,6},{6,4},{8,10},{10,8},{12,14},{14,12},{1,3},{3,1},... | collective-permute-start | bytes 454664 | tf_op jit(solution)/shard_map/ppermute | solution.py:47
  11.4 2.2 %collective-permute-start.5 = (bf16[8,9472]{1,0:T(8,128)(2,1)}, bf16[8,9472]{1,0:T(8,128)(2,1)S(1)}, u32[]{:S(2)}, u32[]{:S(2)}) collective-permute-start(bf16[8,9472]{1,0:T(8,128)(2,1)} %get-tuple-element.32), channel_id=1, source_target_pairs={{0,12},{2,14},{4,0},{6,2},{8,4},{10,6},{12,8},{14,10},{1,13},{3,15... | collective-permute-start | bytes 454664 | tf_op jit(solution)/shard_map/ppermute | solution.py:47
  13.6 2.9 %collective-permute-done.1.refs_2_ = bf16[8,9472]{1,0:T(8,128)(2,1)S(1)} collective-permute-done((bf16[8,9472]{1,0:T(8,128)(2,1)}, bf16[8,9472]{1,0:T(8,128)(2,1)S(1)}, u32[]{:S(2)}, u32[]{:S(2)}) %collective-permute-start.1) | collective-permute-done | bytes 151584 | tf_op jit(solution)/shard_map/ppermute | solution.py:47
  16.6 0.0 collective-permute-done.refs_1_
  16.6 1.5 %collective-permute-start.3 = (bf16[8,9472]{1,0:T(8,128)(2,1)}, bf16[8,9472]{1,0:T(8,128)(2,1)S(1)}, u32[]{:S(2)}, u32[]{:S(2)}) collective-permute-start(bf16[8,9472]{1,0:T(8,128)(2,1)} %get-tuple-element.31), channel_id=1, source_target_pairs={{0,8},{2,10},{4,12},{6,14},{8,0},{10,2},{12,4},{14,6},{1,9},{3,11}... | collective-permute-start | bytes 454664 | tf_op jit(solution)/shard_map/ppermute | solution.py:47
  18.1 3.4 %collective-permute-start.2 = (bf16[8,9472]{1,0:T(8,128)(2,1)S(1)}, bf16[8,9472]{1,0:T(8,128)(2,1)S(1)}, u32[]{:S(2)}, u32[]{:S(2)}) collective-permute-start(bf16[8,9472]{1,0:T(8,128)(2,1)S(1)} %collective-permute-done.1.refs_2_), channel_id=1, source_target_pairs={{0,2},{2,0},{4,6},{6,4},{8,10},{10,8},{12,14},{14,12},{1,3},{3,1},... | collective-permute-start | bytes 454664 | tf_op jit(solution)/shard_map/ppermute | solution.py:47
  21.5 0.0 collective-permute-done.5.refs_6_
  21.5 0.0 collective-permute-start.6
  21.6 4.2 %collective-permute-done.3.refs_4_ = bf16[8,9472]{1,0:T(8,128)(2,1)S(1)} collective-permute-done((bf16[8,9472]{1,0:T(8,128)(2,1)}, bf16[8,9472]{1,0:T(8,128)(2,1)S(1)}, u32[]{:S(2)}, u32[]{:S(2)}) %collective-permute-start.3) | collective-permute-done | bytes 151584 | tf_op jit(solution)/shard_map/ppermute | solution.py:47
  25.8 1.5 %collective-permute-start.4 = (bf16[8,9472]{1,0:T(8,128)(2,1)S(1)}, bf16[8,9472]{1,0:T(8,128)(2,1)S(1)}, u32[]{:S(2)}, u32[]{:S(2)}) collective-permute-start(bf16[8,9472]{1,0:T(8,128)(2,1)S(1)} %collective-permute-done.3.refs_4_), channel_id=1, source_target_pairs={{0,2},{2,0},{4,6},{6,4},{8,10},{10,8},{12,14},{14,12},{1,3},{3,1},... | collective-permute-start | bytes 454664 | tf_op jit(solution)/shard_map/ppermute | solution.py:47
  27.3 0.0 collective-permute-done.2.refs_3_
  27.3 0.0 collective-permute-done.6.refs_7_
  27.3 4.1 %collective-permute-done.4.refs_5_ = bf16[8,9472]{1,0:T(8,128)(2,1)S(1)} collective-permute-done((bf16[8,9472]{1,0:T(8,128)(2,1)S(1)}, bf16[8,9472]{1,0:T(8,128)(2,1)S(1)}, u32[]{:S(2)}, u32[]{:S(2)}) %collective-permute-start.4) | collective-permute-done | bytes 151584 | tf_op jit(solution)/shard_map/ppermute | solution.py:47
  31.4 0.0 copy-start
  31.4 0.0 copy-start.1
  31.4 0.0 collective-permute-start.8
  31.4 0.0 copy-start.3
  31.4 1.1 %copy-done.3 = bf16[8,9472]{1,0:T(8,128)(2,1)S(1)} copy-done((bf16[8,9472]{1,0:T(8,128)(2,1)S(1)}, bf16[8,9472]{1,0:T(8,128)(2,1)}, u32[]{:S(2)}) %copy-start.3) | copy-done | bytes 151576
  32.5 0.0 copy-start.4
  32.5 9.4 %project.1 = (f32[64,512]{1,0:T(8,128)S(1)}, f32[64,512]{1,0:T(8,128)S(1)}, f32[64,128]{1,0:T(8,128)S(1)}) custom-call(bf16[8,9472]{1,0:T(8,128)(2,1)S(1)} %copy-done.3, bf16[8,9472]{1,0:T(8,128)(2,1)S(1)} %collective-permute-done.refs_1_, bf16[8,9472]{1,0:T(8,128)(2,1)S(1)} %collective-permute-done.1.refs_2_, ...), custom_call_target="tpu_custom_call" | custom-call | flops 939524096 | bytes 15990784 | tf_op jit(solution)/shard_map/project/pallas_call | solution.py:305
  41.9 0.1 collective-permute-start.7
  41.9 1.3 %collective-permute-done.7 = f32[64,512]{1,0:T(8,128)S(1)} collective-permute-done((f32[64,512]{1,0:T(8,128)S(1)}, f32[64,512]{1,0:T(8,128)S(1)}, u32[]{:S(2)}, u32[]{:S(2)}) %collective-permute-start.7) | collective-permute-done | bytes 131104 | tf_op jit(solution)/shard_map/ppermute | solution.py:81
  43.3 0.0 collective-permute-done.8.refs_11_.packed_ref
  43.3 0.8 collective-permute-start.10
  44.1 1.5 %collective-permute-start.14 = (bf16[64,512]{1,0:T(8,128)(2,1)S(1)}, bf16[64,512]{1,0:T(8,128)(2,1)S(1)}, u32[]{:S(2)}, u32[]{:S(2)}) collective-permute-start(bf16[64,512]{1,0:T(8,128)(2,1)S(1)} %add_convert_fusion.refs_0_), channel_id=1, source_target_pairs={{0,12},{2,14},{4,8},{6,10},{8,4},{10,6},{12,0},{14,2},{1,13},{3,15... | collective-permute-start | bytes 196616 | tf_op jit(solution)/shard_map/ppermute | solution.py:47
  45.6 1.3 %collective-permute-start.12 = (bf16[64,512]{1,0:T(8,128)(2,1)S(1)}, bf16[64,512]{1,0:T(8,128)(2,1)S(1)}, u32[]{:S(2)}, u32[]{:S(2)}) collective-permute-start(bf16[64,512]{1,0:T(8,128)(2,1)S(1)} %add_convert_fusion.refs_0_), channel_id=1, source_target_pairs={{0,8},{2,10},{4,12},{6,14},{8,0},{10,2},{12,4},{14,6},{1,9},{3,11}... | collective-permute-start | bytes 196616 | tf_op jit(solution)/shard_map/ppermute | solution.py:47
  46.9 0.8 %collective-permute-done.10.refs_2_ = bf16[64,512]{1,0:T(8,128)(2,1)S(1)} collective-permute-done((bf16[64,512]{1,0:T(8,128)(2,1)S(1)}, bf16[64,512]{1,0:T(8,128)(2,1)S(1)}, u32[]{:S(2)}, u32[]{:S(2)}) %collective-permute-start.10) | collective-permute-done | bytes 65568 | tf_op jit(solution)/shard_map/ppermute | solution.py:47
  47.6 1.1 %collective-permute-start.11 = (bf16[64,512]{1,0:T(8,128)(2,1)S(1)}, bf16[64,512]{1,0:T(8,128)(2,1)S(1)}, u32[]{:S(2)}, u32[]{:S(2)}) collective-permute-start(bf16[64,512]{1,0:T(8,128)(2,1)S(1)} %collective-permute-done.10.refs_2_), channel_id=1, source_target_pairs={{0,2},{2,0},{4,6},{6,4},{8,10},{10,8},{12,14},{14,12},{1,3},{3,1},... | collective-permute-start | bytes 196616 | tf_op jit(solution)/shard_map/ppermute | solution.py:47
  48.7 0.9 %collective-permute-start.9 = (bf16[64,512]{1,0:T(8,128)(2,1)S(1)}, bf16[64,512]{1,0:T(8,128)(2,1)S(1)}, u32[]{:S(2)}, u32[]{:S(2)}) collective-permute-start(bf16[64,512]{1,0:T(8,128)(2,1)S(1)} %add_convert_fusion.refs_0_), channel_id=1, source_target_pairs={{0,2},{2,0},{4,6},{6,4},{8,10},{10,8},{12,14},{14,12},{1,3},{3,1},... | collective-permute-start | bytes 196616 | tf_op jit(solution)/shard_map/ppermute | solution.py:47
  49.7 0.9 %collective-permute-done.14.refs_6_ = bf16[64,512]{1,0:T(8,128)(2,1)S(1)} collective-permute-done((bf16[64,512]{1,0:T(8,128)(2,1)S(1)}, bf16[64,512]{1,0:T(8,128)(2,1)S(1)}, u32[]{:S(2)}, u32[]{:S(2)}) %collective-permute-start.14) | collective-permute-done | bytes 65568 | tf_op jit(solution)/shard_map/ppermute | solution.py:47
  50.6 1.0 %collective-permute-start.15 = (bf16[64,512]{1,0:T(8,128)(2,1)S(1)}, bf16[64,512]{1,0:T(8,128)(2,1)S(1)}, u32[]{:S(2)}, u32[]{:S(2)}) collective-permute-start(bf16[64,512]{1,0:T(8,128)(2,1)S(1)} %collective-permute-done.14.refs_6_), channel_id=1, source_target_pairs={{0,2},{2,0},{4,6},{6,4},{8,10},{10,8},{12,14},{14,12},{1,3},{3,1},... | collective-permute-start | bytes 196616 | tf_op jit(solution)/shard_map/ppermute | solution.py:47
  51.5 1.7 %collective-permute-done.12.refs_4_ = bf16[64,512]{1,0:T(8,128)(2,1)S(1)} collective-permute-done((bf16[64,512]{1,0:T(8,128)(2,1)S(1)}, bf16[64,512]{1,0:T(8,128)(2,1)S(1)}, u32[]{:S(2)}, u32[]{:S(2)}) %collective-permute-start.12) | collective-permute-done | bytes 65568 | tf_op jit(solution)/shard_map/ppermute | solution.py:47
  53.2 0.0 collective-permute-done.11.refs_3_
  53.2 1.2 %collective-permute-start.13 = (bf16[64,512]{1,0:T(8,128)(2,1)S(1)}, bf16[64,512]{1,0:T(8,128)(2,1)S(1)}, u32[]{:S(2)}, u32[]{:S(2)}) collective-permute-start(bf16[64,512]{1,0:T(8,128)(2,1)S(1)} %collective-permute-done.12.refs_4_), channel_id=1, source_target_pairs={{0,2},{2,0},{4,6},{6,4},{8,10},{10,8},{12,14},{14,12},{1,3},{3,1},... | collective-permute-start | bytes 196616 | tf_op jit(solution)/shard_map/ppermute | solution.py:47
  54.5 0.0 collective-permute-done.9.refs_1_
  54.5 0.4 collective-permute-done.15.refs_7_
  54.8 2.7 %collective-permute-done.13.refs_5_ = bf16[64,512]{1,0:T(8,128)(2,1)S(1)} collective-permute-done((bf16[64,512]{1,0:T(8,128)(2,1)S(1)}, bf16[64,512]{1,0:T(8,128)(2,1)S(1)}, u32[]{:S(2)}, u32[]{:S(2)}) %collective-permute-start.13) | collective-permute-done | bytes 65568 | tf_op jit(solution)/shard_map/ppermute | solution.py:47
  57.5 0.0 copy-done
  57.5 0.0 copy-done.1
  57.5 0.0 copy-done.4
  57.5 0.0 copy-start.2
  57.5 1.6 %gate_up.1 = (f32[88,768]{1,0:T(8,128)S(1)}, f32[8,2048]{1,0:T(8,128)S(1)}) custom-call(bf16[64,512]{1,0:T(8,128)(2,1)S(1)} %add_convert_fusion.refs_0_, bf16[64,512]{1,0:T(8,128)(2,1)S(1)} %collective-permute-done.9.refs_1_, bf16[64,512]{1,0:T(8,128)(2,1)S(1)} %collective-permute-done.10.refs_2_, bf16[64,512]{1,0:T(8,128)(2,1)S(1)} %collective-permute-done.11.refs_3_, ...), custom_call_target="tpu_custom_call" | custom-call | tf_op jit(solution)/shard_map/gate_up/pallas_call | solution.py:368
  59.2 0.1 collective-permute-start.16
  59.3 1.5 %collective-permute-done.16.far_ref = f32[88,768]{1,0:T(8,128)S(1)} collective-permute-done((f32[88,768]{1,0:T(8,128)S(1)}, f32[88,768]{1,0:T(8,128)S(1)}, u32[]{:S(2)}, u32[]{:S(2)}) %collective-permute-start.16) | collective-permute-done | bytes 270368 | tf_op jit(solution)/shard_map/ppermute | solution.py:81
  60.8 0.0 copy-done.2
  60.8 0.9 %down.1 = (f32[8,3584]{1,0:T(8,128)S(1)}, bf16[8,3584]{1,0:T(8,128)(2,1)S(1)}, bf16[8,3584]{1,0:T(8,128)(2,1)S(1)}, bf16[8,3584]{1,0:T(8,128)(2,1)S(1)}, bf16[8,...) custom-call(f32[88,768]{1,0:T(8,128)S(1)} %get-tuple-element.41.sums, ...), custom_call_target="tpu_custom_call" | custom-call | tf_op jit(solution)/shard_map/down/pallas_call | solution.py:421
  61.7 1.9 %collective-permute-start.17 = (bf16[8,3584]{1,0:T(8,128)(2,1)S(1)}, bf16[8,3584]{1,0:T(8,128)(2,1)S(1)}, u32[]{:S(2)}, u32[]{:S(2)}) collective-permute-start(bf16[8,3584]{1,0:T(8,128)(2,1)S(1)} %get-tuple-element.43), channel_id=1, source_target_pairs={{0,12},{2,14},{4,8},{6,10},{8,4},{10,6},{12,0},{14,2},{1,13},{3,15... | collective-permute-start | bytes 172040 | tf_op jit(solution)/shard_map/ppermute | solution.py:47
  63.6 2.7 %collective-permute-start.18 = (bf16[8,3584]{1,0:T(8,128)(2,1)S(1)}, bf16[8,3584]{1,0:T(8,128)(2,1)S(1)}, u32[]{:S(2)}, u32[]{:S(2)}) collective-permute-start(bf16[8,3584]{1,0:T(8,128)(2,1)S(1)} %get-tuple-element.44), channel_id=1, source_target_pairs={{0,14},{2,12},{4,10},{6,8},{8,6},{10,4},{12,2},{14,0},{1,15},{3,13... | collective-permute-start | bytes 172040 | tf_op jit(solution)/shard_map/ppermute | solution.py:47
  66.2 0.0 collective-permute-start.19
  66.2 3.2 %collective-permute-start.20 = (bf16[8,3584]{1,0:T(8,128)(2,1)S(1)}, bf16[8,3584]{1,0:T(8,128)(2,1)S(1)}, u32[]{:S(2)}, u32[]{:S(2)}) collective-permute-start(bf16[8,3584]{1,0:T(8,128)(2,1)S(1)} %get-tuple-element.46), channel_id=1, source_target_pairs={{0,10},{2,8},{4,14},{6,12},{8,2},{10,0},{12,6},{14,4},{1,11},{3,9}... | collective-permute-start | bytes 172040 | tf_op jit(solution)/shard_map/ppermute | solution.py:47
  69.4 0.0 collective-permute-start.21
  69.4 0.0 collective-permute-done.17.rest_0_
  69.4 2.7 %collective-permute-start.22 = (bf16[8,3584]{1,0:T(8,128)(2,1)S(1)}, bf16[8,3584]{1,0:T(8,128)(2,1)S(1)}, u32[]{:S(2)}, u32[]{:S(2)}) collective-permute-start(bf16[8,3584]{1,0:T(8,128)(2,1)S(1)} %get-tuple-element.48), channel_id=1, source_target_pairs={{0,6},{2,4},{4,2},{6,0},{8,14},{10,12},{12,10},{14,8},{1,7},{3,5},... | collective-permute-start | bytes 172040 | tf_op jit(solution)/shard_map/ppermute | solution.py:47
  72.1 0.0 collective-permute-done.18.rest_1_
  72.1 0.8 %collective-permute-start.23 = (bf16[8,3584]{1,0:T(8,128)(2,1)S(1)}, bf16[8,3584]{1,0:T(8,128)(2,1)S(1)}, u32[]{:S(2)}, u32[]{:S(2)}) collective-permute-start(bf16[8,3584]{1,0:T(8,128)(2,1)S(1)} %get-tuple-element.49), channel_id=1, source_target_pairs={{0,2},{2,0},{4,6},{6,4},{8,10},{10,8},{12,14},{14,12},{1,3},{3,1},... | collective-permute-start | bytes 172040 | tf_op jit(solution)/shard_map/ppermute | solution.py:47
  72.9 1.4 %collective-permute-done.19.rest_2_ = bf16[8,3584]{1,0:T(8,128)(2,1)S(1)} collective-permute-done((bf16[8,3584]{1,0:T(8,128)(2,1)S(1)}, bf16[8,3584]{1,0:T(8,128)(2,1)S(1)}, u32[]{:S(2)}, u32[]{:S(2)}) %collective-permute-start.19) | collective-permute-done | bytes 57376 | tf_op jit(solution)/shard_map/ppermute | solution.py:47
  74.3 1.4 %collective-permute-done.20.rest_3_ = bf16[8,3584]{1,0:T(8,128)(2,1)S(1)} collective-permute-done((bf16[8,3584]{1,0:T(8,128)(2,1)S(1)}, bf16[8,3584]{1,0:T(8,128)(2,1)S(1)}, u32[]{:S(2)}, u32[]{:S(2)}) %collective-permute-start.20) | collective-permute-done | bytes 57376 | tf_op jit(solution)/shard_map/ppermute | solution.py:47
  75.7 0.0 collective-permute-done.21.rest_4_
  75.7 0.9 %collective-permute-done.22.rest_5_ = bf16[8,3584]{1,0:T(8,128)(2,1)S(1)} collective-permute-done((bf16[8,3584]{1,0:T(8,128)(2,1)S(1)}, bf16[8,3584]{1,0:T(8,128)(2,1)S(1)}, u32[]{:S(2)}, u32[]{:S(2)}) %collective-permute-start.22) | collective-permute-done | bytes 57376 | tf_op jit(solution)/shard_map/ppermute | solution.py:47
  76.6 0.3 collective-permute-done.23.rest_6_
  76.9 0.7 finish.1
  (1 shorter events, 0.0 us)
Async XLA Ops:
  6.8 9.8 %collective-permute-start.1 = (bf16[8,9472]{1,0:T(8,128)(2,1)}, bf16[8,9472]{1,0:T(8,128)(2,1)S(1)}, u32[]{:S(2)}, u32[]{:S(2)}) collective-permute-start(bf16[8,9472]{1,0:T(8,128)(2,1)} %get-tuple-element.29), channel_id=1, source_target_pairs={{0,4},{2,6},{4,8},{6,10},{8,12},{10,14},{12,0},{14,2},{1,5},{3,7},... | collective-permute-start | bytes 454664 | tf_op jit(solution)/shard_map/ppermute | solution.py:47
  9.9 6.7 %collective-permute-start = (bf16[8,9472]{1,0:T(8,128)(2,1)}, bf16[8,9472]{1,0:T(8,128)(2,1)S(1)}, u32[]{:S(2)}, u32[]{:S(2)}) collective-permute-start(bf16[8,9472]{1,0:T(8,128)(2,1)} %get-tuple-element.28.refs_0_), channel_id=1, source_target_pairs={{0,2},{2,0},{4,6},{6,4},{8,10},{10,8},{12,14},{14,12},{1,3},{3,1},... | collective-permute-start | bytes 454664 | tf_op jit(solution)/shard_map/ppermute | solution.py:47
  11.4 10.2 %collective-permute-start.5 = (bf16[8,9472]{1,0:T(8,128)(2,1)}, bf16[8,9472]{1,0:T(8,128)(2,1)S(1)}, u32[]{:S(2)}, u32[]{:S(2)}) collective-permute-start(bf16[8,9472]{1,0:T(8,128)(2,1)} %get-tuple-element.32), channel_id=1, source_target_pairs={{0,12},{2,14},{4,0},{6,2},{8,4},{10,6},{12,8},{14,10},{1,13},{3,15... | collective-permute-start | bytes 454664 | tf_op jit(solution)/shard_map/ppermute | solution.py:47
  16.6 9.2 %collective-permute-start.3 = (bf16[8,9472]{1,0:T(8,128)(2,1)}, bf16[8,9472]{1,0:T(8,128)(2,1)S(1)}, u32[]{:S(2)}, u32[]{:S(2)}) collective-permute-start(bf16[8,9472]{1,0:T(8,128)(2,1)} %get-tuple-element.31), channel_id=1, source_target_pairs={{0,8},{2,10},{4,12},{6,14},{8,0},{10,2},{12,4},{14,6},{1,9},{3,11}... | collective-permute-start | bytes 454664 | tf_op jit(solution)/shard_map/ppermute | solution.py:47
  18.1 9.2 %collective-permute-start.2 = (bf16[8,9472]{1,0:T(8,128)(2,1)S(1)}, bf16[8,9472]{1,0:T(8,128)(2,1)S(1)}, u32[]{:S(2)}, u32[]{:S(2)}) collective-permute-start(bf16[8,9472]{1,0:T(8,128)(2,1)S(1)} %collective-permute-done.1.refs_2_), channel_id=1, source_target_pairs={{0,2},{2,0},{4,6},{6,4},{8,10},{10,8},{12,14},{14,12},{1,3},{3,1},... | collective-permute-start | bytes 454664 | tf_op jit(solution)/shard_map/ppermute | solution.py:47
  21.5 5.8 %collective-permute-start.6 = (bf16[8,9472]{1,0:T(8,128)(2,1)S(1)}, bf16[8,9472]{1,0:T(8,128)(2,1)S(1)}, u32[]{:S(2)}, u32[]{:S(2)}) collective-permute-start(bf16[8,9472]{1,0:T(8,128)(2,1)S(1)} %collective-permute-done.5.refs_6_), channel_id=1, source_target_pairs={{0,2},{2,0},{4,6},{6,4},{8,10},{10,8},{12,14},{14,12},{1,3},{3,1},... | collective-permute-start | bytes 454664 | tf_op jit(solution)/shard_map/ppermute | solution.py:47
  25.8 5.6 %collective-permute-start.4 = (bf16[8,9472]{1,0:T(8,128)(2,1)S(1)}, bf16[8,9472]{1,0:T(8,128)(2,1)S(1)}, u32[]{:S(2)}, u32[]{:S(2)}) collective-permute-start(bf16[8,9472]{1,0:T(8,128)(2,1)S(1)} %collective-permute-done.3.refs_4_), channel_id=1, source_target_pairs={{0,2},{2,0},{4,6},{6,4},{8,10},{10,8},{12,14},{14,12},{1,3},{3,1},... | collective-permute-start | bytes 454664 | tf_op jit(solution)/shard_map/ppermute | solution.py:47
  31.4 26.1 %copy-start = (bf16[7168,160]{0,1:T(8,128)(2,1)S(1)}, bf16[7168,160]{0,1:T(8,128)(2,1)}, u32[]{:S(2)}) copy-start(bf16[7168,160]{0,1:T(8,128)(2,1)} %param.21) | copy-start | bytes 6881284
  31.4 26.1 %copy-start.1 = (bf16[7168,160]{0,1:T(8,128)(2,1)S(1)}, bf16[7168,160]{0,1:T(8,128)(2,1)}, u32[]{:S(2)}) copy-start(bf16[7168,160]{0,1:T(8,128)(2,1)} %param.22) | copy-start | bytes 6881284
  31.4 11.9 %collective-permute-start.8 = (bf16[3680,512]{1,0:T(8,128)(2,1)}, bf16[3680,512]{1,0:T(8,128)(2,1)S(1)}, u32[]{:S(2)}, u32[]{:S(2)}) collective-permute-start(bf16[3680,512]{1,0:T(8,128)(2,1)} %get-tuple-element.36), channel_id=1, source_target_pairs={{0,1},{1,0},{2,3},{3,2},{4,5},{5,4},{6,7},{7,6},{8,9},{9,8},{10,11... | collective-permute-start | bytes 11304968 | tf_op jit(solution)/shard_map/ppermute | solution.py:81
  31.4 1.1 %copy-start.3 = (bf16[8,9472]{1,0:T(8,128)(2,1)S(1)}, bf16[8,9472]{1,0:T(8,128)(2,1)}, u32[]{:S(2)}) copy-start(bf16[8,9472]{1,0:T(8,128)(2,1)} %get-tuple-element.28.refs_0_) | copy-start | bytes 454660
  32.5 25.1 %copy-start.4 = (f32[7168]{0:T(1024)S(1)}, f32[7168]{0:T(1024)}, u32[]{:S(2)}) copy-start(f32[7168]{0:T(1024)} %param.18) | copy-start | bytes 86020
  41.9 1.4 %collective-permute-start.7 = (f32[64,512]{1,0:T(8,128)S(1)}, f32[64,512]{1,0:T(8,128)S(1)}, u32[]{:S(2)}, u32[]{:S(2)}) collective-permute-start(f32[64,512]{1,0:T(8,128)S(1)} %get-tuple-element.34), channel_id=1, source_target_pairs={{0,1},{1,0},{2,3},{3,2},{4,5},{5,4},{6,7},{7,6},{8,9},{9,8},{10,11... | collective-permute-start | bytes 393224 | tf_op jit(solution)/shard_map/ppermute | solution.py:81
  43.3 4.3 %collective-permute-start.10 = (bf16[64,512]{1,0:T(8,128)(2,1)S(1)}, bf16[64,512]{1,0:T(8,128)(2,1)S(1)}, u32[]{:S(2)}, u32[]{:S(2)}) collective-permute-start(bf16[64,512]{1,0:T(8,128)(2,1)S(1)} %add_convert_fusion.refs_0_), channel_id=1, source_target_pairs={{0,4},{2,6},{4,0},{6,2},{8,12},{10,14},{12,8},{14,10},{1,5},{3,7},... | collective-permute-start | bytes 196616 | tf_op jit(solution)/shard_map/ppermute | solution.py:47
  44.1 6.5 %collective-permute-start.14 = (bf16[64,512]{1,0:T(8,128)(2,1)S(1)}, bf16[64,512]{1,0:T(8,128)(2,1)S(1)}, u32[]{:S(2)}, u32[]{:S(2)}) collective-permute-start(bf16[64,512]{1,0:T(8,128)(2,1)S(1)} %add_convert_fusion.refs_0_), channel_id=1, source_target_pairs={{0,12},{2,14},{4,8},{6,10},{8,4},{10,6},{12,0},{14,2},{1,13},{3,15... | collective-permute-start | bytes 196616 | tf_op jit(solution)/shard_map/ppermute | solution.py:47
  45.6 7.7 %collective-permute-start.12 = (bf16[64,512]{1,0:T(8,128)(2,1)S(1)}, bf16[64,512]{1,0:T(8,128)(2,1)S(1)}, u32[]{:S(2)}, u32[]{:S(2)}) collective-permute-start(bf16[64,512]{1,0:T(8,128)(2,1)S(1)} %add_convert_fusion.refs_0_), channel_id=1, source_target_pairs={{0,8},{2,10},{4,12},{6,14},{8,0},{10,2},{12,4},{14,6},{1,9},{3,11}... | collective-permute-start | bytes 196616 | tf_op jit(solution)/shard_map/ppermute | solution.py:47
  47.6 5.6 %collective-permute-start.11 = (bf16[64,512]{1,0:T(8,128)(2,1)S(1)}, bf16[64,512]{1,0:T(8,128)(2,1)S(1)}, u32[]{:S(2)}, u32[]{:S(2)}) collective-permute-start(bf16[64,512]{1,0:T(8,128)(2,1)S(1)} %collective-permute-done.10.refs_2_), channel_id=1, source_target_pairs={{0,2},{2,0},{4,6},{6,4},{8,10},{10,8},{12,14},{14,12},{1,3},{3,1},... | collective-permute-start | bytes 196616 | tf_op jit(solution)/shard_map/ppermute | solution.py:47
  48.7 5.7 %collective-permute-start.9 = (bf16[64,512]{1,0:T(8,128)(2,1)S(1)}, bf16[64,512]{1,0:T(8,128)(2,1)S(1)}, u32[]{:S(2)}, u32[]{:S(2)}) collective-permute-start(bf16[64,512]{1,0:T(8,128)(2,1)S(1)} %add_convert_fusion.refs_0_), channel_id=1, source_target_pairs={{0,2},{2,0},{4,6},{6,4},{8,10},{10,8},{12,14},{14,12},{1,3},{3,1},... | collective-permute-start | bytes 196616 | tf_op jit(solution)/shard_map/ppermute | solution.py:47
  50.6 4.3 %collective-permute-start.15 = (bf16[64,512]{1,0:T(8,128)(2,1)S(1)}, bf16[64,512]{1,0:T(8,128)(2,1)S(1)}, u32[]{:S(2)}, u32[]{:S(2)}) collective-permute-start(bf16[64,512]{1,0:T(8,128)(2,1)S(1)} %collective-permute-done.14.refs_6_), channel_id=1, source_target_pairs={{0,2},{2,0},{4,6},{6,4},{8,10},{10,8},{12,14},{14,12},{1,3},{3,1},... | collective-permute-start | bytes 196616 | tf_op jit(solution)/shard_map/ppermute | solution.py:47
  53.2 4.3 %collective-permute-start.13 = (bf16[64,512]{1,0:T(8,128)(2,1)S(1)}, bf16[64,512]{1,0:T(8,128)(2,1)S(1)}, u32[]{:S(2)}, u32[]{:S(2)}) collective-permute-start(bf16[64,512]{1,0:T(8,128)(2,1)S(1)} %collective-permute-done.12.refs_4_), channel_id=1, source_target_pairs={{0,2},{2,0},{4,6},{6,4},{8,10},{10,8},{12,14},{14,12},{1,3},{3,1},... | collective-permute-start | bytes 196616 | tf_op jit(solution)/shard_map/ppermute | solution.py:47
  57.5 3.3 %copy-start.2 = (bf16[160,7168]{1,0:T(8,128)(2,1)S(1)}, bf16[160,7168]{1,0:T(8,128)(2,1)}, u32[]{:S(2)}) copy-start(bf16[160,7168]{1,0:T(8,128)(2,1)} %down_ref.1) | copy-start | bytes 6881284
  59.2 1.6 %collective-permute-start.16 = (f32[88,768]{1,0:T(8,128)S(1)}, f32[88,768]{1,0:T(8,128)S(1)}, u32[]{:S(2)}, u32[]{:S(2)}) collective-permute-start(f32[88,768]{1,0:T(8,128)S(1)} %get-tuple-element.41.sums_ref), channel_id=1, source_target_pairs={{0,1},{1,0},{2,3},{3,2},{4,5},{5,4},{6,7},{7,6},{8,9},{9,8},{10,11... | collective-permute-start | bytes 811016 | tf_op jit(solution)/shard_map/ppermute | solution.py:81
  61.7 7.7 %collective-permute-start.17 = (bf16[8,3584]{1,0:T(8,128)(2,1)S(1)}, bf16[8,3584]{1,0:T(8,128)(2,1)S(1)}, u32[]{:S(2)}, u32[]{:S(2)}) collective-permute-start(bf16[8,3584]{1,0:T(8,128)(2,1)S(1)} %get-tuple-element.43), channel_id=1, source_target_pairs={{0,12},{2,14},{4,8},{6,10},{8,4},{10,6},{12,0},{14,2},{1,13},{3,15... | collective-permute-start | bytes 172040 | tf_op jit(solution)/shard_map/ppermute | solution.py:47
  63.6 8.5 %collective-permute-start.18 = (bf16[8,3584]{1,0:T(8,128)(2,1)S(1)}, bf16[8,3584]{1,0:T(8,128)(2,1)S(1)}, u32[]{:S(2)}, u32[]{:S(2)}) collective-permute-start(bf16[8,3584]{1,0:T(8,128)(2,1)S(1)} %get-tuple-element.44), channel_id=1, source_target_pairs={{0,14},{2,12},{4,10},{6,8},{8,6},{10,4},{12,2},{14,0},{1,15},{3,13... | collective-permute-start | bytes 172040 | tf_op jit(solution)/shard_map/ppermute | solution.py:47
  66.2 8.1 %collective-permute-start.19 = (bf16[8,3584]{1,0:T(8,128)(2,1)S(1)}, bf16[8,3584]{1,0:T(8,128)(2,1)S(1)}, u32[]{:S(2)}, u32[]{:S(2)}) collective-permute-start(bf16[8,3584]{1,0:T(8,128)(2,1)S(1)} %get-tuple-element.45), channel_id=1, source_target_pairs={{0,8},{2,10},{4,12},{6,14},{8,0},{10,2},{12,4},{14,6},{1,9},{3,11}... | collective-permute-start | bytes 172040 | tf_op jit(solution)/shard_map/ppermute | solution.py:47
  66.2 9.5 %collective-permute-start.20 = (bf16[8,3584]{1,0:T(8,128)(2,1)S(1)}, bf16[8,3584]{1,0:T(8,128)(2,1)S(1)}, u32[]{:S(2)}, u32[]{:S(2)}) collective-permute-start(bf16[8,3584]{1,0:T(8,128)(2,1)S(1)} %get-tuple-element.46), channel_id=1, source_target_pairs={{0,10},{2,8},{4,14},{6,12},{8,2},{10,0},{12,6},{14,4},{1,11},{3,9}... | collective-permute-start | bytes 172040 | tf_op jit(solution)/shard_map/ppermute | solution.py:47
  69.4 6.3 %collective-permute-start.21 = (bf16[8,3584]{1,0:T(8,128)(2,1)S(1)}, bf16[8,3584]{1,0:T(8,128)(2,1)S(1)}, u32[]{:S(2)}, u32[]{:S(2)}) collective-permute-start(bf16[8,3584]{1,0:T(8,128)(2,1)S(1)} %get-tuple-element.47), channel_id=1, source_target_pairs={{0,4},{2,6},{4,0},{6,2},{8,12},{10,14},{12,8},{14,10},{1,5},{3,7},... | collective-permute-start | bytes 172040 | tf_op jit(solution)/shard_map/ppermute | solution.py:47
  69.4 7.2 %collective-permute-start.22 = (bf16[8,3584]{1,0:T(8,128)(2,1)S(1)}, bf16[8,3584]{1,0:T(8,128)(2,1)S(1)}, u32[]{:S(2)}, u32[]{:S(2)}) collective-permute-start(bf16[8,3584]{1,0:T(8,128)(2,1)S(1)} %get-tuple-element.48), channel_id=1, source_target_pairs={{0,6},{2,4},{4,2},{6,0},{8,14},{10,12},{12,10},{14,8},{1,7},{3,5},... | collective-permute-start | bytes 172040 | tf_op jit(solution)/shard_map/ppermute | solution.py:47
  72.1 4.8 %collective-permute-start.23 = (bf16[8,3584]{1,0:T(8,128)(2,1)S(1)}, bf16[8,3584]{1,0:T(8,128)(2,1)S(1)}, u32[]{:S(2)}, u32[]{:S(2)}) collective-permute-start(bf16[8,3584]{1,0:T(8,128)(2,1)S(1)} %get-tuple-element.49), channel_id=1, source_target_pairs={{0,2},{2,0},{4,6},{6,4},{8,10},{10,8},{12,14},{14,12},{1,3},{3,1},... | collective-permute-start | bytes 172040 | tf_op jit(solution)/shard_map/ppermute | solution.py:47

commit v10 on v9

--- a/solution.py
+++ b/solution.py
@@ -51,19 +51,20 @@
             got[s, u] = self.send(got[s, 0], 0, u)
 
     def spread(self, own, spaced):
+        early, late = (2, 3) if spaced else (3, 2)
         got = {(0, 0): own[0]}
         got[1, 0] = self.send(own[1], 1, 0)
-        got[3, 0] = self.send(own[3], 3, 0)
+        got[early, 0] = self.send(own[early], early, 0)
         self.along_x(got, 0)
-        far = own[2]
+        leaving = own[late]
         if spaced:
-            far, *_ = lax.optimization_barrier((far, got[1, 0], got[0, self.x - 1]))
-        got[2, 0] = self.send(far, 2, 0)
+            leaving, *_ = lax.optimization_barrier((leaving, got[1, 0], got[0, self.x - 1]))
+        got[late, 0] = self.send(leaving, late, 0)
         self.along_x(got, 1)
-        self.along_x(got, 3)
+        self.along_x(got, early)
         if not spaced:
-            got[2, 0], *_ = lax.optimization_barrier((got[2, 0], got[1, self.x - 1]))
-        self.along_x(got, 2)
+            got[late, 0], *_ = lax.optimization_barrier((got[late, 0], got[1, self.x - 1]))
+        self.along_x(got, late)
         return [got[step] for step in self.steps]
 
     def source(self, step):

time: 77.8 us -> 79.7 us (1.024)
  starting transfers between devices: 32.4 us -> 34.8 us
    ppermute x21, starting transfers between devices: 32.3 us -> 34.7 us  [send(): return lax.ppermute(arr, 'ep', pairs)]
where the time goes in v10:
time: 79.7 us; the launch traced here: 79.5 us
  starting transfers between devices  34.8 us (44%)
  waiting for transfers between devices  24.1 us (30%)
  Pallas kernels  19.4 us (24%)
  local copies, waits for them, and re-layouts  1.08 us (1%)
    ppermute x21, starting transfers between devices, send(): return lax.ppermute(arr, 'ep', pairs)  34.7 us
    ppermute x21, waiting for transfers between devices, send(): return lax.ppermute(arr, 'ep', pairs)  21.2 us
    pallas_call x1, Pallas kernels, project(): pl.pallas_call(kernel, name='project', grid=(blocks,), out_shape=outs, in...  9.38 us
    pallas_call x1, Pallas kernels, attention(): pl.pallas_call(kernel, name='attention', out_shape=[shape_of((rows, width...  6.82 us
    ppermute x3, waiting for transfers between devices, swap(): return lax.ppermute(arr, 'tp', [(0, 1), (1, 0)])  2.87 us
    pallas_call x1, Pallas kernels, gate_up(): pl.pallas_call(kernel, name='gate_up', out_shape=[shape_of((tall + extra...  1.67 us
  transfers between devices with their start and end apart: 24, of which 14 were waited for; matrix products, arithmetic and copies ran while one was open for 0% of the time, Pallas kernels for 12%

profile of v10, /device:TPU:0, one launch (start us, length us, event | category | flops | bytes accessed | tf_op | source)
XLA Modules:
  0.0 79.5 jit_solution(8304248379615265546)
XLA Ops:
  0.0 6.8 %attention.1 = (bf16[8,9472]{1,0:T(8,128)(2,1)}, bf16[8,9472]{1,0:T(8,128)(2,1)}, bf16[8,9472]{1,0:T(8,128)(2,1)}, bf16[8,9472]{1,0:T(8,128)(2,1)}, bf16[3680,512]{1,0:T(8,128)(2,1)}) custom-call(bf16[8,8192]{1,0:T(8,128)(2,1)} %refs_0_.1, bf16[8,512]{1,0:T(8,128)(2,1)} %refs_1_.1, bf16[8,7168]{1,0:T(8,128)(2,1)} %refs_2_.1, s32[3,8]{1,0:T(4,128)} %bitcast.10, ...), custom_call_target="tpu_custom_call" | custom-call | tf_op jit(solution)/shard_map/attention/pallas_call | solution.py:220
  6.8 3.1 %collective-permute-start.1 = (bf16[8,9472]{1,0:T(8,128)(2,1)}, bf16[8,9472]{1,0:T(8,128)(2,1)S(1)}, u32[]{:S(2)}, u32[]{:S(2)}) collective-permute-start(bf16[8,9472]{1,0:T(8,128)(2,1)} %get-tuple-element.29), channel_id=1, source_target_pairs={{0,4},{2,6},{4,8},{6,10},{8,12},{10,14},{12,0},{14,2},{1,5},{3,7},... | collective-permute-start | bytes 454664 | tf_op jit(solution)/shard_map/ppermute | solution.py:47
  9.9 1.5 %collective-permute-start = (bf16[8,9472]{1,0:T(8,128)(2,1)}, bf16[8,9472]{1,0:T(8,128)(2,1)S(1)}, u32[]{:S(2)}, u32[]{:S(2)}) collective-permute-start(bf16[8,9472]{1,0:T(8,128)(2,1)} %get-tuple-element.28.refs_0_), channel_id=1, source_target_pairs={{0,2},{2,0},{4,6},{6,4},{8,10},{10,8},{12,14},{14,12},{1,3},{3,1},... | collective-permute-start | bytes 454664 | tf_op jit(solution)/shard_map/ppermute | solution.py:47
  11.4 2.6 %collective-permute-start.3 = (bf16[8,9472]{1,0:T(8,128)(2,1)}, bf16[8,9472]{1,0:T(8,128)(2,1)S(1)}, u32[]{:S(2)}, u32[]{:S(2)}) collective-permute-start(bf16[8,9472]{1,0:T(8,128)(2,1)} %get-tuple-element.30), channel_id=1, source_target_pairs={{0,8},{2,10},{4,12},{6,14},{8,0},{10,2},{12,4},{14,6},{1,9},{3,11}... | collective-permute-start | bytes 454664 | tf_op jit(solution)/shard_map/ppermute | solution.py:47
  14.0 2.8 %collective-permute-done.1.refs_2_ = bf16[8,9472]{1,0:T(8,128)(2,1)S(1)} collective-permute-done((bf16[8,9472]{1,0:T(8,128)(2,1)}, bf16[8,9472]{1,0:T(8,128)(2,1)S(1)}, u32[]{:S(2)}, u32[]{:S(2)}) %collective-permute-start.1) | collective-permute-done | bytes 151584 | tf_op jit(solution)/shard_map/ppermute | solution.py:47
  16.8 0.0 collective-permute-done.refs_1_
  16.8 1.6 %collective-permute-start.5 = (bf16[8,9472]{1,0:T(8,128)(2,1)}, bf16[8,9472]{1,0:T(8,128)(2,1)S(1)}, u32[]{:S(2)}, u32[]{:S(2)}) collective-permute-start(bf16[8,9472]{1,0:T(8,128)(2,1)} %get-tuple-element.32), channel_id=1, source_target_pairs={{0,12},{2,14},{4,0},{6,2},{8,4},{10,6},{12,8},{14,10},{1,13},{3,15... | collective-permute-start | bytes 454664 | tf_op jit(solution)/shard_map/ppermute | solution.py:47
  18.4 1.5 %collective-permute-start.2 = (bf16[8,9472]{1,0:T(8,128)(2,1)S(1)}, bf16[8,9472]{1,0:T(8,128)(2,1)S(1)}, u32[]{:S(2)}, u32[]{:S(2)}) collective-permute-start(bf16[8,9472]{1,0:T(8,128)(2,1)S(1)} %collective-permute-done.1.refs_2_), channel_id=1, source_target_pairs={{0,2},{2,0},{4,6},{6,4},{8,10},{10,8},{12,14},{14,12},{1,3},{3,1},... | collective-permute-start | bytes 454664 | tf_op jit(solution)/shard_map/ppermute | solution.py:47
  19.9 2.8 %collective-permute-done.3.refs_4_ = bf16[8,9472]{1,0:T(8,128)(2,1)S(1)} collective-permute-done((bf16[8,9472]{1,0:T(8,128)(2,1)}, bf16[8,9472]{1,0:T(8,128)(2,1)S(1)}, u32[]{:S(2)}, u32[]{:S(2)}) %collective-permute-start.3) | collective-permute-done | bytes 151584 | tf_op jit(solution)/shard_map/ppermute | solution.py:47
  22.7 1.5 %collective-permute-start.4 = (bf16[8,9472]{1,0:T(8,128)(2,1)S(1)}, bf16[8,9472]{1,0:T(8,128)(2,1)S(1)}, u32[]{:S(2)}, u32[]{:S(2)}) collective-permute-start(bf16[8,9472]{1,0:T(8,128)(2,1)S(1)} %collective-permute-done.3.refs_4_), channel_id=1, source_target_pairs={{0,2},{2,0},{4,6},{6,4},{8,10},{10,8},{12,14},{14,12},{1,3},{3,1},... | collective-permute-start | bytes 454664 | tf_op jit(solution)/shard_map/ppermute | solution.py:47
  24.2 0.4 collective-permute-done.5.refs_6_
  24.6 1.3 %collective-permute-start.6 = (bf16[8,9472]{1,0:T(8,128)(2,1)S(1)}, bf16[8,9472]{1,0:T(8,128)(2,1)S(1)}, u32[]{:S(2)}, u32[]{:S(2)}) collective-permute-start(bf16[8,9472]{1,0:T(8,128)(2,1)S(1)} %collective-permute-done.5.refs_6_), channel_id=1, source_target_pairs={{0,2},{2,0},{4,6},{6,4},{8,10},{10,8},{12,14},{14,12},{1,3},{3,1},... | collective-permute-start | bytes 454664 | tf_op jit(solution)/shard_map/ppermute | solution.py:47
  25.8 0.0 collective-permute-done.2.refs_3_
  25.8 3.7 %collective-permute-done.4.refs_5_ = bf16[8,9472]{1,0:T(8,128)(2,1)S(1)} collective-permute-done((bf16[8,9472]{1,0:T(8,128)(2,1)S(1)}, bf16[8,9472]{1,0:T(8,128)(2,1)S(1)}, u32[]{:S(2)}, u32[]{:S(2)}) %collective-permute-start.4) | collective-permute-done | bytes 151584 | tf_op jit(solution)/shard_map/ppermute | solution.py:47
  29.5 2.2 %collective-permute-done.6.refs_7_ = bf16[8,9472]{1,0:T(8,128)(2,1)S(1)} collective-permute-done((bf16[8,9472]{1,0:T(8,128)(2,1)S(1)}, bf16[8,9472]{1,0:T(8,128)(2,1)S(1)}, u32[]{:S(2)}, u32[]{:S(2)}) %collective-permute-start.6) | collective-permute-done | bytes 151584 | tf_op jit(solution)/shard_map/ppermute | solution.py:47
  31.7 0.0 copy-start
  31.7 0.0 copy-start.1
  31.7 0.0 collective-permute-start.8
  31.7 0.0 copy-start.3
  31.7 1.1 %copy-done.3 = bf16[8,9472]{1,0:T(8,128)(2,1)S(1)} copy-done((bf16[8,9472]{1,0:T(8,128)(2,1)S(1)}, bf16[8,9472]{1,0:T(8,128)(2,1)}, u32[]{:S(2)}) %copy-start.3) | copy-done | bytes 151576
  32.8 0.0 copy-start.4
  32.8 9.4 %project.1 = (f32[64,512]{1,0:T(8,128)S(1)}, f32[64,512]{1,0:T(8,128)S(1)}, f32[64,128]{1,0:T(8,128)S(1)}) custom-call(bf16[8,9472]{1,0:T(8,128)(2,1)S(1)} %copy-done.3, bf16[8,9472]{1,0:T(8,128)(2,1)S(1)} %collective-permute-done.refs_1_, bf16[8,9472]{1,0:T(8,128)(2,1)S(1)} %collective-permute-done.1.refs_2_, ...), custom_call_target="tpu_custom_call" | custom-call | flops 939524096 | bytes 15990784 | tf_op jit(solution)/shard_map/project/pallas_call | solution.py:306
  42.2 0.1 collective-permute-start.7
  42.3 1.3 %collective-permute-done.7 = f32[64,512]{1,0:T(8,128)S(1)} collective-permute-done((f32[64,512]{1,0:T(8,128)S(1)}, f32[64,512]{1,0:T(8,128)S(1)}, u32[]{:S(2)}, u32[]{:S(2)}) %collective-permute-start.7) | collective-permute-done | bytes 131104 | tf_op jit(solution)/shard_map/ppermute | solution.py:82
  43.6 0.0 collective-permute-done.8.refs_11_.packed_ref
  43.6 1.4 %collective-permute-start.10 = (bf16[64,512]{1,0:T(8,128)(2,1)S(1)}, bf16[64,512]{1,0:T(8,128)(2,1)S(1)}, u32[]{:S(2)}, u32[]{:S(2)}) collective-permute-start(bf16[64,512]{1,0:T(8,128)(2,1)S(1)} %add_convert_fusion.refs_0_), channel_id=1, source_target_pairs={{0,4},{2,6},{4,0},{6,2},{8,12},{10,14},{12,8},{14,10},{1,5},{3,7},... | collective-permute-start | bytes 196616 | tf_op jit(solution)/shard_map/ppermute | solution.py:47
  45.0 2.8 %collective-permute-start.14 = (bf16[64,512]{1,0:T(8,128)(2,1)S(1)}, bf16[64,512]{1,0:T(8,128)(2,1)S(1)}, u32[]{:S(2)}, u32[]{:S(2)}) collective-permute-start(bf16[64,512]{1,0:T(8,128)(2,1)S(1)} %add_convert_fusion.refs_0_), channel_id=1, source_target_pairs={{0,12},{2,14},{4,8},{6,10},{8,4},{10,6},{12,0},{14,2},{1,13},{3,15... | collective-permute-start | bytes 196616 | tf_op jit(solution)/shard_map/ppermute | solution.py:47
  47.8 0.5 collective-permute-start.12
  48.3 0.0 collective-permute-done.10.refs_2_
  48.3 1.7 %collective-permute-start.11 = (bf16[64,512]{1,0:T(8,128)(2,1)S(1)}, bf16[64,512]{1,0:T(8,128)(2,1)S(1)}, u32[]{:S(2)}, u32[]{:S(2)}) collective-permute-start(bf16[64,512]{1,0:T(8,128)(2,1)S(1)} %collective-permute-done.10.refs_2_), channel_id=1, source_target_pairs={{0,2},{2,0},{4,6},{6,4},{8,10},{10,8},{12,14},{14,12},{1,3},{3,1},... | collective-permute-start | bytes 196616 | tf_op jit(solution)/shard_map/ppermute | solution.py:47
  50.0 0.3 collective-permute-start.9
  50.3 1.4 %collective-permute-done.14.refs_6_ = bf16[64,512]{1,0:T(8,128)(2,1)S(1)} collective-permute-done((bf16[64,512]{1,0:T(8,128)(2,1)S(1)}, bf16[64,512]{1,0:T(8,128)(2,1)S(1)}, u32[]{:S(2)}, u32[]{:S(2)}) %collective-permute-start.14) | collective-permute-done | bytes 65568 | tf_op jit(solution)/shard_map/ppermute | solution.py:47
  51.7 1.7 %collective-permute-start.15 = (bf16[64,512]{1,0:T(8,128)(2,1)S(1)}, bf16[64,512]{1,0:T(8,128)(2,1)S(1)}, u32[]{:S(2)}, u32[]{:S(2)}) collective-permute-start(bf16[64,512]{1,0:T(8,128)(2,1)S(1)} %collective-permute-done.14.refs_6_), channel_id=1, source_target_pairs={{0,2},{2,0},{4,6},{6,4},{8,10},{10,8},{12,14},{14,12},{1,3},{3,1},... | collective-permute-start | bytes 196616 | tf_op jit(solution)/shard_map/ppermute | solution.py:47
  53.4 1.2 %collective-permute-done.12.refs_4_ = bf16[64,512]{1,0:T(8,128)(2,1)S(1)} collective-permute-done((bf16[64,512]{1,0:T(8,128)(2,1)S(1)}, bf16[64,512]{1,0:T(8,128)(2,1)S(1)}, u32[]{:S(2)}, u32[]{:S(2)}) %collective-permute-start.12) | collective-permute-done | bytes 65568 | tf_op jit(solution)/shard_map/ppermute | solution.py:47
  54.7 0.0 collective-permute-done.11.refs_3_
  54.7 1.7 %collective-permute-start.13 = (bf16[64,512]{1,0:T(8,128)(2,1)S(1)}, bf16[64,512]{1,0:T(8,128)(2,1)S(1)}, u32[]{:S(2)}, u32[]{:S(2)}) collective-permute-start(bf16[64,512]{1,0:T(8,128)(2,1)S(1)} %collective-permute-done.12.refs_4_), channel_id=1, source_target_pairs={{0,2},{2,0},{4,6},{6,4},{8,10},{10,8},{12,14},{14,12},{1,3},{3,1},... | collective-permute-start | bytes 196616 | tf_op jit(solution)/shard_map/ppermute | solution.py:47
  56.4 0.0 collective-permute-done.9.refs_1_
  56.4 0.0 collective-permute-done.15.refs_7_
  56.4 2.5 %collective-permute-done.13.refs_5_ = bf16[64,512]{1,0:T(8,128)(2,1)S(1)} collective-permute-done((bf16[64,512]{1,0:T(8,128)(2,1)S(1)}, bf16[64,512]{1,0:T(8,128)(2,1)S(1)}, u32[]{:S(2)}, u32[]{:S(2)}) %collective-permute-start.13) | collective-permute-done | bytes 65568 | tf_op jit(solution)/shard_map/ppermute | solution.py:47
  58.9 0.0 copy-done
  58.9 0.0 copy-done.1
  58.9 0.0 copy-done.4
  58.9 0.0 copy-start.2
  58.9 1.7 %gate_up.1 = (f32[88,768]{1,0:T(8,128)S(1)}, f32[8,2048]{1,0:T(8,128)S(1)}) custom-call(bf16[64,512]{1,0:T(8,128)(2,1)S(1)} %add_convert_fusion.refs_0_, bf16[64,512]{1,0:T(8,128)(2,1)S(1)} %collective-permute-done.9.refs_1_, bf16[64,512]{1,0:T(8,128)(2,1)S(1)} %collective-permute-done.10.refs_2_, bf16[64,512]{1,0:T(8,128)(2,1)S(1)} %collective-permute-done.11.refs_3_, ...), custom_call_target="tpu_custom_call" | custom-call | tf_op jit(solution)/shard_map/gate_up/pallas_call | solution.py:369
  60.6 0.1 collective-permute-start.16
  60.7 1.5 %collective-permute-done.16.far_ref = f32[88,768]{1,0:T(8,128)S(1)} collective-permute-done((f32[88,768]{1,0:T(8,128)S(1)}, f32[88,768]{1,0:T(8,128)S(1)}, u32[]{:S(2)}, u32[]{:S(2)}) %collective-permute-start.16) | collective-permute-done | bytes 270368 | tf_op jit(solution)/shard_map/ppermute | solution.py:82
  62.2 0.0 copy-done.2
  62.2 0.9 %down.1 = (f32[8,3584]{1,0:T(8,128)S(1)}, bf16[8,3584]{1,0:T(8,128)(2,1)S(1)}, bf16[8,3584]{1,0:T(8,128)(2,1)S(1)}, bf16[8,3584]{1,0:T(8,128)(2,1)S(1)}, bf16[8,...) custom-call(f32[88,768]{1,0:T(8,128)S(1)} %get-tuple-element.41.sums, ...), custom_call_target="tpu_custom_call" | custom-call | tf_op jit(solution)/shard_map/down/pallas_call | solution.py:422
  63.1 2.7 %collective-permute-start.17 = (bf16[8,3584]{1,0:T(8,128)(2,1)S(1)}, bf16[8,3584]{1,0:T(8,128)(2,1)S(1)}, u32[]{:S(2)}, u32[]{:S(2)}) collective-permute-start(bf16[8,3584]{1,0:T(8,128)(2,1)S(1)} %get-tuple-element.43), channel_id=1, source_target_pairs={{0,12},{2,14},{4,8},{6,10},{8,4},{10,6},{12,0},{14,2},{1,13},{3,15... | collective-permute-start | bytes 172040 | tf_op jit(solution)/shard_map/ppermute | solution.py:47
  65.8 2.4 %collective-permute-start.18 = (bf16[8,3584]{1,0:T(8,128)(2,1)S(1)}, bf16[8,3584]{1,0:T(8,128)(2,1)S(1)}, u32[]{:S(2)}, u32[]{:S(2)}) collective-permute-start(bf16[8,3584]{1,0:T(8,128)(2,1)S(1)} %get-tuple-element.44), channel_id=1, source_target_pairs={{0,14},{2,12},{4,10},{6,8},{8,6},{10,4},{12,2},{14,0},{1,15},{3,13... | collective-permute-start | bytes 172040 | tf_op jit(solution)/shard_map/ppermute | solution.py:47
  68.1 0.0 collective-permute-start.19
  68.1 2.7 %collective-permute-start.20 = (bf16[8,3584]{1,0:T(8,128)(2,1)S(1)}, bf16[8,3584]{1,0:T(8,128)(2,1)S(1)}, u32[]{:S(2)}, u32[]{:S(2)}) collective-permute-start(bf16[8,3584]{1,0:T(8,128)(2,1)S(1)} %get-tuple-element.46), channel_id=1, source_target_pairs={{0,10},{2,8},{4,14},{6,12},{8,2},{10,0},{12,6},{14,4},{1,11},{3,9}... | collective-permute-start | bytes 172040 | tf_op jit(solution)/shard_map/ppermute | solution.py:47
  70.8 0.5 collective-permute-start.21
  71.3 0.0 collective-permute-done.17.rest_0_
  71.3 2.7 %collective-permute-start.22 = (bf16[8,3584]{1,0:T(8,128)(2,1)S(1)}, bf16[8,3584]{1,0:T(8,128)(2,1)S(1)}, u32[]{:S(2)}, u32[]{:S(2)}) collective-permute-start(bf16[8,3584]{1,0:T(8,128)(2,1)S(1)} %get-tuple-element.48), channel_id=1, source_target_pairs={{0,6},{2,4},{4,2},{6,0},{8,14},{10,12},{12,10},{14,8},{1,7},{3,5},... | collective-permute-start | bytes 172040 | tf_op jit(solution)/shard_map/ppermute | solution.py:47
  74.0 0.0 collective-permute-done.18.rest_1_
  74.0 0.7 collective-permute-start.23
  74.7 1.6 %collective-permute-done.19.rest_2_ = bf16[8,3584]{1,0:T(8,128)(2,1)S(1)} collective-permute-done((bf16[8,3584]{1,0:T(8,128)(2,1)S(1)}, bf16[8,3584]{1,0:T(8,128)(2,1)S(1)}, u32[]{:S(2)}, u32[]{:S(2)}) %collective-permute-start.19) | collective-permute-done | bytes 57376 | tf_op jit(solution)/shard_map/ppermute | solution.py:47
  76.3 1.3 %collective-permute-done.20.rest_3_ = bf16[8,3584]{1,0:T(8,128)(2,1)S(1)} collective-permute-done((bf16[8,3584]{1,0:T(8,128)(2,1)S(1)}, bf16[8,3584]{1,0:T(8,128)(2,1)S(1)}, u32[]{:S(2)}, u32[]{:S(2)}) %collective-permute-start.20) | collective-permute-done | bytes 57376 | tf_op jit(solution)/shard_map/ppermute | solution.py:47
  77.6 0.0 collective-permute-done.21.rest_4_
  77.6 0.9 %collective-permute-done.22.rest_5_ = bf16[8,3584]{1,0:T(8,128)(2,1)S(1)} collective-permute-done((bf16[8,3584]{1,0:T(8,128)(2,1)S(1)}, bf16[8,3584]{1,0:T(8,128)(2,1)S(1)}, u32[]{:S(2)}, u32[]{:S(2)}) %collective-permute-start.22) | collective-permute-done | bytes 57376 | tf_op jit(solution)/shard_map/ppermute | solution.py:47
  78.5 0.3 collective-permute-done.23.rest_6_
  78.8 0.7 finish.1
  (1 shorter events, 0.0 us)
Async XLA Ops:
  6.8 10.0 %collective-permute-start.1 = (bf16[8,9472]{1,0:T(8,128)(2,1)}, bf16[8,9472]{1,0:T(8,128)(2,1)S(1)}, u32[]{:S(2)}, u32[]{:S(2)}) collective-permute-start(bf16[8,9472]{1,0:T(8,128)(2,1)} %get-tuple-element.29), channel_id=1, source_target_pairs={{0,4},{2,6},{4,8},{6,10},{8,12},{10,14},{12,0},{14,2},{1,5},{3,7},... | collective-permute-start | bytes 454664 | tf_op jit(solution)/shard_map/ppermute | solution.py:47
  9.9 6.9 %collective-permute-start = (bf16[8,9472]{1,0:T(8,128)(2,1)}, bf16[8,9472]{1,0:T(8,128)(2,1)S(1)}, u32[]{:S(2)}, u32[]{:S(2)}) collective-permute-start(bf16[8,9472]{1,0:T(8,128)(2,1)} %get-tuple-element.28.refs_0_), channel_id=1, source_target_pairs={{0,2},{2,0},{4,6},{6,4},{8,10},{10,8},{12,14},{14,12},{1,3},{3,1},... | collective-permute-start | bytes 454664 | tf_op jit(solution)/shard_map/ppermute | solution.py:47
  11.4 11.3 %collective-permute-start.3 = (bf16[8,9472]{1,0:T(8,128)(2,1)}, bf16[8,9472]{1,0:T(8,128)(2,1)S(1)}, u32[]{:S(2)}, u32[]{:S(2)}) collective-permute-start(bf16[8,9472]{1,0:T(8,128)(2,1)} %get-tuple-element.30), channel_id=1, source_target_pairs={{0,8},{2,10},{4,12},{6,14},{8,0},{10,2},{12,4},{14,6},{1,9},{3,11}... | collective-permute-start | bytes 454664 | tf_op jit(solution)/shard_map/ppermute | solution.py:47
  16.8 7.8 %collective-permute-start.5 = (bf16[8,9472]{1,0:T(8,128)(2,1)}, bf16[8,9472]{1,0:T(8,128)(2,1)S(1)}, u32[]{:S(2)}, u32[]{:S(2)}) collective-permute-start(bf16[8,9472]{1,0:T(8,128)(2,1)} %get-tuple-element.32), channel_id=1, source_target_pairs={{0,12},{2,14},{4,0},{6,2},{8,4},{10,6},{12,8},{14,10},{1,13},{3,15... | collective-permute-start | bytes 454664 | tf_op jit(solution)/shard_map/ppermute | solution.py:47
  18.4 7.4 %collective-permute-start.2 = (bf16[8,9472]{1,0:T(8,128)(2,1)S(1)}, bf16[8,9472]{1,0:T(8,128)(2,1)S(1)}, u32[]{:S(2)}, u32[]{:S(2)}) collective-permute-start(bf16[8,9472]{1,0:T(8,128)(2,1)S(1)} %collective-permute-done.1.refs_2_), channel_id=1, source_target_pairs={{0,2},{2,0},{4,6},{6,4},{8,10},{10,8},{12,14},{14,12},{1,3},{3,1},... | collective-permute-start | bytes 454664 | tf_op jit(solution)/shard_map/ppermute | solution.py:47
  22.7 6.8 %collective-permute-start.4 = (bf16[8,9472]{1,0:T(8,128)(2,1)S(1)}, bf16[8,9472]{1,0:T(8,128)(2,1)S(1)}, u32[]{:S(2)}, u32[]{:S(2)}) collective-permute-start(bf16[8,9472]{1,0:T(8,128)(2,1)S(1)} %collective-permute-done.3.refs_4_), channel_id=1, source_target_pairs={{0,2},{2,0},{4,6},{6,4},{8,10},{10,8},{12,14},{14,12},{1,3},{3,1},... | collective-permute-start | bytes 454664 | tf_op jit(solution)/shard_map/ppermute | solution.py:47
  24.6 7.2 %collective-permute-start.6 = (bf16[8,9472]{1,0:T(8,128)(2,1)S(1)}, bf16[8,9472]{1,0:T(8,128)(2,1)S(1)}, u32[]{:S(2)}, u32[]{:S(2)}) collective-permute-start(bf16[8,9472]{1,0:T(8,128)(2,1)S(1)} %collective-permute-done.5.refs_6_), channel_id=1, source_target_pairs={{0,2},{2,0},{4,6},{6,4},{8,10},{10,8},{12,14},{14,12},{1,3},{3,1},... | collective-permute-start | bytes 454664 | tf_op jit(solution)/shard_map/ppermute | solution.py:47
  31.7 27.2 %copy-start = (bf16[7168,160]{0,1:T(8,128)(2,1)S(1)}, bf16[7168,160]{0,1:T(8,128)(2,1)}, u32[]{:S(2)}) copy-start(bf16[7168,160]{0,1:T(8,128)(2,1)} %param.21) | copy-start | bytes 6881284
  31.7 27.2 %copy-start.1 = (bf16[7168,160]{0,1:T(8,128)(2,1)S(1)}, bf16[7168,160]{0,1:T(8,128)(2,1)}, u32[]{:S(2)}) copy-start(bf16[7168,160]{0,1:T(8,128)(2,1)} %param.22) | copy-start | bytes 6881284
  31.7 11.9 %collective-permute-start.8 = (bf16[3680,512]{1,0:T(8,128)(2,1)}, bf16[3680,512]{1,0:T(8,128)(2,1)S(1)}, u32[]{:S(2)}, u32[]{:S(2)}) collective-permute-start(bf16[3680,512]{1,0:T(8,128)(2,1)} %get-tuple-element.36), channel_id=1, source_target_pairs={{0,1},{1,0},{2,3},{3,2},{4,5},{5,4},{6,7},{7,6},{8,9},{9,8},{10,11... | collective-permute-start | bytes 11304968 | tf_op jit(solution)/shard_map/ppermute | solution.py:82
  31.7 1.1 %copy-start.3 = (bf16[8,9472]{1,0:T(8,128)(2,1)S(1)}, bf16[8,9472]{1,0:T(8,128)(2,1)}, u32[]{:S(2)}) copy-start(bf16[8,9472]{1,0:T(8,128)(2,1)} %get-tuple-element.28.refs_0_) | copy-start | bytes 454660
  32.8 26.1 %copy-start.4 = (f32[7168]{0:T(1024)S(1)}, f32[7168]{0:T(1024)}, u32[]{:S(2)}) copy-start(f32[7168]{0:T(1024)} %param.18) | copy-start | bytes 86020
  42.2 1.4 %collective-permute-start.7 = (f32[64,512]{1,0:T(8,128)S(1)}, f32[64,512]{1,0:T(8,128)S(1)}, u32[]{:S(2)}, u32[]{:S(2)}) collective-permute-start(f32[64,512]{1,0:T(8,128)S(1)} %get-tuple-element.34), channel_id=1, source_target_pairs={{0,1},{1,0},{2,3},{3,2},{4,5},{5,4},{6,7},{7,6},{8,9},{9,8},{10,11... | collective-permute-start | bytes 393224 | tf_op jit(solution)/shard_map/ppermute | solution.py:82
  43.6 4.7 %collective-permute-start.10 = (bf16[64,512]{1,0:T(8,128)(2,1)S(1)}, bf16[64,512]{1,0:T(8,128)(2,1)S(1)}, u32[]{:S(2)}, u32[]{:S(2)}) collective-permute-start(bf16[64,512]{1,0:T(8,128)(2,1)S(1)} %add_convert_fusion.refs_0_), channel_id=1, source_target_pairs={{0,4},{2,6},{4,0},{6,2},{8,12},{10,14},{12,8},{14,10},{1,5},{3,7},... | collective-permute-start | bytes 196616 | tf_op jit(solution)/shard_map/ppermute | solution.py:47
  45.0 6.7 %collective-permute-start.14 = (bf16[64,512]{1,0:T(8,128)(2,1)S(1)}, bf16[64,512]{1,0:T(8,128)(2,1)S(1)}, u32[]{:S(2)}, u32[]{:S(2)}) collective-permute-start(bf16[64,512]{1,0:T(8,128)(2,1)S(1)} %add_convert_fusion.refs_0_), channel_id=1, source_target_pairs={{0,12},{2,14},{4,8},{6,10},{8,4},{10,6},{12,0},{14,2},{1,13},{3,15... | collective-permute-start | bytes 196616 | tf_op jit(solution)/shard_map/ppermute | solution.py:47
  47.8 6.9 %collective-permute-start.12 = (bf16[64,512]{1,0:T(8,128)(2,1)S(1)}, bf16[64,512]{1,0:T(8,128)(2,1)S(1)}, u32[]{:S(2)}, u32[]{:S(2)}) collective-permute-start(bf16[64,512]{1,0:T(8,128)(2,1)S(1)} %add_convert_fusion.refs_0_), channel_id=1, source_target_pairs={{0,8},{2,10},{4,12},{6,14},{8,0},{10,2},{12,4},{14,6},{1,9},{3,11}... | collective-permute-start | bytes 196616 | tf_op jit(solution)/shard_map/ppermute | solution.py:47
  48.3 6.4 %collective-permute-start.11 = (bf16[64,512]{1,0:T(8,128)(2,1)S(1)}, bf16[64,512]{1,0:T(8,128)(2,1)S(1)}, u32[]{:S(2)}, u32[]{:S(2)}) collective-permute-start(bf16[64,512]{1,0:T(8,128)(2,1)S(1)} %collective-permute-done.10.refs_2_), channel_id=1, source_target_pairs={{0,2},{2,0},{4,6},{6,4},{8,10},{10,8},{12,14},{14,12},{1,3},{3,1},... | collective-permute-start | bytes 196616 | tf_op jit(solution)/shard_map/ppermute | solution.py:47
  50.0 6.4 %collective-permute-start.9 = (bf16[64,512]{1,0:T(8,128)(2,1)S(1)}, bf16[64,512]{1,0:T(8,128)(2,1)S(1)}, u32[]{:S(2)}, u32[]{:S(2)}) collective-permute-start(bf16[64,512]{1,0:T(8,128)(2,1)S(1)} %add_convert_fusion.refs_0_), channel_id=1, source_target_pairs={{0,2},{2,0},{4,6},{6,4},{8,10},{10,8},{12,14},{14,12},{1,3},{3,1},... | collective-permute-start | bytes 196616 | tf_op jit(solution)/shard_map/ppermute | solution.py:47
  51.7 4.7 %collective-permute-start.15 = (bf16[64,512]{1,0:T(8,128)(2,1)S(1)}, bf16[64,512]{1,0:T(8,128)(2,1)S(1)}, u32[]{:S(2)}, u32[]{:S(2)}) collective-permute-start(bf16[64,512]{1,0:T(8,128)(2,1)S(1)} %collective-permute-done.14.refs_6_), channel_id=1, source_target_pairs={{0,2},{2,0},{4,6},{6,4},{8,10},{10,8},{12,14},{14,12},{1,3},{3,1},... | collective-permute-start | bytes 196616 | tf_op jit(solution)/shard_map/ppermute | solution.py:47
  54.7 4.3 %collective-permute-start.13 = (bf16[64,512]{1,0:T(8,128)(2,1)S(1)}, bf16[64,512]{1,0:T(8,128)(2,1)S(1)}, u32[]{:S(2)}, u32[]{:S(2)}) collective-permute-start(bf16[64,512]{1,0:T(8,128)(2,1)S(1)} %collective-permute-done.12.refs_4_), channel_id=1, source_target_pairs={{0,2},{2,0},{4,6},{6,4},{8,10},{10,8},{12,14},{14,12},{1,3},{3,1},... | collective-permute-start | bytes 196616 | tf_op jit(solution)/shard_map/ppermute | solution.py:47
  58.9 3.3 %copy-start.2 = (bf16[160,7168]{1,0:T(8,128)(2,1)S(1)}, bf16[160,7168]{1,0:T(8,128)(2,1)}, u32[]{:S(2)}) copy-start(bf16[160,7168]{1,0:T(8,128)(2,1)} %down_ref.1) | copy-start | bytes 6881284
  60.6 1.6 %collective-permute-start.16 = (f32[88,768]{1,0:T(8,128)S(1)}, f32[88,768]{1,0:T(8,128)S(1)}, u32[]{:S(2)}, u32[]{:S(2)}) collective-permute-start(f32[88,768]{1,0:T(8,128)S(1)} %get-tuple-element.41.sums_ref), channel_id=1, source_target_pairs={{0,1},{1,0},{2,3},{3,2},{4,5},{5,4},{6,7},{7,6},{8,9},{9,8},{10,11... | collective-permute-start | bytes 811016 | tf_op jit(solution)/shard_map/ppermute | solution.py:82
  63.1 8.2 %collective-permute-start.17 = (bf16[8,3584]{1,0:T(8,128)(2,1)S(1)}, bf16[8,3584]{1,0:T(8,128)(2,1)S(1)}, u32[]{:S(2)}, u32[]{:S(2)}) collective-permute-start(bf16[8,3584]{1,0:T(8,128)(2,1)S(1)} %get-tuple-element.43), channel_id=1, source_target_pairs={{0,12},{2,14},{4,8},{6,10},{8,4},{10,6},{12,0},{14,2},{1,13},{3,15... | collective-permute-start | bytes 172040 | tf_op jit(solution)/shard_map/ppermute | solution.py:47
  65.8 8.2 %collective-permute-start.18 = (bf16[8,3584]{1,0:T(8,128)(2,1)S(1)}, bf16[8,3584]{1,0:T(8,128)(2,1)S(1)}, u32[]{:S(2)}, u32[]{:S(2)}) collective-permute-start(bf16[8,3584]{1,0:T(8,128)(2,1)S(1)} %get-tuple-element.44), channel_id=1, source_target_pairs={{0,14},{2,12},{4,10},{6,8},{8,6},{10,4},{12,2},{14,0},{1,15},{3,13... | collective-permute-start | bytes 172040 | tf_op jit(solution)/shard_map/ppermute | solution.py:47
  68.1 8.1 %collective-permute-start.19 = (bf16[8,3584]{1,0:T(8,128)(2,1)S(1)}, bf16[8,3584]{1,0:T(8,128)(2,1)S(1)}, u32[]{:S(2)}, u32[]{:S(2)}) collective-permute-start(bf16[8,3584]{1,0:T(8,128)(2,1)S(1)} %get-tuple-element.45), channel_id=1, source_target_pairs={{0,8},{2,10},{4,12},{6,14},{8,0},{10,2},{12,4},{14,6},{1,9},{3,11}... | collective-permute-start | bytes 172040 | tf_op jit(solution)/shard_map/ppermute | solution.py:47
  68.1 9.5 %collective-permute-start.20 = (bf16[8,3584]{1,0:T(8,128)(2,1)S(1)}, bf16[8,3584]{1,0:T(8,128)(2,1)S(1)}, u32[]{:S(2)}, u32[]{:S(2)}) collective-permute-start(bf16[8,3584]{1,0:T(8,128)(2,1)S(1)} %get-tuple-element.46), channel_id=1, source_target_pairs={{0,10},{2,8},{4,14},{6,12},{8,2},{10,0},{12,6},{14,4},{1,11},{3,9}... | collective-permute-start | bytes 172040 | tf_op jit(solution)/shard_map/ppermute | solution.py:47
  70.8 6.8 %collective-permute-start.21 = (bf16[8,3584]{1,0:T(8,128)(2,1)S(1)}, bf16[8,3584]{1,0:T(8,128)(2,1)S(1)}, u32[]{:S(2)}, u32[]{:S(2)}) collective-permute-start(bf16[8,3584]{1,0:T(8,128)(2,1)S(1)} %get-tuple-element.47), channel_id=1, source_target_pairs={{0,4},{2,6},{4,0},{6,2},{8,12},{10,14},{12,8},{14,10},{1,5},{3,7},... | collective-permute-start | bytes 172040 | tf_op jit(solution)/shard_map/ppermute | solution.py:47
  71.3 7.2 %collective-permute-start.22 = (bf16[8,3584]{1,0:T(8,128)(2,1)S(1)}, bf16[8,3584]{1,0:T(8,128)(2,1)S(1)}, u32[]{:S(2)}, u32[]{:S(2)}) collective-permute-start(bf16[8,3584]{1,0:T(8,128)(2,1)S(1)} %get-tuple-element.48), channel_id=1, source_target_pairs={{0,6},{2,4},{4,2},{6,0},{8,14},{10,12},{12,10},{14,8},{1,7},{3,5},... | collective-permute-start | bytes 172040 | tf_op jit(solution)/shard_map/ppermute | solution.py:47
  74.0 4.8 %collective-permute-start.23 = (bf16[8,3584]{1,0:T(8,128)(2,1)S(1)}, bf16[8,3584]{1,0:T(8,128)(2,1)S(1)}, u32[]{:S(2)}, u32[]{:S(2)}) collective-permute-start(bf16[8,3584]{1,0:T(8,128)(2,1)S(1)} %get-tuple-element.49), channel_id=1, source_target_pairs={{0,2},{2,0},{4,6},{6,4},{8,10},{10,8},{12,14},{14,12},{1,3},{3,1},... | collective-permute-start | bytes 172040 | tf_op jit(solution)/shard_map/ppermute | solution.py:47

commit v11 on v9

--- a/solution.py
+++ b/solution.py
@@ -263,16 +263,12 @@
 
     def kernel(*refs):
         chunk_refs, rest = refs[:count], refs[count:]
-        w_ref, ours_ref, theirs_ref, weight_ref, stacked, total = rest
+        w_ref, ours_ref, theirs_ref, weight_ref, total = rest
         k = pl.program_id(0)
 
-        @pl.when(k == 0)
-        def _():
-            both = jnp.concatenate([ref[:, :depth] for ref in chunk_refs], axis=0)
-            for i in range(blocks):
-                stacked[i] = both[:, i * block : (i + 1) * block]
-
-        product = jnp.dot(stacked[k], w_ref[...], preferred_element_type=jnp.float32)
+        lanes = pl.ds(pl.multiple_of(k * block, LANES), block)
+        stacked = jnp.concatenate([ref[:, lanes] for ref in chunk_refs], axis=0)
+        product = jnp.dot(stacked, w_ref[...], preferred_element_type=jnp.float32)
 
         @pl.when(k == 0)
         def _():
@@ -310,7 +306,6 @@
         in_specs=[whole(c) for c in chunks] + [pl.BlockSpec((block, cols), lambda k: (k, 0))],
         out_specs=[whole(o) for o in outs],
         scratch_shapes=[
-            pltpu.VMEM((blocks, tall, block), jnp.bfloat16),
             pltpu.VMEM((tall, cols), jnp.float32),
         ],
         cost_estimate=pl.CostEstimate(

time: 77.8 us -> 77.7 us (level)
  no operation moved by 1% of the time
where the time goes in v11:
time: 77.7 us; the launch traced here: 77.5 us
  starting transfers between devices  32.4 us (42%)
  waiting for transfers between devices  24.6 us (32%)
  Pallas kernels  19.3 us (25%)
  local copies, waits for them, and re-layouts  1.08 us (1%)
    ppermute x21, starting transfers between devices, send(): return lax.ppermute(arr, 'ep', pairs)  32.3 us
    ppermute x21, waiting for transfers between devices, send(): return lax.ppermute(arr, 'ep', pairs)  21.7 us
    pallas_call x1, Pallas kernels, project(): pl.pallas_call(kernel, name='project', grid=(blocks,), out_shape=outs, in...  9.26 us
    pallas_call x1, Pallas kernels, attention(): pl.pallas_call(kernel, name='attention', out_shape=[shape_of((rows, width...  6.82 us
    ppermute x3, waiting for transfers between devices, swap(): return lax.ppermute(arr, 'tp', [(0, 1), (1, 0)])  2.87 us
    pallas_call x1, Pallas kernels, gate_up(): pl.pallas_call(kernel, name='gate_up', out_shape=[shape_of((tall + extra...  1.67 us
  transfers between devices with their start and end apart: 24, of which 14 were waited for; matrix products, arithmetic and copies ran while one was open for 0% of the time, Pallas kernels for 12%

profile of v11, /device:TPU:0, one launch (start us, length us, event | category | flops | bytes accessed | tf_op | source)
XLA Modules:
  0.0 77.5 jit_solution(10446319299330665946)
XLA Ops:
  0.0 6.8 %attention.1 = (bf16[8,9472]{1,0:T(8,128)(2,1)}, bf16[8,9472]{1,0:T(8,128)(2,1)}, bf16[8,9472]{1,0:T(8,128)(2,1)}, bf16[8,9472]{1,0:T(8,128)(2,1)}, bf16[3680,512]{1,0:T(8,128)(2,1)}) custom-call(bf16[8,8192]{1,0:T(8,128)(2,1)} %refs_0_.1, bf16[8,512]{1,0:T(8,128)(2,1)} %refs_1_.1, bf16[8,7168]{1,0:T(8,128)(2,1)} %refs_2_.1, s32[3,8]{1,0:T(4,128)} %bitcast.10, ...), custom_call_target="tpu_custom_call" | custom-call | tf_op jit(solution)/shard_map/attention/pallas_call | solution.py:219
  6.8 3.1 %collective-permute-start.1 = (bf16[8,9472]{1,0:T(8,128)(2,1)}, bf16[8,9472]{1,0:T(8,128)(2,1)S(1)}, u32[]{:S(2)}, u32[]{:S(2)}) collective-permute-start(bf16[8,9472]{1,0:T(8,128)(2,1)} %get-tuple-element.29), channel_id=1, source_target_pairs={{0,4},{2,6},{4,8},{6,10},{8,12},{10,14},{12,0},{14,2},{1,5},{3,7},... | collective-permute-start | bytes 454664 | tf_op jit(solution)/shard_map/ppermute | solution.py:47
  9.9 1.5 %collective-permute-start = (bf16[8,9472]{1,0:T(8,128)(2,1)}, bf16[8,9472]{1,0:T(8,128)(2,1)S(1)}, u32[]{:S(2)}, u32[]{:S(2)}) collective-permute-start(bf16[8,9472]{1,0:T(8,128)(2,1)} %get-tuple-element.28.refs_0_), channel_id=1, source_target_pairs={{0,2},{2,0},{4,6},{6,4},{8,10},{10,8},{12,14},{14,12},{1,3},{3,1},... | collective-permute-start | bytes 454664 | tf_op jit(solution)/shard_map/ppermute | solution.py:47
  11.4 2.2 %collective-permute-start.5 = (bf16[8,9472]{1,0:T(8,128)(2,1)}, bf16[8,9472]{1,0:T(8,128)(2,1)S(1)}, u32[]{:S(2)}, u32[]{:S(2)}) collective-permute-start(bf16[8,9472]{1,0:T(8,128)(2,1)} %get-tuple-element.32), channel_id=1, source_target_pairs={{0,12},{2,14},{4,0},{6,2},{8,4},{10,6},{12,8},{14,10},{1,13},{3,15... | collective-permute-start | bytes 454664 | tf_op jit(solution)/shard_map/ppermute | solution.py:47
  13.6 2.9 %collective-permute-done.1.refs_2_ = bf16[8,9472]{1,0:T(8,128)(2,1)S(1)} collective-permute-done((bf16[8,9472]{1,0:T(8,128)(2,1)}, bf16[8,9472]{1,0:T(8,128)(2,1)S(1)}, u32[]{:S(2)}, u32[]{:S(2)}) %collective-permute-start.1) | collective-permute-done | bytes 151584 | tf_op jit(solution)/shard_map/ppermute | solution.py:47
  16.6 0.0 collective-permute-done.refs_1_
  16.6 1.5 %collective-permute-start.3 = (bf16[8,9472]{1,0:T(8,128)(2,1)}, bf16[8,9472]{1,0:T(8,128)(2,1)S(1)}, u32[]{:S(2)}, u32[]{:S(2)}) collective-permute-start(bf16[8,9472]{1,0:T(8,128)(2,1)} %get-tuple-element.31), channel_id=1, source_target_pairs={{0,8},{2,10},{4,12},{6,14},{8,0},{10,2},{12,4},{14,6},{1,9},{3,11}... | collective-permute-start | bytes 454664 | tf_op jit(solution)/shard_map/ppermute | solution.py:47
  18.1 3.4 %collective-permute-start.2 = (bf16[8,9472]{1,0:T(8,128)(2,1)S(1)}, bf16[8,9472]{1,0:T(8,128)(2,1)S(1)}, u32[]{:S(2)}, u32[]{:S(2)}) collective-permute-start(bf16[8,9472]{1,0:T(8,128)(2,1)S(1)} %collective-permute-done.1.refs_2_), channel_id=1, source_target_pairs={{0,2},{2,0},{4,6},{6,4},{8,10},{10,8},{12,14},{14,12},{1,3},{3,1},... | collective-permute-start | bytes 454664 | tf_op jit(solution)/shard_map/ppermute | solution.py:47
  21.5 0.0 collective-permute-done.5.refs_6_
  21.5 0.0 collective-permute-start.6
  21.6 4.2 %collective-permute-done.3.refs_4_ = bf16[8,9472]{1,0:T(8,128)(2,1)S(1)} collective-permute-done((bf16[8,9472]{1,0:T(8,128)(2,1)}, bf16[8,9472]{1,0:T(8,128)(2,1)S(1)}, u32[]{:S(2)}, u32[]{:S(2)}) %collective-permute-start.3) | collective-permute-done | bytes 151584 | tf_op jit(solution)/shard_map/ppermute | solution.py:47
  25.8 1.5 %collective-permute-start.4 = (bf16[8,9472]{1,0:T(8,128)(2,1)S(1)}, bf16[8,9472]{1,0:T(8,128)(2,1)S(1)}, u32[]{:S(2)}, u32[]{:S(2)}) collective-permute-start(bf16[8,9472]{1,0:T(8,128)(2,1)S(1)} %collective-permute-done.3.refs_4_), channel_id=1, source_target_pairs={{0,2},{2,0},{4,6},{6,4},{8,10},{10,8},{12,14},{14,12},{1,3},{3,1},... | collective-permute-start | bytes 454664 | tf_op jit(solution)/shard_map/ppermute | solution.py:47
  27.3 0.0 collective-permute-done.2.refs_3_
  27.3 0.0 collective-permute-done.6.refs_7_
  27.3 4.1 %collective-permute-done.4.refs_5_ = bf16[8,9472]{1,0:T(8,128)(2,1)S(1)} collective-permute-done((bf16[8,9472]{1,0:T(8,128)(2,1)S(1)}, bf16[8,9472]{1,0:T(8,128)(2,1)S(1)}, u32[]{:S(2)}, u32[]{:S(2)}) %collective-permute-start.4) | collective-permute-done | bytes 151584 | tf_op jit(solution)/shard_map/ppermute | solution.py:47
  31.4 0.0 copy-start
  31.4 0.0 copy-start.1
  31.4 0.0 collective-permute-start.8
  31.4 0.0 copy-start.3
  31.4 1.1 %copy-done.3 = bf16[8,9472]{1,0:T(8,128)(2,1)S(1)} copy-done((bf16[8,9472]{1,0:T(8,128)(2,1)S(1)}, bf16[8,9472]{1,0:T(8,128)(2,1)}, u32[]{:S(2)}) %copy-start.3) | copy-done | bytes 151576
  32.5 0.0 copy-start.4
  32.5 9.3 %project.1 = (f32[64,512]{1,0:T(8,128)S(1)}, f32[64,512]{1,0:T(8,128)S(1)}, f32[64,128]{1,0:T(8,128)S(1)}) custom-call(bf16[8,9472]{1,0:T(8,128)(2,1)S(1)} %copy-done.3, bf16[8,9472]{1,0:T(8,128)(2,1)S(1)} %collective-permute-done.refs_1_, bf16[8,9472]{1,0:T(8,128)(2,1)S(1)} %collective-permute-done.1.refs_2_, ...), custom_call_target="tpu_custom_call" | custom-call | flops 939524096 | bytes 15990784 | tf_op jit(solution)/shard_map/project/pallas_call | solution.py:301
  41.7 0.1 collective-permute-start.7
  41.8 1.3 %collective-permute-done.7 = f32[64,512]{1,0:T(8,128)S(1)} collective-permute-done((f32[64,512]{1,0:T(8,128)S(1)}, f32[64,512]{1,0:T(8,128)S(1)}, u32[]{:S(2)}, u32[]{:S(2)}) %collective-permute-start.7) | collective-permute-done | bytes 131104 | tf_op jit(solution)/shard_map/ppermute | solution.py:81
  43.2 0.0 collective-permute-done.8.refs_11_.packed_ref
  43.2 0.8 collective-permute-start.10
  43.9 1.5 %collective-permute-start.14 = (bf16[64,512]{1,0:T(8,128)(2,1)S(1)}, bf16[64,512]{1,0:T(8,128)(2,1)S(1)}, u32[]{:S(2)}, u32[]{:S(2)}) collective-permute-start(bf16[64,512]{1,0:T(8,128)(2,1)S(1)} %add_convert_fusion.refs_0_), channel_id=1, source_target_pairs={{0,12},{2,14},{4,8},{6,10},{8,4},{10,6},{12,0},{14,2},{1,13},{3,15... | collective-permute-start | bytes 196616 | tf_op jit(solution)/shard_map/ppermute | solution.py:47
  45.5 1.3 %collective-permute-start.12 = (bf16[64,512]{1,0:T(8,128)(2,1)S(1)}, bf16[64,512]{1,0:T(8,128)(2,1)S(1)}, u32[]{:S(2)}, u32[]{:S(2)}) collective-permute-start(bf16[64,512]{1,0:T(8,128)(2,1)S(1)} %add_convert_fusion.refs_0_), channel_id=1, source_target_pairs={{0,8},{2,10},{4,12},{6,14},{8,0},{10,2},{12,4},{14,6},{1,9},{3,11}... | collective-permute-start | bytes 196616 | tf_op jit(solution)/shard_map/ppermute | solution.py:47
  46.7 0.8 %collective-permute-done.10.refs_2_ = bf16[64,512]{1,0:T(8,128)(2,1)S(1)} collective-permute-done((bf16[64,512]{1,0:T(8,128)(2,1)S(1)}, bf16[64,512]{1,0:T(8,128)(2,1)S(1)}, u32[]{:S(2)}, u32[]{:S(2)}) %collective-permute-start.10) | collective-permute-done | bytes 65568 | tf_op jit(solution)/shard_map/ppermute | solution.py:47
  47.5 1.1 %collective-permute-start.11 = (bf16[64,512]{1,0:T(8,128)(2,1)S(1)}, bf16[64,512]{1,0:T(8,128)(2,1)S(1)}, u32[]{:S(2)}, u32[]{:S(2)}) collective-permute-start(bf16[64,512]{1,0:T(8,128)(2,1)S(1)} %collective-permute-done.10.refs_2_), channel_id=1, source_target_pairs={{0,2},{2,0},{4,6},{6,4},{8,10},{10,8},{12,14},{14,12},{1,3},{3,1},... | collective-permute-start | bytes 196616 | tf_op jit(solution)/shard_map/ppermute | solution.py:47
  48.6 0.9 %collective-permute-start.9 = (bf16[64,512]{1,0:T(8,128)(2,1)S(1)}, bf16[64,512]{1,0:T(8,128)(2,1)S(1)}, u32[]{:S(2)}, u32[]{:S(2)}) collective-permute-start(bf16[64,512]{1,0:T(8,128)(2,1)S(1)} %add_convert_fusion.refs_0_), channel_id=1, source_target_pairs={{0,2},{2,0},{4,6},{6,4},{8,10},{10,8},{12,14},{14,12},{1,3},{3,1},... | collective-permute-start | bytes 196616 | tf_op jit(solution)/shard_map/ppermute | solution.py:47
  49.5 0.9 %collective-permute-done.14.refs_6_ = bf16[64,512]{1,0:T(8,128)(2,1)S(1)} collective-permute-done((bf16[64,512]{1,0:T(8,128)(2,1)S(1)}, bf16[64,512]{1,0:T(8,128)(2,1)S(1)}, u32[]{:S(2)}, u32[]{:S(2)}) %collective-permute-start.14) | collective-permute-done | bytes 65568 | tf_op jit(solution)/shard_map/ppermute | solution.py:47
  50.4 1.0 %collective-permute-start.15 = (bf16[64,512]{1,0:T(8,128)(2,1)S(1)}, bf16[64,512]{1,0:T(8,128)(2,1)S(1)}, u32[]{:S(2)}, u32[]{:S(2)}) collective-permute-start(bf16[64,512]{1,0:T(8,128)(2,1)S(1)} %collective-permute-done.14.refs_6_), channel_id=1, source_target_pairs={{0,2},{2,0},{4,6},{6,4},{8,10},{10,8},{12,14},{14,12},{1,3},{3,1},... | collective-permute-start | bytes 196616 | tf_op jit(solution)/shard_map/ppermute | solution.py:47
  51.4 1.7 %collective-permute-done.12.refs_4_ = bf16[64,512]{1,0:T(8,128)(2,1)S(1)} collective-permute-done((bf16[64,512]{1,0:T(8,128)(2,1)S(1)}, bf16[64,512]{1,0:T(8,128)(2,1)S(1)}, u32[]{:S(2)}, u32[]{:S(2)}) %collective-permute-start.12) | collective-permute-done | bytes 65568 | tf_op jit(solution)/shard_map/ppermute | solution.py:47
  53.1 0.0 collective-permute-done.11.refs_3_
  53.1 1.2 %collective-permute-start.13 = (bf16[64,512]{1,0:T(8,128)(2,1)S(1)}, bf16[64,512]{1,0:T(8,128)(2,1)S(1)}, u32[]{:S(2)}, u32[]{:S(2)}) collective-permute-start(bf16[64,512]{1,0:T(8,128)(2,1)S(1)} %collective-permute-done.12.refs_4_), channel_id=1, source_target_pairs={{0,2},{2,0},{4,6},{6,4},{8,10},{10,8},{12,14},{14,12},{1,3},{3,1},... | collective-permute-start | bytes 196616 | tf_op jit(solution)/shard_map/ppermute | solution.py:47
  54.3 0.0 collective-permute-done.9.refs_1_
  54.3 0.4 collective-permute-done.15.refs_7_
  54.7 2.7 %collective-permute-done.13.refs_5_ = bf16[64,512]{1,0:T(8,128)(2,1)S(1)} collective-permute-done((bf16[64,512]{1,0:T(8,128)(2,1)S(1)}, bf16[64,512]{1,0:T(8,128)(2,1)S(1)}, u32[]{:S(2)}, u32[]{:S(2)}) %collective-permute-start.13) | collective-permute-done | bytes 65568 | tf_op jit(solution)/shard_map/ppermute | solution.py:47
  57.4 0.0 copy-done
  57.4 0.0 copy-done.1
  57.4 0.0 copy-done.4
  57.4 0.0 copy-start.2
  57.4 1.7 %gate_up.1 = (f32[88,768]{1,0:T(8,128)S(1)}, f32[8,2048]{1,0:T(8,128)S(1)}) custom-call(bf16[64,512]{1,0:T(8,128)(2,1)S(1)} %add_convert_fusion.refs_0_, bf16[64,512]{1,0:T(8,128)(2,1)S(1)} %collective-permute-done.9.refs_1_, bf16[64,512]{1,0:T(8,128)(2,1)S(1)} %collective-permute-done.10.refs_2_, bf16[64,512]{1,0:T(8,128)(2,1)S(1)} %collective-permute-done.11.refs_3_, ...), custom_call_target="tpu_custom_call" | custom-call | tf_op jit(solution)/shard_map/gate_up/pallas_call | solution.py:363
  59.1 0.1 collective-permute-start.16
  59.2 1.5 %collective-permute-done.16.far_ref = f32[88,768]{1,0:T(8,128)S(1)} collective-permute-done((f32[88,768]{1,0:T(8,128)S(1)}, f32[88,768]{1,0:T(8,128)S(1)}, u32[]{:S(2)}, u32[]{:S(2)}) %collective-permute-start.16) | collective-permute-done | bytes 270368 | tf_op jit(solution)/shard_map/ppermute | solution.py:81
  60.7 0.0 copy-done.2
  60.7 0.9 %down.1 = (f32[8,3584]{1,0:T(8,128)S(1)}, bf16[8,3584]{1,0:T(8,128)(2,1)S(1)}, bf16[8,3584]{1,0:T(8,128)(2,1)S(1)}, bf16[8,3584]{1,0:T(8,128)(2,1)S(1)}, bf16[8,...) custom-call(f32[88,768]{1,0:T(8,128)S(1)} %get-tuple-element.41.sums, ...), custom_call_target="tpu_custom_call" | custom-call | tf_op jit(solution)/shard_map/down/pallas_call | solution.py:416
  61.6 1.9 %collective-permute-start.17 = (bf16[8,3584]{1,0:T(8,128)(2,1)S(1)}, bf16[8,3584]{1,0:T(8,128)(2,1)S(1)}, u32[]{:S(2)}, u32[]{:S(2)}) collective-permute-start(bf16[8,3584]{1,0:T(8,128)(2,1)S(1)} %get-tuple-element.43), channel_id=1, source_target_pairs={{0,12},{2,14},{4,8},{6,10},{8,4},{10,6},{12,0},{14,2},{1,13},{3,15... | collective-permute-start | bytes 172040 | tf_op jit(solution)/shard_map/ppermute | solution.py:47
  63.5 2.6 %collective-permute-start.18 = (bf16[8,3584]{1,0:T(8,128)(2,1)S(1)}, bf16[8,3584]{1,0:T(8,128)(2,1)S(1)}, u32[]{:S(2)}, u32[]{:S(2)}) collective-permute-start(bf16[8,3584]{1,0:T(8,128)(2,1)S(1)} %get-tuple-element.44), channel_id=1, source_target_pairs={{0,14},{2,12},{4,10},{6,8},{8,6},{10,4},{12,2},{14,0},{1,15},{3,13... | collective-permute-start | bytes 172040 | tf_op jit(solution)/shard_map/ppermute | solution.py:47
  66.1 0.0 collective-permute-start.19
  66.1 3.2 %collective-permute-start.20 = (bf16[8,3584]{1,0:T(8,128)(2,1)S(1)}, bf16[8,3584]{1,0:T(8,128)(2,1)S(1)}, u32[]{:S(2)}, u32[]{:S(2)}) collective-permute-start(bf16[8,3584]{1,0:T(8,128)(2,1)S(1)} %get-tuple-element.46), channel_id=1, source_target_pairs={{0,10},{2,8},{4,14},{6,12},{8,2},{10,0},{12,6},{14,4},{1,11},{3,9}... | collective-permute-start | bytes 172040 | tf_op jit(solution)/shard_map/ppermute | solution.py:47
  69.3 0.0 collective-permute-start.21
  69.3 0.0 collective-permute-done.17.rest_0_
  69.3 2.7 %collective-permute-start.22 = (bf16[8,3584]{1,0:T(8,128)(2,1)S(1)}, bf16[8,3584]{1,0:T(8,128)(2,1)S(1)}, u32[]{:S(2)}, u32[]{:S(2)}) collective-permute-start(bf16[8,3584]{1,0:T(8,128)(2,1)S(1)} %get-tuple-element.48), channel_id=1, source_target_pairs={{0,6},{2,4},{4,2},{6,0},{8,14},{10,12},{12,10},{14,8},{1,7},{3,5},... | collective-permute-start | bytes 172040 | tf_op jit(solution)/shard_map/ppermute | solution.py:47
  72.0 0.0 collective-permute-done.18.rest_1_
  72.0 0.8 %collective-permute-start.23 = (bf16[8,3584]{1,0:T(8,128)(2,1)S(1)}, bf16[8,3584]{1,0:T(8,128)(2,1)S(1)}, u32[]{:S(2)}, u32[]{:S(2)}) collective-permute-start(bf16[8,3584]{1,0:T(8,128)(2,1)S(1)} %get-tuple-element.49), channel_id=1, source_target_pairs={{0,2},{2,0},{4,6},{6,4},{8,10},{10,8},{12,14},{14,12},{1,3},{3,1},... | collective-permute-start | bytes 172040 | tf_op jit(solution)/shard_map/ppermute | solution.py:47
  72.8 1.4 %collective-permute-done.19.rest_2_ = bf16[8,3584]{1,0:T(8,128)(2,1)S(1)} collective-permute-done((bf16[8,3584]{1,0:T(8,128)(2,1)S(1)}, bf16[8,3584]{1,0:T(8,128)(2,1)S(1)}, u32[]{:S(2)}, u32[]{:S(2)}) %collective-permute-start.19) | collective-permute-done | bytes 57376 | tf_op jit(solution)/shard_map/ppermute | solution.py:47
  74.2 1.4 %collective-permute-done.20.rest_3_ = bf16[8,3584]{1,0:T(8,128)(2,1)S(1)} collective-permute-done((bf16[8,3584]{1,0:T(8,128)(2,1)S(1)}, bf16[8,3584]{1,0:T(8,128)(2,1)S(1)}, u32[]{:S(2)}, u32[]{:S(2)}) %collective-permute-start.20) | collective-permute-done | bytes 57376 | tf_op jit(solution)/shard_map/ppermute | solution.py:47
  75.6 0.0 collective-permute-done.21.rest_4_
  75.6 0.9 %collective-permute-done.22.rest_5_ = bf16[8,3584]{1,0:T(8,128)(2,1)S(1)} collective-permute-done((bf16[8,3584]{1,0:T(8,128)(2,1)S(1)}, bf16[8,3584]{1,0:T(8,128)(2,1)S(1)}, u32[]{:S(2)}, u32[]{:S(2)}) %collective-permute-start.22) | collective-permute-done | bytes 57376 | tf_op jit(solution)/shard_map/ppermute | solution.py:47
  76.5 0.3 collective-permute-done.23.rest_6_
  76.8 0.7 finish.1
  (1 shorter events, 0.0 us)
Async XLA Ops:
  6.8 9.8 %collective-permute-start.1 = (bf16[8,9472]{1,0:T(8,128)(2,1)}, bf16[8,9472]{1,0:T(8,128)(2,1)S(1)}, u32[]{:S(2)}, u32[]{:S(2)}) collective-permute-start(bf16[8,9472]{1,0:T(8,128)(2,1)} %get-tuple-element.29), channel_id=1, source_target_pairs={{0,4},{2,6},{4,8},{6,10},{8,12},{10,14},{12,0},{14,2},{1,5},{3,7},... | collective-permute-start | bytes 454664 | tf_op jit(solution)/shard_map/ppermute | solution.py:47
  9.9 6.7 %collective-permute-start = (bf16[8,9472]{1,0:T(8,128)(2,1)}, bf16[8,9472]{1,0:T(8,128)(2,1)S(1)}, u32[]{:S(2)}, u32[]{:S(2)}) collective-permute-start(bf16[8,9472]{1,0:T(8,128)(2,1)} %get-tuple-element.28.refs_0_), channel_id=1, source_target_pairs={{0,2},{2,0},{4,6},{6,4},{8,10},{10,8},{12,14},{14,12},{1,3},{3,1},... | collective-permute-start | bytes 454664 | tf_op jit(solution)/shard_map/ppermute | solution.py:47
  11.4 10.2 %collective-permute-start.5 = (bf16[8,9472]{1,0:T(8,128)(2,1)}, bf16[8,9472]{1,0:T(8,128)(2,1)S(1)}, u32[]{:S(2)}, u32[]{:S(2)}) collective-permute-start(bf16[8,9472]{1,0:T(8,128)(2,1)} %get-tuple-element.32), channel_id=1, source_target_pairs={{0,12},{2,14},{4,0},{6,2},{8,4},{10,6},{12,8},{14,10},{1,13},{3,15... | collective-permute-start | bytes 454664 | tf_op jit(solution)/shard_map/ppermute | solution.py:47
  16.6 9.2 %collective-permute-start.3 = (bf16[8,9472]{1,0:T(8,128)(2,1)}, bf16[8,9472]{1,0:T(8,128)(2,1)S(1)}, u32[]{:S(2)}, u32[]{:S(2)}) collective-permute-start(bf16[8,9472]{1,0:T(8,128)(2,1)} %get-tuple-element.31), channel_id=1, source_target_pairs={{0,8},{2,10},{4,12},{6,14},{8,0},{10,2},{12,4},{14,6},{1,9},{3,11}... | collective-permute-start | bytes 454664 | tf_op jit(solution)/shard_map/ppermute | solution.py:47
  18.1 9.2 %collective-permute-start.2 = (bf16[8,9472]{1,0:T(8,128)(2,1)S(1)}, bf16[8,9472]{1,0:T(8,128)(2,1)S(1)}, u32[]{:S(2)}, u32[]{:S(2)}) collective-permute-start(bf16[8,9472]{1,0:T(8,128)(2,1)S(1)} %collective-permute-done.1.refs_2_), channel_id=1, source_target_pairs={{0,2},{2,0},{4,6},{6,4},{8,10},{10,8},{12,14},{14,12},{1,3},{3,1},... | collective-permute-start | bytes 454664 | tf_op jit(solution)/shard_map/ppermute | solution.py:47
  21.5 5.8 %collective-permute-start.6 = (bf16[8,9472]{1,0:T(8,128)(2,1)S(1)}, bf16[8,9472]{1,0:T(8,128)(2,1)S(1)}, u32[]{:S(2)}, u32[]{:S(2)}) collective-permute-start(bf16[8,9472]{1,0:T(8,128)(2,1)S(1)} %collective-permute-done.5.refs_6_), channel_id=1, source_target_pairs={{0,2},{2,0},{4,6},{6,4},{8,10},{10,8},{12,14},{14,12},{1,3},{3,1},... | collective-permute-start | bytes 454664 | tf_op jit(solution)/shard_map/ppermute | solution.py:47
  25.8 5.6 %collective-permute-start.4 = (bf16[8,9472]{1,0:T(8,128)(2,1)S(1)}, bf16[8,9472]{1,0:T(8,128)(2,1)S(1)}, u32[]{:S(2)}, u32[]{:S(2)}) collective-permute-start(bf16[8,9472]{1,0:T(8,128)(2,1)S(1)} %collective-permute-done.3.refs_4_), channel_id=1, source_target_pairs={{0,2},{2,0},{4,6},{6,4},{8,10},{10,8},{12,14},{14,12},{1,3},{3,1},... | collective-permute-start | bytes 454664 | tf_op jit(solution)/shard_map/ppermute | solution.py:47
  31.4 26.0 %copy-start = (bf16[7168,160]{0,1:T(8,128)(2,1)S(1)}, bf16[7168,160]{0,1:T(8,128)(2,1)}, u32[]{:S(2)}) copy-start(bf16[7168,160]{0,1:T(8,128)(2,1)} %param.21) | copy-start | bytes 6881284
  31.4 26.0 %copy-start.1 = (bf16[7168,160]{0,1:T(8,128)(2,1)S(1)}, bf16[7168,160]{0,1:T(8,128)(2,1)}, u32[]{:S(2)}) copy-start(bf16[7168,160]{0,1:T(8,128)(2,1)} %param.22) | copy-start | bytes 6881284
  31.4 11.8 %collective-permute-start.8 = (bf16[3680,512]{1,0:T(8,128)(2,1)}, bf16[3680,512]{1,0:T(8,128)(2,1)S(1)}, u32[]{:S(2)}, u32[]{:S(2)}) collective-permute-start(bf16[3680,512]{1,0:T(8,128)(2,1)} %get-tuple-element.36), channel_id=1, source_target_pairs={{0,1},{1,0},{2,3},{3,2},{4,5},{5,4},{6,7},{7,6},{8,9},{9,8},{10,11... | collective-permute-start | bytes 11304968 | tf_op jit(solution)/shard_map/ppermute | solution.py:81
  31.4 1.1 %copy-start.3 = (bf16[8,9472]{1,0:T(8,128)(2,1)S(1)}, bf16[8,9472]{1,0:T(8,128)(2,1)}, u32[]{:S(2)}) copy-start(bf16[8,9472]{1,0:T(8,128)(2,1)} %get-tuple-element.28.refs_0_) | copy-start | bytes 454660
  32.5 24.9 %copy-start.4 = (f32[7168]{0:T(1024)S(1)}, f32[7168]{0:T(1024)}, u32[]{:S(2)}) copy-start(f32[7168]{0:T(1024)} %param.18) | copy-start | bytes 86020
  41.7 1.4 %collective-permute-start.7 = (f32[64,512]{1,0:T(8,128)S(1)}, f32[64,512]{1,0:T(8,128)S(1)}, u32[]{:S(2)}, u32[]{:S(2)}) collective-permute-start(f32[64,512]{1,0:T(8,128)S(1)} %get-tuple-element.34), channel_id=1, source_target_pairs={{0,1},{1,0},{2,3},{3,2},{4,5},{5,4},{6,7},{7,6},{8,9},{9,8},{10,11... | collective-permute-start | bytes 393224 | tf_op jit(solution)/shard_map/ppermute | solution.py:81
  43.2 4.3 %collective-permute-start.10 = (bf16[64,512]{1,0:T(8,128)(2,1)S(1)}, bf16[64,512]{1,0:T(8,128)(2,1)S(1)}, u32[]{:S(2)}, u32[]{:S(2)}) collective-permute-start(bf16[64,512]{1,0:T(8,128)(2,1)S(1)} %add_convert_fusion.refs_0_), channel_id=1, source_target_pairs={{0,4},{2,6},{4,0},{6,2},{8,12},{10,14},{12,8},{14,10},{1,5},{3,7},... | collective-permute-start | bytes 196616 | tf_op jit(solution)/shard_map/ppermute | solution.py:47
  43.9 6.5 %collective-permute-start.14 = (bf16[64,512]{1,0:T(8,128)(2,1)S(1)}, bf16[64,512]{1,0:T(8,128)(2,1)S(1)}, u32[]{:S(2)}, u32[]{:S(2)}) collective-permute-start(bf16[64,512]{1,0:T(8,128)(2,1)S(1)} %add_convert_fusion.refs_0_), channel_id=1, source_target_pairs={{0,12},{2,14},{4,8},{6,10},{8,4},{10,6},{12,0},{14,2},{1,13},{3,15... | collective-permute-start | bytes 196616 | tf_op jit(solution)/shard_map/ppermute | solution.py:47
  45.5 7.7 %collective-permute-start.12 = (bf16[64,512]{1,0:T(8,128)(2,1)S(1)}, bf16[64,512]{1,0:T(8,128)(2,1)S(1)}, u32[]{:S(2)}, u32[]{:S(2)}) collective-permute-start(bf16[64,512]{1,0:T(8,128)(2,1)S(1)} %add_convert_fusion.refs_0_), channel_id=1, source_target_pairs={{0,8},{2,10},{4,12},{6,14},{8,0},{10,2},{12,4},{14,6},{1,9},{3,11}... | collective-permute-start | bytes 196616 | tf_op jit(solution)/shard_map/ppermute | solution.py:47
  47.5 5.6 %collective-permute-start.11 = (bf16[64,512]{1,0:T(8,128)(2,1)S(1)}, bf16[64,512]{1,0:T(8,128)(2,1)S(1)}, u32[]{:S(2)}, u32[]{:S(2)}) collective-permute-start(bf16[64,512]{1,0:T(8,128)(2,1)S(1)} %collective-permute-done.10.refs_2_), channel_id=1, source_target_pairs={{0,2},{2,0},{4,6},{6,4},{8,10},{10,8},{12,14},{14,12},{1,3},{3,1},... | collective-permute-start | bytes 196616 | tf_op jit(solution)/shard_map/ppermute | solution.py:47
  48.6 5.7 %collective-permute-start.9 = (bf16[64,512]{1,0:T(8,128)(2,1)S(1)}, bf16[64,512]{1,0:T(8,128)(2,1)S(1)}, u32[]{:S(2)}, u32[]{:S(2)}) collective-permute-start(bf16[64,512]{1,0:T(8,128)(2,1)S(1)} %add_convert_fusion.refs_0_), channel_id=1, source_target_pairs={{0,2},{2,0},{4,6},{6,4},{8,10},{10,8},{12,14},{14,12},{1,3},{3,1},... | collective-permute-start | bytes 196616 | tf_op jit(solution)/shard_map/ppermute | solution.py:47
  50.4 4.3 %collective-permute-start.15 = (bf16[64,512]{1,0:T(8,128)(2,1)S(1)}, bf16[64,512]{1,0:T(8,128)(2,1)S(1)}, u32[]{:S(2)}, u32[]{:S(2)}) collective-permute-start(bf16[64,512]{1,0:T(8,128)(2,1)S(1)} %collective-permute-done.14.refs_6_), channel_id=1, source_target_pairs={{0,2},{2,0},{4,6},{6,4},{8,10},{10,8},{12,14},{14,12},{1,3},{3,1},... | collective-permute-start | bytes 196616 | tf_op jit(solution)/shard_map/ppermute | solution.py:47
  53.1 4.3 %collective-permute-start.13 = (bf16[64,512]{1,0:T(8,128)(2,1)S(1)}, bf16[64,512]{1,0:T(8,128)(2,1)S(1)}, u32[]{:S(2)}, u32[]{:S(2)}) collective-permute-start(bf16[64,512]{1,0:T(8,128)(2,1)S(1)} %collective-permute-done.12.refs_4_), channel_id=1, source_target_pairs={{0,2},{2,0},{4,6},{6,4},{8,10},{10,8},{12,14},{14,12},{1,3},{3,1},... | collective-permute-start | bytes 196616 | tf_op jit(solution)/shard_map/ppermute | solution.py:47
  57.4 3.3 %copy-start.2 = (bf16[160,7168]{1,0:T(8,128)(2,1)S(1)}, bf16[160,7168]{1,0:T(8,128)(2,1)}, u32[]{:S(2)}) copy-start(bf16[160,7168]{1,0:T(8,128)(2,1)} %down_ref.1) | copy-start | bytes 6881284
  59.1 1.6 %collective-permute-start.16 = (f32[88,768]{1,0:T(8,128)S(1)}, f32[88,768]{1,0:T(8,128)S(1)}, u32[]{:S(2)}, u32[]{:S(2)}) collective-permute-start(f32[88,768]{1,0:T(8,128)S(1)} %get-tuple-element.41.sums_ref), channel_id=1, source_target_pairs={{0,1},{1,0},{2,3},{3,2},{4,5},{5,4},{6,7},{7,6},{8,9},{9,8},{10,11... | collective-permute-start | bytes 811016 | tf_op jit(solution)/shard_map/ppermute | solution.py:81
  61.6 7.7 %collective-permute-start.17 = (bf16[8,3584]{1,0:T(8,128)(2,1)S(1)}, bf16[8,3584]{1,0:T(8,128)(2,1)S(1)}, u32[]{:S(2)}, u32[]{:S(2)}) collective-permute-start(bf16[8,3584]{1,0:T(8,128)(2,1)S(1)} %get-tuple-element.43), channel_id=1, source_target_pairs={{0,12},{2,14},{4,8},{6,10},{8,4},{10,6},{12,0},{14,2},{1,13},{3,15... | collective-permute-start | bytes 172040 | tf_op jit(solution)/shard_map/ppermute | solution.py:47
  63.5 8.5 %collective-permute-start.18 = (bf16[8,3584]{1,0:T(8,128)(2,1)S(1)}, bf16[8,3584]{1,0:T(8,128)(2,1)S(1)}, u32[]{:S(2)}, u32[]{:S(2)}) collective-permute-start(bf16[8,3584]{1,0:T(8,128)(2,1)S(1)} %get-tuple-element.44), channel_id=1, source_target_pairs={{0,14},{2,12},{4,10},{6,8},{8,6},{10,4},{12,2},{14,0},{1,15},{3,13... | collective-permute-start | bytes 172040 | tf_op jit(solution)/shard_map/ppermute | solution.py:47
  66.1 8.1 %collective-permute-start.19 = (bf16[8,3584]{1,0:T(8,128)(2,1)S(1)}, bf16[8,3584]{1,0:T(8,128)(2,1)S(1)}, u32[]{:S(2)}, u32[]{:S(2)}) collective-permute-start(bf16[8,3584]{1,0:T(8,128)(2,1)S(1)} %get-tuple-element.45), channel_id=1, source_target_pairs={{0,8},{2,10},{4,12},{6,14},{8,0},{10,2},{12,4},{14,6},{1,9},{3,11}... | collective-permute-start | bytes 172040 | tf_op jit(solution)/shard_map/ppermute | solution.py:47
  66.1 9.5 %collective-permute-start.20 = (bf16[8,3584]{1,0:T(8,128)(2,1)S(1)}, bf16[8,3584]{1,0:T(8,128)(2,1)S(1)}, u32[]{:S(2)}, u32[]{:S(2)}) collective-permute-start(bf16[8,3584]{1,0:T(8,128)(2,1)S(1)} %get-tuple-element.46), channel_id=1, source_target_pairs={{0,10},{2,8},{4,14},{6,12},{8,2},{10,0},{12,6},{14,4},{1,11},{3,9}... | collective-permute-start | bytes 172040 | tf_op jit(solution)/shard_map/ppermute | solution.py:47
  69.3 6.3 %collective-permute-start.21 = (bf16[8,3584]{1,0:T(8,128)(2,1)S(1)}, bf16[8,3584]{1,0:T(8,128)(2,1)S(1)}, u32[]{:S(2)}, u32[]{:S(2)}) collective-permute-start(bf16[8,3584]{1,0:T(8,128)(2,1)S(1)} %get-tuple-element.47), channel_id=1, source_target_pairs={{0,4},{2,6},{4,0},{6,2},{8,12},{10,14},{12,8},{14,10},{1,5},{3,7},... | collective-permute-start | bytes 172040 | tf_op jit(solution)/shard_map/ppermute | solution.py:47
  69.3 7.2 %collective-permute-start.22 = (bf16[8,3584]{1,0:T(8,128)(2,1)S(1)}, bf16[8,3584]{1,0:T(8,128)(2,1)S(1)}, u32[]{:S(2)}, u32[]{:S(2)}) collective-permute-start(bf16[8,3584]{1,0:T(8,128)(2,1)S(1)} %get-tuple-element.48), channel_id=1, source_target_pairs={{0,6},{2,4},{4,2},{6,0},{8,14},{10,12},{12,10},{14,8},{1,7},{3,5},... | collective-permute-start | bytes 172040 | tf_op jit(solution)/shard_map/ppermute | solution.py:47
  72.0 4.8 %collective-permute-start.23 = (bf16[8,3584]{1,0:T(8,128)(2,1)S(1)}, bf16[8,3584]{1,0:T(8,128)(2,1)S(1)}, u32[]{:S(2)}, u32[]{:S(2)}) collective-permute-start(bf16[8,3584]{1,0:T(8,128)(2,1)S(1)} %get-tuple-element.49), channel_id=1, source_target_pairs={{0,2},{2,0},{4,6},{6,4},{8,10},{10,8},{12,14},{14,12},{1,3},{3,1},... | collective-permute-start | bytes 172040 | tf_op jit(solution)/shard_map/ppermute | solution.py:47

commit v12 on v11

--- a/solution.py
+++ b/solution.py
@@ -257,7 +257,7 @@
     depth, cols = w_out.shape
     count = len(chunks)
     tall = rows * count
-    blocks = 8
+    blocks = 16
     block = depth // blocks
     note = piece + LANES
 

time: 77.7 us -> 81.9 us (1.054)
  Pallas kernels: 19.3 us -> 23.4 us
    pallas_call x1, Pallas kernels: 9.26 us -> 13.3 us  [project(): pl.pallas_call(kernel, name='project', grid=(blocks,), out_shape=outs, in...]
  transfers between devices with their start and end apart: 24 -> 24, of which waited for: 14 -> 14; matrix products, arithmetic and copies ran while one was open for 0% -> 0% of each run, Pallas kernels for 12% -> 16%
where the time goes in v12:
time: 81.9 us; the launch traced here: 81.5 us
  starting transfers between devices  32.4 us (40%)
  waiting for transfers between devices  24.6 us (30%)
  Pallas kernels  23.4 us (29%)
  local copies, waits for them, and re-layouts  1.08 us (1%)
    ppermute x21, starting transfers between devices, send(): return lax.ppermute(arr, 'ep', pairs)  32.3 us
    ppermute x21, waiting for transfers between devices, send(): return lax.ppermute(arr, 'ep', pairs)  21.7 us
    pallas_call x1, Pallas kernels, project(): pl.pallas_call(kernel, name='project', grid=(blocks,), out_shape=outs, in...  13.3 us
    pallas_call x1, Pallas kernels, attention(): pl.pallas_call(kernel, name='attention', out_shape=[shape_of((rows, width...  6.82 us
    ppermute x3, waiting for transfers between devices, swap(): return lax.ppermute(arr, 'tp', [(0, 1), (1, 0)])  2.87 us
    pallas_call x1, Pallas kernels, gate_up(): pl.pallas_call(kernel, name='gate_up', out_shape=[shape_of((tall + extra...  1.65 us
  transfers between devices with their start and end apart: 24, of which 14 were waited for; matrix products, arithmetic and copies ran while one was open for 0% of the time, Pallas kernels for 16%

profile of v12, /device:TPU:0, one launch (start us, length us, event | category | flops | bytes accessed | tf_op | source)
XLA Modules:
  0.0 81.5 jit_solution(7317931659541738788)
XLA Ops:
  0.0 6.8 %attention.1 = (bf16[8,9472]{1,0:T(8,128)(2,1)}, bf16[8,9472]{1,0:T(8,128)(2,1)}, bf16[8,9472]{1,0:T(8,128)(2,1)}, bf16[8,9472]{1,0:T(8,128)(2,1)}, bf16[3680,512]{1,0:T(8,128)(2,1)}) custom-call(bf16[8,8192]{1,0:T(8,128)(2,1)} %refs_0_.1, bf16[8,512]{1,0:T(8,128)(2,1)} %refs_1_.1, bf16[8,7168]{1,0:T(8,128)(2,1)} %refs_2_.1, s32[3,8]{1,0:T(4,128)} %bitcast.10, ...), custom_call_target="tpu_custom_call" | custom-call | tf_op jit(solution)/shard_map/attention/pallas_call | solution.py:219
  6.8 3.1 %collective-permute-start.1 = (bf16[8,9472]{1,0:T(8,128)(2,1)}, bf16[8,9472]{1,0:T(8,128)(2,1)S(1)}, u32[]{:S(2)}, u32[]{:S(2)}) collective-permute-start(bf16[8,9472]{1,0:T(8,128)(2,1)} %get-tuple-element.29), channel_id=1, source_target_pairs={{0,4},{2,6},{4,8},{6,10},{8,12},{10,14},{12,0},{14,2},{1,5},{3,7},... | collective-permute-start | bytes 454664 | tf_op jit(solution)/shard_map/ppermute | solution.py:47
  9.9 1.5 %collective-permute-start = (bf16[8,9472]{1,0:T(8,128)(2,1)}, bf16[8,9472]{1,0:T(8,128)(2,1)S(1)}, u32[]{:S(2)}, u32[]{:S(2)}) collective-permute-start(bf16[8,9472]{1,0:T(8,128)(2,1)} %get-tuple-element.28.refs_0_), channel_id=1, source_target_pairs={{0,2},{2,0},{4,6},{6,4},{8,10},{10,8},{12,14},{14,12},{1,3},{3,1},... | collective-permute-start | bytes 454664 | tf_op jit(solution)/shard_map/ppermute | solution.py:47
  11.4 2.2 %collective-permute-start.5 = (bf16[8,9472]{1,0:T(8,128)(2,1)}, bf16[8,9472]{1,0:T(8,128)(2,1)S(1)}, u32[]{:S(2)}, u32[]{:S(2)}) collective-permute-start(bf16[8,9472]{1,0:T(8,128)(2,1)} %get-tuple-element.32), channel_id=1, source_target_pairs={{0,12},{2,14},{4,0},{6,2},{8,4},{10,6},{12,8},{14,10},{1,13},{3,15... | collective-permute-start | bytes 454664 | tf_op jit(solution)/shard_map/ppermute | solution.py:47
  13.6 2.9 %collective-permute-done.1.refs_2_ = bf16[8,9472]{1,0:T(8,128)(2,1)S(1)} collective-permute-done((bf16[8,9472]{1,0:T(8,128)(2,1)}, bf16[8,9472]{1,0:T(8,128)(2,1)S(1)}, u32[]{:S(2)}, u32[]{:S(2)}) %collective-permute-start.1) | collective-permute-done | bytes 151584 | tf_op jit(solution)/shard_map/ppermute | solution.py:47
  16.6 0.0 collective-permute-done.refs_1_
  16.6 1.5 %collective-permute-start.3 = (bf16[8,9472]{1,0:T(8,128)(2,1)}, bf16[8,9472]{1,0:T(8,128)(2,1)S(1)}, u32[]{:S(2)}, u32[]{:S(2)}) collective-permute-start(bf16[8,9472]{1,0:T(8,128)(2,1)} %get-tuple-element.31), channel_id=1, source_target_pairs={{0,8},{2,10},{4,12},{6,14},{8,0},{10,2},{12,4},{14,6},{1,9},{3,11}... | collective-permute-start | bytes 454664 | tf_op jit(solution)/shard_map/ppermute | solution.py:47
  18.1 3.4 %collective-permute-start.2 = (bf16[8,9472]{1,0:T(8,128)(2,1)S(1)}, bf16[8,9472]{1,0:T(8,128)(2,1)S(1)}, u32[]{:S(2)}, u32[]{:S(2)}) collective-permute-start(bf16[8,9472]{1,0:T(8,128)(2,1)S(1)} %collective-permute-done.1.refs_2_), channel_id=1, source_target_pairs={{0,2},{2,0},{4,6},{6,4},{8,10},{10,8},{12,14},{14,12},{1,3},{3,1},... | collective-permute-start | bytes 454664 | tf_op jit(solution)/shard_map/ppermute | solution.py:47
  21.5 0.0 collective-permute-done.5.refs_6_
  21.5 0.0 collective-permute-start.6
  21.6 4.2 %collective-permute-done.3.refs_4_ = bf16[8,9472]{1,0:T(8,128)(2,1)S(1)} collective-permute-done((bf16[8,9472]{1,0:T(8,128)(2,1)}, bf16[8,9472]{1,0:T(8,128)(2,1)S(1)}, u32[]{:S(2)}, u32[]{:S(2)}) %collective-permute-start.3) | collective-permute-done | bytes 151584 | tf_op jit(solution)/shard_map/ppermute | solution.py:47
  25.8 1.5 %collective-permute-start.4 = (bf16[8,9472]{1,0:T(8,128)(2,1)S(1)}, bf16[8,9472]{1,0:T(8,128)(2,1)S(1)}, u32[]{:S(2)}, u32[]{:S(2)}) collective-permute-start(bf16[8,9472]{1,0:T(8,128)(2,1)S(1)} %collective-permute-done.3.refs_4_), channel_id=1, source_target_pairs={{0,2},{2,0},{4,6},{6,4},{8,10},{10,8},{12,14},{14,12},{1,3},{3,1},... | collective-permute-start | bytes 454664 | tf_op jit(solution)/shard_map/ppermute | solution.py:47
  27.3 0.0 collective-permute-done.2.refs_3_
  27.3 0.0 collective-permute-done.6.refs_7_
  27.3 4.1 %collective-permute-done.4.refs_5_ = bf16[8,9472]{1,0:T(8,128)(2,1)S(1)} collective-permute-done((bf16[8,9472]{1,0:T(8,128)(2,1)S(1)}, bf16[8,9472]{1,0:T(8,128)(2,1)S(1)}, u32[]{:S(2)}, u32[]{:S(2)}) %collective-permute-start.4) | collective-permute-done | bytes 151584 | tf_op jit(solution)/shard_map/ppermute | solution.py:47
  31.4 0.0 copy-start
  31.4 0.0 copy-start.1
  31.4 0.0 collective-permute-start.8
  31.4 0.0 copy-start.3
  31.4 1.1 %copy-done.3 = bf16[8,9472]{1,0:T(8,128)(2,1)S(1)} copy-done((bf16[8,9472]{1,0:T(8,128)(2,1)S(1)}, bf16[8,9472]{1,0:T(8,128)(2,1)}, u32[]{:S(2)}) %copy-start.3) | copy-done | bytes 151576
  32.5 0.0 copy-start.4
  32.5 13.3 %project.1 = (f32[64,512]{1,0:T(8,128)S(1)}, f32[64,512]{1,0:T(8,128)S(1)}, f32[64,128]{1,0:T(8,128)S(1)}) custom-call(bf16[8,9472]{1,0:T(8,128)(2,1)S(1)} %copy-done.3, bf16[8,9472]{1,0:T(8,128)(2,1)S(1)} %collective-permute-done.refs_1_, bf16[8,9472]{1,0:T(8,128)(2,1)S(1)} %collective-permute-done.1.refs_2_, ...), custom_call_target="tpu_custom_call" | custom-call | flops 939524096 | bytes 15990784 | tf_op jit(solution)/shard_map/project/pallas_call | solution.py:301
  45.8 0.1 collective-permute-start.7
  45.9 1.3 %collective-permute-done.7 = f32[64,512]{1,0:T(8,128)S(1)} collective-permute-done((f32[64,512]{1,0:T(8,128)S(1)}, f32[64,512]{1,0:T(8,128)S(1)}, u32[]{:S(2)}, u32[]{:S(2)}) %collective-permute-start.7) | collective-permute-done | bytes 131104 | tf_op jit(solution)/shard_map/ppermute | solution.py:81
  47.2 0.0 collective-permute-done.8.refs_11_.packed_ref
  47.2 0.8 collective-permute-start.10
  48.0 1.5 %collective-permute-start.14 = (bf16[64,512]{1,0:T(8,128)(2,1)S(1)}, bf16[64,512]{1,0:T(8,128)(2,1)S(1)}, u32[]{:S(2)}, u32[]{:S(2)}) collective-permute-start(bf16[64,512]{1,0:T(8,128)(2,1)S(1)} %add_convert_fusion.refs_0_), channel_id=1, source_target_pairs={{0,12},{2,14},{4,8},{6,10},{8,4},{10,6},{12,0},{14,2},{1,13},{3,15... | collective-permute-start | bytes 196616 | tf_op jit(solution)/shard_map/ppermute | solution.py:47
  49.5 1.3 %collective-permute-start.12 = (bf16[64,512]{1,0:T(8,128)(2,1)S(1)}, bf16[64,512]{1,0:T(8,128)(2,1)S(1)}, u32[]{:S(2)}, u32[]{:S(2)}) collective-permute-start(bf16[64,512]{1,0:T(8,128)(2,1)S(1)} %add_convert_fusion.refs_0_), channel_id=1, source_target_pairs={{0,8},{2,10},{4,12},{6,14},{8,0},{10,2},{12,4},{14,6},{1,9},{3,11}... | collective-permute-start | bytes 196616 | tf_op jit(solution)/shard_map/ppermute | solution.py:47
  50.8 0.8 collective-permute-done.10.refs_2_
  51.6 1.1 %collective-permute-start.11 = (bf16[64,512]{1,0:T(8,128)(2,1)S(1)}, bf16[64,512]{1,0:T(8,128)(2,1)S(1)}, u32[]{:S(2)}, u32[]{:S(2)}) collective-permute-start(bf16[64,512]{1,0:T(8,128)(2,1)S(1)} %collective-permute-done.10.refs_2_), channel_id=1, source_target_pairs={{0,2},{2,0},{4,6},{6,4},{8,10},{10,8},{12,14},{14,12},{1,3},{3,1},... | collective-permute-start | bytes 196616 | tf_op jit(solution)/shard_map/ppermute | solution.py:47
  52.7 0.9 %collective-permute-start.9 = (bf16[64,512]{1,0:T(8,128)(2,1)S(1)}, bf16[64,512]{1,0:T(8,128)(2,1)S(1)}, u32[]{:S(2)}, u32[]{:S(2)}) collective-permute-start(bf16[64,512]{1,0:T(8,128)(2,1)S(1)} %add_convert_fusion.refs_0_), channel_id=1, source_target_pairs={{0,2},{2,0},{4,6},{6,4},{8,10},{10,8},{12,14},{14,12},{1,3},{3,1},... | collective-permute-start | bytes 196616 | tf_op jit(solution)/shard_map/ppermute | solution.py:47
  53.6 0.9 %collective-permute-done.14.refs_6_ = bf16[64,512]{1,0:T(8,128)(2,1)S(1)} collective-permute-done((bf16[64,512]{1,0:T(8,128)(2,1)S(1)}, bf16[64,512]{1,0:T(8,128)(2,1)S(1)}, u32[]{:S(2)}, u32[]{:S(2)}) %collective-permute-start.14) | collective-permute-done | bytes 65568 | tf_op jit(solution)/shard_map/ppermute | solution.py:47
  54.5 1.0 %collective-permute-start.15 = (bf16[64,512]{1,0:T(8,128)(2,1)S(1)}, bf16[64,512]{1,0:T(8,128)(2,1)S(1)}, u32[]{:S(2)}, u32[]{:S(2)}) collective-permute-start(bf16[64,512]{1,0:T(8,128)(2,1)S(1)} %collective-permute-done.14.refs_6_), channel_id=1, source_target_pairs={{0,2},{2,0},{4,6},{6,4},{8,10},{10,8},{12,14},{14,12},{1,3},{3,1},... | collective-permute-start | bytes 196616 | tf_op jit(solution)/shard_map/ppermute | solution.py:47
  55.5 1.7 %collective-permute-done.12.refs_4_ = bf16[64,512]{1,0:T(8,128)(2,1)S(1)} collective-permute-done((bf16[64,512]{1,0:T(8,128)(2,1)S(1)}, bf16[64,512]{1,0:T(8,128)(2,1)S(1)}, u32[]{:S(2)}, u32[]{:S(2)}) %collective-permute-start.12) | collective-permute-done | bytes 65568 | tf_op jit(solution)/shard_map/ppermute | solution.py:47
  57.2 0.0 collective-permute-done.11.refs_3_
  57.2 1.2 %collective-permute-start.13 = (bf16[64,512]{1,0:T(8,128)(2,1)S(1)}, bf16[64,512]{1,0:T(8,128)(2,1)S(1)}, u32[]{:S(2)}, u32[]{:S(2)}) collective-permute-start(bf16[64,512]{1,0:T(8,128)(2,1)S(1)} %collective-permute-done.12.refs_4_), channel_id=1, source_target_pairs={{0,2},{2,0},{4,6},{6,4},{8,10},{10,8},{12,14},{14,12},{1,3},{3,1},... | collective-permute-start | bytes 196616 | tf_op jit(solution)/shard_map/ppermute | solution.py:47
  58.4 0.0 collective-permute-done.9.refs_1_
  58.4 0.4 collective-permute-done.15.refs_7_
  58.8 2.7 %collective-permute-done.13.refs_5_ = bf16[64,512]{1,0:T(8,128)(2,1)S(1)} collective-permute-done((bf16[64,512]{1,0:T(8,128)(2,1)S(1)}, bf16[64,512]{1,0:T(8,128)(2,1)S(1)}, u32[]{:S(2)}, u32[]{:S(2)}) %collective-permute-start.13) | collective-permute-done | bytes 65568 | tf_op jit(solution)/shard_map/ppermute | solution.py:47
  61.4 0.0 copy-done
  61.4 0.0 copy-done.1
  61.4 0.0 copy-done.4
  61.5 0.0 copy-start.2
  61.5 1.6 %gate_up.1 = (f32[88,768]{1,0:T(8,128)S(1)}, f32[8,2048]{1,0:T(8,128)S(1)}) custom-call(bf16[64,512]{1,0:T(8,128)(2,1)S(1)} %add_convert_fusion.refs_0_, bf16[64,512]{1,0:T(8,128)(2,1)S(1)} %collective-permute-done.9.refs_1_, bf16[64,512]{1,0:T(8,128)(2,1)S(1)} %collective-permute-done.10.refs_2_, bf16[64,512]{1,0:T(8,128)(2,1)S(1)} %collective-permute-done.11.refs_3_, ...), custom_call_target="tpu_custom_call" | custom-call | tf_op jit(solution)/shard_map/gate_up/pallas_call | solution.py:363
  63.1 0.1 collective-permute-start.16
  63.2 1.5 %collective-permute-done.16.far_ref = f32[88,768]{1,0:T(8,128)S(1)} collective-permute-done((f32[88,768]{1,0:T(8,128)S(1)}, f32[88,768]{1,0:T(8,128)S(1)}, u32[]{:S(2)}, u32[]{:S(2)}) %collective-permute-start.16) | collective-permute-done | bytes 270368 | tf_op jit(solution)/shard_map/ppermute | solution.py:81
  64.7 0.0 copy-done.2
  64.7 0.9 %down.1 = (f32[8,3584]{1,0:T(8,128)S(1)}, bf16[8,3584]{1,0:T(8,128)(2,1)S(1)}, bf16[8,3584]{1,0:T(8,128)(2,1)S(1)}, bf16[8,3584]{1,0:T(8,128)(2,1)S(1)}, bf16[8,...) custom-call(f32[88,768]{1,0:T(8,128)S(1)} %get-tuple-element.41.sums, ...), custom_call_target="tpu_custom_call" | custom-call | tf_op jit(solution)/shard_map/down/pallas_call | solution.py:416
  65.6 1.9 %collective-permute-start.17 = (bf16[8,3584]{1,0:T(8,128)(2,1)S(1)}, bf16[8,3584]{1,0:T(8,128)(2,1)S(1)}, u32[]{:S(2)}, u32[]{:S(2)}) collective-permute-start(bf16[8,3584]{1,0:T(8,128)(2,1)S(1)} %get-tuple-element.43), channel_id=1, source_target_pairs={{0,12},{2,14},{4,8},{6,10},{8,4},{10,6},{12,0},{14,2},{1,13},{3,15... | collective-permute-start | bytes 172040 | tf_op jit(solution)/shard_map/ppermute | solution.py:47
  67.5 2.7 %collective-permute-start.18 = (bf16[8,3584]{1,0:T(8,128)(2,1)S(1)}, bf16[8,3584]{1,0:T(8,128)(2,1)S(1)}, u32[]{:S(2)}, u32[]{:S(2)}) collective-permute-start(bf16[8,3584]{1,0:T(8,128)(2,1)S(1)} %get-tuple-element.44), channel_id=1, source_target_pairs={{0,14},{2,12},{4,10},{6,8},{8,6},{10,4},{12,2},{14,0},{1,15},{3,13... | collective-permute-start | bytes 172040 | tf_op jit(solution)/shard_map/ppermute | solution.py:47
  70.2 0.0 collective-permute-start.19
  70.2 3.2 %collective-permute-start.20 = (bf16[8,3584]{1,0:T(8,128)(2,1)S(1)}, bf16[8,3584]{1,0:T(8,128)(2,1)S(1)}, u32[]{:S(2)}, u32[]{:S(2)}) collective-permute-start(bf16[8,3584]{1,0:T(8,128)(2,1)S(1)} %get-tuple-element.46), channel_id=1, source_target_pairs={{0,10},{2,8},{4,14},{6,12},{8,2},{10,0},{12,6},{14,4},{1,11},{3,9}... | collective-permute-start | bytes 172040 | tf_op jit(solution)/shard_map/ppermute | solution.py:47
  73.3 0.0 collective-permute-start.21
  73.3 0.0 collective-permute-done.17.rest_0_
  73.3 2.7 %collective-permute-start.22 = (bf16[8,3584]{1,0:T(8,128)(2,1)S(1)}, bf16[8,3584]{1,0:T(8,128)(2,1)S(1)}, u32[]{:S(2)}, u32[]{:S(2)}) collective-permute-start(bf16[8,3584]{1,0:T(8,128)(2,1)S(1)} %get-tuple-element.48), channel_id=1, source_target_pairs={{0,6},{2,4},{4,2},{6,0},{8,14},{10,12},{12,10},{14,8},{1,7},{3,5},... | collective-permute-start | bytes 172040 | tf_op jit(solution)/shard_map/ppermute | solution.py:47
  76.0 0.0 collective-permute-done.18.rest_1_
  76.0 0.8 collective-permute-start.23
  76.8 1.5 %collective-permute-done.19.rest_2_ = bf16[8,3584]{1,0:T(8,128)(2,1)S(1)} collective-permute-done((bf16[8,3584]{1,0:T(8,128)(2,1)S(1)}, bf16[8,3584]{1,0:T(8,128)(2,1)S(1)}, u32[]{:S(2)}, u32[]{:S(2)}) %collective-permute-start.19) | collective-permute-done | bytes 57376 | tf_op jit(solution)/shard_map/ppermute | solution.py:47
  78.3 1.3 %collective-permute-done.20.rest_3_ = bf16[8,3584]{1,0:T(8,128)(2,1)S(1)} collective-permute-done((bf16[8,3584]{1,0:T(8,128)(2,1)S(1)}, bf16[8,3584]{1,0:T(8,128)(2,1)S(1)}, u32[]{:S(2)}, u32[]{:S(2)}) %collective-permute-start.20) | collective-permute-done | bytes 57376 | tf_op jit(solution)/shard_map/ppermute | solution.py:47
  79.6 0.0 collective-permute-done.21.rest_4_
  79.6 0.9 %collective-permute-done.22.rest_5_ = bf16[8,3584]{1,0:T(8,128)(2,1)S(1)} collective-permute-done((bf16[8,3584]{1,0:T(8,128)(2,1)S(1)}, bf16[8,3584]{1,0:T(8,128)(2,1)S(1)}, u32[]{:S(2)}, u32[]{:S(2)}) %collective-permute-start.22) | collective-permute-done | bytes 57376 | tf_op jit(solution)/shard_map/ppermute | solution.py:47
  80.5 0.3 collective-permute-done.23.rest_6_
  80.8 0.7 finish.1
  (1 shorter events, 0.0 us)
Async XLA Ops:
  6.8 9.8 %collective-permute-start.1 = (bf16[8,9472]{1,0:T(8,128)(2,1)}, bf16[8,9472]{1,0:T(8,128)(2,1)S(1)}, u32[]{:S(2)}, u32[]{:S(2)}) collective-permute-start(bf16[8,9472]{1,0:T(8,128)(2,1)} %get-tuple-element.29), channel_id=1, source_target_pairs={{0,4},{2,6},{4,8},{6,10},{8,12},{10,14},{12,0},{14,2},{1,5},{3,7},... | collective-permute-start | bytes 454664 | tf_op jit(solution)/shard_map/ppermute | solution.py:47
  9.9 6.7 %collective-permute-start = (bf16[8,9472]{1,0:T(8,128)(2,1)}, bf16[8,9472]{1,0:T(8,128)(2,1)S(1)}, u32[]{:S(2)}, u32[]{:S(2)}) collective-permute-start(bf16[8,9472]{1,0:T(8,128)(2,1)} %get-tuple-element.28.refs_0_), channel_id=1, source_target_pairs={{0,2},{2,0},{4,6},{6,4},{8,10},{10,8},{12,14},{14,12},{1,3},{3,1},... | collective-permute-start | bytes 454664 | tf_op jit(solution)/shard_map/ppermute | solution.py:47
  11.4 10.2 %collective-permute-start.5 = (bf16[8,9472]{1,0:T(8,128)(2,1)}, bf16[8,9472]{1,0:T(8,128)(2,1)S(1)}, u32[]{:S(2)}, u32[]{:S(2)}) collective-permute-start(bf16[8,9472]{1,0:T(8,128)(2,1)} %get-tuple-element.32), channel_id=1, source_target_pairs={{0,12},{2,14},{4,0},{6,2},{8,4},{10,6},{12,8},{14,10},{1,13},{3,15... | collective-permute-start | bytes 454664 | tf_op jit(solution)/shard_map/ppermute | solution.py:47
  16.6 9.2 %collective-permute-start.3 = (bf16[8,9472]{1,0:T(8,128)(2,1)}, bf16[8,9472]{1,0:T(8,128)(2,1)S(1)}, u32[]{:S(2)}, u32[]{:S(2)}) collective-permute-start(bf16[8,9472]{1,0:T(8,128)(2,1)} %get-tuple-element.31), channel_id=1, source_target_pairs={{0,8},{2,10},{4,12},{6,14},{8,0},{10,2},{12,4},{14,6},{1,9},{3,11}... | collective-permute-start | bytes 454664 | tf_op jit(solution)/shard_map/ppermute | solution.py:47
  18.1 9.2 %collective-permute-start.2 = (bf16[8,9472]{1,0:T(8,128)(2,1)S(1)}, bf16[8,9472]{1,0:T(8,128)(2,1)S(1)}, u32[]{:S(2)}, u32[]{:S(2)}) collective-permute-start(bf16[8,9472]{1,0:T(8,128)(2,1)S(1)} %collective-permute-done.1.refs_2_), channel_id=1, source_target_pairs={{0,2},{2,0},{4,6},{6,4},{8,10},{10,8},{12,14},{14,12},{1,3},{3,1},... | collective-permute-start | bytes 454664 | tf_op jit(solution)/shard_map/ppermute | solution.py:47
  21.5 5.8 %collective-permute-start.6 = (bf16[8,9472]{1,0:T(8,128)(2,1)S(1)}, bf16[8,9472]{1,0:T(8,128)(2,1)S(1)}, u32[]{:S(2)}, u32[]{:S(2)}) collective-permute-start(bf16[8,9472]{1,0:T(8,128)(2,1)S(1)} %collective-permute-done.5.refs_6_), channel_id=1, source_target_pairs={{0,2},{2,0},{4,6},{6,4},{8,10},{10,8},{12,14},{14,12},{1,3},{3,1},... | collective-permute-start | bytes 454664 | tf_op jit(solution)/shard_map/ppermute | solution.py:47
  25.8 5.6 %collective-permute-start.4 = (bf16[8,9472]{1,0:T(8,128)(2,1)S(1)}, bf16[8,9472]{1,0:T(8,128)(2,1)S(1)}, u32[]{:S(2)}, u32[]{:S(2)}) collective-permute-start(bf16[8,9472]{1,0:T(8,128)(2,1)S(1)} %collective-permute-done.3.refs_4_), channel_id=1, source_target_pairs={{0,2},{2,0},{4,6},{6,4},{8,10},{10,8},{12,14},{14,12},{1,3},{3,1},... | collective-permute-start | bytes 454664 | tf_op jit(solution)/shard_map/ppermute | solution.py:47
  31.4 30.1 %copy-start = (bf16[7168,160]{0,1:T(8,128)(2,1)S(1)}, bf16[7168,160]{0,1:T(8,128)(2,1)}, u32[]{:S(2)}) copy-start(bf16[7168,160]{0,1:T(8,128)(2,1)} %param.21) | copy-start | bytes 6881284
  31.4 30.1 %copy-start.1 = (bf16[7168,160]{0,1:T(8,128)(2,1)S(1)}, bf16[7168,160]{0,1:T(8,128)(2,1)}, u32[]{:S(2)}) copy-start(bf16[7168,160]{0,1:T(8,128)(2,1)} %param.22) | copy-start | bytes 6881284
  31.4 15.8 %collective-permute-start.8 = (bf16[3680,512]{1,0:T(8,128)(2,1)}, bf16[3680,512]{1,0:T(8,128)(2,1)S(1)}, u32[]{:S(2)}, u32[]{:S(2)}) collective-permute-start(bf16[3680,512]{1,0:T(8,128)(2,1)} %get-tuple-element.36), channel_id=1, source_target_pairs={{0,1},{1,0},{2,3},{3,2},{4,5},{5,4},{6,7},{7,6},{8,9},{9,8},{10,11... | collective-permute-start | bytes 11304968 | tf_op jit(solution)/shard_map/ppermute | solution.py:81
  31.4 1.1 %copy-start.3 = (bf16[8,9472]{1,0:T(8,128)(2,1)S(1)}, bf16[8,9472]{1,0:T(8,128)(2,1)}, u32[]{:S(2)}) copy-start(bf16[8,9472]{1,0:T(8,128)(2,1)} %get-tuple-element.28.refs_0_) | copy-start | bytes 454660
  32.5 29.0 %copy-start.4 = (f32[7168]{0:T(1024)S(1)}, f32[7168]{0:T(1024)}, u32[]{:S(2)}) copy-start(f32[7168]{0:T(1024)} %param.18) | copy-start | bytes 86020
  45.8 1.4 %collective-permute-start.7 = (f32[64,512]{1,0:T(8,128)S(1)}, f32[64,512]{1,0:T(8,128)S(1)}, u32[]{:S(2)}, u32[]{:S(2)}) collective-permute-start(f32[64,512]{1,0:T(8,128)S(1)} %get-tuple-element.34), channel_id=1, source_target_pairs={{0,1},{1,0},{2,3},{3,2},{4,5},{5,4},{6,7},{7,6},{8,9},{9,8},{10,11... | collective-permute-start | bytes 393224 | tf_op jit(solution)/shard_map/ppermute | solution.py:81
  47.2 4.3 %collective-permute-start.10 = (bf16[64,512]{1,0:T(8,128)(2,1)S(1)}, bf16[64,512]{1,0:T(8,128)(2,1)S(1)}, u32[]{:S(2)}, u32[]{:S(2)}) collective-permute-start(bf16[64,512]{1,0:T(8,128)(2,1)S(1)} %add_convert_fusion.refs_0_), channel_id=1, source_target_pairs={{0,4},{2,6},{4,0},{6,2},{8,12},{10,14},{12,8},{14,10},{1,5},{3,7},... | collective-permute-start | bytes 196616 | tf_op jit(solution)/shard_map/ppermute | solution.py:47
  48.0 6.5 %collective-permute-start.14 = (bf16[64,512]{1,0:T(8,128)(2,1)S(1)}, bf16[64,512]{1,0:T(8,128)(2,1)S(1)}, u32[]{:S(2)}, u32[]{:S(2)}) collective-permute-start(bf16[64,512]{1,0:T(8,128)(2,1)S(1)} %add_convert_fusion.refs_0_), channel_id=1, source_target_pairs={{0,12},{2,14},{4,8},{6,10},{8,4},{10,6},{12,0},{14,2},{1,13},{3,15... | collective-permute-start | bytes 196616 | tf_op jit(solution)/shard_map/ppermute | solution.py:47
  49.5 7.7 %collective-permute-start.12 = (bf16[64,512]{1,0:T(8,128)(2,1)S(1)}, bf16[64,512]{1,0:T(8,128)(2,1)S(1)}, u32[]{:S(2)}, u32[]{:S(2)}) collective-permute-start(bf16[64,512]{1,0:T(8,128)(2,1)S(1)} %add_convert_fusion.refs_0_), channel_id=1, source_target_pairs={{0,8},{2,10},{4,12},{6,14},{8,0},{10,2},{12,4},{14,6},{1,9},{3,11}... | collective-permute-start | bytes 196616 | tf_op jit(solution)/shard_map/ppermute | solution.py:47
  51.6 5.6 %collective-permute-start.11 = (bf16[64,512]{1,0:T(8,128)(2,1)S(1)}, bf16[64,512]{1,0:T(8,128)(2,1)S(1)}, u32[]{:S(2)}, u32[]{:S(2)}) collective-permute-start(bf16[64,512]{1,0:T(8,128)(2,1)S(1)} %collective-permute-done.10.refs_2_), channel_id=1, source_target_pairs={{0,2},{2,0},{4,6},{6,4},{8,10},{10,8},{12,14},{14,12},{1,3},{3,1},... | collective-permute-start | bytes 196616 | tf_op jit(solution)/shard_map/ppermute | solution.py:47
  52.7 5.7 %collective-permute-start.9 = (bf16[64,512]{1,0:T(8,128)(2,1)S(1)}, bf16[64,512]{1,0:T(8,128)(2,1)S(1)}, u32[]{:S(2)}, u32[]{:S(2)}) collective-permute-start(bf16[64,512]{1,0:T(8,128)(2,1)S(1)} %add_convert_fusion.refs_0_), channel_id=1, source_target_pairs={{0,2},{2,0},{4,6},{6,4},{8,10},{10,8},{12,14},{14,12},{1,3},{3,1},... | collective-permute-start | bytes 196616 | tf_op jit(solution)/shard_map/ppermute | solution.py:47
  54.5 4.3 %collective-permute-start.15 = (bf16[64,512]{1,0:T(8,128)(2,1)S(1)}, bf16[64,512]{1,0:T(8,128)(2,1)S(1)}, u32[]{:S(2)}, u32[]{:S(2)}) collective-permute-start(bf16[64,512]{1,0:T(8,128)(2,1)S(1)} %collective-permute-done.14.refs_6_), channel_id=1, source_target_pairs={{0,2},{2,0},{4,6},{6,4},{8,10},{10,8},{12,14},{14,12},{1,3},{3,1},... | collective-permute-start | bytes 196616 | tf_op jit(solution)/shard_map/ppermute | solution.py:47
  57.2 4.3 %collective-permute-start.13 = (bf16[64,512]{1,0:T(8,128)(2,1)S(1)}, bf16[64,512]{1,0:T(8,128)(2,1)S(1)}, u32[]{:S(2)}, u32[]{:S(2)}) collective-permute-start(bf16[64,512]{1,0:T(8,128)(2,1)S(1)} %collective-permute-done.12.refs_4_), channel_id=1, source_target_pairs={{0,2},{2,0},{4,6},{6,4},{8,10},{10,8},{12,14},{14,12},{1,3},{3,1},... | collective-permute-start | bytes 196616 | tf_op jit(solution)/shard_map/ppermute | solution.py:47
  61.5 3.3 %copy-start.2 = (bf16[160,7168]{1,0:T(8,128)(2,1)S(1)}, bf16[160,7168]{1,0:T(8,128)(2,1)}, u32[]{:S(2)}) copy-start(bf16[160,7168]{1,0:T(8,128)(2,1)} %down_ref.1) | copy-start | bytes 6881284
  63.1 1.6 %collective-permute-start.16 = (f32[88,768]{1,0:T(8,128)S(1)}, f32[88,768]{1,0:T(8,128)S(1)}, u32[]{:S(2)}, u32[]{:S(2)}) collective-permute-start(f32[88,768]{1,0:T(8,128)S(1)} %get-tuple-element.41.sums_ref), channel_id=1, source_target_pairs={{0,1},{1,0},{2,3},{3,2},{4,5},{5,4},{6,7},{7,6},{8,9},{9,8},{10,11... | collective-permute-start | bytes 811016 | tf_op jit(solution)/shard_map/ppermute | solution.py:81
  65.6 7.7 %collective-permute-start.17 = (bf16[8,3584]{1,0:T(8,128)(2,1)S(1)}, bf16[8,3584]{1,0:T(8,128)(2,1)S(1)}, u32[]{:S(2)}, u32[]{:S(2)}) collective-permute-start(bf16[8,3584]{1,0:T(8,128)(2,1)S(1)} %get-tuple-element.43), channel_id=1, source_target_pairs={{0,12},{2,14},{4,8},{6,10},{8,4},{10,6},{12,0},{14,2},{1,13},{3,15... | collective-permute-start | bytes 172040 | tf_op jit(solution)/shard_map/ppermute | solution.py:47
  67.5 8.5 %collective-permute-start.18 = (bf16[8,3584]{1,0:T(8,128)(2,1)S(1)}, bf16[8,3584]{1,0:T(8,128)(2,1)S(1)}, u32[]{:S(2)}, u32[]{:S(2)}) collective-permute-start(bf16[8,3584]{1,0:T(8,128)(2,1)S(1)} %get-tuple-element.44), channel_id=1, source_target_pairs={{0,14},{2,12},{4,10},{6,8},{8,6},{10,4},{12,2},{14,0},{1,15},{3,13... | collective-permute-start | bytes 172040 | tf_op jit(solution)/shard_map/ppermute | solution.py:47
  70.2 8.1 %collective-permute-start.19 = (bf16[8,3584]{1,0:T(8,128)(2,1)S(1)}, bf16[8,3584]{1,0:T(8,128)(2,1)S(1)}, u32[]{:S(2)}, u32[]{:S(2)}) collective-permute-start(bf16[8,3584]{1,0:T(8,128)(2,1)S(1)} %get-tuple-element.45), channel_id=1, source_target_pairs={{0,8},{2,10},{4,12},{6,14},{8,0},{10,2},{12,4},{14,6},{1,9},{3,11}... | collective-permute-start | bytes 172040 | tf_op jit(solution)/shard_map/ppermute | solution.py:47
  70.2 9.5 %collective-permute-start.20 = (bf16[8,3584]{1,0:T(8,128)(2,1)S(1)}, bf16[8,3584]{1,0:T(8,128)(2,1)S(1)}, u32[]{:S(2)}, u32[]{:S(2)}) collective-permute-start(bf16[8,3584]{1,0:T(8,128)(2,1)S(1)} %get-tuple-element.46), channel_id=1, source_target_pairs={{0,10},{2,8},{4,14},{6,12},{8,2},{10,0},{12,6},{14,4},{1,11},{3,9}... | collective-permute-start | bytes 172040 | tf_op jit(solution)/shard_map/ppermute | solution.py:47
  73.3 6.3 %collective-permute-start.21 = (bf16[8,3584]{1,0:T(8,128)(2,1)S(1)}, bf16[8,3584]{1,0:T(8,128)(2,1)S(1)}, u32[]{:S(2)}, u32[]{:S(2)}) collective-permute-start(bf16[8,3584]{1,0:T(8,128)(2,1)S(1)} %get-tuple-element.47), channel_id=1, source_target_pairs={{0,4},{2,6},{4,0},{6,2},{8,12},{10,14},{12,8},{14,10},{1,5},{3,7},... | collective-permute-start | bytes 172040 | tf_op jit(solution)/shard_map/ppermute | solution.py:47
  73.3 7.2 %collective-permute-start.22 = (bf16[8,3584]{1,0:T(8,128)(2,1)S(1)}, bf16[8,3584]{1,0:T(8,128)(2,1)S(1)}, u32[]{:S(2)}, u32[]{:S(2)}) collective-permute-start(bf16[8,3584]{1,0:T(8,128)(2,1)S(1)} %get-tuple-element.48), channel_id=1, source_target_pairs={{0,6},{2,4},{4,2},{6,0},{8,14},{10,12},{12,10},{14,8},{1,7},{3,5},... | collective-permute-start | bytes 172040 | tf_op jit(solution)/shard_map/ppermute | solution.py:47
  76.0 4.8 %collective-permute-start.23 = (bf16[8,3584]{1,0:T(8,128)(2,1)S(1)}, bf16[8,3584]{1,0:T(8,128)(2,1)S(1)}, u32[]{:S(2)}, u32[]{:S(2)}) collective-permute-start(bf16[8,3584]{1,0:T(8,128)(2,1)S(1)} %get-tuple-element.49), channel_id=1, source_target_pairs={{0,2},{2,0},{4,6},{6,4},{8,10},{10,8},{12,14},{14,12},{1,3},{3,1},... | collective-permute-start | bytes 172040 | tf_op jit(solution)/shard_map/ppermute | solution.py:47
